TPU v7x, 128 devices: a whole 4x4x4 slice. The times are simulated.
128 devices in a mesh: section: 2 (over core), dp: 8 (over z, y_lo), tensor: 8 (over y_hi, x).
Axes of the slice: x: 4, y: 4 (y_hi: 2, y_lo: 2; y = y_hi * 2 + y_lo), z: 4, core: 2. Of those that a mesh axis runs over, the one named last changes fastest.
Arguments:
- inputs: bfloat16 [2, 1, 1024, 1024], P(None, None, 'dp'), may hold values from -6 to 6
- cotangent: bfloat16 [2, 1, 1024, 1024], P(None, None, 'dp'), may hold values from -6 to 6
- query_key_value_weight: bfloat16 [2, 1024, 3, 1024], P('section', 'dp', None, 'tensor'), may hold values from -0.1875 to 0.1875
- attention_out_weight: bfloat16 [2, 1024, 1024], P('section', 'tensor', 'dp'), may hold values from -0.5 to 0.5
- up_weight: bfloat16 [2, 1024, 4096], P('section', 'dp', 'tensor'), may hold values from -0.1875 to 0.1875
- down_weight: bfloat16 [2, 4096, 1024], P('section', 'tensor', 'dp'), may hold values from -0.09375 to 0.09375
- ln_gain: bfloat16 [2, 2, 1024], P('section', None, 'dp'), may hold values from 0.099609375 to 1.8984375
- ln_bias: bfloat16 [2, 2, 1024], P('section', None, 'dp'), may hold values from -3 to 3
- in_bias: bfloat16 [2, 2, 1024], P('section', None, 'tensor'), may hold values from -3 to 3
- output_biases: bfloat16 [2, 2, 1024], P('section', None, 'dp'), may hold values from -3 to 3
- expand_bias: bfloat16 [2, 4096], P('section', 'tensor'), may hold values from -3 to 3
Outputs:
- activations: bfloat16 [2, 2, 1, 1024, 1024], P('section', None, None, 'dp')
- input_grads: bfloat16 [2, 2, 1, 1024, 1024], P('section', None, None, 'dp')
- grad_qkv: float32 [2, 1024, 3, 1024], P('section', 'dp', None, 'tensor')
- grad_out: float32 [2, 1024, 1024], P('section', 'tensor', 'dp')
- grad_up: float32 [2, 1024, 4096], P('section', 'dp', 'tensor')
- grad_down: float32 [2, 4096, 1024], P('section', 'tensor', 'dp')
- grad_ln_gain: float32 [2, 2, 1024], P('section', None, 'dp')
- grad_ln_bias: float32 [2, 2, 1024], P('section', None, 'dp')
- grad_in_bias: float32 [2, 2, 1024], P('section', None, 'tensor')
- grad_out_bias: float32 [2, 2, 1024], P('section', None, 'dp')
- grad_up_bias: float32 [2, 4096], P('section', 'tensor')
All inputs are finite; a program needn't handle non-finite values.
Results may differ from a plain program's by a relative error of at most 0.02.
Values may be sent and summed in bfloat16 or wider, within the bound.
No kernel may reach another device: no remote copies, remote signals or barrier semaphores. Data moves between devices by JAX's collectives and lax.ppermute only.
A program may use at most 128 MiB of HBM per device.

v0:
```python
import math

import jax
import jax.numpy as jnp
from jax import lax
from jax.sharding import PartitionSpec as P

HD = 64


EPSILON = 1e-05
MASKED = -1e30


def in_blocks(shard, dim, length):
    shape = shard.shape
    pieces = shard.reshape(*shape[:dim], length, shape[dim] // length, *shape[dim + 1 :])
    return jnp.moveaxis(pieces, dim, 0)


def sum_at_owner(shard, axis, dim):
    length = lax.axis_size(axis)
    pieces = lax.all_to_all(in_blocks(shard, dim, length), axis, 0, 0, tiled=True)
    return jnp.sum(pieces.astype(jnp.float32), axis=0)


def copy_for_each(shard, axis):
    copies = jnp.broadcast_to(shard, (lax.axis_size(axis), *shard.shape))
    return lax.all_to_all(copies, axis, split_axis=0, concat_axis=0, tiled=True)


def in_order(pieces, dim):
    shape = list(pieces.shape[1:])
    shape[dim] *= pieces.shape[0]
    return jnp.moveaxis(pieces, 0, dim).reshape(shape)


def gathered_copies(shard, axis, dim):
    pieces = copy_for_each(shard, axis)
    return in_order(pieces, dim)


def in_one_piece(arrays, axis, dim, along):
    widths = [a.shape[along] for a in arrays]
    both = jnp.concatenate(arrays, axis=along)
    filled = lax.all_gather(both, axis, axis=dim, tiled=True)
    return tuple(jnp.split(filled, [sum(widths[:k]) for k in range(1, len(widths))], axis=along))


def in_one_piece_2(arrays, axis, dim, along):
    ends, at = ([], 0)
    for a in arrays[:-1]:
        at += a.shape[along]
        ends.append(at)
    both = jnp.concatenate(arrays, axis=along)
    return tuple(jnp.split(sum_at_owner(both, axis, dim), ends, axis=along))


def turned_gather(arrays, axis, dims):
    turned = [jnp.moveaxis(a, dim, 0) for a, dim in zip(arrays, dims)]
    widths = [t[0].size for t in turned]
    both = jnp.concatenate([t.reshape(-1, w) for t, w in zip(turned, widths)], axis=1)
    filled = lax.all_gather(both, axis, axis=0, tiled=True)
    pieces = jnp.split(filled, [sum(widths[:k]) for k in range(1, len(widths))], axis=1)
    return tuple(
        (
            jnp.moveaxis(b.reshape(-1, *t.shape[1:]), 0, dim)
            for b, t, dim in zip(pieces, turned, dims)
        )
    )


def from_behind(value, axis, steps):
    count = lax.axis_size(axis)
    first, last = (max(0, -steps), min(count, count - steps))
    return lax.ppermute(value, axis, [(source, source + steps) for source in range(first, last)])


def of_everyone(shard, axis):
    return copy_for_each(shard, axis).sum(axis=0)


def together(arrays, axis):
    line, at, gathered = (jnp.concatenate([a.reshape(-1) for a in arrays]), 0, [])
    subtotal = of_everyone(line, axis)
    for a in arrays:
        gathered.append(subtotal[at : at + a.size].reshape(a.shape))
        at += a.size
    return tuple(gathered)


def side_by_side(arrays, axis, dim, along):
    ends, at = ([], 0)
    for a in arrays[:-1]:
        at += a.shape[along]
        ends.append(at)
    both = jnp.concatenate(arrays, axis=along)
    return tuple(
        jnp.split(lax.psum_scatter(both, axis, scatter_dimension=dim, tiled=True), ends, axis=along)
    )


def layer_norm(layer_entry, norm_gain, norm_shift):
    row_mean = jnp.mean(layer_entry, axis=-1, keepdims=True)
    centred = layer_entry - row_mean
    variance = jnp.mean(centred * centred, axis=-1, keepdims=True)
    return centred * lax.rsqrt(variance + EPSILON) * norm_gain + norm_shift


def gelu_tanh(argument):
    return (
        0.5
        * argument
        * (
            1.0
            + jnp.tanh(0.7978845608028654 * (argument + 0.044715 * argument * argument * argument))
        )
    )


def row_share(partial_value):
    return sum_at_owner(partial_value.astype(jnp.bfloat16), "tensor", 1)


def row_join(rows):
    return gathered_copies(rows, "tensor", 1)


def own_rows(full_rows):
    share = full_rows.shape[1] // lax.axis_size("tensor")
    return lax.dynamic_slice_in_dim(full_rows, lax.axis_index("tensor") * share, share, 1)


def causal_scores(queries, all_keys):
    seq_count, block_len, feature_cols = queries.shape
    length = all_keys.shape[1]
    head_count = feature_cols // HD
    query_heads = queries.reshape(seq_count, block_len, head_count, HD)
    key_heads = all_keys.reshape(seq_count, length, head_count, HD)
    raw_scores = jnp.einsum(
        "sqhe,skhe->shqk", query_heads, key_heads, preferred_element_type=jnp.float32
    ) * (1.0 / math.sqrt(HD))
    query_pos = lax.axis_index("dp") * block_len + lax.broadcasted_iota(
        jnp.int32, (block_len, length), 0
    )
    key_pos = lax.broadcasted_iota(jnp.int32, (block_len, length), 1)
    return jnp.where((key_pos <= query_pos)[None, None], raw_scores, MASKED)


def layer_forward(layer_entry, weights, bias_inner, bias_upper):
    mat_qkv, mat_out, mat_up, mat_down, norm_gains, norm_shifts, bias_outer = weights
    gains_float = norm_gains.astype(jnp.float32)
    shifts_float = norm_shifts.astype(jnp.float32)
    outer_float = bias_outer.astype(jnp.float32)
    inner_float = bias_inner.astype(jnp.float32)
    first_normalized = layer_norm(layer_entry, gains_float[0], shifts_float[0]).astype(jnp.bfloat16)
    projected_rows = jnp.einsum(
        "scd,dje->scje", first_normalized, mat_qkv, preferred_element_type=jnp.float32
    )
    queries = (projected_rows[:, :, 0] + inner_float[0]).astype(jnp.bfloat16)
    key_rows = projected_rows[:, :, 1].astype(jnp.bfloat16)
    value_rows = (projected_rows[:, :, 2] + inner_float[1]).astype(jnp.bfloat16)
    all_keys, all_values = in_one_piece((key_rows, value_rows), "dp", 1, 0)
    seq_count, block_len, feature_cols = queries.shape
    length = all_keys.shape[1]
    head_count = feature_cols // HD
    scores = causal_scores(queries, all_keys)
    row_max = jnp.max(scores, axis=-1, keepdims=True)
    exponent = jnp.exp(scores - row_max)
    row_total = jnp.sum(exponent, axis=-1, keepdims=True)
    probability = (exponent / row_total).astype(jnp.bfloat16)
    log_total = row_max + jnp.log(row_total)
    value_heads = all_values.reshape(seq_count, length, head_count, HD)
    mixture = jnp.einsum(
        "shqk,skhe->sqhe", probability, value_heads, preferred_element_type=jnp.float32
    )
    attention_result = mixture.reshape(seq_count, block_len, feature_cols).astype(jnp.bfloat16)
    branch_part = jnp.einsum(
        "sce,ed->scd", attention_result, mat_out, preferred_element_type=jnp.float32
    )
    residual_middle = own_rows(layer_entry) + (row_share(branch_part) + outer_float[0])
    second_normalized = row_join(
        layer_norm(residual_middle, gains_float[1], shifts_float[1]).astype(jnp.bfloat16)
    )
    hidden_preactivation = jnp.einsum(
        "scd,df->scf", second_normalized, mat_up, preferred_element_type=jnp.float32
    ) + bias_upper.astype(jnp.float32)
    activated_hidden = gelu_tanh(hidden_preactivation).astype(jnp.bfloat16)
    feed_part = jnp.einsum(
        "scf,fd->scd", activated_hidden, mat_down, preferred_element_type=jnp.float32
    )
    layer_result = row_join(
        (residual_middle + (row_share(feed_part) + outer_float[1])).astype(jnp.bfloat16)
    )
    saved_state = (
        layer_entry,
        first_normalized,
        queries,
        all_keys,
        all_values,
        log_total,
        attention_result,
        residual_middle,
        second_normalized,
        hidden_preactivation,
        activated_hidden,
    )
    return (layer_result, saved_state)


def layer_backward(grad_output, saved_state, weights):
    mat_qkv, mat_out, mat_up, mat_down, norm_gains, norm_shifts, bias_outer = weights
    (
        layer_entry,
        first_normalized,
        queries,
        all_keys,
        all_values,
        log_total,
        attention_result,
        residual_middle,
        second_normalized,
        hidden_preactivation,
        activated_hidden,
    ) = saved_state
    gains_float = norm_gains.astype(jnp.float32)
    shifts_float = norm_shifts.astype(jnp.float32)
    seq_count, block_len, feature_cols = queries.shape
    length = all_keys.shape[1]
    head_count = feature_cols // HD
    score_scale = 1.0 / math.sqrt(HD)
    output_low = grad_output.astype(jnp.bfloat16)
    grad_down = jnp.einsum(
        "scf,scd->fd", activated_hidden, output_low, preferred_element_type=jnp.float32
    )
    grad_bias_two = jnp.sum(grad_output, axis=(0, 1))
    grad_active = jnp.einsum(
        "scd,fd->scf", output_low, mat_down, preferred_element_type=jnp.float32
    )
    unused_value, gelu_back = jax.vjp(gelu_tanh, hidden_preactivation)
    grad_pre = gelu_back(grad_active)[0].astype(jnp.bfloat16)
    grad_upbias = jnp.sum(grad_pre.astype(jnp.float32), axis=(0, 1))
    grad_up = jnp.einsum(
        "scd,scf->df", second_normalized, grad_pre, preferred_element_type=jnp.float32
    )
    normed_two_part = jnp.einsum(
        "scf,df->scd", grad_pre, mat_up, preferred_element_type=jnp.float32
    )
    grad_normed_two = row_share(normed_two_part)
    unused_norm, norm_back_two = jax.vjp(
        layer_norm, residual_middle, gains_float[1], shifts_float[1]
    )
    grad_from_norm, grad_gain_two, grad_shift_two = norm_back_two(grad_normed_two)
    grad_middle = own_rows(grad_output) + grad_from_norm
    branch_grad = row_join(grad_middle.astype(jnp.bfloat16))
    grad_bias_one = jnp.sum(branch_grad.astype(jnp.float32), axis=(0, 1))
    grad_wout = jnp.einsum(
        "sce,scd->ed", attention_result, branch_grad, preferred_element_type=jnp.float32
    )
    grad_attended = jnp.einsum(
        "scd,ed->sce", branch_grad, mat_out, preferred_element_type=jnp.float32
    ).astype(jnp.bfloat16)
    scores = causal_scores(queries, all_keys)
    soft_probs = jnp.exp(scores - log_total)
    attended_heads = grad_attended.reshape(seq_count, block_len, head_count, HD)
    value_heads = all_values.reshape(seq_count, length, head_count, HD)
    key_heads = all_keys.reshape(seq_count, length, head_count, HD)
    query_heads = queries.reshape(seq_count, block_len, head_count, HD)
    grad_prob = jnp.einsum(
        "sqhe,skhe->shqk", attended_heads, value_heads, preferred_element_type=jnp.float32
    )
    grad_values_all = jnp.einsum(
        "shqk,sqhe->skhe",
        soft_probs.astype(jnp.bfloat16),
        attended_heads,
        preferred_element_type=jnp.float32,
    ).reshape(seq_count, length, feature_cols)
    row_inner = jnp.sum(soft_probs * grad_prob, axis=-1, keepdims=True)
    grad_scores = (soft_probs * (grad_prob - row_inner)).astype(jnp.bfloat16)
    grad_queries = (
        (
            jnp.einsum(
                "shqk,skhe->sqhe", grad_scores, key_heads, preferred_element_type=jnp.float32
            )
            * score_scale
        )
        .reshape(seq_count, block_len, feature_cols)
        .astype(jnp.bfloat16)
    )
    grad_keys_all = (
        jnp.einsum(
            "shqk,sqhe->skhe", grad_scores, query_heads, preferred_element_type=jnp.float32
        ).reshape(seq_count, length, feature_cols)
        * score_scale
    )
    grad_keys, grad_values = in_one_piece_2(
        (grad_keys_all.astype(jnp.bfloat16), grad_values_all.astype(jnp.bfloat16)), "dp", 1, 0
    )
    grad_keys = grad_keys.astype(jnp.bfloat16)
    grad_values = grad_values.astype(jnp.bfloat16)
    grad_proj = jnp.stack((grad_queries, grad_keys, grad_values), axis=2)
    grad_qkv = jnp.einsum(
        "scd,scje->dje", first_normalized, grad_proj, preferred_element_type=jnp.float32
    )
    grad_inbias = jnp.stack(
        (
            jnp.sum(grad_queries.astype(jnp.float32), axis=(0, 1)),
            jnp.sum(grad_values.astype(jnp.float32), axis=(0, 1)),
        )
    )
    normed_part = jnp.einsum(
        "scje,dje->scd", grad_proj, mat_qkv, preferred_element_type=jnp.float32
    )
    grad_normed = row_share(normed_part)
    unused_first, norm_back_one = jax.vjp(
        layer_norm, own_rows(layer_entry), gains_float[0], shifts_float[0]
    )
    grad_from_first, grad_gain_one, grad_shift_one = norm_back_one(grad_normed)
    grad_input = row_join((grad_middle + grad_from_first).astype(jnp.bfloat16))
    weight_grads = (
        grad_qkv,
        grad_wout,
        grad_up,
        grad_down,
        jnp.stack((grad_gain_one, grad_gain_two)),
        jnp.stack((grad_shift_one, grad_shift_two)),
        jnp.stack((grad_bias_one, grad_bias_two)),
    )
    return (grad_input, weight_grads, (grad_inbias, grad_upbias))


def local(
    inputs,
    cotangent,
    query_key_value_weight,
    attention_out_weight,
    up_weight,
    down_weight,
    ln_gain,
    ln_bias,
    in_bias,
    output_biases,
    expand_bias,
):
    micro_count = inputs.shape[0]
    on_first = lax.axis_index("section") == 0
    gathered = turned_gather(
        (
            query_key_value_weight,
            attention_out_weight,
            up_weight,
            down_weight,
            ln_gain,
            ln_bias,
            output_biases,
        ),
        "dp",
        (1, 2, 1, 2, 2, 2, 2),
    )
    forward_weights = tuple((piece[0] for piece in gathered))
    bias_inner = in_bias[0]
    bias_upper = expand_bias[0]
    received = jnp.zeros(inputs.shape[1:], jnp.bfloat16)
    section_outputs = []
    saved_states = []
    for tick_index in range(micro_count + 1):
        own_input = inputs[min(tick_index, micro_count - 1)]
        layer_entry = jnp.where(on_first, own_input, received).astype(jnp.float32)
        layer_output, saved_state = layer_forward(
            layer_entry, forward_weights, bias_inner, bias_upper
        )
        section_outputs.append(layer_output)
        saved_states.append(saved_state)
        if tick_index < micro_count:
            received = from_behind(layer_output, "section", 1)
    activations = jnp.stack(
        [
            jnp.where(on_first, section_outputs[micro_index], section_outputs[micro_index + 1])
            for micro_index in range(micro_count)
        ]
    )
    regathered = turned_gather(
        (
            query_key_value_weight,
            attention_out_weight,
            up_weight,
            down_weight,
            ln_gain,
            ln_bias,
            output_biases,
        ),
        "dp",
        (1, 2, 1, 2, 2, 2, 2),
    )
    backward_weights = tuple((piece[0] for piece in regathered))
    received_grad = jnp.zeros(cotangent.shape[1:], jnp.bfloat16)
    input_grad_list = []
    grad_sums = None
    small_sums = None
    for tick_index in range(micro_count + 1):
        own_grad = cotangent[min(tick_index, micro_count - 1)]
        grad_output = jnp.where(on_first, received_grad, own_grad).astype(jnp.float32)
        saved_state = jax.tree.map(
            lambda early_part, late_part: jnp.where(on_first, early_part, late_part),
            saved_states[max(tick_index - 1, 0)],
            saved_states[min(tick_index + 1, micro_count)],
        )
        live_weight = jnp.where(
            on_first, 1.0 if tick_index >= 1 else 0.0, 1.0 if tick_index < micro_count else 0.0
        ).astype(jnp.float32)
        grad_input, weight_grads, small_grads = layer_backward(
            grad_output, saved_state, backward_weights
        )
        weight_grads = jax.tree.map(lambda grad_term: grad_term * live_weight, weight_grads)
        small_grads = jax.tree.map(lambda grad_term: grad_term * live_weight, small_grads)
        if grad_sums is None:
            grad_sums = weight_grads
            small_sums = small_grads
        else:
            grad_sums = jax.tree.map(lambda summed, added: summed + added, grad_sums, weight_grads)
            small_sums = jax.tree.map(lambda summed, added: summed + added, small_sums, small_grads)
        input_grad_list.append(grad_input)
        if tick_index < micro_count:
            received_grad = from_behind(grad_input, "section", -1)
    input_grads = jnp.stack(
        [
            jnp.where(on_first, input_grad_list[micro_index + 1], input_grad_list[micro_index])
            for micro_index in range(micro_count)
        ]
    )
    gain_total, shift_total = together((grad_sums[4], grad_sums[5]), "tensor")
    grad_sums = (
        grad_sums[0],
        grad_sums[1],
        grad_sums[2],
        grad_sums[3],
        gain_total,
        shift_total,
        grad_sums[6],
    )
    shards = (
        lax.psum_scatter(
            grad_sums[0].astype(jnp.bfloat16), "dp", scatter_dimension=0, tiled=True
        ).astype(jnp.float32),
        lax.psum_scatter(
            grad_sums[1].astype(jnp.bfloat16), "dp", scatter_dimension=1, tiled=True
        ).astype(jnp.float32),
        lax.psum_scatter(
            grad_sums[2].astype(jnp.bfloat16), "dp", scatter_dimension=0, tiled=True
        ).astype(jnp.float32),
        *tuple(
            (
                part.astype(jnp.float32)
                for part in side_by_side(
                    (
                        grad_sums[3].astype(jnp.bfloat16),
                        grad_sums[4].astype(jnp.bfloat16),
                        grad_sums[5].astype(jnp.bfloat16),
                        grad_sums[6].astype(jnp.bfloat16),
                    ),
                    "dp",
                    1,
                    0,
                )
            )
        ),
    )
    small_totals = jax.tree.map(lambda part: of_everyone(part, "dp"), small_sums)
    return (
        activations[None],
        input_grads[None],
        shards[0][None],
        shards[1][None],
        shards[2][None],
        shards[3][None],
        shards[4][None],
        shards[5][None],
        small_totals[0][None],
        shards[6][None],
        small_totals[1][None],
    )


def solution(mesh):
    return jax.shard_map(
        local,
        mesh=mesh,
        in_specs=(
            P(None, None, "dp", None),
            P(None, None, "dp", None),
            P("section", "dp", None, "tensor"),
            P("section", "tensor", "dp"),
            P("section", "dp", "tensor"),
            P("section", "tensor", "dp"),
            P("section", None, "dp"),
            P("section", None, "dp"),
            P("section", None, "tensor"),
            P("section", None, "dp"),
            P("section", "tensor"),
        ),
        out_specs=(
            P("section", None, None, "dp", None),
            P("section", None, None, "dp", None),
            P("section", "dp", None, "tensor"),
            P("section", "tensor", "dp"),
            P("section", "dp", "tensor"),
            P("section", "tensor", "dp"),
            P("section", None, "dp"),
            P("section", None, "dp"),
            P("section", None, "tensor"),
            P("section", None, "dp"),
            P("section", "tensor"),
        ),
        check_vma=False,
    )
```

profile of v0, /device:TPU:1, one launch (start us, length us, event | category | flops | bytes accessed | tf_op | source)
XLA Modules:
  0.0 736.8 jit_solution(13458962859753043575)
XLA Ops:
  9.3 5.6 concatenate.31
  17.2 71.2 %all-gather.2.cloned.1.call-done = bf16[1024,1542]{0,1:T(8,128)(2,1)} async-done(((bf16[128,1542]{0,1:T(8,128)(2,1)}), bf16[1024,1542]{0,1:T(8,128)(2,1)}) %all-gather.2.cloned.1.call-update) | async-done | bytes 3158032 | tf_op jit(solution)/shard_map/all_gather | solution.py:63
  91.0 22.3 %all_gather.14 = bf16[2,1024,128]{1,2,0:T(8,128)(2,1)S(1)} all-gather(bf16[2,128,128]{1,2,0:T(8,128)(2,1)S(1)} %pad_maximum_fusion.1), channel_id=1, replica_groups=mesh['section'=2,'dp'=8,'tensor'=8] {'dp'}, dimensions={1}, use_global_device_ids=true | all-gather | bytes 589824 | tf_op jit(solution)/shard_map/all_gather | solution.py:46
  116.7 6.1 all-to-all-start
  123.7 6.8 all-to-all-done
  131.7 3.4 all-to-all-start.1
  135.1 7.5 %all-to-all-done.1 = bf16[8,1,16,1024]{3,2,1,0:T(8,128)(2,1)S(1)} async-done(((bf16[8,1,16,1024]{3,2,1,0:T(8,128)(2,1)}), bf16[8,1,16,1024]{3,2,1,0:T(8,128)(2,1)S(1)}, u32[]{:S(2)}, u32[]{:S(2)}) %all-to-all-start.1) | async-done | bytes 262176 | tf_op jit(solution)/shard_map/all_to_all | solution.py:29
  146.2 10.1 %all_to_all.152 = bf16[8,1,16,1024]{3,2,1,0:T(8,128)(2,1)S(1)} all-to-all(bf16[8,1,16,1024]{3,2,1,0:T(8,128)(2,1)S(1)} %bitcast.749), channel_id=1, replica_groups=mesh['section'=2,'dp'=8,'tensor'=8] {'tensor'}, dimensions={0} | all-to-all | bytes 524288 | tf_op jit(solution)/shard_map/all_to_all | solution.py:23
  156.3 10.1 %all_to_all.153 = bf16[8,1,16,1024]{3,2,1,0:T(8,128)(2,1)S(1)} all-to-all(bf16[8,1,16,1024]{3,2,1,0:T(8,128)(2,1)S(1)} %broadcast_in_dim.224), channel_id=1, replica_groups=mesh['section'=2,'dp'=8,'tensor'=8] {'tensor'}, dimensions={0} | all-to-all | bytes 524288 | tf_op jit(solution)/shard_map/all_to_all | solution.py:29
  168.3 11.1 %collective-permute-done = bf16[1,128,1024]{2,1,0:T(8,128)(2,1)S(1)} collective-permute-done((bf16[1,128,1024]{2,1,0:T(8,128)(2,1)S(1)}, bf16[1,128,1024]{2,1,0:T(8,128)(2,1)S(1)}, u32[]{:S(2)}, u32[]{:S(2)}) %collective-permute-start) | collective-permute-done | bytes 262176 | tf_op jit(solution)/shard_map/ppermute | solution.py:76
  182.4 21.8 %all_gather.15 = bf16[2,1024,128]{1,2,0:T(8,128)(2,1)S(1)} all-gather(bf16[2,128,128]{1,2,0:T(8,128)(2,1)S(1)} %pad_maximum_fusion.2), channel_id=1, replica_groups=mesh['section'=2,'dp'=8,'tensor'=8] {'dp'}, dimensions={1}, use_global_device_ids=true | all-gather | bytes 589824 | tf_op jit(solution)/shard_map/all_gather | solution.py:46
  207.7 3.4 all-to-all-start.4
  213.1 5.5 all-to-all-done.4
  220.9 3.4 all-to-all-start.5
  224.5 7.3 all-to-all-done.5
  236.7 3.4 all-to-all-start.6
  243.2 4.4 all-to-all-done.6
  248.5 3.4 all-to-all-start.7
  254.2 5.3 all-to-all-done.7
  259.5 4.0 all-to-all-start.12
  267.7 3.4 all-to-all-done.12
  280.1 21.9 %all_gather.16 = bf16[2,1024,128]{1,2,0:T(8,128)(2,1)S(1)} all-gather(bf16[2,128,128]{1,2,0:T(8,128)(2,1)S(1)} %pad_maximum_fusion.3), channel_id=1, replica_groups=mesh['section'=2,'dp'=8,'tensor'=8] {'dp'}, dimensions={1}, use_global_device_ids=true | all-gather | bytes 589824 | tf_op jit(solution)/shard_map/all_gather | solution.py:46
  307.1 7.3 all-to-all-start.8
  315.0 7.0 all-to-all-done.8
  326.1 3.4 all-to-all-start.13
  332.8 4.3 all-to-all-done.13
  341.2 4.3 all-to-all-start.14
  346.5 6.5 all-to-all-done.14
  355.4 3.4 all-to-all-start.15
  360.7 5.7 all-to-all-done.15
  367.2 3.4 all-to-all-start.9
  373.2 4.9 all-to-all-done.9
  378.9 3.4 all-to-all-start.16
  384.1 5.8 all-to-all-done.16
  389.9 19.0 %collective-permute-start.2 = (bf16[1,128,1024]{2,1,0:T(8,128)(2,1)S(1)}, bf16[1,128,1024]{2,1,0:T(8,128)(2,1)S(1)}, u32[]{:S(2)}, u32[]{:S(2)}) collective-permute-start(bf16[1,128,1024]{2,1,0:T(8,128)(2,1)S(1)} %bitcast.673), channel_id=1, source_target_pairs={{64,0},{65,1},{66,2},{67,3},{68,4},{69,5},{70,6},{71,7},{72,8},{73... | collective-permute-start | bytes 786440 | tf_op jit(solution)/shard_map/ppermute | solution.py:76
  415.5 4.2 all-to-all-start.17
  422.0 6.6 all-to-all-done.17
  435.1 3.4 all-to-all-start.18
  440.9 5.3 all-to-all-done.18
  452.5 4.1 all-to-all-start.19
  464.8 3.4 all-to-all-start.10
  470.6 5.2 all-to-all-done.10
  476.5 4.0 all-to-all-start.20
  481.6 6.6 all-to-all-done.20
  488.9 3.4 all-to-all-start.11
  501.4 5.4 all-to-all-start.21
  510.0 4.5 all-to-all-done.21
  514.5 9.1 %collective-permute-start.3 = (bf16[1,128,1024]{2,1,0:T(8,128)(2,1)S(1)}, bf16[1,128,1024]{2,1,0:T(8,128)(2,1)S(1)}, u32[]{:S(2)}, u32[]{:S(2)}) collective-permute-start(bf16[1,128,1024]{2,1,0:T(8,128)(2,1)S(1)} %bitcast.676), channel_id=1, source_target_pairs={{64,0},{65,1},{66,2},{67,3},{68,4},{69,5},{70,6},{71,7},{72,8},{73... | collective-permute-start | bytes 786440 | tf_op jit(solution)/shard_map/ppermute | solution.py:76
  532.0 4.0 all-to-all-start.22
  539.8 5.2 all-to-all-done.22
  552.2 4.0 all-to-all-start.23
  560.6 4.6 all-to-all-done.23
  579.8 4.2 all-to-all-start.24
  584.0 3.5 add_convert_fusion
  588.1 6.5 all-to-all-done.24
  600.3 3.4 all-to-all-start.25
  604.8 6.5 all-to-all-done.25
  612.5 3.4 all-to-all-start.27
  616.1 6.7 all-to-all-done.27
  636.7 4.2 all-to-all-done.28
  641.6 3.4 all-to-all-start.26
  648.6 4.0 all-to-all-done.26
  655.1 27.6 %reduce-scatter.9.cloned.1.call-done = bf16[128,3,128]{2,0,1:T(8,128)(2,1)} async-done(((bf16[1024,3,128]{2,0,1:T(8,128)(2,1)}), bf16[128,3,128]{2,0,1:T(8,128)(2,1)}) %reduce-scatter.9.cloned.1.call-update) | async-done | bytes 98320 | tf_op jit(solution)/shard_map/reduce_scatter | solution.py:442
  684.3 41.3 %reduce-scatter.15.cloned.1.call-done = bf16[128,518]{1,0:T(8,128)(2,1)} async-done(((bf16[1024,518]{1,0:T(8,128)(2,1)}), bf16[128,518]{1,0:T(8,128)(2,1)}) %reduce-scatter.15.cloned.1.call-update) | async-done | bytes 132624
  (627 shorter events, 202.2 us)
Async XLA Ops:
  7.2 81.1 %all-gather.2.cloned.1.call-start = ((), (), s32[]{:S(2)}) async-start(), calls=%async_computation.34 | async-start | bytes 3557376 | tf_op jit(solution)/shard_map/all_gather | solution.py:63
  15.6 166.7 %copy-start.109 = (f32[128]{0:T(128)}, f32[128]{0:T(128)S(1)}, u32[]{:S(2)}) copy-start(f32[128]{0:T(128)S(1)} %get-tuple-element.133) | copy-start | bytes 1540
  15.7 188.6 %copy-start.103 = (f32[2,64]{1,0:T(2,128)}, f32[2,64]{1,0:T(2,128)S(1)}, u32[]{:S(2)}) copy-start(f32[2,64]{1,0:T(2,128)S(1)} %add.624) | copy-start | bytes 1540
  16.8 96.5 %copy-start.145 = (f32[128]{0:T(128)}, f32[128]{0:T(128)S(1)}, u32[]{:S(2)}) copy-start(f32[128]{0:T(128)S(1)} %broadcast_multiply_fusion.11) | copy-start | bytes 1540
  17.0 96.3 %copy-start.160 = (f32[128]{0:T(128)}, f32[128]{0:T(128)S(1)}, u32[]{:S(2)}) copy-start(f32[128]{0:T(128)S(1)} %add_rsqrt_fusion.5) | copy-start | bytes 1540
  89.2 188.8 %copy-start.88 = (f32[1,1,1024]{2,1,0:T(1,128)}, f32[1,1,1024]{2,1,0:T(1,128)S(1)}, u32[]{:S(2)}) copy-start(f32[1,1,1024]{2,1,0:T(1,128)S(1)} %get-tuple-element.126) | copy-start | bytes 12292
  89.2 129.5 %copy-start.82 = (f32[1,1,1024]{2,1,0:T(1,128)}, f32[1,1,1024]{2,1,0:T(1,128)S(1)}, u32[]{:S(2)}) copy-start(f32[1,1,1024]{2,1,0:T(1,128)S(1)} %get-tuple-element.122) | copy-start | bytes 12292
  116.7 13.8 %all-to-all-start = ((bf16[8,1,16,1024]{3,2,1,0:T(8,128)(2,1)}), bf16[8,1,16,1024]{3,2,1,0:T(8,128)(2,1)S(1)}, u32[]{:S(2)}, u32[]{:S(2)}) async-start(bf16[8,1,16,1024]{3,2,1,0:T(8,128)(2,1)} %bitcast.39), calls=%async_computation | async-start | bytes 524288 | tf_op jit(solution)/shard_map/all_to_all | solution.py:23
  131.7 11.0 %all-to-all-start.1 = ((bf16[8,1,16,1024]{3,2,1,0:T(8,128)(2,1)}), bf16[8,1,16,1024]{3,2,1,0:T(8,128)(2,1)S(1)}, u32[]{:S(2)}, u32[]{:S(2)}) async-start(bf16[8,1,16,1024]{3,2,1,0:T(8,128)(2,1)} %broadcast_in_dim.223), calls=%async_computation.1 | async-start | bytes 524288 | tf_op jit(solution)/shard_map/all_to_all | solution.py:29
  135.1 96.8 %copy-start.140 = (f32[1,512]{1,0:T(1,128)}, f32[1,512]{1,0:T(1,128)S(1)}, u32[]{:S(2)}) copy-start(f32[1,512]{1,0:T(1,128)S(1)} %convert_element_type.1007) | copy-start | bytes 6148
  166.4 13.1 %collective-permute-start = (bf16[1,128,1024]{2,1,0:T(8,128)(2,1)S(1)}, bf16[1,128,1024]{2,1,0:T(8,128)(2,1)S(1)}, u32[]{:S(2)}, u32[]{:S(2)}) collective-permute-start(bf16[1,128,1024]{2,1,0:T(8,128)(2,1)S(1)} %bitcast.674), channel_id=1, source_target_pairs={{0,64},{1,65},{2,66},{3,67},{4,68},{5,69},{6,70},{7,71},{8,72},{9,... | collective-permute-start | bytes 786440 | tf_op jit(solution)/shard_map/ppermute | solution.py:76
  204.4 135.6 %copy-start.22 = (bf16[128,2,64]{0,2,1:T(8,128)(2,1)}, bf16[128,2,64]{0,2,1:T(8,128)(2,1)S(1)}, u32[]{:S(2)}) copy-start(bf16[128,2,64]{0,2,1:T(8,128)(2,1)S(1)} %add_convert_fusion.13) | copy-start | bytes 98308
  207.7 11.0 %all-to-all-start.4 = ((bf16[8,1,16,1024]{3,2,1,0:T(8,128)(2,1)}), bf16[8,1,16,1024]{3,2,1,0:T(8,128)(2,1)S(1)}, u32[]{:S(2)}, u32[]{:S(2)}) async-start(bf16[8,1,16,1024]{3,2,1,0:T(8,128)(2,1)} %bitcast.78), calls=%async_computation.4 | async-start | bytes 524288 | tf_op jit(solution)/shard_map/all_to_all | solution.py:23
  219.7 53.1 %copy-start.52 = (f32[1,16,1024]{2,1,0:T(8,128)}, f32[1,16,1024]{2,1,0:T(8,128)S(1)}, u32[]{:S(2)}) copy-start(f32[1,16,1024]{2,1,0:T(8,128)S(1)} %get-tuple-element.63) | copy-start | bytes 196612
  220.9 11.0 %all-to-all-start.5 = ((bf16[8,1,16,1024]{3,2,1,0:T(8,128)(2,1)}), bf16[8,1,16,1024]{3,2,1,0:T(8,128)(2,1)S(1)}, u32[]{:S(2)}, u32[]{:S(2)}) async-start(bf16[8,1,16,1024]{3,2,1,0:T(8,128)(2,1)} %broadcast_in_dim.225), calls=%async_computation.5 | async-start | bytes 524288 | tf_op jit(solution)/shard_map/all_to_all | solution.py:29
  224.3 48.5 %copy-start.117 = (f32[16]{0:T(128)}, f32[16]{0:T(128)S(1)}, u32[]{:S(2)}) copy-start(f32[16]{0:T(128)S(1)} %broadcast_multiply_fusion.5) | copy-start | bytes 196
  224.5 48.3 %copy-start.131 = (f32[16]{0:T(128)}, f32[16]{0:T(128)S(1)}, u32[]{:S(2)}) copy-start(f32[16]{0:T(128)S(1)} %fusion.161) | copy-start | bytes 196
  236.7 11.0 %all-to-all-start.6 = ((bf16[8,1,16,1024]{3,2,1,0:T(8,128)(2,1)}), bf16[8,1,16,1024]{3,2,1,0:T(8,128)(2,1)S(1)}, u32[]{:S(2)}, u32[]{:S(2)}) async-start(bf16[8,1,16,1024]{3,2,1,0:T(8,128)(2,1)} %bitcast.748), calls=%async_computation.6 | async-start | bytes 524288 | tf_op jit(solution)/shard_map/all_to_all | solution.py:23
  248.5 11.0 %all-to-all-start.7 = ((bf16[8,1,16,1024]{3,2,1,0:T(8,128)(2,1)}), bf16[8,1,16,1024]{3,2,1,0:T(8,128)(2,1)S(1)}, u32[]{:S(2)}, u32[]{:S(2)}) async-start(bf16[8,1,16,1024]{3,2,1,0:T(8,128)(2,1)} %broadcast_in_dim.226), calls=%async_computation.7 | async-start | bytes 524288 | tf_op jit(solution)/shard_map/all_to_all | solution.py:29
  259.5 11.7 %all-to-all-start.12 = ((bf16[8,1,16,1024]{3,2,1,0:T(8,128)(2,1)}), bf16[8,1,16,1024]{3,2,1,0:T(8,128)(2,1)}, u32[]{:S(2)}, u32[]{:S(2)}) async-start(bf16[8,1,16,1024]{3,2,1,0:T(8,128)(2,1)} %bitcast.746), calls=%async_computation.12 | async-start | bytes 524288 | tf_op jit(solution)/shard_map/all_to_all | solution.py:23
  263.5 12.3 %collective-permute-start.1 = (bf16[1,128,1024]{2,1,0:T(8,128)(2,1)S(1)}, bf16[1,128,1024]{2,1,0:T(8,128)(2,1)}, u32[]{:S(2)}, u32[]{:S(2)}) collective-permute-start(bf16[1,128,1024]{2,1,0:T(8,128)(2,1)S(1)} %bitcast.675), channel_id=1, source_target_pairs={{0,64},{1,65},{2,66},{3,67},{4,68},{5,69},{6,70},{7,71},{8,72},{9,... | collective-permute-start | bytes 786440 | tf_op jit(solution)/shard_map/ppermute | solution.py:76
  303.1 145.8 %copy-start.17 = (bf16[1,1024,128]{1,2,0:T(8,128)(2,1)}, bf16[1,1024,128]{1,2,0:T(8,128)(2,1)S(1)}, u32[]{:S(2)}) copy-start(bf16[1,1024,128]{1,2,0:T(8,128)(2,1)S(1)} %get-tuple-element.91) | copy-start | bytes 786436
  307.1 31.4 %copy-start.59 = (bf16[1,1024,128]{1,2,0:T(8,128)(2,1)S(1)}, bf16[1,1024,128]{1,2,0:T(8,128)(2,1)}, u32[]{:S(2)}) copy-start(bf16[1,1024,128]{1,2,0:T(8,128)(2,1)} %get-tuple-element.90) | copy-start | bytes 786436
  307.1 15.0 %all-to-all-start.8 = ((bf16[8,1,16,1024]{3,2,1,0:T(8,128)(2,1)}), bf16[8,1,16,1024]{3,2,1,0:T(8,128)(2,1)S(1)}, u32[]{:S(2)}, u32[]{:S(2)}) async-start(bf16[8,1,16,1024]{3,2,1,0:T(8,128)(2,1)} %bitcast.105), calls=%async_computation.8 | async-start | bytes 524288 | tf_op jit(solution)/shard_map/all_to_all | solution.py:23
  326.1 11.0 %all-to-all-start.13 = ((bf16[8,1,16,1024]{3,2,1,0:T(8,128)(2,1)}), bf16[8,1,16,1024]{3,2,1,0:T(8,128)(2,1)S(1)}, u32[]{:S(2)}, u32[]{:S(2)}) async-start(bf16[8,1,16,1024]{3,2,1,0:T(8,128)(2,1)} %broadcast_in_dim.232), calls=%async_computation.13 | async-start | bytes 524288 | tf_op jit(solution)/shard_map/all_to_all | solution.py:29
  341.2 25.3 %copy-start.81 = (bf16[16,1024]{1,0:T(8,128)(2,1)S(1)}, bf16[16,1024]{1,0:T(8,128)(2,1)}, u32[]{:S(2)}) copy-start(bf16[16,1024]{1,0:T(8,128)(2,1)} %get-tuple-element.113) | copy-start | bytes 98308
  341.2 11.8 %all-to-all-start.14 = ((bf16[8,2,128,128]{2,3,1,0:T(8,128)(2,1)}), bf16[8,2,128,128]{2,3,1,0:T(8,128)(2,1)}, u32[]{:S(2)}, u32[]{:S(2)}) async-start(bf16[8,2,128,128]{2,3,1,0:T(8,128)(2,1)} %maximum_bitcast_fusion.1), calls=%async_computation.14 | async-start | bytes 1048576 | tf_op jit(solution)/shard_map/all_to_all | solution.py:23
  346.4 24.9 %copy-start.55 = (f32[1,16,1024]{2,1,0:T(8,128)S(1)}, f32[1,16,1024]{2,1,0:T(8,128)}, u32[]{:S(2)}) copy-start(f32[1,16,1024]{2,1,0:T(8,128)} %copy-done.54) | copy-start | bytes 196612
  346.4 24.9 %copy-start.120 = (f32[16]{0:T(128)S(1)}, f32[16]{0:T(128)}, u32[]{:S(2)}) copy-start(f32[16]{0:T(128)} %copy-done.119) | copy-start | bytes 196
  346.4 25.6 %copy-start.156 = (f32[16]{0:T(128)S(1)}, f32[16]{0:T(128)}, u32[]{:S(2)}) copy-start(f32[16]{0:T(128)} %copy-done.155) | copy-start | bytes 196
  346.5 25.7 %copy-start.68 = (f32[1,16,1024]{2,1,0:T(8,128)S(1)}, f32[1,16,1024]{2,1,0:T(8,128)}, u32[]{:S(2)}) copy-start(f32[1,16,1024]{2,1,0:T(8,128)} %copy-done.67) | copy-start | bytes 196612
  346.5 25.7 %copy-start.134 = (f32[16]{0:T(128)S(1)}, f32[16]{0:T(128)}, u32[]{:S(2)}) copy-start(f32[16]{0:T(128)} %copy-done.133) | copy-start | bytes 196
  354.4 27.9 %copy-start.141 = (f32[1,512]{1,0:T(1,128)S(1)}, f32[1,512]{1,0:T(1,128)}, u32[]{:S(2)}) copy-start(f32[1,512]{1,0:T(1,128)} %copy-done.140) | copy-start | bytes 6148
  355.4 11.0 %all-to-all-start.15 = ((bf16[8,1,16,1024]{3,2,1,0:T(8,128)(2,1)}), bf16[8,1,16,1024]{3,2,1,0:T(8,128)(2,1)S(1)}, u32[]{:S(2)}, u32[]{:S(2)}) async-start(bf16[8,1,16,1024]{3,2,1,0:T(8,128)(2,1)} %bitcast.139), calls=%async_computation.15 | async-start | bytes 524288 | tf_op jit(solution)/shard_map/all_to_all | solution.py:23
  360.7 48.2 %copy-start.45 = (bf16[8,1,16,1024]{3,2,1,0:T(8,128)(2,1)S(1)}, bf16[8,1,16,1024]{3,2,1,0:T(8,128)(2,1)}, u32[]{:S(2)}) copy-start(bf16[8,1,16,1024]{3,2,1,0:T(8,128)(2,1)} %copy-done.44) | copy-start | bytes 786436
  360.7 48.2 %copy-start.47 = (bf16[8,1,16,1024]{3,2,1,0:T(8,128)(2,1)S(1)}, bf16[8,1,16,1024]{3,2,1,0:T(8,128)(2,1)}, u32[]{:S(2)}) copy-start(bf16[8,1,16,1024]{3,2,1,0:T(8,128)(2,1)} %copy-done.46) | copy-start | bytes 786436
  367.2 11.0 %all-to-all-start.9 = ((bf16[8,1,16,1024]{3,2,1,0:T(8,128)(2,1)}), bf16[8,1,16,1024]{3,2,1,0:T(8,128)(2,1)S(1)}, u32[]{:S(2)}, u32[]{:S(2)}) async-start(bf16[8,1,16,1024]{3,2,1,0:T(8,128)(2,1)} %broadcast_in_dim.227), calls=%async_computation.9 | async-start | bytes 524288 | tf_op jit(solution)/shard_map/all_to_all | solution.py:29
  378.9 11.0 %all-to-all-start.16 = ((bf16[8,1,16,1024]{3,2,1,0:T(8,128)(2,1)}), bf16[8,1,16,1024]{3,2,1,0:T(8,128)(2,1)S(1)}, u32[]{:S(2)}, u32[]{:S(2)}) async-start(bf16[8,1,16,1024]{3,2,1,0:T(8,128)(2,1)} %broadcast_in_dim.235), calls=%async_computation.16 | async-start | bytes 524288 | tf_op jit(solution)/shard_map/all_to_all | solution.py:29
  382.3 28.4 %copy-start.57 = (f32[128,512]{1,0:T(8,128)S(1)}, f32[128,512]{1,0:T(8,128)}, u32[]{:S(2)}) copy-start(f32[128,512]{1,0:T(8,128)} %copy-done.56) | copy-start | bytes 786436
  384.1 29.2 %copy-start.60 = (f32[128,512]{1,0:T(8,128)}, f32[128,512]{1,0:T(8,128)S(1)}, u32[]{:S(2)}) copy-start(f32[128,512]{1,0:T(8,128)S(1)} %convolution_add_fusion.1) | copy-start | bytes 786436
  389.9 20.2 %collective-permute-start.2 = (bf16[1,128,1024]{2,1,0:T(8,128)(2,1)S(1)}, bf16[1,128,1024]{2,1,0:T(8,128)(2,1)S(1)}, u32[]{:S(2)}, u32[]{:S(2)}) collective-permute-start(bf16[1,128,1024]{2,1,0:T(8,128)(2,1)S(1)} %bitcast.673), channel_id=1, source_target_pairs={{64,0},{65,1},{66,2},{67,3},{68,4},{69,5},{70,6},{71,7},{72,8},{73... | collective-permute-start | bytes 786440 | tf_op jit(solution)/shard_map/ppermute | solution.py:76
  415.5 13.1 %all-to-all-start.17 = ((bf16[8,1,16,1024]{3,2,1,0:T(8,128)(2,1)}), bf16[8,1,16,1024]{3,2,1,0:T(8,128)(2,1)}, u32[]{:S(2)}, u32[]{:S(2)}) async-start(bf16[8,1,16,1024]{3,2,1,0:T(8,128)(2,1)} %bitcast.146), calls=%async_computation.17 | async-start | bytes 524288 | tf_op jit(solution)/shard_map/all_to_all | solution.py:23
  435.1 11.1 %all-to-all-start.18 = ((bf16[8,1,16,1024]{3,2,1,0:T(8,128)(2,1)}), bf16[8,1,16,1024]{3,2,1,0:T(8,128)(2,1)S(1)}, u32[]{:S(2)}, u32[]{:S(2)}) async-start(bf16[8,1,16,1024]{3,2,1,0:T(8,128)(2,1)} %broadcast_in_dim.238), calls=%async_computation.18 | async-start | bytes 524288 | tf_op jit(solution)/shard_map/all_to_all | solution.py:29
  452.5 12.3 %all-to-all-start.19 = ((bf16[8,2,128,128]{2,3,1,0:T(8,128)(2,1)}), bf16[8,2,128,128]{2,3,1,0:T(8,128)(2,1)}, u32[]{:S(2)}, u32[]{:S(2)}) async-start(bf16[8,2,128,128]{2,3,1,0:T(8,128)(2,1)} %maximum_bitcast_fusion.2), calls=%async_computation.19 | async-start | bytes 1048576 | tf_op jit(solution)/shard_map/all_to_all | solution.py:23
  464.8 11.0 %all-to-all-start.10 = ((bf16[8,1,16,1024]{3,2,1,0:T(8,128)(2,1)}), bf16[8,1,16,1024]{3,2,1,0:T(8,128)(2,1)S(1)}, u32[]{:S(2)}, u32[]{:S(2)}) async-start(bf16[8,1,16,1024]{3,2,1,0:T(8,128)(2,1)} %bitcast.745), calls=%async_computation.10 | async-start | bytes 524288 | tf_op jit(solution)/shard_map/all_to_all | solution.py:23
  476.5 11.7 %all-to-all-start.20 = ((bf16[8,1,16,1024]{3,2,1,0:T(8,128)(2,1)}), bf16[8,1,16,1024]{3,2,1,0:T(8,128)(2,1)}, u32[]{:S(2)}, u32[]{:S(2)}) async-start(bf16[8,1,16,1024]{3,2,1,0:T(8,128)(2,1)} %bitcast.699), calls=%async_computation.20 | async-start | bytes 524288 | tf_op jit(solution)/shard_map/all_to_all | solution.py:23
  480.5 43.1 %copy-start.3 = (bf16[1,128,1024]{2,1,0:T(8,128)(2,1)S(1)}, bf16[1,128,1024]{2,1,0:T(8,128)(2,1)}, u32[]{:S(2)}) copy-start(bf16[1,128,1024]{2,1,0:T(8,128)(2,1)} %copy-done.2) | copy-start | bytes 786436
  480.6 43.1 %copy-start.89 = (f32[1,1,1024]{2,1,0:T(1,128)S(1)}, f32[1,1,1024]{2,1,0:T(1,128)}, u32[]{:S(2)}) copy-start(f32[1,1,1024]{2,1,0:T(1,128)} %copy-done.88) | copy-start | bytes 12292
  488.9 11.0 %all-to-all-start.11 = ((bf16[8,1,16,1024]{3,2,1,0:T(8,128)(2,1)}), bf16[8,1,16,1024]{3,2,1,0:T(8,128)(2,1)S(1)}, u32[]{:S(2)}, u32[]{:S(2)}) async-start(bf16[8,1,16,1024]{3,2,1,0:T(8,128)(2,1)} %broadcast_in_dim.228), calls=%async_computation.11 | async-start | bytes 524288 | tf_op jit(solution)/shard_map/all_to_all | solution.py:29
  501.4 13.0 %all-to-all-start.21 = ((bf16[8,1,16,1024]{3,2,1,0:T(8,128)(2,1)}), bf16[8,1,16,1024]{3,2,1,0:T(8,128)(2,1)S(1)}, u32[]{:S(2)}, u32[]{:S(2)}) async-start(bf16[8,1,16,1024]{3,2,1,0:T(8,128)(2,1)} %broadcast_in_dim.241), calls=%async_computation.21 | async-start | bytes 524288 | tf_op jit(solution)/shard_map/all_to_all | solution.py:29
  514.5 11.9 %collective-permute-start.3 = (bf16[1,128,1024]{2,1,0:T(8,128)(2,1)S(1)}, bf16[1,128,1024]{2,1,0:T(8,128)(2,1)S(1)}, u32[]{:S(2)}, u32[]{:S(2)}) collective-permute-start(bf16[1,128,1024]{2,1,0:T(8,128)(2,1)S(1)} %bitcast.676), channel_id=1, source_target_pairs={{64,0},{65,1},{66,2},{67,3},{68,4},{69,5},{70,6},{71,7},{72,8},{73... | collective-permute-start | bytes 786440 | tf_op jit(solution)/shard_map/ppermute | solution.py:76
  532.0 13.1 %all-to-all-start.22 = ((bf16[8,1,16,1024]{3,2,1,0:T(8,128)(2,1)}), bf16[8,1,16,1024]{3,2,1,0:T(8,128)(2,1)}, u32[]{:S(2)}, u32[]{:S(2)}) async-start(bf16[8,1,16,1024]{3,2,1,0:T(8,128)(2,1)} %bitcast.747), calls=%async_computation.22 | async-start | bytes 524288 | tf_op jit(solution)/shard_map/all_to_all | solution.py:23
  552.2 13.0 %all-to-all-start.23 = ((bf16[8,1,16,1024]{3,2,1,0:T(8,128)(2,1)}), bf16[8,1,16,1024]{3,2,1,0:T(8,128)(2,1)}, u32[]{:S(2)}, u32[]{:S(2)}) async-start(bf16[8,1,16,1024]{3,2,1,0:T(8,128)(2,1)} %broadcast_in_dim.244), calls=%async_computation.23 | async-start | bytes 524288 | tf_op jit(solution)/shard_map/all_to_all | solution.py:29
  556.2 90.9 %reduce-scatter.13.cloned.1.call-start = ((), (), s32[]{:S(2)}) async-start(), calls=%async_computation.37 | async-start | bytes 294912
  570.2 83.3 %reduce-scatter.11.cloned.1.call-start = ((), (), s32[]{:S(2)}) async-start(), calls=%async_computation.36 | async-start | bytes 1179648 | tf_op jit(solution)/shard_map/reduce_scatter | solution.py:448
  579.8 14.8 %all-to-all-start.24 = ((bf16[8,2,128,128]{2,3,1,0:T(8,128)(2,1)}), bf16[8,2,128,128]{2,3,1,0:T(8,128)(2,1)}, u32[]{:S(2)}, u32[]{:S(2)}) async-start(bf16[8,2,128,128]{2,3,1,0:T(8,128)(2,1)} %maximum_bitcast_fusion.3), calls=%async_computation.24 | async-start | bytes 1048576 | tf_op jit(solution)/shard_map/all_to_all | solution.py:23
  584.0 98.7 %reduce-scatter.9.cloned.1.call-start = ((), (), s32[]{:S(2)}) async-start(), calls=%async_computation.35 | async-start | bytes 884736 | tf_op jit(solution)/shard_map/reduce_scatter | solution.py:442
  599.3 27.7 %copy-start.9 = (bf16[512,1024]{1,0:T(8,128)(2,1)S(1)}, bf16[512,1024]{1,0:T(8,128)(2,1)}, u32[]{:S(2)}) copy-start(bf16[512,1024]{1,0:T(8,128)(2,1)} %add_convert_fusion) | copy-start | bytes 3145732
  600.3 11.0 %all-to-all-start.25 = ((bf16[8,1,16,1024]{3,2,1,0:T(8,128)(2,1)}), bf16[8,1,16,1024]{3,2,1,0:T(8,128)(2,1)S(1)}, u32[]{:S(2)}, u32[]{:S(2)}) async-start(bf16[8,1,16,1024]{3,2,1,0:T(8,128)(2,1)} %bitcast.194), calls=%async_computation.25 | async-start | bytes 524288 | tf_op jit(solution)/shard_map/all_to_all | solution.py:23
  612.5 10.3 %all-to-all-start.27 = ((f32[8,1,4096]{2,1,0:T(1,128)}), f32[8,1,4096]{2,1,0:T(1,128)S(1)}, u32[]{:S(2)}, u32[]{:S(2)}) async-start(f32[8,1,4096]{2,1,0:T(1,128)} %broadcast_in_dim.255), calls=%async_computation.29 | async-start | bytes 262144 | tf_op jit(solution)/shard_map/all_to_all | solution.py:29
  623.4 8.4 %all-to-all-start.29 = ((f32[8,1,512]{2,1,0:T(1,128)}), f32[8,1,512]{2,1,0:T(1,128)S(1)}, u32[]{:S(2)}, u32[]{:S(2)}) async-start(f32[8,1,512]{2,1,0:T(1,128)} %broadcast_in_dim.266), calls=%async_computation.31 | async-start | bytes 32768 | tf_op jit(solution)/shard_map/all_to_all | solution.py:29
  626.8 98.8 %reduce-scatter.15.cloned.1.call-start = ((), (), s32[]{:S(2)}) async-start(), calls=%async_computation.38 | async-start | bytes 1474560
  632.4 8.5 %all-to-all-start.28 = ((f32[8,2,128]{2,1,0:T(2,128)}), f32[8,2,128]{2,1,0:T(2,128)S(1)}, u32[]{:S(2)}, u32[]{:S(2)}) async-start(f32[8,2,128]{2,1,0:T(2,128)} %broadcast_in_dim.262), calls=%async_computation.30 | async-start | bytes 16384 | tf_op jit(solution)/shard_map/all_to_all | solution.py:29
  641.6 11.0 %all-to-all-start.26 = ((bf16[8,1,16,1024]{3,2,1,0:T(8,128)(2,1)}), bf16[8,1,16,1024]{3,2,1,0:T(8,128)(2,1)S(1)}, u32[]{:S(2)}, u32[]{:S(2)}) async-start(bf16[8,1,16,1024]{3,2,1,0:T(8,128)(2,1)} %broadcast_in_dim.247), calls=%async_computation.26 | async-start | bytes 524288 | tf_op jit(solution)/shard_map/all_to_all | solution.py:29
  (134 other events, 1295.2 us)
Sparse Core Ops, SparseCore 0:
  15.0 73.2 all-gather.1
  570.3 28.3 reduce-scatter.12
  601.3 40.5 reduce-scatter.10
  644.2 38.4 reduce-scatter.8
  685.0 40.5 reduce-scatter.14
where the time goes:
time: 747 us; the launch traced here: 737 us
  waiting for transfers between devices  301 us (40%)
  starting transfers between devices  141 us (19%)
  blocking collectives  86.1 us (12%)
  matrix products  85.6 us (11%)
  other arithmetic  71.5 us (10%)
  local copies, waits for them, and re-layouts  35.4 us (5%)
  between operations  16.6 us (2%)
    all_to_all x14, waiting for transfers between devices, sum_at_owner(): lax.all_to_all(in_blocks(shard, dim, length), axis, 0, 0, tiled=True)  78.9 us
    all_gather x1, waiting for transfers between devices, turned_gather(): filled = lax.all_gather(both, axis, axis=0, tiled=True)  71.2 us
    all_to_all x14, waiting for transfers between devices, copy_for_each(): return lax.all_to_all(copies, axis, split_axis=0, concat_axis=0, tiled=True)  68.5 us
    all_gather x3, blocking collectives, in_one_piece(): filled = lax.all_gather(both, axis, axis=dim, tiled=True)  66 us
    all_to_all x14, starting transfers between devices, sum_at_owner(): lax.all_to_all(in_blocks(shard, dim, length), axis, 0, 0, tiled=True)  59.4 us
    all_to_all x14, starting transfers between devices, copy_for_each(): return lax.all_to_all(copies, axis, split_axis=0, concat_axis=0, tiled=True)  50.2 us
    unnamed x7, waiting for transfers between devices  41.4 us
    ppermute x4, starting transfers between devices, from_behind(): lax.ppermute(value, axis, [(source, source + steps) for source in range(f...  30.7 us
  transfers between devices with their start and end apart: 37, of which 34 were waited for; matrix products, arithmetic and copies ran while one was open for 13% of the time, Pallas kernels for 0%

commit v1 on v0

v1 whole, which is shorter than its diff:
```python
import math

import jax
import jax.numpy as jnp
from jax import lax
from jax.sharding import Mesh, PartitionSpec as P

HD = 64
EPSILON = 1e-05
MASKED = -1e30
BF = jnp.bfloat16
F32 = jnp.float32
CHIPS = ("yh", "z", "yl")
TOKENS = ("z", "yl", "yh")


def swap_cores(v):
    return lax.ppermute(v, "s", [(0, 1), (1, 0)])


def spread(piece):
    copies = jnp.broadcast_to(piece, (16, *piece.shape))
    return lax.all_to_all(copies, CHIPS, 0, 0, tiled=True)


def sum_over_x(part):
    got = [
        lax.ppermute(part, "x", [(i, i ^ k) for i in range(4)]).astype(F32) for k in (1, 3, 2)
    ]
    return (part.astype(F32) + got[0]) + (got[2] + got[1])


def layer_norm(v, gain, shift):
    mean = jnp.mean(v, axis=-1, keepdims=True)
    centred = v - mean
    variance = jnp.mean(centred * centred, axis=-1, keepdims=True)
    return centred * lax.rsqrt(variance + EPSILON) * gain + shift


def layer_norm_back(v, gain, grad):
    mean = jnp.mean(v, axis=-1, keepdims=True)
    centred = v - mean
    variance = jnp.mean(centred * centred, axis=-1, keepdims=True)
    inverse = lax.rsqrt(variance + EPSILON)
    xhat = centred * inverse
    d = grad * gain
    back = inverse * (
        d - jnp.mean(d, axis=-1, keepdims=True) - xhat * jnp.mean(d * xhat, axis=-1, keepdims=True)
    )
    return back, jnp.sum(grad * xhat, axis=0), jnp.sum(grad, axis=0)


def gelu(u):
    return 0.5 * u * (1.0 + jnp.tanh(0.7978845608028654 * (u + 0.044715 * u * u * u)))


def gelu_slope(u):
    t = jnp.tanh(0.7978845608028654 * (u + 0.044715 * u * u * u))
    return 0.5 * (1.0 + t) + 0.5 * u * (1.0 - t * t) * 0.7978845608028654 * (
        1.0 + 3.0 * 0.044715 * u * u
    )


def ein(form, a, b):
    return jnp.einsum(form, a, b, preferred_element_type=F32)


def forward(x, wa, wf, par):
    ln, qb, vb, ub = par
    n1 = layer_norm(x, ln[0], ln[2]).astype(BF)
    proj = ein("cd,hdk->hck", n1, wa[:, :, :192])
    q = (proj[:, :, :64] + qb[:, None]).astype(BF)
    k = proj[:, :, 64:128].astype(BF)
    v = (proj[:, :, 128:] + vb[:, None]).astype(BF)
    kv = jnp.concatenate([k, v], axis=-1)
    kv = lax.all_to_all(jnp.broadcast_to(kv, (16, *kv.shape)), TOKENS, 0, 0, tiled=True)
    kv = jnp.moveaxis(kv, 0, 1).reshape(4, 1024, 128)
    scores = ein("hqe,hke->hqk", q, kv[:, :, :64]) * (1.0 / math.sqrt(HD))
    first = lax.axis_index(TOKENS) * 64
    qpos = first + lax.broadcasted_iota(jnp.int32, (64, 1024), 0)
    kpos = lax.broadcasted_iota(jnp.int32, (64, 1024), 1)
    scores = jnp.where(kpos <= qpos, scores, MASKED)
    top = jnp.max(scores, axis=-1, keepdims=True)
    e = jnp.exp(scores - top)
    p = e / jnp.sum(e, axis=-1, keepdims=True)
    att = ein("hqk,hke->hqe", p.astype(BF), kv[:, :, 64:]).astype(BF)
    part = ein("hce,hde->cd", att, wa[:, :, 192:]).astype(BF)
    mid = x + (sum_over_x(part) + ln[4])
    n2 = layer_norm(mid, ln[1], ln[3]).astype(BF)
    pre = ein("cd,hdf->hcf", n2, wf[:, :, :256]) + ub[:, None]
    act = gelu(pre).astype(BF)
    part = ein("hcf,hdf->cd", act, wf[:, :, 256:]).astype(BF)
    y = (mid + (sum_over_x(part) + ln[5])).astype(BF)
    return y, (x, n1, q, kv, p, att, mid, n2, pre, act)


def backward(g, saved, wa, wf, par):
    x, n1, q, kv, p, att, mid, n2, pre, act = saved
    ln = par[0]
    gl = g.astype(BF)
    gf_down = ein("cd,hcf->hdf", gl, act)
    ob1 = jnp.sum(g, axis=0)
    dact = ein("cd,hdf->hcf", gl, wf[:, :, 256:])
    dpre = (dact * gelu_slope(pre)).astype(BF)
    gub = jnp.sum(dpre.astype(F32), axis=1)
    gf_up = ein("cd,hcf->hdf", n2, dpre)
    part = ein("hcf,hdf->cd", dpre, wf[:, :, :256]).astype(BF)
    back, gg1, gs1 = layer_norm_back(mid, ln[1], sum_over_x(part))
    dmid = g + back
    bg = dmid.astype(BF)
    ob0 = jnp.sum(bg.astype(F32), axis=0)
    ga_out = ein("cd,hce->hde", bg, att)
    datt = ein("cd,hde->hce", bg, wa[:, :, 192:]).astype(BF)
    dp = ein("hqe,hke->hqk", datt, kv[:, :, 64:])
    ds = (p * (dp - jnp.sum(p * dp, axis=-1, keepdims=True))).astype(BF)
    dq = (ein("hqk,hke->hqe", ds, kv[:, :, :64]) * (1.0 / math.sqrt(HD))).astype(BF)
    dk = ein("hqk,hqe->hke", ds, q) * (1.0 / math.sqrt(HD))
    dv = ein("hqk,hqe->hke", p.astype(BF), datt)
    dkv = jnp.concatenate([dk, dv], axis=-1).astype(BF).reshape(4, 16, 64, 128)
    dkv = lax.all_to_all(jnp.moveaxis(dkv, 1, 0), TOKENS, 0, 0, tiled=True)
    dkv = jnp.sum(dkv.astype(F32), axis=0).astype(BF)
    dproj = jnp.concatenate([dq, dkv], axis=-1)
    gib = jnp.sum(dproj.astype(F32), axis=1)
    ga_qkv = ein("cd,hcj->hdj", n1, dproj)
    part = ein("hcj,hdj->cd", dproj, wa[:, :, :192]).astype(BF)
    back, gg0, gs0 = layer_norm_back(x, ln[0], sum_over_x(part))
    dx = (dmid + back).astype(BF)
    ga = jnp.concatenate([ga_qkv, ga_out], axis=-1).astype(BF)
    gf = jnp.concatenate([gf_up, gf_down], axis=-1).astype(BF)
    rows = jnp.stack([gg0, gg1, gs0, gs1, ob0, ob1])
    return dx, ga, gf, (rows, gib, gub)


def by_owner(rows, gib, gub, s):
    dpart = jnp.moveaxis(rows.reshape(6, 8, 128), 1, 0)
    def natural(v):
        pair = v.reshape(2, 2, -1)
        return jnp.where(s == 0, pair, pair[::-1])
    qb = natural(gib[:, :64])
    vb = natural(gib[:, 128:])
    ub = natural(gub)
    tpart = jnp.concatenate(
        [
            jnp.moveaxis(qb, 0, 1).reshape(2, 1, 128),
            jnp.moveaxis(vb, 0, 1).reshape(2, 1, 128),
            jnp.moveaxis(ub, 0, 1).reshape(2, 4, 128),
        ],
        axis=1,
    )
    both = jnp.concatenate(
        [
            jnp.broadcast_to(dpart[None], (2, 8, 6, 128)),
            jnp.broadcast_to(tpart[:, None], (2, 8, 6, 128)),
        ],
        axis=2,
    )
    return both.reshape(16, 6, 256).astype(BF)


def reduce_layer(ga, gf, small):
    ga, gf = ga.reshape(2, 16, 128, 256), gf.reshape(2, 16, 128, 512)
    mf = (gf[0].astype(F32) + swap_cores(gf[1]).astype(F32)).astype(BF)
    rf = jnp.sum(lax.all_to_all(mf, CHIPS, 0, 0, tiled=True).astype(F32), axis=0)
    ma = (ga[0].astype(F32) + swap_cores(ga[1]).astype(F32)).astype(BF)
    sm = (small.astype(F32) + swap_cores(small).astype(F32)).astype(BF)
    ma = jnp.concatenate([ma, sm, jnp.zeros((16, 10, 256), BF)], axis=1)
    ra = jnp.sum(lax.all_to_all(ma, CHIPS, 0, 0, tiled=True).astype(F32), axis=0)
    return jnp.concatenate([ra[:128], rf], axis=1), ra[128:134].reshape(12, 128)


def local(inputs, cotangent, wqkv, wout, wup, wdown, gain, shift, inb, outb, upb):
    s = lax.axis_index("s")
    yh = lax.axis_index("yh")
    attn = jnp.concatenate([wqkv[0], wout[0].T[:, None]], axis=1).reshape(128, 4, 2, 64)
    attn = jnp.moveaxis(attn, 2, 0).reshape(2, 128, 256)
    up = jnp.moveaxis(wup[0].reshape(128, 2, 256), 1, 0)
    down = jnp.moveaxis(wdown[0].T.reshape(128, 2, 256), 1, 0)
    small = jnp.concatenate([gain[0], shift[0], outb[0], inb[0], upb[0].reshape(4, 128)])
    small = jnp.broadcast_to(small.reshape(1, 2, 768), (2, 2, 768))
    own = jnp.concatenate([attn, up, down], axis=2)
    own = jnp.concatenate([own, small, jnp.zeros((2, 14, 768), BF)], axis=1)
    both = lax.all_to_all(own, "s", 0, 0, tiled=True)
    urgent = jnp.concatenate(
        [both[0, :128, :256], both[:, 128:130].reshape(12, 256), jnp.zeros((4, 256), BF)]
    )
    g0a = spread(urgent)
    g0f = spread(both[0, :128, 256:])
    g1 = spread(both[1, :128])

    def whole(mine):
        mine = mine.reshape(2, 1024, -1)
        return jnp.concatenate([mine, swap_cores(mine)])

    wa = [whole(g0a[:, :128]), whole(g1[:, :, :256])]
    wf = [whole(g0f), whole(g1[:, :, 256:])]
    par = g0a[:, 128:140].reshape(2, 8, 2, 12, 128).astype(F32)
    pars = []
    for l in range(2):
        ln = jnp.moveaxis(par[0, :, l, :6], 0, 1).reshape(6, 1024)
        def split(v):
            v = jnp.moveaxis(v.reshape(2, 2, -1), 1, 0)
            return jnp.where(s == 0, v, v[::-1]).reshape(4, -1)
        pars.append(
            (ln, split(par[:, 0, l, 6]), split(par[:, 0, l, 7]), split(par[:, 0, l, 8:12]))
        )
    def own_rows(v):
        return lax.dynamic_slice(v, (s, 0, yh * 64, 0), (1, 1, 64, 1024)).reshape(64, 1024)

    y0, saved0 = forward(own_rows(inputs).astype(F32), wa[0], wf[0], pars[0])
    y1, saved1 = forward(y0.astype(F32), wa[1], wf[1], pars[1])

    def collect(a, b):
        rows = jnp.broadcast_to(jnp.stack([a, b])[:, None], (2, 2, 64, 1024))
        rows = lax.all_to_all(rows.reshape(4, 64, 1024), ("s", "yh"), 0, 0, tiled=True)
        return rows.reshape(1, 2, 1, 128, 1024)

    acts = collect(y0, y1)
    d1, ga1, gf1, sm1 = backward(own_rows(cotangent).astype(F32), saved1, wa[1], wf[1], pars[1])
    r1, t1 = reduce_layer(ga1, gf1, by_owner(*sm1, s))
    d0, ga0, gf0, sm0 = backward(d1.astype(F32), saved0, wa[0], wf[0], pars[0])
    r0, t0 = reduce_layer(ga0, gf0, by_owner(*sm0, s))
    grads = collect(d0, d1)
    w = lax.all_to_all(jnp.stack([r0, r1]), "s", 0, 0, tiled=True)
    t = jnp.where(s == 0, t0, t1)
    at = jnp.moveaxis(w[:, :, :256].reshape(2, 128, 4, 64), 0, 2).reshape(128, 4, 128)
    gup = jnp.moveaxis(w[:, :, 256:512], 0, 1).reshape(1, 128, 512)
    gdown = jnp.moveaxis(w[:, :, 512:], 0, 1).reshape(128, 512).T
    return (
        acts,
        grads,
        at[None, :, :3],
        at[None, :, 3].swapaxes(1, 2),
        gup,
        gdown[None],
        t[None, 0:2],
        t[None, 2:4],
        t[None, 6:8],
        t[None, 4:6],
        t[8:12].reshape(1, 512),
    )


def solution(mesh):
    parts = Mesh(mesh.devices.reshape(2, 4, 2, 2, 4), ("s", "z", "yl", "yh", "x"))
    dp, tp = ("z", "yl"), ("yh", "x")
    return jax.shard_map(
        local,
        mesh=parts,
        in_specs=(
            P(None, None, dp, None),
            P(None, None, dp, None),
            P("s", dp, None, tp),
            P("s", tp, dp),
            P("s", dp, tp),
            P("s", tp, dp),
            P("s", None, dp),
            P("s", None, dp),
            P("s", None, tp),
            P("s", None, dp),
            P("s", tp),
        ),
        out_specs=(
            P("s", None, None, dp, None),
            P("s", None, None, dp, None),
            P("s", dp, None, tp),
            P("s", tp, dp),
            P("s", dp, tp),
            P("s", tp, dp),
            P("s", None, dp),
            P("s", None, dp),
            P("s", None, tp),
            P("s", None, dp),
            P("s", tp),
        ),
        check_vma=False,
    )
```

time: 747 us -> 547 us (0.73)
  waiting for transfers between devices: 301 us -> 159 us
  local copies, waits for them, and re-layouts: 35.4 us -> 97.2 us
  blocking collectives: 86.1 us -> 33.7 us
  matrix products: 85.6 us -> 55.3 us
  starting transfers between devices: 141 us -> 118 us
  between operations: 16.6 us -> 2.79 us
    all_gather x1 -> x0, waiting for transfers between devices: 71.2 us -> none  [turned_gather(): filled = lax.all_gather(both, axis, axis=0, tiled=True)]
    all_gather x3 -> x0, blocking collectives: 66 us -> none  [in_one_piece(): filled = lax.all_gather(both, axis, axis=dim, tiled=True)]
    unnamed x7 -> x0, waiting for transfers between devices: 41.4 us -> none
    all_to_all x28 -> x12, starting transfers between devices: 110 us -> 74.2 us  [the longest x3 18.4 us: spread(): return lax.all_to_all(copies, CHIPS, 0, 0, tiled=True)]
    reduce_scatter x2 -> x0, waiting for transfers between devices: 27.6 us -> none  [the longest x1 27.6 us: local(): lax.psum_scatter(grad_sums[0].astype(jnp.bfloat16), 'dp', scatter_dimensi...]
    dot_general x54 -> x36, matrix products: 80.8 us -> 55.3 us  [ein(): return jnp.einsum(form, a, b, preferred_element_type=F32)]
    concatenate x5 -> x15, other arithmetic: 0.12 us -> 22.6 us  [the longest x2 8.66 us: backward(): gf = jnp.concatenate([gf_up, gf_down], axis=-1).astype(BF)]
    slice x7 -> x21, local copies, waits for them, and re-layouts: 0.07 us -> 21.6 us  [the longest x2 8.12 us: reduce_layer(): mf = (gf[0].astype(F32) + swap_cores(gf[1]).astype(F32)).astype(BF)]
  transfers between devices with their start and end apart: 37 -> 46, of which waited for: 34 -> 21; matrix products, arithmetic and copies ran while one was open for 13% -> 32% of each run, Pallas kernels for 0% -> 0%
where the time goes in v1:
time: 547 us; the launch traced here: 536 us
  waiting for transfers between devices  159 us (29%)
  starting transfers between devices  118 us (22%)
  local copies, waits for them, and re-layouts  97.2 us (18%)
  other arithmetic  70 us (13%)
  matrix products  55.3 us (10%)
  blocking collectives  33.7 us (6%)
    all_to_all x3, waiting for transfers between devices, spread(): return lax.all_to_all(copies, CHIPS, 0, 0, tiled=True)  62.7 us
    dot_general x36, matrix products, ein(): return jnp.einsum(form, a, b, preferred_element_type=F32)  55.3 us
    all_to_all x2, waiting for transfers between devices, reduce_layer(): lax.all_to_all(mf, CHIPS, 0, 0, tiled=True).astype(F32)  44.4 us
    ppermute x24, starting transfers between devices, sum_over_x(): lax.ppermute(part, 'x', [(i, i ^ k) for i in range(4)]).astype(F32)  26.9 us
    all_to_all x2, waiting for transfers between devices, forward(): lax.all_to_all(jnp.broadcast_to(kv, (16, *kv.shape)), TOKENS, 0, 0, tiled...  23.8 us
    all_to_all x1, blocking collectives, reduce_layer(): lax.all_to_all(ma, CHIPS, 0, 0, tiled=True).astype(F32)  22.1 us
    concatenate x8, local copies, waits for them, and re-layouts, backward(): dkv = jnp.concatenate([dk, dv], axis=-1).astype(BF).reshape(4, 16, 64, 128)  18.5 us
    all_to_all x3, starting transfers between devices, spread(): return lax.all_to_all(copies, CHIPS, 0, 0, tiled=True)  18.4 us
  transfers between devices with their start and end apart: 46, of which 21 were waited for; matrix products, arithmetic and copies ran while one was open for 32% of the time, Pallas kernels for 0%

profile of v1, /device:TPU:1, one launch (start us, length us, event | category | flops | bytes accessed | tf_op | source)
XLA Modules:
  0.0 535.9 jit_solution(14736263070664716533)
XLA Ops:
  6.6 5.1 all_to_all.75
  13.1 7.9 %all-to-all-start.1 = ((bf16[16,144,256]{2,1,0:T(8,128)(2,1)}), bf16[16,144,256]{2,1,0:T(8,128)(2,1)S(1)}, u32[]{:S(2)}, u32[]{:S(2)}) async-start(bf16[16,144,256]{2,1,0:T(8,128)(2,1)} %broadcast_in_dim.57), calls=%async_computation.1 | async-start | bytes 2359296 | tf_op jit(solution)/shard_map/all_to_all | solution.py:23
  22.0 17.2 %all-to-all-done.1 = bf16[16,144,256]{2,1,0:T(8,128)(2,1)S(1)} async-done(((bf16[16,144,256]{2,1,0:T(8,128)(2,1)}), bf16[16,144,256]{2,1,0:T(8,128)(2,1)S(1)}, u32[]{:S(2)}, u32[]{:S(2)}) %all-to-all-start.1) | async-done | bytes 1179680 | tf_op jit(solution)/shard_map/all_to_all | solution.py:23
  40.8 5.1 all-to-all-start.3
  57.0 18.2 %all-to-all-done.3 = bf16[16,128,512]{2,1,0:T(8,128)(2,1)S(1)} async-done(((bf16[16,128,512]{2,1,0:T(8,128)(2,1)}), bf16[16,128,512]{2,1,0:T(8,128)(2,1)S(1)}, u32[]{:S(2)}, u32[]{:S(2)}) %all-to-all-start.3) | async-done | bytes 2097184 | tf_op jit(solution)/shard_map/all_to_all | solution.py:23
  76.5 6.2 %all-to-all-start.2 = ((bf16[16,4,64,128]{3,2,1,0:T(8,128)(2,1)}), bf16[16,4,64,128]{3,2,1,0:T(8,128)(2,1)S(1)}, u32[]{:S(2)}, u32[]{:S(2)}) async-start(bf16[16,4,64,128]{3,2,1,0:T(8,128)(2,1)} %broadcast_in_dim.58), calls=%async_computation.2 | async-start | bytes 2097152 | tf_op jit(solution)/shard_map/all_to_all | solution.py:76
  84.3 12.4 %all-to-all-done.2 = bf16[16,4,64,128]{3,2,1,0:T(8,128)(2,1)S(1)} async-done(((bf16[16,4,64,128]{3,2,1,0:T(8,128)(2,1)}), bf16[16,4,64,128]{3,2,1,0:T(8,128)(2,1)S(1)}, u32[]{:S(2)}, u32[]{:S(2)}) %all-to-all-start.2) | async-done | bytes 1048608 | tf_op jit(solution)/shard_map/all_to_all | solution.py:76
  96.7 3.1 broadcast_in_dim.61
  99.8 5.5 %all-to-all-start.4 = ((bf16[16,128,768]{2,1,0:T(8,128)(2,1)}), bf16[16,128,768]{2,1,0:T(8,128)(2,1)}, u32[]{:S(2)}, u32[]{:S(2)}) async-start(bf16[16,128,768]{2,1,0:T(8,128)(2,1)} %broadcast_in_dim.61), calls=%async_computation.4 | async-start | bytes 6291456 | tf_op jit(solution)/shard_map/all_to_all | solution.py:23
  106.5 2.5 collective-permute-start.4
  112.9 2.8 convolution_convert_fusion.9
  115.9 2.6 collective-permute-start.3
  119.5 27.3 %all-to-all-done.4 = bf16[16,128,768]{2,1,0:T(8,128)(2,1)} async-done(((bf16[16,128,768]{2,1,0:T(8,128)(2,1)}), bf16[16,128,768]{2,1,0:T(8,128)(2,1)}, u32[]{:S(2)}, u32[]{:S(2)}) %all-to-all-start.4) | async-done | bytes 3145760 | tf_op jit(solution)/shard_map/all_to_all | solution.py:23
  146.8 2.3 slice.356
  149.1 2.3 copy.262
  151.4 3.6 collective-permute-start.8
  160.6 2.6 collective-permute-start.7
  164.0 3.3 slice.372
  173.6 8.6 %all-to-all-start.5 = ((bf16[16,4,64,128]{3,2,1,0:T(8,128)(2,1)}), bf16[16,4,64,128]{3,2,1,0:T(8,128)(2,1)}, u32[]{:S(2)}, u32[]{:S(2)}) async-start(bf16[16,4,64,128]{3,2,1,0:T(8,128)(2,1)} %broadcast_in_dim.62), calls=%async_computation.5 | async-start | bytes 2097152 | tf_op jit(solution)/shard_map/all_to_all | solution.py:76
  185.1 11.5 %all-to-all-done.5 = bf16[16,4,64,128]{3,2,1,0:T(8,128)(2,1)} async-done(((bf16[16,4,64,128]{3,2,1,0:T(8,128)(2,1)}), bf16[16,4,64,128]{3,2,1,0:T(8,128)(2,1)}, u32[]{:S(2)}, u32[]{:S(2)}) %all-to-all-start.5) | async-done | bytes 1048608 | tf_op jit(solution)/shard_map/all_to_all | solution.py:76
  201.3 3.5 convolution_convert_fusion.8
  205.9 2.6 collective-permute-start.11
  214.9 2.7 convert_reduce_fusion.8
  232.7 3.3 collective-permute-done.13
  239.1 2.3 convolution_convert_fusion.3
  243.0 2.6 copy.272
  245.6 2.4 multiply_reduce_fusion.1
  251.1 2.5 copy.271
  253.6 3.2 maximum_bitcast_fusion
  256.8 5.6 %all-to-all-start.7 = ((bf16[16,4,64,128]{3,2,1,0:T(8,128)(2,1)}), bf16[16,4,64,128]{3,2,1,0:T(8,128)(2,1)}, u32[]{:S(2)}, u32[]{:S(2)}) async-start(bf16[16,4,64,128]{3,2,1,0:T(8,128)(2,1)} %maximum_bitcast_fusion), calls=%async_computation.7 | async-start | bytes 2097152 | tf_op jit(solution)/shard_map/all_to_all | solution.py:120
  262.4 4.5 pad_maximum_fusion
  266.9 5.4 %copy.305 = f32[2,1024,512]{2,1,0:T(8,128)} copy(f32[2,1024,512]{1,2,0:T(8,128)} %get-tuple-element.94) | data formatting | bytes 8388608 | tf_op jit(solution)/shard_map/convert_element_type | solution.py:162
  272.2 4.0 copy.306
  276.3 4.4 collective-permute-start.33
  286.4 2.6 fusion.34
  294.4 3.6 pad_maximum_fusion.4
  299.3 2.9 copy.295
  302.2 2.3 copy.296
  310.0 2.5 convert_reduce_fusion.11
  326.9 2.4 multiply_reduce_fusion
  329.3 2.9 convolution_convert_fusion.2
  332.2 2.6 concatenate.124
  334.8 2.5 copy.278
  340.7 2.6 concatenate.123
  343.3 2.5 copy.277
  345.8 2.8 maximum_bitcast_fusion.1
  348.6 6.9 %all-to-all-start.8 = ((bf16[16,4,64,128]{3,2,1,0:T(8,128)(2,1)}), bf16[16,4,64,128]{3,2,1,0:T(8,128)(2,1)}, u32[]{:S(2)}, u32[]{:S(2)}) async-start(bf16[16,4,64,128]{3,2,1,0:T(8,128)(2,1)} %maximum_bitcast_fusion.1), calls=%async_computation.8 | async-start | bytes 2097152 | tf_op jit(solution)/shard_map/all_to_all | solution.py:120
  355.5 4.2 pad_maximum_fusion.1
  360.4 4.1 copy.293
  367.8 2.5 all-to-all-done.8
  372.1 6.8 %all-to-all-start.6 = ((bf16[4,64,1024]{2,1,0:T(8,128)(2,1)}), bf16[4,64,1024]{2,1,0:T(8,128)(2,1)S(1)}, u32[]{:S(2)}, u32[]{:S(2)}) async-start(bf16[4,64,1024]{2,1,0:T(8,128)(2,1)} %bitcast.72), calls=%async_computation.6 | async-start | bytes 1048576 | tf_op jit(solution)/shard_map/all_to_all | solution.py:214
  385.5 3.9 add_convert_fusion
  393.6 5.5 %all-to-all-start.9 = ((bf16[4,64,1024]{2,1,0:T(8,128)(2,1)}), bf16[4,64,1024]{2,1,0:T(8,128)(2,1)S(1)}, u32[]{:S(2)}, u32[]{:S(2)}) async-start(bf16[4,64,1024]{2,1,0:T(8,128)(2,1)} %bitcast.89), calls=%async_computation.9 | async-start | bytes 1048576 | tf_op jit(solution)/shard_map/all_to_all | solution.py:214
  400.8 7.8 %all-to-all-done.9 = bf16[4,64,1024]{2,1,0:T(8,128)(2,1)S(1)} async-done(((bf16[4,64,1024]{2,1,0:T(8,128)(2,1)}), bf16[4,64,1024]{2,1,0:T(8,128)(2,1)S(1)}, u32[]{:S(2)}, u32[]{:S(2)}) %all-to-all-start.9) | async-done | bytes 524320 | tf_op jit(solution)/shard_map/all_to_all | solution.py:214
  409.4 4.7 all-to-all-start.13
  425.6 18.6 %all-to-all-done.13 = bf16[16,128,512]{2,1,0:T(8,128)(2,1)} async-done(((bf16[16,128,512]{2,1,0:T(8,128)(2,1)}), bf16[16,128,512]{2,1,0:T(8,128)(2,1)}, u32[]{:S(2)}, u32[]{:S(2)}) %all-to-all-start.13) | async-done | bytes 2097184 | tf_op jit(solution)/shard_map/all_to_all | solution.py:163
  444.2 22.1 %all_to_all.76 = bf16[16,144,256]{2,1,0:T(8,128)(2,1)S(1)} all-to-all(bf16[16,144,256]{2,1,0:T(8,128)(2,1)S(1)} %get-tuple-element.129), channel_id=1, replica_groups=mesh['s'=2,'z'=4,'yl'=2,'yh'=2,'x'=4] {'yh','z','yl'}, dimensions={0} | all-to-all | bytes 2359296 | tf_op jit(solution)/shard_map/all_to_all | solution.py:167
  466.4 3.7 all-to-all-start.10
  470.1 5.4 %copy.292 = f32[2,1024,512]{2,1,0:T(8,128)} copy(f32[2,1024,512]{1,2,0:T(8,128)} %get-tuple-element.92) | data formatting | bytes 8388608 | tf_op jit(solution)/shard_map/convert_element_type | solution.py:162
  475.4 4.9 add_convert_fusion.1
  480.4 5.0 all-to-all-done.10
  486.4 7.7 %all-to-all-start.11 = ((bf16[16,128,512]{2,1,0:T(8,128)(2,1)}), bf16[16,128,512]{2,1,0:T(8,128)(2,1)S(1)}, u32[]{:S(2)}, u32[]{:S(2)}) async-start(bf16[16,128,512]{2,1,0:T(8,128)(2,1)} %add_convert_fusion.1), calls=%async_computation.11 | async-start | bytes 4194304 | tf_op jit(solution)/shard_map/all_to_all | solution.py:163
  497.7 25.7 %all-to-all-done.11 = bf16[16,128,512]{2,1,0:T(8,128)(2,1)S(1)} async-done(((bf16[16,128,512]{2,1,0:T(8,128)(2,1)}), bf16[16,128,512]{2,1,0:T(8,128)(2,1)S(1)}, u32[]{:S(2)}, u32[]{:S(2)}) %all-to-all-start.11) | async-done | bytes 2097184 | tf_op jit(solution)/shard_map/all_to_all | solution.py:163
  523.8 6.4 %all_to_all.77 = f32[2,128,768]{2,1,0:T(8,128)S(1)} all-to-all(f32[2,128,768]{2,1,0:T(8,128)S(1)} %pad_maximum_fusion.6), channel_id=1, replica_groups=mesh['s'=2,'z'=4,'yl'=2,'yh'=2,'x'=4] {'s'}, dimensions={0} | all-to-all | bytes 1572864 | tf_op jit(solution)/shard_map/all_to_all | solution.py:223
  (466 shorter events, 155.9 us)
Async XLA Ops:
  11.7 10.2 %copy-start.33 = (bf16[2,144,768]{2,1,0:T(8,128)(2,1)}, bf16[2,144,768]{2,1,0:T(8,128)(2,1)S(1)}, u32[]{:S(2)}) copy-start(bf16[2,144,768]{2,1,0:T(8,128)(2,1)S(1)} %all_to_all.75) | copy-start | bytes 1327108
  13.1 26.2 %all-to-all-start.1 = ((bf16[16,144,256]{2,1,0:T(8,128)(2,1)}), bf16[16,144,256]{2,1,0:T(8,128)(2,1)S(1)}, u32[]{:S(2)}, u32[]{:S(2)}) async-start(bf16[16,144,256]{2,1,0:T(8,128)(2,1)} %broadcast_in_dim.57), calls=%async_computation.1 | async-start | bytes 2359296 | tf_op jit(solution)/shard_map/all_to_all | solution.py:23
  40.8 34.5 %all-to-all-start.3 = ((bf16[16,128,512]{2,1,0:T(8,128)(2,1)}), bf16[16,128,512]{2,1,0:T(8,128)(2,1)S(1)}, u32[]{:S(2)}, u32[]{:S(2)}) async-start(bf16[16,128,512]{2,1,0:T(8,128)(2,1)} %broadcast_in_dim.60), calls=%async_computation.3 | async-start | bytes 4194304 | tf_op jit(solution)/shard_map/all_to_all | solution.py:23
  50.9 3.9 collective-permute-start
  53.6 104.2 %copy-start.51 = (f32[1,8,128]{2,0,1:T(1,128)}, f32[1,8,128]{2,0,1:T(1,128)S(1)}, u32[]{:S(2)}) copy-start(f32[1,8,128]{2,0,1:T(1,128)S(1)} %get-tuple-element.145) | copy-start | bytes 12292
  53.6 117.0 %copy-start.60 = (f32[1,8,128]{2,0,1:T(1,128)}, f32[1,8,128]{2,0,1:T(1,128)S(1)}, u32[]{:S(2)}) copy-start(f32[1,8,128]{2,0,1:T(1,128)S(1)} %get-tuple-element.112) | copy-start | bytes 12292
  56.8 53.4 %copy-start.36 = (f32[4,64,192]{2,1,0:T(8,128)}, f32[4,64,192]{2,1,0:T(8,128)S(1)}, u32[]{:S(2)}) copy-start(f32[4,64,192]{2,1,0:T(8,128)S(1)} %convolution_bitcast_fusion.11) | copy-start | bytes 589828
  76.5 20.2 %all-to-all-start.2 = ((bf16[16,4,64,128]{3,2,1,0:T(8,128)(2,1)}), bf16[16,4,64,128]{3,2,1,0:T(8,128)(2,1)S(1)}, u32[]{:S(2)}, u32[]{:S(2)}) async-start(bf16[16,4,64,128]{3,2,1,0:T(8,128)(2,1)} %broadcast_in_dim.58), calls=%async_computation.2 | async-start | bytes 2097152 | tf_op jit(solution)/shard_map/all_to_all | solution.py:76
  99.8 47.0 %all-to-all-start.4 = ((bf16[16,128,768]{2,1,0:T(8,128)(2,1)}), bf16[16,128,768]{2,1,0:T(8,128)(2,1)}, u32[]{:S(2)}, u32[]{:S(2)}) async-start(bf16[16,128,768]{2,1,0:T(8,128)(2,1)} %broadcast_in_dim.61), calls=%async_computation.4 | async-start | bytes 6291456 | tf_op jit(solution)/shard_map/all_to_all | solution.py:23
  106.5 49.9 %collective-permute-start.4 = (bf16[2,1024,512]{2,1,0:T(8,128)(2,1)S(1)}, bf16[2,1024,512]{2,1,0:T(8,128)(2,1)}, u32[]{:S(2)}, u32[]{:S(2)}) collective-permute-start(bf16[2,1024,512]{2,1,0:T(8,128)(2,1)S(1)} %bitcast.361), channel_id=1, source_target_pairs={{0,64},{64,0},{1,65},{65,1},{2,66},{66,2},{3,67},{67,3},{4,68},{68... | collective-permute-start | bytes 6291464 | tf_op jit(solution)/shard_map/ppermute | solution.py:18
  115.7 35.7 %copy-start.46 = (bf16[4,64,64]{2,1,0:T(8,128)(2,1)}, bf16[4,64,64]{2,1,0:T(8,128)(2,1)S(1)}, u32[]{:S(2)}) copy-start(bf16[4,64,64]{2,1,0:T(8,128)(2,1)S(1)} %convolution_convert_fusion.9) | copy-start | bytes 98308
  115.9 39.1 %collective-permute-start.3 = (bf16[64,1024]{1,0:T(8,128)(2,1)S(1)}, bf16[64,1024]{1,0:T(8,128)(2,1)S(1)}, u32[]{:S(2)}, u32[]{:S(2)}) collective-permute-start(bf16[64,1024]{1,0:T(8,128)(2,1)S(1)} %fusion.32), channel_id=1, source_target_pairs={{0,3},{1,2},{2,1},{3,0},{4,7},{5,6},{6,5},{7,4},{8,11},{9,10},{10,... | collective-permute-start | bytes 393224 | tf_op jit(solution)/shard_map/ppermute | solution.py:28
  118.5 36.5 %collective-permute-start.2 = (bf16[64,1024]{1,0:T(8,128)(2,1)S(1)}, bf16[64,1024]{1,0:T(8,128)(2,1)S(1)}, u32[]{:S(2)}, u32[]{:S(2)}) collective-permute-start(bf16[64,1024]{1,0:T(8,128)(2,1)S(1)} %fusion.32), channel_id=1, source_target_pairs={{0,2},{1,3},{2,0},{3,1},{4,6},{5,7},{6,4},{7,5},{8,10},{9,11},{10,... | collective-permute-start | bytes 393224 | tf_op jit(solution)/shard_map/ppermute | solution.py:28
  119.0 36.0 %collective-permute-start.1 = (bf16[64,1024]{1,0:T(8,128)(2,1)S(1)}, bf16[64,1024]{1,0:T(8,128)(2,1)S(1)}, u32[]{:S(2)}, u32[]{:S(2)}) collective-permute-start(bf16[64,1024]{1,0:T(8,128)(2,1)S(1)} %fusion.32), channel_id=1, source_target_pairs={{0,1},{1,0},{2,3},{3,2},{4,5},{5,4},{6,7},{7,6},{8,9},{9,8},{10,11... | collective-permute-start | bytes 393224 | tf_op jit(solution)/shard_map/ppermute | solution.py:28
  151.4 19.2 %collective-permute-start.8 = (bf16[2,1024,256]{1,2,0:T(8,128)(2,1)}, bf16[2,1024,256]{1,2,0:T(8,128)(2,1)S(1)}, u32[]{:S(2)}, u32[]{:S(2)}) collective-permute-start(bf16[2,1024,256]{1,2,0:T(8,128)(2,1)} %copy.262), channel_id=1, source_target_pairs={{0,64},{64,0},{1,65},{65,1},{2,66},{66,2},{3,67},{67,3},{4,68},{68... | collective-permute-start | bytes 3145736 | tf_op jit(solution)/shard_map/ppermute | solution.py:18
  160.6 8.1 %collective-permute-start.7 = (bf16[64,1024]{1,0:T(8,128)(2,1)S(1)}, bf16[64,1024]{1,0:T(8,128)(2,1)S(1)}, u32[]{:S(2)}, u32[]{:S(2)}) collective-permute-start(bf16[64,1024]{1,0:T(8,128)(2,1)S(1)} %fusion.26), channel_id=1, source_target_pairs={{0,3},{1,2},{2,1},{3,0},{4,7},{5,6},{6,5},{7,4},{8,11},{9,10},{10,... | collective-permute-start | bytes 393224 | tf_op jit(solution)/shard_map/ppermute | solution.py:28
  163.2 6.3 %collective-permute-start.6 = (bf16[64,1024]{1,0:T(8,128)(2,1)S(1)}, bf16[64,1024]{1,0:T(8,128)(2,1)S(1)}, u32[]{:S(2)}, u32[]{:S(2)}) collective-permute-start(bf16[64,1024]{1,0:T(8,128)(2,1)S(1)} %fusion.26), channel_id=1, source_target_pairs={{0,2},{1,3},{2,0},{3,1},{4,6},{5,7},{6,4},{7,5},{8,10},{9,11},{10,... | collective-permute-start | bytes 393224 | tf_op jit(solution)/shard_map/ppermute | solution.py:28
  163.7 6.4 %collective-permute-start.5 = (bf16[64,1024]{1,0:T(8,128)(2,1)S(1)}, bf16[64,1024]{1,0:T(8,128)(2,1)S(1)}, u32[]{:S(2)}, u32[]{:S(2)}) collective-permute-start(bf16[64,1024]{1,0:T(8,128)(2,1)S(1)} %fusion.26), channel_id=1, source_target_pairs={{0,1},{1,0},{2,3},{3,2},{4,5},{5,4},{6,7},{7,6},{8,9},{9,8},{10,11... | collective-permute-start | bytes 393224 | tf_op jit(solution)/shard_map/ppermute | solution.py:28
  167.2 42.0 %collective-permute-start.12 = (bf16[2,1024,512]{2,1,0:T(8,128)(2,1)}, bf16[2,1024,512]{2,1,0:T(8,128)(2,1)}, u32[]{:S(2)}, u32[]{:S(2)}) collective-permute-start(bf16[2,1024,512]{2,1,0:T(8,128)(2,1)} %bitcast.63), channel_id=1, source_target_pairs={{0,64},{64,0},{1,65},{65,1},{2,66},{66,2},{3,67},{67,3},{4,68},{68... | collective-permute-start | bytes 6291464 | tf_op jit(solution)/shard_map/ppermute | solution.py:18
  173.6 23.0 %all-to-all-start.5 = ((bf16[16,4,64,128]{3,2,1,0:T(8,128)(2,1)}), bf16[16,4,64,128]{3,2,1,0:T(8,128)(2,1)}, u32[]{:S(2)}, u32[]{:S(2)}) async-start(bf16[16,4,64,128]{3,2,1,0:T(8,128)(2,1)} %broadcast_in_dim.62), calls=%async_computation.5 | async-start | bytes 2097152 | tf_op jit(solution)/shard_map/all_to_all | solution.py:76
  205.9 8.0 %copy-start.63 = (f32[1,8,128]{2,0,1:T(1,128)S(1)}, f32[1,8,128]{2,0,1:T(1,128)}, u32[]{:S(2)}) copy-start(f32[1,8,128]{2,0,1:T(1,128)} %get-tuple-element.111) | copy-start | bytes 12292
  205.9 8.4 %copy-start.53 = (f32[1,8,128]{2,0,1:T(1,128)S(1)}, f32[1,8,128]{2,0,1:T(1,128)}, u32[]{:S(2)}) copy-start(f32[1,8,128]{2,0,1:T(1,128)} %get-tuple-element.109) | copy-start | bytes 12292
  205.9 8.4 %copy-start.71 = (f32[4,256]{1,0:T(4,128)S(1)}, f32[4,256]{1,0:T(4,128)}, u32[]{:S(2)}) copy-start(f32[4,256]{1,0:T(4,128)} %add.410) | copy-start | bytes 12292
  205.9 5.9 %collective-permute-start.11 = (bf16[64,1024]{1,0:T(8,128)(2,1)S(1)}, bf16[64,1024]{1,0:T(8,128)(2,1)S(1)}, u32[]{:S(2)}, u32[]{:S(2)}) collective-permute-start(bf16[64,1024]{1,0:T(8,128)(2,1)S(1)} %fusion.33), channel_id=1, source_target_pairs={{0,3},{1,2},{2,1},{3,0},{4,7},{5,6},{6,5},{7,4},{8,11},{9,10},{10,... | collective-permute-start | bytes 393224 | tf_op jit(solution)/shard_map/ppermute | solution.py:28
  208.5 5.4 %collective-permute-start.10 = (bf16[64,1024]{1,0:T(8,128)(2,1)S(1)}, bf16[64,1024]{1,0:T(8,128)(2,1)S(1)}, u32[]{:S(2)}, u32[]{:S(2)}) collective-permute-start(bf16[64,1024]{1,0:T(8,128)(2,1)S(1)} %fusion.33), channel_id=1, source_target_pairs={{0,2},{1,3},{2,0},{3,1},{4,6},{5,7},{6,4},{7,5},{8,10},{9,11},{10,... | collective-permute-start | bytes 393224 | tf_op jit(solution)/shard_map/ppermute | solution.py:28
  209.1 4.9 collective-permute-start.9
  218.3 12.3 %collective-permute-start.18 = (bf16[64,1024]{1,0:T(8,128)(2,1)S(1)}, bf16[64,1024]{1,0:T(8,128)(2,1)S(1)}, u32[]{:S(2)}, u32[]{:S(2)}) collective-permute-start(bf16[64,1024]{1,0:T(8,128)(2,1)S(1)} %fusion.28), channel_id=1, source_target_pairs={{0,3},{1,2},{2,1},{3,0},{4,7},{5,6},{6,5},{7,4},{8,11},{9,10},{10,... | collective-permute-start | bytes 393224 | tf_op jit(solution)/shard_map/ppermute | solution.py:28
  220.3 11.3 %collective-permute-start.17 = (bf16[64,1024]{1,0:T(8,128)(2,1)S(1)}, bf16[64,1024]{1,0:T(8,128)(2,1)S(1)}, u32[]{:S(2)}, u32[]{:S(2)}) collective-permute-start(bf16[64,1024]{1,0:T(8,128)(2,1)S(1)} %fusion.28), channel_id=1, source_target_pairs={{0,2},{1,3},{2,0},{3,1},{4,6},{5,7},{6,4},{7,5},{8,10},{9,11},{10,... | collective-permute-start | bytes 393224 | tf_op jit(solution)/shard_map/ppermute | solution.py:28
  220.8 10.8 %collective-permute-start.16 = (bf16[64,1024]{1,0:T(8,128)(2,1)S(1)}, bf16[64,1024]{1,0:T(8,128)(2,1)S(1)}, u32[]{:S(2)}, u32[]{:S(2)}) collective-permute-start(bf16[64,1024]{1,0:T(8,128)(2,1)S(1)} %fusion.28), channel_id=1, source_target_pairs={{0,1},{1,0},{2,3},{3,2},{4,5},{5,4},{6,7},{7,6},{8,9},{9,8},{10,11... | collective-permute-start | bytes 393224 | tf_op jit(solution)/shard_map/ppermute | solution.py:28
  224.0 8.4 %collective-permute-start.15 = (bf16[64,1024]{1,0:T(8,128)(2,1)S(1)}, bf16[64,1024]{1,0:T(8,128)(2,1)S(1)}, u32[]{:S(2)}, u32[]{:S(2)}) collective-permute-start(bf16[64,1024]{1,0:T(8,128)(2,1)S(1)} %fusion.27), channel_id=1, source_target_pairs={{0,3},{1,2},{2,1},{3,0},{4,7},{5,6},{6,5},{7,4},{8,11},{9,10},{10,... | collective-permute-start | bytes 393224 | tf_op jit(solution)/shard_map/ppermute | solution.py:28
  225.9 6.8 %collective-permute-start.14 = (bf16[64,1024]{1,0:T(8,128)(2,1)S(1)}, bf16[64,1024]{1,0:T(8,128)(2,1)S(1)}, u32[]{:S(2)}, u32[]{:S(2)}) collective-permute-start(bf16[64,1024]{1,0:T(8,128)(2,1)S(1)} %fusion.27), channel_id=1, source_target_pairs={{0,2},{1,3},{2,0},{3,1},{4,6},{5,7},{6,4},{7,5},{8,10},{9,11},{10,... | collective-permute-start | bytes 393224 | tf_op jit(solution)/shard_map/ppermute | solution.py:28
  228.6 7.5 %copy-start.62 = (f32[1,8,128]{2,0,1:T(1,128)S(1)}, f32[1,8,128]{2,0,1:T(1,128)}, u32[]{:S(2)}) copy-start(f32[1,8,128]{2,0,1:T(1,128)} %get-tuple-element.108) | copy-start | bytes 12292
  230.7 5.4 %collective-permute-start.13 = (bf16[64,1024]{1,0:T(8,128)(2,1)S(1)}, bf16[64,1024]{1,0:T(8,128)(2,1)S(1)}, u32[]{:S(2)}, u32[]{:S(2)}) collective-permute-start(bf16[64,1024]{1,0:T(8,128)(2,1)S(1)} %fusion.27), channel_id=1, source_target_pairs={{0,1},{1,0},{2,3},{3,2},{4,5},{5,4},{6,7},{7,6},{8,9},{9,8},{10,11... | collective-permute-start | bytes 393224 | tf_op jit(solution)/shard_map/ppermute | solution.py:28
  256.8 28.1 %all-to-all-start.7 = ((bf16[16,4,64,128]{3,2,1,0:T(8,128)(2,1)}), bf16[16,4,64,128]{3,2,1,0:T(8,128)(2,1)}, u32[]{:S(2)}, u32[]{:S(2)}) async-start(bf16[16,4,64,128]{3,2,1,0:T(8,128)(2,1)} %maximum_bitcast_fusion), calls=%async_computation.7 | async-start | bytes 2097152 | tf_op jit(solution)/shard_map/all_to_all | solution.py:120
  272.2 8.4 %copy-start.90 = (bf16[4,256]{1,0:T(4,128)(2,1)S(1)}, bf16[4,256]{1,0:T(4,128)(2,1)}, u32[]{:S(2)}) copy-start(bf16[4,256]{1,0:T(4,128)(2,1)} %get-tuple-element.140) | copy-start | bytes 6148
  272.2 9.1 %copy-start.43 = (bf16[1,64,1024]{2,1,0:T(8,128)(2,1)S(1)}, bf16[1,64,1024]{2,1,0:T(8,128)(2,1)}, u32[]{:S(2)}) copy-start(bf16[1,64,1024]{2,1,0:T(8,128)(2,1)} %get-tuple-element.103) | copy-start | bytes 393220
  272.2 9.9 %copy-start.17 = (f32[64,1024]{1,0:T(8,128)S(1)}, f32[64,1024]{1,0:T(8,128)}, u32[]{:S(2)}) copy-start(f32[64,1024]{1,0:T(8,128)} %copy-done.16) | copy-start | bytes 786436
  272.2 9.9 %copy-start.48 = (bf16[4,64,64]{2,1,0:T(8,128)(2,1)S(1)}, bf16[4,64,64]{2,1,0:T(8,128)(2,1)}, u32[]{:S(2)}) copy-start(bf16[4,64,64]{2,1,0:T(8,128)(2,1)} %convolution_convert_fusion.8) | copy-start | bytes 98308
  276.3 108.3 %collective-permute-start.33 = (bf16[16,128,512]{2,1,0:T(8,128)(2,1)}, bf16[16,128,512]{2,1,0:T(8,128)(2,1)}, u32[]{:S(2)}, u32[]{:S(2)}) collective-permute-start(bf16[16,128,512]{2,1,0:T(8,128)(2,1)} %bitcast.381), channel_id=1, source_target_pairs={{0,64},{64,0},{1,65},{65,1},{2,66},{66,2},{3,67},{67,3},{4,68},{68... | collective-permute-start | bytes 6291464 | tf_op jit(solution)/shard_map/ppermute | solution.py:18
  289.0 17.7 %collective-permute-start.21 = (bf16[64,1024]{1,0:T(8,128)(2,1)}, bf16[64,1024]{1,0:T(8,128)(2,1)}, u32[]{:S(2)}, u32[]{:S(2)}) collective-permute-start(bf16[64,1024]{1,0:T(8,128)(2,1)} %fusion.34), channel_id=1, source_target_pairs={{0,3},{1,2},{2,1},{3,0},{4,7},{5,6},{6,5},{7,4},{8,11},{9,10},{10,... | collective-permute-start | bytes 393224 | tf_op jit(solution)/shard_map/ppermute | solution.py:28
  290.8 15.9 %collective-permute-start.20 = (bf16[64,1024]{1,0:T(8,128)(2,1)}, bf16[64,1024]{1,0:T(8,128)(2,1)}, u32[]{:S(2)}, u32[]{:S(2)}) collective-permute-start(bf16[64,1024]{1,0:T(8,128)(2,1)} %fusion.34), channel_id=1, source_target_pairs={{0,2},{1,3},{2,0},{3,1},{4,6},{5,7},{6,4},{7,5},{8,10},{9,11},{10,... | collective-permute-start | bytes 393224 | tf_op jit(solution)/shard_map/ppermute | solution.py:28
  291.8 14.9 %collective-permute-start.19 = (bf16[64,1024]{1,0:T(8,128)(2,1)}, bf16[64,1024]{1,0:T(8,128)(2,1)}, u32[]{:S(2)}, u32[]{:S(2)}) collective-permute-start(bf16[64,1024]{1,0:T(8,128)(2,1)} %fusion.34), channel_id=1, source_target_pairs={{0,1},{1,0},{2,3},{3,2},{4,5},{5,4},{6,7},{7,6},{8,9},{9,8},{10,11... | collective-permute-start | bytes 393224 | tf_op jit(solution)/shard_map/ppermute | solution.py:28
  302.2 7.8 %copy-start.23 = (f32[4,64,256]{2,1,0:T(8,128)S(1)}, f32[4,64,256]{2,1,0:T(8,128)}, u32[]{:S(2)}) copy-start(f32[4,64,256]{2,1,0:T(8,128)} %copy-done.22) | copy-start | bytes 786436
  304.5 114.1 %collective-permute-start.31 = (bf16[16,128,256]{2,1,0:T(8,128)(2,1)}, bf16[16,128,256]{2,1,0:T(8,128)(2,1)}, u32[]{:S(2)}, u32[]{:S(2)}) collective-permute-start(bf16[16,128,256]{2,1,0:T(8,128)(2,1)} %bitcast.385), channel_id=1, source_target_pairs={{0,64},{64,0},{1,65},{65,1},{2,66},{66,2},{3,67},{67,3},{4,68},{68... | collective-permute-start | bytes 3145736 | tf_op jit(solution)/shard_map/ppermute | solution.py:18
  310.0 7.6 %copy-start.27 = (bf16[64,1024]{1,0:T(8,128)(2,1)}, bf16[64,1024]{1,0:T(8,128)(2,1)S(1)}, u32[]{:S(2)}) copy-start(bf16[64,1024]{1,0:T(8,128)(2,1)S(1)} %get-tuple-element.76) | copy-start | bytes 393220
  313.3 8.9 %collective-permute-start.24 = (bf16[64,1024]{1,0:T(8,128)(2,1)S(1)}, bf16[64,1024]{1,0:T(8,128)(2,1)S(1)}, u32[]{:S(2)}, u32[]{:S(2)}) collective-permute-start(bf16[64,1024]{1,0:T(8,128)(2,1)S(1)} %fusion.29), channel_id=1, source_target_pairs={{0,3},{1,2},{2,1},{3,0},{4,7},{5,6},{6,5},{7,4},{8,11},{9,10},{10,... | collective-permute-start | bytes 393224 | tf_op jit(solution)/shard_map/ppermute | solution.py:28
  315.2 8.0 %collective-permute-start.23 = (bf16[64,1024]{1,0:T(8,128)(2,1)S(1)}, bf16[64,1024]{1,0:T(8,128)(2,1)}, u32[]{:S(2)}, u32[]{:S(2)}) collective-permute-start(bf16[64,1024]{1,0:T(8,128)(2,1)S(1)} %fusion.29), channel_id=1, source_target_pairs={{0,2},{1,3},{2,0},{3,1},{4,6},{5,7},{6,4},{7,5},{8,10},{9,11},{10,... | collective-permute-start | bytes 393224 | tf_op jit(solution)/shard_map/ppermute | solution.py:28
  316.2 7.0 %collective-permute-start.22 = (bf16[64,1024]{1,0:T(8,128)(2,1)S(1)}, bf16[64,1024]{1,0:T(8,128)(2,1)}, u32[]{:S(2)}, u32[]{:S(2)}) collective-permute-start(bf16[64,1024]{1,0:T(8,128)(2,1)S(1)} %fusion.29), channel_id=1, source_target_pairs={{0,1},{1,0},{2,3},{3,2},{4,5},{5,4},{6,7},{7,6},{8,9},{9,8},{10,11... | collective-permute-start | bytes 393224 | tf_op jit(solution)/shard_map/ppermute | solution.py:28
  322.1 43.5 %collective-permute-start.32 = (bf16[16,6,256]{2,1,0:T(8,128)(2,1)S(1)}, bf16[16,6,256]{2,1,0:T(8,128)(2,1)}, u32[]{:S(2)}, u32[]{:S(2)}) collective-permute-start(bf16[16,6,256]{2,1,0:T(8,128)(2,1)S(1)} %convert_element_type.448), channel_id=1, source_target_pairs={{0,64},{64,0},{1,65},{65,1},{2,66},{66,2},{3,67},{67,3},{4,68},{68... | collective-permute-start | bytes 147464 | tf_op jit(solution)/shard_map/ppermute | solution.py:18
  348.6 21.7 %all-to-all-start.8 = ((bf16[16,4,64,128]{3,2,1,0:T(8,128)(2,1)}), bf16[16,4,64,128]{3,2,1,0:T(8,128)(2,1)}, u32[]{:S(2)}, u32[]{:S(2)}) async-start(bf16[16,4,64,128]{3,2,1,0:T(8,128)(2,1)} %maximum_bitcast_fusion.1), calls=%async_computation.8 | async-start | bytes 2097152 | tf_op jit(solution)/shard_map/all_to_all | solution.py:120
  364.5 110.9 %collective-permute-start.30 = (bf16[16,128,512]{2,1,0:T(8,128)(2,1)}, bf16[16,128,512]{2,1,0:T(8,128)(2,1)}, u32[]{:S(2)}, u32[]{:S(2)}) collective-permute-start(bf16[16,128,512]{2,1,0:T(8,128)(2,1)} %bitcast.382), channel_id=1, source_target_pairs={{0,64},{64,0},{1,65},{65,1},{2,66},{66,2},{3,67},{67,3},{4,68},{68... | collective-permute-start | bytes 6291464 | tf_op jit(solution)/shard_map/ppermute | solution.py:18
  366.8 13.4 %copy-start.10 = (bf16[2,1024,256]{1,2,0:T(8,128)(2,1)S(1)}, bf16[2,1024,256]{1,2,0:T(8,128)(2,1)}, u32[]{:S(2)}) copy-start(bf16[2,1024,256]{1,2,0:T(8,128)(2,1)} %copy.254) | copy-start | bytes 3145732
  367.8 12.5 %copy-start.45 = (bf16[4,64,64]{2,1,0:T(8,128)(2,1)S(1)}, bf16[4,64,64]{2,1,0:T(8,128)(2,1)}, u32[]{:S(2)}) copy-start(bf16[4,64,64]{2,1,0:T(8,128)(2,1)} %fusion.37) | copy-start | bytes 98308
  372.1 20.6 %all-to-all-start.6 = ((bf16[4,64,1024]{2,1,0:T(8,128)(2,1)}), bf16[4,64,1024]{2,1,0:T(8,128)(2,1)S(1)}, u32[]{:S(2)}, u32[]{:S(2)}) async-start(bf16[4,64,1024]{2,1,0:T(8,128)(2,1)} %bitcast.72), calls=%async_computation.6 | async-start | bytes 1048576 | tf_op jit(solution)/shard_map/all_to_all | solution.py:214
  382.1 8.7 %collective-permute-start.27 = (bf16[64,1024]{1,0:T(8,128)(2,1)S(1)}, bf16[64,1024]{1,0:T(8,128)(2,1)S(1)}, u32[]{:S(2)}, u32[]{:S(2)}) collective-permute-start(bf16[64,1024]{1,0:T(8,128)(2,1)S(1)} %fusion.35), channel_id=1, source_target_pairs={{0,3},{1,2},{2,1},{3,0},{4,7},{5,6},{6,5},{7,4},{8,11},{9,10},{10,... | collective-permute-start | bytes 393224 | tf_op jit(solution)/shard_map/ppermute | solution.py:28
  384.1 6.7 %collective-permute-start.26 = (bf16[64,1024]{1,0:T(8,128)(2,1)S(1)}, bf16[64,1024]{1,0:T(8,128)(2,1)S(1)}, u32[]{:S(2)}, u32[]{:S(2)}) collective-permute-start(bf16[64,1024]{1,0:T(8,128)(2,1)S(1)} %fusion.35), channel_id=1, source_target_pairs={{0,2},{1,3},{2,0},{3,1},{4,6},{5,7},{6,4},{7,5},{8,10},{9,11},{10,... | collective-permute-start | bytes 393224 | tf_op jit(solution)/shard_map/ppermute | solution.py:28
  384.6 7.0 %collective-permute-start.25 = (bf16[64,1024]{1,0:T(8,128)(2,1)S(1)}, bf16[64,1024]{1,0:T(8,128)(2,1)S(1)}, u32[]{:S(2)}, u32[]{:S(2)}) collective-permute-start(bf16[64,1024]{1,0:T(8,128)(2,1)S(1)} %fusion.35), channel_id=1, source_target_pairs={{0,1},{1,0},{2,3},{3,2},{4,5},{5,4},{6,7},{7,6},{8,9},{9,8},{10,11... | collective-permute-start | bytes 393224 | tf_op jit(solution)/shard_map/ppermute | solution.py:28
  389.3 9.8 %copy-start.59 = (f32[1,8,128]{2,0,1:T(1,128)S(1)}, f32[1,8,128]{2,0,1:T(1,128)}, u32[]{:S(2)}) copy-start(f32[1,8,128]{2,0,1:T(1,128)} %copy-done.58) | copy-start | bytes 12292
  393.6 15.0 %all-to-all-start.9 = ((bf16[4,64,1024]{2,1,0:T(8,128)(2,1)}), bf16[4,64,1024]{2,1,0:T(8,128)(2,1)S(1)}, u32[]{:S(2)}, u32[]{:S(2)}) async-start(bf16[4,64,1024]{2,1,0:T(8,128)(2,1)} %bitcast.89), calls=%async_computation.9 | async-start | bytes 1048576 | tf_op jit(solution)/shard_map/all_to_all | solution.py:214
  409.4 34.8 %all-to-all-start.13 = ((bf16[16,128,512]{2,1,0:T(8,128)(2,1)}), bf16[16,128,512]{2,1,0:T(8,128)(2,1)}, u32[]{:S(2)}, u32[]{:S(2)}) async-start(bf16[16,128,512]{2,1,0:T(8,128)(2,1)} %add_convert_fusion), calls=%async_computation.13 | async-start | bytes 4194304 | tf_op jit(solution)/shard_map/all_to_all | solution.py:163
  417.2 4.9 collective-permute-start.28
  418.5 3.6 collective-permute-start.29
  466.4 19.0 %all-to-all-start.10 = ((bf16[16,144,256]{2,1,0:T(8,128)(2,1)}), bf16[16,144,256]{2,1,0:T(8,128)(2,1)S(1)}, u32[]{:S(2)}, u32[]{:S(2)}) async-start(bf16[16,144,256]{2,1,0:T(8,128)(2,1)} %get-tuple-element.128), calls=%async_computation.10 | async-start | bytes 2359296 | tf_op jit(solution)/shard_map/all_to_all | solution.py:167
  486.4 37.1 %all-to-all-start.11 = ((bf16[16,128,512]{2,1,0:T(8,128)(2,1)}), bf16[16,128,512]{2,1,0:T(8,128)(2,1)S(1)}, u32[]{:S(2)}, u32[]{:S(2)}) async-start(bf16[16,128,512]{2,1,0:T(8,128)(2,1)} %add_convert_fusion.1), calls=%async_computation.11 | async-start | bytes 4194304 | tf_op jit(solution)/shard_map/all_to_all | solution.py:163
  (75 other events, 253.1 us)

commit v2 on v1

v2 whole, which is shorter than its diff:
```python
import functools
import math

import jax
import jax.numpy as jnp
from jax import lax
from jax.experimental import pallas as pl
from jax.experimental.pallas import tpu as pltpu
from jax.sharding import Mesh, PartitionSpec as P

EPSILON = 1e-05
MASKED = -1e30
SCALE = 1.0 / math.sqrt(64)
BF = jnp.bfloat16
F32 = jnp.float32
CHIPS = ("z", "yl", "yh")
ROWS = 64
D = 1024


def sds(*shape, dtype=BF):
    return jax.ShapeDtypeStruct(shape, dtype)


def call(kernel, outs, ins, us=3):
    specs, arrays = [], []
    for item in ins:
        if isinstance(item, tuple):
            array, block, index = item
            if block is None:
                specs.append(pl.BlockSpec(memory_space=pltpu.SMEM))
            else:
                specs.append(pl.BlockSpec(block, functools.partial(lambda at, i: at, index)))
        else:
            array = item
            specs.append(
                pl.BlockSpec(
                    array.shape, functools.partial(lambda n, i: (0,) * n, array.ndim)
                )
            )
        arrays.append(array)
    out_specs = [
        pl.BlockSpec(o.shape, functools.partial(lambda n, i: (0,) * n, len(o.shape)))
        for o in outs
    ]
    return pl.pallas_call(
        kernel,
        grid=(1,),
        out_shape=outs,
        in_specs=specs,
        out_specs=out_specs,
        compiler_params=pltpu.CompilerParams(vmem_limit_bytes=48 * 1024 * 1024),
        cost_estimate=pl.CostEstimate(
            flops=0, bytes_accessed=us * 3_000_000, transcendentals=0
        ),
    )(*arrays)


def nn(a, b):
    return jnp.dot(a, b, preferred_element_type=F32)


def nt(a, b):
    return lax.dot_general(a, b, (((1,), (1,)), ((), ())), preferred_element_type=F32)


def tn(a, b):
    return lax.dot_general(a, b, (((0,), (0,)), ((), ())), preferred_element_type=F32)


def heads():
    return [(k, side, yh) for k, (side, yh) in enumerate([(0, 0), (0, 1), (1, 0), (1, 1)])]


def attn_tile(ref, yh):
    if len(ref.shape) == 5:
        return ref[0, :, yh, 0:128, :].reshape(D, 256)
    return ref[:, yh, 0:128, :].reshape(D, 256)


def ffn_tile(ref, yh, part):
    return ref[:, yh, 0:128, part * 256 : part * 256 + 256].reshape(D, 256)


def low_half(v):
    lane = lax.broadcasted_iota(jnp.int32, v.shape, 1)
    return jnp.where(lane < 64, v, 0.0)


def high_half(v):
    lane = lax.broadcasted_iota(jnp.int32, v.shape, 1)
    return jnp.where(lane >= 64, v, 0.0)


def mean_of(v):
    return jnp.sum(v, axis=-1, keepdims=True) * (1.0 / D)


def normal(v):
    centred = v - mean_of(v)
    inverse = lax.rsqrt(mean_of(centred * centred) + EPSILON)
    return centred * inverse, inverse


def layer_norm(v, gain, shift):
    return normal(v)[0] * gain + shift


def layer_norm_back(v, gain, grad):
    xhat, inverse = normal(v)
    d = grad * gain
    back = inverse * (d - mean_of(d) - xhat * mean_of(d * xhat))
    return (
        back,
        jnp.sum(grad * xhat, axis=0, keepdims=True),
        jnp.sum(grad, axis=0, keepdims=True),
    )


def gelu(u):
    return 0.5 * u * (1.0 + jnp.tanh(0.7978845608028654 * (u + 0.044715 * u * u * u)))


def gelu_slope(u):
    t = jnp.tanh(0.7978845608028654 * (u + 0.044715 * u * u * u))
    return 0.5 * (1.0 + t) + 0.5 * u * (1.0 - t * t) * (
        0.7978845608028654 * (1.0 + 3.0 * 0.044715 * u * u)
    )


def total(parts):
    a, b, c, d = [p[...].astype(F32) for p in parts]
    return (a + b) + (c + d)


def ln_row(lnp, layer, which, kind):
    return lnp[which, layer * 8 + 4 + kind : layer * 8 + 5 + kind, :]


def project(x, lnp, bias, wm, wo, layer, n1, q, kv):
    normed = layer_norm(x, ln_row(lnp, layer, 0, 0), ln_row(lnp, layer, 0, 1)).astype(BF)
    n1[...] = normed
    for k, side, yh in heads():
        tile = nn(normed, attn_tile((wm, wo)[side], yh))
        tile = tile + bias[yh, layer * 8 + side : layer * 8 + side + 1, :]
        q[k] = low_half(tile[:, 128:]).astype(BF)
        pair = tile[:, :128].astype(BF)
        for g in range(16):
            kv[g, kv.shape[1] - ROWS :, k * 128 : k * 128 + 128] = pair


def pack_kernel(qkv, out, up, down, gain, shift, inb, outb, upb, msg, ffn):
    wt = out[...].astype(F32).T
    dt = down[...].astype(F32).T
    inb_, gain_, shift_, outb_ = [r[...].astype(F32) for r in (inb, gain, shift, outb)]
    upb_ = upb[...].astype(F32)
    zero = jnp.zeros((1, 64), F32)
    def flat(v):
        return jnp.concatenate([v[0:1], v[1:2]], axis=1)
    rows = []
    for j in range(2):
        cols = slice(j * 64, j * 64 + 64)
        rows.append(jnp.concatenate([zero, inb_[1:2, cols], inb_[0:1, cols], zero], axis=1))
    ups = [upb_[:, :256], upb_[:, 256:]]
    tail = [flat(gain_), flat(shift_), flat(outb_), jnp.zeros((9, 256), F32)]
    for j in range(2):
        cols = slice(j * 64, j * 64 + 64)
        tile = jnp.concatenate(
            [
                qkv[1, :, cols].astype(F32),
                qkv[2, :, cols].astype(F32),
                qkv[0, :, cols].astype(F32),
                wt[:, cols],
            ],
            axis=1,
        ).astype(BF)
        small = jnp.concatenate([rows[j], rows[1 - j], ups[j], ups[1 - j], *tail]).astype(BF)
        for g in range(16):
            msg[j, g, 0:128, :] = tile
            msg[j, g, 128:144, :] = small
        ffn[j, :, 0:256] = up[:, j * 256 : j * 256 + 256]
        ffn[j, :, 256:512] = dt[:, j * 256 : j * 256 + 256].astype(BF)


def first_kernel(x, params, wm, wo, piece, n1, q, msg, lnp, bias):
    for layer in range(2):
        blocks = [params[layer, d, 0].astype(F32) for d in range(8)]
        for half in range(2):
            cols = slice(half * 128, half * 128 + 128)
            lnp[half, layer * 8 : layer * 8 + 8, :] = jnp.concatenate(
                [b[0:8, cols] for b in blocks], axis=1
            )
        for yh in range(2):
            bias[yh, layer * 8 : layer * 8 + 8, :] = params[layer, 0, yh].astype(F32)[0:8]
    project(x[...].astype(F32), lnp, bias, wm, wo, 0, n1, q, msg)
    rest = piece[...]
    for g in range(16):
        msg[g, 0:128, :] = rest


def next_kernel(mid, p0, p1, p2, p3, lnp, bias, wm, wo, y, n1, q, msg):
    out = (mid[...] + (total((p0, p1, p2, p3)) + ln_row(lnp, 0, 1, 2))).astype(BF)
    y[...] = out
    project(out.astype(F32), lnp, bias, wm, wo, 1, n1, q, msg)


def attend_kernel(first, q, kv, wm, wo, part, prob, att):
    length = 16 * ROWS
    qpos = first[0] + lax.broadcasted_iota(jnp.int32, (ROWS, length), 0)
    kpos = lax.broadcasted_iota(jnp.int32, (ROWS, length), 1)
    allowed = kpos <= qpos
    acc = None
    for k, side, yh in heads():
        pair = kv[:, :, k * 128 : k * 128 + 128].reshape(length, 128)
        scores = jnp.where(allowed, nt(q[k], pair) * SCALE, MASKED)
        e = jnp.exp(scores - jnp.max(scores, axis=-1, keepdims=True))
        p = e / jnp.sum(e, axis=-1, keepdims=True)
        prob[k] = p
        mixed = high_half(nn(p.astype(BF), pair)).astype(BF)
        att[k] = mixed
        term = nt(mixed, attn_tile((wm, wo)[side], yh)[:, 128:])
        acc = term if acc is None else acc + term
    part[...] = acc.astype(BF)


def feed(x, parts, lnp, bias, wm, wo, layer, part, mid, n2, pre, act):
    middle = x[...].astype(F32) + (total(parts) + ln_row(lnp, layer, 0, 2))
    mid[...] = middle
    normed = layer_norm(middle, ln_row(lnp, layer, 1, 0), ln_row(lnp, layer, 1, 1)).astype(BF)
    n2[...] = normed
    acc = None
    for k, side, yh in heads():
        w = (wm, wo)[side]
        u = nn(normed, ffn_tile(w, yh, 0))
        u = u + bias[yh, layer * 8 + 2 + side : layer * 8 + 3 + side, :]
        pre[k] = u
        a = gelu(u).astype(BF)
        act[k] = a
        term = nt(a, ffn_tile(w, yh, 1))
        acc = term if acc is None else acc + term
    part[...] = acc.astype(BF)


def feed_back(g, pre, wm, wo, dpre, part):
    acc = None
    for k, side, yh in heads():
        w = (wm, wo)[side]
        d = (nn(g, ffn_tile(w, yh, 1)) * gelu_slope(pre[k])).astype(BF)
        dpre[k] = d
        term = nt(d, ffn_tile(w, yh, 0))
        acc = term if acc is None else acc + term
    part[...] = acc.astype(BF)


def feed_kernel(x, p0, p1, p2, p3, lnp, bias, wm, wo, part, mid, n2, pre, act):
    feed(x, (p0, p1, p2, p3), lnp, bias, wm, wo, 0, part, mid, n2, pre, act)


def turn_kernel(x, p0, p1, p2, p3, lnp, bias, wm, wo, g, part, mid, n2, pre, act, dpre, back):
    feed(x, (p0, p1, p2, p3), lnp, bias, wm, wo, 1, part, mid, n2, pre, act)
    feed_back(g[...], pre, wm, wo, dpre, back)


def grad_ffn_kernel(n2, g, dpre, act, mine, other, sums, row):
    for k, side, yh in heads():
        out = (mine, other)[side]
        out[:, yh, :, 0:256] = tn(n2[...], dpre[k]).astype(BF).reshape(8, 128, 256)
        out[:, yh, :, 256:512] = tn(g[...], act[k]).astype(BF).reshape(8, 128, 256)
        sums[k : k + 1, :] = jnp.sum(dpre[k].astype(F32), axis=0, keepdims=True)
    row[...] = jnp.sum(g[...].astype(F32), axis=0, keepdims=True)


def attend_back(layer, g, mid, parts, lnp, wm, wo, prob, q, kv, dmid, bg, dq, dkv, rows):
    back, gg, gs = layer_norm_back(mid[...], ln_row(lnp, layer, 1, 0), total(parts))
    dm = g[...].astype(F32) + back
    dmid[...] = dm
    low = dm.astype(BF)
    bg[...] = low
    rows[0:1, :] = gg
    rows[1:2, :] = gs
    rows[2:3, :] = jnp.sum(low.astype(F32), axis=0, keepdims=True)
    at = dkv.shape[1] - ROWS
    for k, side, yh in heads():
        pair = kv[:, :, k * 128 : k * 128 + 128].reshape(16 * ROWS, 128)
        da = high_half(nn(low, attn_tile((wm, wo)[side], yh)[:, 128:])).astype(BF)
        p = prob[k]
        dp = nt(da, pair)
        ds = (p * (dp - jnp.sum(p * dp, axis=-1, keepdims=True))).astype(BF)
        dq[k] = low_half(nn(ds, pair) * SCALE).astype(BF)
        both = tn(ds, q[k]) * SCALE + tn(p.astype(BF), da)
        dkv[:, at:, k * 128 : k * 128 + 128] = both.astype(BF).reshape(16, ROWS, 128)


def attend_back_kernel(g, mid, p0, p1, p2, p3, lnp, wm, wo, prob, q, kv, dmid, bg, dq, dkv, rows):
    attend_back(1, g, mid, (p0, p1, p2, p3), lnp, wm, wo, prob, q, kv, dmid, bg, dq, dkv, rows)


def attend_back_first_kernel(
    g, mid, p0, p1, p2, p3, lnp, wm, wo, prob, q, kv, gm, gr, dmid, bg, dq, msg, rows
):
    attend_back(0, g, mid, (p0, p1, p2, p3), lnp, wm, wo, prob, q, kv, dmid, bg, dq, msg, rows)
    for i in range(8):
        for j in range(2):
            msg[2 * i + j, 0:128, :] = (gm[i, j].astype(F32) + gr[i, j].astype(F32)).astype(BF)


def project_back_kernel(dkv, dq, wm, wo, dproj, part, sums):
    pairs = jnp.sum(dkv[...].astype(F32), axis=0).astype(BF)
    acc = None
    for k, side, yh in heads():
        tile = jnp.concatenate([pairs[:, k * 128 : k * 128 + 128], dq[k]], axis=1)
        dproj[k] = tile
        sums[k : k + 1, :] = jnp.sum(tile.astype(F32), axis=0, keepdims=True)
        term = nt(tile, attn_tile((wm, wo)[side], yh))
        acc = term if acc is None else acc + term
    part[...] = acc.astype(BF)


def grad_attn_kernel(n1, bg, att, dproj, mine, other):
    for k, side, yh in heads():
        out = (mine, other)[side]
        first = tn(n1[...], dproj[k])
        second = tn(bg[...], att[k])
        out[:, yh, :, 0:128] = first[:, :128].astype(BF).reshape(8, 128, 128)
        out[:, yh, :, 128:] = (first[:, 128:] + second).astype(BF).reshape(8, 128, 128)


def hand_down_kernel(x, dmid, p0, p1, p2, p3, lnp, pre, wm, wo, dx, dpre, part, rows):
    back, gg, gs = layer_norm_back(
        x[...].astype(F32), ln_row(lnp, 1, 0, 0), total((p0, p1, p2, p3))
    )
    g = (dmid[...] + back).astype(BF)
    dx[...] = g
    rows[0:1, :] = gg
    rows[1:2, :] = gs
    feed_back(g, pre, wm, wo, dpre, part)


def last_kernel(
    x, dmid, p0, p1, p2, p3, lnp, gm, gr,
    r0, o0, a0, u0, h1, r1, o1, a1, u1, dx, msg,
):
    back, gg, gs = layer_norm_back(
        x[...].astype(F32), ln_row(lnp, 0, 0, 0), total((p0, p1, p2, p3))
    )
    dx[...] = (dmid[...] + back).astype(BF)
    lines = []
    for first, rows, ob, a, u in (
        ((gg, gs), r0, o0, a0, u0),
        ((h1[0:1, :], h1[1:2, :]), r1, o1, a1, u1),
    ):
        lines.append(
            (
                a[...],
                u[...],
                (
                    (first[0], rows[0:1, :]),
                    (first[1], rows[1:2, :]),
                    (rows[2:3, :], ob[...]),
                ),
            )
        )
    for d in range(8):
        cols = slice(d * 128, d * 128 + 128)
        for yh in range(2):
            block = []
            for a, u, pairs in lines:
                block += [a[yh : yh + 1], a[2 + yh : 3 + yh], u[yh : yh + 1], u[2 + yh : 3 + yh]]
                block += [jnp.concatenate([f[:, cols], s[:, cols]], axis=1) for f, s in pairs]
            block.append(jnp.zeros((2, 256), F32))
            g = 2 * d + yh
            msg[g, 0:128, :] = (gm[d, yh].astype(F32) + gr[d, yh].astype(F32)).astype(BF)
            msg[g, 128:144, :] = jnp.concatenate(block).astype(BF)


def combine_kernel(am, ar, fm, fr, msg):
    msg[0, :, 0:256] = (am[0].astype(F32) + ar[0].astype(F32)).astype(BF)
    msg[0, :, 256:768] = (fm[0].astype(F32) + fr[0].astype(F32)).astype(BF)


def settle_kernel(tail, l0, l1, out):
    t = jnp.sum(tail[...].astype(F32), axis=0)
    out[0, 0:128, 0:256] = t[0:128]
    out[1, 0:128, 0:256] = jnp.sum(l1[:, :, 0:256].astype(F32), axis=0)
    for j in range(2):
        cols = slice(256 + j * 256, 512 + j * 256)
        out[0, 0:128, cols] = jnp.sum(l0[:, 0:128, j * 256 : j * 256 + 256].astype(F32), axis=0)
        out[1, 0:128, cols] = jnp.sum(l1[:, :, cols].astype(F32), axis=0)
    small = t[128:144]
    pad = jnp.zeros((1, 256), F32)
    out[0, 128:136, 0:256] = jnp.concatenate([small[0:7], pad])
    out[1, 128:136, 0:256] = jnp.concatenate([small[7:14], pad])


def unpack_kernel(r, qkv, out, up, down, gain, shift, inb, outb, upb):
    a = [r[j, 0:128, 0:256] for j in range(2)]
    for i, at in enumerate((128, 0, 64)):
        qkv[i] = jnp.concatenate([t[:, at : at + 64] for t in a], axis=1)
    out[...] = jnp.concatenate([t[:, 192:256] for t in a], axis=1).T
    for j in range(2):
        up[:, j * 256 : j * 256 + 256] = r[j, 0:128, 256:512]
        down[j * 256 : j * 256 + 256, :] = r[j, 0:128, 512:768].T
    s0, s1 = r[0, 128:136, 0:256], r[1, 128:136, 0:256]
    for row, ref in ((4, gain), (5, shift), (6, outb)):
        t = s0[row : row + 1] + s1[row : row + 1]
        ref[0:1, :] = t[:, 0:128]
        ref[1:2, :] = t[:, 128:256]
    sides = [s0[0:1] + s1[1:2], s0[1:2] + s1[0:1]]
    inb[0:1, :] = jnp.concatenate([t[:, 128:192] for t in sides], axis=1)
    inb[1:2, :] = jnp.concatenate([t[:, 64:128] for t in sides], axis=1)
    upb[...] = jnp.concatenate([s0[2:3] + s1[3:4], s0[3:4] + s1[2:3]], axis=1)


def swap_cores(v):
    return lax.ppermute(v, "s", [(0, 1), (1, 0)])


def all_parts(part):
    got = [lax.ppermute(part, "x", [(i, i ^ k) for i in range(4)]) for k in (1, 3, 2)]
    return part, got[0], got[2], got[1]


def exchange(v, axes=CHIPS):
    return lax.all_to_all(v, axes, 0, 0, tiled=True)


def by_layer(mine, first, second):
    return jnp.where(mine == 0, first, second)


def whole_rows(s, yh, a, b):
    keep, send = by_layer(s, a, b), by_layer(s, b, a)
    got = swap_cores(send)
    rows = jnp.stack([by_layer(s, keep, got), by_layer(s, got, keep)])
    far = lax.ppermute(rows, "yh", [(0, 1), (1, 0)])
    return jnp.concatenate([by_layer(yh, rows, far), by_layer(yh, far, rows)], axis=1).reshape(
        1, 2, 1, 128, D
    )


def local(inputs, cotangent, wqkv, wout, wup, wdown, gain, shift, inb, outb, upb):
    s, yh = lax.axis_index("s"), lax.axis_index("yh")
    first = (lax.axis_index(CHIPS) * ROWS).astype(jnp.int32).reshape(1)

    def own_rows(v):
        return lax.dynamic_slice(v, (s, 0, yh * ROWS, 0), (1, 1, ROWS, D)).reshape(ROWS, D)

    x, cot = own_rows(inputs), own_rows(cotangent)
    msg, ffn = call(
        pack_kernel,
        [sds(2, 16, 144, 256), sds(2, 128, 512)],
        [
            jnp.moveaxis(wqkv[0], 1, 0), wout[0], wup[0], wdown[0],
            gain[0], shift[0], inb[0], outb[0], upb,
        ],
    )
    u = exchange(msg.reshape(32, 144, 256), ("s", *CHIPS)).reshape(2, 16, 144, 256)
    got = swap_cores(by_layer(s, ffn[1], ffn[0]))
    piece0, piece1 = by_layer(s, ffn[0], got), by_layer(s, got, ffn[1])
    u = u.reshape(2, 8, 2, 144, 256)
    am = [(u, (1, 8, 2, 144, 256), (l, 0, 0, 0, 0)) for l in range(2)]
    ao = [swap_cores(u[l]) for l in range(2)]
    kinds = dict(n1=sds(ROWS, D), q=sds(4, ROWS, 128))
    n10, q0, msg, lnp, bias = call(
        first_kernel,
        [kinds["n1"], kinds["q"], sds(16, 192, 512), sds(2, 16, D, dtype=F32), sds(2, 16, 256, dtype=F32)],
        [x, (u, (2, 8, 2, 16, 256), (0, 0, 0, 8, 0)), am[0], ao[0], piece0],
    )
    got0 = exchange(msg)
    kv0 = (got0, (16, ROWS, 512), (0, 2, 0))
    f0 = (got0.reshape(8, 2, 192, 512), (8, 2, 128, 512), (0, 0, 0, 0))
    f0o = (swap_cores(got0).reshape(8, 2, 192, 512), (8, 2, 128, 512), (0, 0, 0, 0))
    attend_outs = [sds(ROWS, D), sds(4, ROWS, D, dtype=F32), sds(4, ROWS, 128)]
    feed_outs = [
        sds(ROWS, D), sds(ROWS, D, dtype=F32), sds(ROWS, D),
        sds(4, ROWS, 256, dtype=F32), sds(4, ROWS, 256),
    ]
    part, prob0, att0 = call(attend_kernel, attend_outs, [(first, None, None), q0, kv0, am[0], ao[0]])
    f1 = exchange(jnp.broadcast_to(piece1, (16, 128, 512))).reshape(8, 2, 128, 512)
    f1o = swap_cores(f1)
    part, mid0, n20, pre0, act0 = call(
        feed_kernel, feed_outs, [x, *all_parts(part), lnp, bias, f0, f0o]
    )
    y0, n11, q1, msg = call(
        next_kernel,
        [sds(ROWS, D), kinds["n1"], kinds["q"], sds(16, ROWS, 512)],
        [mid0, *all_parts(part), lnp, bias, am[1], ao[1]],
    )
    kv1 = exchange(msg)
    part, prob1, att1 = call(attend_kernel, attend_outs, [(first, None, None), q1, kv1, am[1], ao[1]])
    part, mid1, n21, pre1, act1, dpre1, back = call(
        turn_kernel,
        feed_outs + [sds(4, ROWS, 256), sds(ROWS, D)],
        [y0, *all_parts(part), lnp, bias, f1, f1o, cot],
    )
    backs = all_parts(back)
    a, b, c, d = [p.astype(F32) for p in all_parts(part)]
    y1 = (mid1 + (((a + b) + (c + d)) + lnp[1, 14:15])).astype(BF)
    grad_ffn_outs = [
        sds(8, 2, 128, 512), sds(8, 2, 128, 512), sds(4, 256, dtype=F32), sds(1, D, dtype=F32)
    ]
    gfm1, gfo1, gub1, ob11 = call(grad_ffn_kernel, grad_ffn_outs, [n21, cot, dpre1, act1])
    gfr1 = swap_cores(gfo1)
    back_outs = [sds(ROWS, D, dtype=F32), sds(ROWS, D), sds(4, ROWS, 128)]
    rows_out = sds(8, D, dtype=F32)
    dmid1, bg1, dq1, dkv, rows1 = call(
        attend_back_kernel,
        back_outs + [sds(16, ROWS, 512), rows_out],
        [cot, mid1, *backs, lnp, am[1], ao[1], prob1, q1, kv1],
    )
    dkv = exchange(dkv)
    project_outs = [sds(4, ROWS, 256), sds(ROWS, D), sds(4, 256, dtype=F32)]
    dproj1, part, gib1 = call(project_back_kernel, project_outs, [dkv, dq1, am[1], ao[1]])
    backs = all_parts(part)
    grad_attn_outs = [sds(8, 2, 128, 256), sds(8, 2, 128, 256)]
    gam1, gao1 = call(grad_attn_kernel, grad_attn_outs, [n11, bg1, att1, dproj1])
    gar1 = swap_cores(gao1)
    dx1, dpre0, part, head1 = call(
        hand_down_kernel,
        [sds(ROWS, D), sds(4, ROWS, 256), sds(ROWS, D), rows_out],
        [y0, dmid1, *backs, lnp, pre0, f0, f0o],
    )
    backs = all_parts(part)
    gfm0, gfo0, gub0, ob10 = call(grad_ffn_kernel, grad_ffn_outs, [n20, dx1, dpre0, act0])
    gfr0 = swap_cores(gfo0)
    def flat(v):
        return v.reshape(16, 128, v.shape[-1])
    msg1 = pl.pallas_call(
        combine_kernel,
        grid=(16,),
        out_shape=sds(16, 128, 768),
        in_specs=[pl.BlockSpec((1, 128, w), lambda i: (i, 0, 0)) for w in (256, 256, 512, 512)],
        out_specs=pl.BlockSpec((1, 128, 768), lambda i: (i, 0, 0)),
        compiler_params=pltpu.CompilerParams(vmem_limit_bytes=32 * 1024 * 1024),
        cost_estimate=pl.CostEstimate(flops=0, bytes_accessed=9_000_000, transcendentals=0),
    )(flat(gam1), flat(gar1), flat(gfm1), flat(gfr1))
    l1 = exchange(msg1)
    dmid0, bg0, dq0, msg, rows0 = call(
        attend_back_first_kernel,
        back_outs + [sds(16, 192, 512), rows_out],
        [dx1, mid0, *backs, lnp, am[0], ao[0], prob0, q0, kv0, gfm0, gfr0],
    )
    l0 = exchange(msg)
    dproj0, part, gib0 = call(
        project_back_kernel, project_outs, [(l0, (16, ROWS, 512), (0, 2, 0)), dq0, am[0], ao[0]]
    )
    backs = all_parts(part)
    gam0, gao0 = call(grad_attn_kernel, grad_attn_outs, [n10, bg0, att0, dproj0])
    gar0 = swap_cores(gao0)
    dx0, msg = call(
        last_kernel,
        [sds(ROWS, D), sds(16, 144, 256)],
        [x, dmid0, *backs, lnp, gam0, gar0, rows0, ob10, gib0, gub0, head1, rows1, ob11, gib1, gub1],
    )
    tail = exchange(msg)
    acts = whole_rows(s, yh, y0, y1)
    grads = whole_rows(s, yh, dx0, dx1)
    (settled,) = call(settle_kernel, [sds(2, 144, 768, dtype=F32)], [tail, l0, l1])
    settled = exchange(settled, "s")
    f = functools.partial(sds, dtype=F32)
    gq, go, gu, gd, gg, gs, gi, gb, gub = call(
        unpack_kernel,
        [f(3, 128, 128), f(128, 128), f(128, 512), f(512, 128), f(2, 128), f(2, 128), f(2, 128), f(2, 128), f(1, 512)],
        [settled],
    )
    return (
        acts, grads, jnp.moveaxis(gq, 0, 1)[None], go[None], gu[None], gd[None],
        gg[None], gs[None], gi[None], gb[None], gub,
    )


def solution(mesh):
    parts = Mesh(mesh.devices.reshape(2, 4, 2, 2, 4), ("s", "z", "yl", "yh", "x"))
    dp, tp = ("z", "yl"), ("yh", "x")
    return jax.shard_map(
        local,
        mesh=parts,
        in_specs=(
            P(None, None, dp, None),
            P(None, None, dp, None),
            P("s", dp, None, tp),
            P("s", tp, dp),
            P("s", dp, tp),
            P("s", tp, dp),
            P("s", None, dp),
            P("s", None, dp),
            P("s", None, tp),
            P("s", None, dp),
            P("s", tp),
        ),
        out_specs=(
            P("s", None, None, dp, None),
            P("s", None, None, dp, None),
            P("s", dp, None, tp),
            P("s", tp, dp),
            P("s", dp, tp),
            P("s", tp, dp),
            P("s", None, dp),
            P("s", None, dp),
            P("s", None, tp),
            P("s", None, dp),
            P("s", tp),
        ),
        check_vma=False,
    )
```

time: 547 us -> 424 us (0.78); the launches traced: 536 us -> 422 us
  blocking collectives: 33.7 us -> 134 us
  local copies, waits for them, and re-layouts: 97.2 us -> 23.5 us
  other arithmetic: 70 us -> 2.98 us
  Pallas kernels: 0 us -> 56.7 us
  matrix products: 55.3 us -> 0 us
  starting transfers between devices: 118 us -> 70.5 us
  waiting for transfers between devices: 159 us -> 134 us
    all_to_all x3 -> x5, blocking collectives: 33.7 us -> 134 us  [exchange(): return lax.all_to_all(v, axes, 0, 0, tiled=True)]
    all_to_all x12 -> x4, waiting for transfers between devices: 146 us -> 62.4 us  [exchange(): return lax.all_to_all(v, axes, 0, 0, tiled=True)]
    pallas_call x0 -> x20, Pallas kernels: none -> 56.7 us  [the longest x19 55.8 us: call(): pl.pallas_call(kernel, grid=(1,), out_shape=outs, in_specs=specs, out_spe...]
    dot_general x36 -> x0, matrix products: 55.3 us -> none  [ein(): return jnp.einsum(form, a, b, preferred_element_type=F32)]
    ppermute x24 -> x26, waiting for transfers between devices: 11.7 us -> 64.4 us  [the longest x24 42.7 us: all_parts(): lax.ppermute(part, 'x', [(i, i ^ k) for i in range(4)])]
    all_to_all x12 -> x4, starting transfers between devices: 74.2 us -> 22 us  [exchange(): return lax.all_to_all(v, axes, 0, 0, tiled=True)]
    concatenate x15 -> x0, other arithmetic: 22.6 us -> none  [the longest x2 8.66 us: backward(): gf = jnp.concatenate([gf_up, gf_down], axis=-1).astype(BF)]
    concatenate x13 -> x0, local copies, waits for them, and re-layouts: 20.3 us -> none  [the longest x8 18.5 us: backward(): dkv = jnp.concatenate([dk, dv], axis=-1).astype(BF).reshape(4, 16, 64, 128)]
  transfers between devices with their start and end apart: 46 -> 41, of which waited for: 21 -> 27; matrix products, arithmetic and copies ran while one was open for 32% -> 1% of each run, Pallas kernels for 0% -> 5%
where the time goes in v2:
time: 424 us; the launch traced here: 422 us
  blocking collectives  134 us (32%)
  waiting for transfers between devices  134 us (32%)
  starting transfers between devices  70.5 us (17%)
  Pallas kernels  56.7 us (13%)
  local copies, waits for them, and re-layouts  23.5 us (6%)
    all_to_all x5, blocking collectives, exchange(): return lax.all_to_all(v, axes, 0, 0, tiled=True)  134 us
    all_to_all x4, waiting for transfers between devices, exchange(): return lax.all_to_all(v, axes, 0, 0, tiled=True)  62.4 us
    pallas_call x19, Pallas kernels, call(): pl.pallas_call(kernel, grid=(1,), out_shape=outs, in_specs=specs, out_spe...  55.8 us
    ppermute x24, waiting for transfers between devices, all_parts(): lax.ppermute(part, 'x', [(i, i ^ k) for i in range(4)])  42.7 us
    ppermute x24, starting transfers between devices, all_parts(): lax.ppermute(part, 'x', [(i, i ^ k) for i in range(4)])  31.3 us
    all_to_all x4, starting transfers between devices, exchange(): return lax.all_to_all(v, axes, 0, 0, tiled=True)  22 us
    ppermute x2, waiting for transfers between devices, whole_rows(): far = lax.ppermute(rows, 'yh', [(0, 1), (1, 0)])  21.7 us
    unnamed x80, local copies, waits for them, and re-layouts  19.3 us
  transfers between devices with their start and end apart: 41, of which 27 were waited for; matrix products, arithmetic and copies ran while one was open for 1% of the time, Pallas kernels for 5%

profile of v2, /device:TPU:1, one launch (start us, length us, event | category | flops | bytes accessed | tf_op | source)
XLA Modules:
  0.0 422.3 jit_solution(13534371005620366844)
XLA Ops:
  7.8 41.0 %all_to_all.45 = bf16[32,144,256]{2,1,0:T(8,128)(2,1)S(1)} all-to-all(bf16[32,144,256]{2,1,0:T(8,128)(2,1)S(1)} %bitcast.68), channel_id=1, replica_groups=mesh['s'=2,'z'=4,'yl'=2,'yh'=2,'x'=4] {'s','z','yl','yh'}, dimensions={0} | all-to-all | bytes 4718592 | tf_op jit(solution)/shard_map/all_to_all | solution.py:424
  48.8 1.8 fusion
  51.1 2.4 collective-permute-done.1
  53.7 3.8 shard_map.195
  57.5 42.5 %all_to_all.46.kv = bf16[16,192,512]{2,1,0:T(8,128)(2,1)} all-to-all(bf16[16,192,512]{2,1,0:T(8,128)(2,1)} %get-tuple-element.85), channel_id=1, replica_groups=mesh['s'=2,'z'=4,'yl'=2,'yh'=2,'x'=4] {'z','yl','yh'}, dimensions={0} | all-to-all | bytes 6291456 | tf_op jit(solution)/shard_map/all_to_all | solution.py:424
  100.1 1.8 collective-permute-start.5
  101.9 1.5 broadcast_in_dim.27
  103.4 4.4 %all-to-all-start.3 = ((bf16[16,128,512]{2,1,0:T(8,128)(2,1)}), bf16[16,128,512]{2,1,0:T(8,128)(2,1)}, u32[]{:S(2)}, u32[]{:S(2)}) async-start(bf16[16,128,512]{2,1,0:T(8,128)(2,1)} %broadcast_in_dim.27), calls=%async_computation.3 | async-start | bytes 4194304 | tf_op jit(solution)/shard_map/all_to_all | solution.py:424
  107.9 28.3 %all-to-all-done.3 = bf16[16,128,512]{2,1,0:T(8,128)(2,1)} async-done(((bf16[16,128,512]{2,1,0:T(8,128)(2,1)}), bf16[16,128,512]{2,1,0:T(8,128)(2,1)}, u32[]{:S(2)}, u32[]{:S(2)}) %all-to-all-start.3) | async-done | bytes 2097184 | tf_op jit(solution)/shard_map/all_to_all | solution.py:424
  137.0 4.0 shard_map.196
  142.9 2.4 collective-permute-start.3
  145.3 1.5 collective-permute-done.2.p1
  146.8 2.5 collective-permute-start.4
  149.3 2.5 collective-permute-done.3.p2
  151.8 3.0 collective-permute-done.4.p3
  154.8 3.8 shard_map.197
  159.4 3.2 collective-permute-start.8
  163.3 2.1 collective-permute-done.7.p2
  165.3 2.3 collective-permute-done.8.p3
  167.7 2.1 shard_map.198
  169.8 19.5 %all_to_all.47.kv = bf16[16,64,512]{2,1,0:T(8,128)(2,1)S(1)} all-to-all(bf16[16,64,512]{2,1,0:T(8,128)(2,1)S(1)} %get-tuple-element.93), channel_id=1, replica_groups=mesh['s'=2,'z'=4,'yl'=2,'yh'=2,'x'=4] {'z','yl','yh'}, dimensions={0} | all-to-all | bytes 2097152 | tf_op jit(solution)/shard_map/all_to_all | solution.py:424
  189.3 3.7 shard_map.199
  193.1 5.0 %collective-permute-start.11 = (bf16[64,1024]{1,0:T(8,128)(2,1)S(1)}, bf16[64,1024]{1,0:T(8,128)(2,1)S(1)}, u32[]{:S(2)}, u32[]{:S(2)}) collective-permute-start(bf16[64,1024]{1,0:T(8,128)(2,1)S(1)} %get-tuple-element.94.p0), channel_id=1, source_target_pairs={{0,2},{1,3},{2,0},{3,1},{4,6},{5,7},{6,4},{7,5},{8,10},{9,11},{10,... | collective-permute-start | bytes 393224 | tf_op jit(solution)/shard_map/ppermute | solution.py:419
  199.1 2.8 collective-permute-done.11.p2
  201.9 1.4 collective-permute-done.12.p3
  203.3 5.1 %shard_map.200 = (bf16[64,1024]{1,0:T(8,128)(2,1)}, f32[64,1024]{1,0:T(8,128)S(1)}, bf16[64,1024]{1,0:T(8,128)(2,1)S(1)}, f32[4,64,256]{2,1,0:T(8,128)}, bf16[4,...) custom-call(bf16[64,1024]{1,0:T(8,128)(2,1)S(1)} %get-tuple-element.91.x, ...), custom_call_target="tpu_custom_call" | custom-call | bytes 9000000 | tf_op jit(solution)/shard_map/pallas_call | solution.py:46
  208.7 1.7 collective-permute-start.20
  210.3 2.2 collective-permute-start.21
  212.5 1.6 collective-permute-done.20.p2
  214.1 1.4 collective-permute-done.21.p3
  215.5 4.7 %shard_map.201 = (f32[64,1024]{1,0:T(8,128)S(1)}, bf16[64,1024]{1,0:T(8,128)(2,1)S(1)}, bf16[4,64,128]{2,1,0:T(8,128)(2,1)S(1)}, bf16[16,64,512]{2,1,0:T(8,128)(2,1)S(1)}, f32[8,1024]{1,0:T(8,128)S(1)}) custom-call(bf16[64,1024]{1,0:T(8,128)(2,1)S(1)} %dynamic-slice_bitcast_fusion.g, f32[64,1024]{1,0:T(8,128)S(1)} %get-tuple-element.95.mid, ...), custom_call_target="tpu_custom_call" | custom-call | bytes 9000000 | tf_op jit(solution)/shard_map/pallas_call | solution.py:46
  220.2 23.6 %all_to_all.48.dkv = bf16[16,64,512]{2,1,0:T(8,128)(2,1)S(1)} all-to-all(bf16[16,64,512]{2,1,0:T(8,128)(2,1)S(1)} %get-tuple-element.100), channel_id=1, replica_groups=mesh['s'=2,'z'=4,'yl'=2,'yh'=2,'x'=4] {'z','yl','yh'}, dimensions={0} | all-to-all | bytes 2097152 | tf_op jit(solution)/shard_map/all_to_all | solution.py:424
  243.8 2.0 shard_map.202
  246.0 2.0 collective-permute-start.23
  248.0 1.8 collective-permute-start.24
  249.8 2.0 collective-permute-done.23.p2
  253.2 3.9 shard_map.203
  258.3 5.6 %collective-permute-start.28 = (bf16[8,2,128,512]{3,2,1,0:T(8,128)(2,1)S(1)}, bf16[8,2,128,512]{3,2,1,0:T(8,128)(2,1)S(1)}, u32[]{:S(2)}, u32[]{:S(2)}) collective-permute-start(bf16[8,2,128,512]{3,2,1,0:T(8,128)(2,1)S(1)} %get-tuple-element.111), channel_id=1, source_target_pairs={{0,64},{64,0},{1,65},{65,1},{2,66},{66,2},{3,67},{67,3},{4,68},{68... | collective-permute-start | bytes 6291464 | tf_op jit(solution)/shard_map/ppermute | solution.py:415
  263.9 2.8 collective-permute-start.26
  269.0 4.2 collective-permute-done.26.p2
  273.1 2.5 collective-permute-done.27.p3
  275.7 1.4 copy-done.39
  277.1 7.9 %shard_map.205 = (f32[64,1024]{1,0:T(8,128)S(1)}, bf16[64,1024]{1,0:T(8,128)(2,1)S(1)}, bf16[4,64,128]{2,1,0:T(8,128)(2,1)S(1)}, bf16[16,192,512]{2,1,0:T(8,128)(2,1)}, f32[8,1024]{1,0:T(8,128)S(1)}) custom-call(bf16[64,1024]{1,0:T(8,128)(2,1)S(1)} %get-tuple-element.104.g, f32[64,1024]{1,0:T(8,128)S(1)} %get-tuple-element.89.mid, ...), custom_call_target="tpu_custom_call" | custom-call | bytes 9000000 | tf_op jit(solution)/shard_map/pallas_call | solution.py:46
  287.6 4.5 %all-to-all-start.5 = ((bf16[16,192,512]{2,1,0:T(8,128)(2,1)}), bf16[16,192,512]{2,1,0:T(8,128)(2,1)}, u32[]{:S(2)}, u32[]{:S(2)}) async-start(bf16[16,192,512]{2,1,0:T(8,128)(2,1)} %get-tuple-element.113), calls=%async_computation.5 | async-start | bytes 6291456 | tf_op jit(solution)/shard_map/all_to_all | solution.py:424
  295.6 2.6 collective-permute-done.36
  298.3 1.5 collective-permute-done.35
  300.7 1.7 copy-done.5
  302.4 29.1 %all-to-all-done.5.dkv.l0 = bf16[16,192,512]{2,1,0:T(8,128)(2,1)} async-done(((bf16[16,192,512]{2,1,0:T(8,128)(2,1)}), bf16[16,192,512]{2,1,0:T(8,128)(2,1)}, u32[]{:S(2)}, u32[]{:S(2)}) %all-to-all-start.5) | async-done | bytes 3145760 | tf_op jit(solution)/shard_map/all_to_all | solution.py:424
  331.6 6.9 %all-to-all-start.7 = ((bf16[16,128,768]{2,1,0:T(8,128)(2,1)}), bf16[16,128,768]{2,1,0:T(8,128)(2,1)}, u32[]{:S(2)}, u32[]{:S(2)}) async-start(bf16[16,128,768]{2,1,0:T(8,128)(2,1)} %copy-done.5), calls=%async_computation.7 | async-start | bytes 6291456 | tf_op jit(solution)/shard_map/all_to_all | solution.py:424
  339.4 2.4 shard_map.206
  342.5 2.0 shard_map.207
  344.5 1.9 collective-permute-start.32
  347.5 2.2 collective-permute-start.14
  349.7 6.1 %collective-permute-done.16 = bf16[64,1024]{1,0:T(8,128)(2,1)S(1)} collective-permute-done((bf16[64,1024]{1,0:T(8,128)(2,1)}, bf16[64,1024]{1,0:T(8,128)(2,1)S(1)}, u32[]{:S(2)}, u32[]{:S(2)}) %collective-permute-start.16) | collective-permute-done | bytes 131104 | tf_op jit(solution)/shard_map/ppermute | solution.py:419
  359.1 3.2 collective-permute-done.30.p2
  362.3 2.9 collective-permute-done.31.p3
  369.8 1.7 shard_map.209
  372.4 5.0 %all-to-all-done.7.l1 = bf16[16,128,768]{2,1,0:T(8,128)(2,1)} async-done(((bf16[16,128,768]{2,1,0:T(8,128)(2,1)}), bf16[16,128,768]{2,1,0:T(8,128)(2,1)}, u32[]{:S(2)}, u32[]{:S(2)}) %all-to-all-start.7) | async-done | bytes 3145760 | tf_op jit(solution)/shard_map/all_to_all | solution.py:424
  377.4 6.1 %all-to-all-start.6 = ((bf16[16,144,256]{2,1,0:T(8,128)(2,1)}), bf16[16,144,256]{2,1,0:T(8,128)(2,1)S(1)}, u32[]{:S(2)}, u32[]{:S(2)}) async-start(bf16[16,144,256]{2,1,0:T(8,128)(2,1)} %get-tuple-element.135), calls=%async_computation.6 | async-start | bytes 2359296 | tf_op jit(solution)/shard_map/all_to_all | solution.py:424
  383.6 2.9 collective-permute-start.18
  386.8 17.0 %collective-permute-done.18 = bf16[2,64,1024]{2,1,0:T(8,128)(2,1)S(1)} collective-permute-done((bf16[2,64,1024]{2,1,0:T(8,128)(2,1)S(1)}, bf16[2,64,1024]{2,1,0:T(8,128)(2,1)S(1)}, u32[]{:S(2)}, u32[]{:S(2)}) %collective-permute-start.18) | collective-permute-done | bytes 262176 | tf_op jit(solution)/shard_map/ppermute | solution.py:435
  404.6 4.7 %collective-permute-done.34 = bf16[2,64,1024]{2,1,0:T(8,128)(2,1)S(1)} collective-permute-done((bf16[2,64,1024]{2,1,0:T(8,128)(2,1)S(1)}, bf16[2,64,1024]{2,1,0:T(8,128)(2,1)S(1)}, u32[]{:S(2)}, u32[]{:S(2)}) %collective-permute-start.34) | collective-permute-done | bytes 262176 | tf_op jit(solution)/shard_map/ppermute | solution.py:435
  410.3 3.7 shard_map.212
  414.0 7.2 %all_to_all.49.r = f32[2,144,768]{2,1,0:T(8,128)S(1)} all-to-all(f32[2,144,768]{2,1,0:T(8,128)S(1)} %shard_map.212), channel_id=1, replica_groups=mesh['s'=2,'z'=4,'yl'=2,'yh'=2,'x'=4] {'s'}, dimensions={0} | all-to-all | bytes 1769472 | tf_op jit(solution)/shard_map/all_to_all | solution.py:424
  (140 shorter events, 39.8 us)
Async XLA Ops:
  0.6 50.5 %copy-start = (bf16[2,1,128,1024]{3,2,1,0:T(8,128)(2,1)S(1)}, bf16[2,1,128,1024]{3,2,1,0:T(8,128)(2,1)}, u32[]{:S(2)}) copy-start(bf16[2,1,128,1024]{3,2,1,0:T(8,128)(2,1)} %param.11) | copy-start | bytes 1572868
  0.7 1.0 copy-start.8
  1.6 0.9 copy-start.9
  2.5 0.9 copy-start.16
  48.8 140.5 %copy-start.2 = (bf16[32,144,256]{2,1,0:T(8,128)(2,1)}, bf16[32,144,256]{2,1,0:T(8,128)(2,1)S(1)}, u32[]{:S(2)}) copy-start(bf16[32,144,256]{2,1,0:T(8,128)(2,1)S(1)} %all_to_all.45) | copy-start | bytes 7077892
  50.5 3.2 collective-permute-start
  50.9 2.6 collective-permute-start.1
  57.5 42.5 %copy-start.10 = (bf16[64,1024]{1,0:T(8,128)(2,1)}, bf16[64,1024]{1,0:T(8,128)(2,1)S(1)}, u32[]{:S(2)}) copy-start(bf16[64,1024]{1,0:T(8,128)(2,1)S(1)} %get-tuple-element.116.n1) | copy-start | bytes 393220
  100.1 54.8 %collective-permute-start.5 = (bf16[16,192,512]{2,1,0:T(8,128)(2,1)}, bf16[16,192,512]{2,1,0:T(8,128)(2,1)}, u32[]{:S(2)}, u32[]{:S(2)}) collective-permute-start(bf16[16,192,512]{2,1,0:T(8,128)(2,1)} %all_to_all.46.kv), channel_id=1, source_target_pairs={{0,64},{64,0},{1,65},{65,1},{2,66},{66,2},{3,67},{67,3},{4,68},{68... | collective-permute-start | bytes 9437192 | tf_op jit(solution)/shard_map/ppermute | solution.py:415
  103.4 32.8 %all-to-all-start.3 = ((bf16[16,128,512]{2,1,0:T(8,128)(2,1)}), bf16[16,128,512]{2,1,0:T(8,128)(2,1)}, u32[]{:S(2)}, u32[]{:S(2)}) async-start(bf16[16,128,512]{2,1,0:T(8,128)(2,1)} %broadcast_in_dim.27), calls=%async_computation.3 | async-start | bytes 4194304 | tf_op jit(solution)/shard_map/all_to_all | solution.py:424
  107.8 54.8 %collective-permute-start.9 = (bf16[8,2,144,256]{3,2,1,0:T(8,128)(2,1)}, bf16[8,2,144,256]{3,2,1,0:T(8,128)(2,1)}, u32[]{:S(2)}, u32[]{:S(2)}) collective-permute-start(bf16[8,2,144,256]{3,2,1,0:T(8,128)(2,1)} %bitcast.81), channel_id=1, source_target_pairs={{0,64},{64,0},{1,65},{65,1},{2,66},{66,2},{3,67},{67,3},{4,68},{68... | collective-permute-start | bytes 3538952 | tf_op jit(solution)/shard_map/ppermute | solution.py:415
  136.2 62.8 %collective-permute-start.13 = (bf16[8,2,128,512]{3,2,1,0:T(8,128)(2,1)}, bf16[8,2,128,512]{3,2,1,0:T(8,128)(2,1)}, u32[]{:S(2)}, u32[]{:S(2)}) collective-permute-start(bf16[8,2,128,512]{3,2,1,0:T(8,128)(2,1)} %bitcast.19.wm), channel_id=1, source_target_pairs={{0,64},{64,0},{1,65},{65,1},{2,66},{66,2},{3,67},{67,3},{4,68},{68... | collective-permute-start | bytes 6291464 | tf_op jit(solution)/shard_map/ppermute | solution.py:415
  141.6 5.1 %collective-permute-start.2 = (bf16[64,1024]{1,0:T(8,128)(2,1)S(1)}, bf16[64,1024]{1,0:T(8,128)(2,1)S(1)}, u32[]{:S(2)}, u32[]{:S(2)}) collective-permute-start(bf16[64,1024]{1,0:T(8,128)(2,1)S(1)} %get-tuple-element.86.p0), channel_id=1, source_target_pairs={{0,1},{1,0},{2,3},{3,2},{4,5},{5,4},{6,7},{7,6},{8,9},{9,8},{10,11... | collective-permute-start | bytes 393224 | tf_op jit(solution)/shard_map/ppermute | solution.py:419
  142.9 8.9 %collective-permute-start.3 = (bf16[64,1024]{1,0:T(8,128)(2,1)S(1)}, bf16[64,1024]{1,0:T(8,128)(2,1)S(1)}, u32[]{:S(2)}, u32[]{:S(2)}) collective-permute-start(bf16[64,1024]{1,0:T(8,128)(2,1)S(1)} %get-tuple-element.86.p0), channel_id=1, source_target_pairs={{0,2},{1,3},{2,0},{3,1},{4,6},{5,7},{6,4},{7,5},{8,10},{9,11},{10,... | collective-permute-start | bytes 393224 | tf_op jit(solution)/shard_map/ppermute | solution.py:419
  146.8 8.0 %collective-permute-start.4 = (bf16[64,1024]{1,0:T(8,128)(2,1)S(1)}, bf16[64,1024]{1,0:T(8,128)(2,1)S(1)}, u32[]{:S(2)}, u32[]{:S(2)}) collective-permute-start(bf16[64,1024]{1,0:T(8,128)(2,1)S(1)} %get-tuple-element.86.p0), channel_id=1, source_target_pairs={{0,3},{1,2},{2,1},{3,0},{4,7},{5,6},{6,5},{7,4},{8,11},{9,10},{10,... | collective-permute-start | bytes 393224 | tf_op jit(solution)/shard_map/ppermute | solution.py:419
  158.7 4.6 %collective-permute-start.6 = (bf16[64,1024]{1,0:T(8,128)(2,1)S(1)}, bf16[64,1024]{1,0:T(8,128)(2,1)S(1)}, u32[]{:S(2)}, u32[]{:S(2)}) collective-permute-start(bf16[64,1024]{1,0:T(8,128)(2,1)S(1)} %get-tuple-element.90.p0), channel_id=1, source_target_pairs={{0,1},{1,0},{2,3},{3,2},{4,5},{5,4},{6,7},{7,6},{8,9},{9,8},{10,11... | collective-permute-start | bytes 393224 | tf_op jit(solution)/shard_map/ppermute | solution.py:419
  158.8 6.6 %collective-permute-start.7 = (bf16[64,1024]{1,0:T(8,128)(2,1)S(1)}, bf16[64,1024]{1,0:T(8,128)(2,1)S(1)}, u32[]{:S(2)}, u32[]{:S(2)}) collective-permute-start(bf16[64,1024]{1,0:T(8,128)(2,1)S(1)} %get-tuple-element.90.p0), channel_id=1, source_target_pairs={{0,2},{1,3},{2,0},{3,1},{4,6},{5,7},{6,4},{7,5},{8,10},{9,11},{10,... | collective-permute-start | bytes 393224 | tf_op jit(solution)/shard_map/ppermute | solution.py:419
  159.4 8.2 %collective-permute-start.8 = (bf16[64,1024]{1,0:T(8,128)(2,1)S(1)}, bf16[64,1024]{1,0:T(8,128)(2,1)S(1)}, u32[]{:S(2)}, u32[]{:S(2)}) collective-permute-start(bf16[64,1024]{1,0:T(8,128)(2,1)S(1)} %get-tuple-element.90.p0), channel_id=1, source_target_pairs={{0,3},{1,2},{2,1},{3,0},{4,7},{5,6},{6,5},{7,4},{8,11},{9,10},{10,... | collective-permute-start | bytes 393224 | tf_op jit(solution)/shard_map/ppermute | solution.py:419
  193.0 15.4 %copy-start.21 = (bf16[4,64,128]{2,1,0:T(8,128)(2,1)}, bf16[4,64,128]{2,1,0:T(8,128)(2,1)S(1)}, u32[]{:S(2)}) copy-start(bf16[4,64,128]{2,1,0:T(8,128)(2,1)S(1)} %get-tuple-element.138.att) | copy-start | bytes 196612
  193.0 6.0 %collective-permute-start.10 = (bf16[64,1024]{1,0:T(8,128)(2,1)S(1)}, bf16[64,1024]{1,0:T(8,128)(2,1)S(1)}, u32[]{:S(2)}, u32[]{:S(2)}) collective-permute-start(bf16[64,1024]{1,0:T(8,128)(2,1)S(1)} %get-tuple-element.94.p0), channel_id=1, source_target_pairs={{0,1},{1,0},{2,3},{3,2},{4,5},{5,4},{6,7},{7,6},{8,9},{9,8},{10,11... | collective-permute-start | bytes 393224 | tf_op jit(solution)/shard_map/ppermute | solution.py:419
  193.1 8.8 %collective-permute-start.11 = (bf16[64,1024]{1,0:T(8,128)(2,1)S(1)}, bf16[64,1024]{1,0:T(8,128)(2,1)S(1)}, u32[]{:S(2)}, u32[]{:S(2)}) collective-permute-start(bf16[64,1024]{1,0:T(8,128)(2,1)S(1)} %get-tuple-element.94.p0), channel_id=1, source_target_pairs={{0,2},{1,3},{2,0},{3,1},{4,6},{5,7},{6,4},{7,5},{8,10},{9,11},{10,... | collective-permute-start | bytes 393224 | tf_op jit(solution)/shard_map/ppermute | solution.py:419
  198.1 5.2 %collective-permute-start.12 = (bf16[64,1024]{1,0:T(8,128)(2,1)S(1)}, bf16[64,1024]{1,0:T(8,128)(2,1)S(1)}, u32[]{:S(2)}, u32[]{:S(2)}) collective-permute-start(bf16[64,1024]{1,0:T(8,128)(2,1)S(1)} %get-tuple-element.94.p0), channel_id=1, source_target_pairs={{0,3},{1,2},{2,1},{3,0},{4,7},{5,6},{6,5},{7,4},{8,11},{9,10},{10,... | collective-permute-start | bytes 393224 | tf_op jit(solution)/shard_map/ppermute | solution.py:419
  208.4 4.1 collective-permute-start.19
  208.7 5.4 %collective-permute-start.20 = (bf16[64,1024]{1,0:T(8,128)(2,1)S(1)}, bf16[64,1024]{1,0:T(8,128)(2,1)S(1)}, u32[]{:S(2)}, u32[]{:S(2)}) collective-permute-start(bf16[64,1024]{1,0:T(8,128)(2,1)S(1)} %get-tuple-element.97.p0), channel_id=1, source_target_pairs={{0,2},{1,3},{2,0},{3,1},{4,6},{5,7},{6,4},{7,5},{8,10},{9,11},{10,... | collective-permute-start | bytes 393224 | tf_op jit(solution)/shard_map/ppermute | solution.py:419
  210.3 5.2 %collective-permute-start.21 = (bf16[64,1024]{1,0:T(8,128)(2,1)S(1)}, bf16[64,1024]{1,0:T(8,128)(2,1)S(1)}, u32[]{:S(2)}, u32[]{:S(2)}) collective-permute-start(bf16[64,1024]{1,0:T(8,128)(2,1)S(1)} %get-tuple-element.97.p0), channel_id=1, source_target_pairs={{0,3},{1,2},{2,1},{3,0},{4,7},{5,6},{6,5},{7,4},{8,11},{9,10},{10,... | collective-permute-start | bytes 393224 | tf_op jit(solution)/shard_map/ppermute | solution.py:419
  215.5 28.3 %copy-start.3 = (bf16[32,144,256]{2,1,0:T(8,128)(2,1)S(1)}, bf16[32,144,256]{2,1,0:T(8,128)(2,1)}, u32[]{:S(2)}) copy-start(bf16[32,144,256]{2,1,0:T(8,128)(2,1)} %copy-done.2) | copy-start | bytes 7077892
  220.2 25.6 %copy-start.23 = (f32[8,1024]{1,0:T(8,128)}, f32[8,1024]{1,0:T(8,128)S(1)}, u32[]{:S(2)}) copy-start(f32[8,1024]{1,0:T(8,128)S(1)} %get-tuple-element.127.r1) | copy-start | bytes 98308
  245.9 3.9 collective-permute-start.22
  246.0 5.8 %collective-permute-start.23 = (bf16[64,1024]{1,0:T(8,128)(2,1)S(1)}, bf16[64,1024]{1,0:T(8,128)(2,1)S(1)}, u32[]{:S(2)}, u32[]{:S(2)}) collective-permute-start(bf16[64,1024]{1,0:T(8,128)(2,1)S(1)} %get-tuple-element.102.p0), channel_id=1, source_target_pairs={{0,2},{1,3},{2,0},{3,1},{4,6},{5,7},{6,4},{7,5},{8,10},{9,11},{10,... | collective-permute-start | bytes 393224 | tf_op jit(solution)/shard_map/ppermute | solution.py:419
  248.0 5.2 %collective-permute-start.24 = (bf16[64,1024]{1,0:T(8,128)(2,1)S(1)}, bf16[64,1024]{1,0:T(8,128)(2,1)S(1)}, u32[]{:S(2)}, u32[]{:S(2)}) collective-permute-start(bf16[64,1024]{1,0:T(8,128)(2,1)S(1)} %get-tuple-element.102.p0), channel_id=1, source_target_pairs={{0,3},{1,2},{2,1},{3,0},{4,7},{5,6},{6,5},{7,4},{8,11},{9,10},{10,... | collective-permute-start | bytes 393224 | tf_op jit(solution)/shard_map/ppermute | solution.py:419
  257.0 28.0 %copy-start.25 = (f32[8,1024]{1,0:T(8,128)}, f32[8,1024]{1,0:T(8,128)S(1)}, u32[]{:S(2)}) copy-start(f32[8,1024]{1,0:T(8,128)S(1)} %get-tuple-element.126.h1) | copy-start | bytes 98308
  258.3 17.3 %collective-permute-start.28 = (bf16[8,2,128,512]{3,2,1,0:T(8,128)(2,1)S(1)}, bf16[8,2,128,512]{3,2,1,0:T(8,128)(2,1)S(1)}, u32[]{:S(2)}, u32[]{:S(2)}) collective-permute-start(bf16[8,2,128,512]{3,2,1,0:T(8,128)(2,1)S(1)} %get-tuple-element.111), channel_id=1, source_target_pairs={{0,64},{64,0},{1,65},{65,1},{2,66},{66,2},{3,67},{67,3},{4,68},{68... | collective-permute-start | bytes 6291464 | tf_op jit(solution)/shard_map/ppermute | solution.py:415
  263.9 5.1 %collective-permute-start.25 = (bf16[64,1024]{1,0:T(8,128)(2,1)S(1)}, bf16[64,1024]{1,0:T(8,128)(2,1)S(1)}, u32[]{:S(2)}, u32[]{:S(2)}) collective-permute-start(bf16[64,1024]{1,0:T(8,128)(2,1)S(1)} %get-tuple-element.105.p0), channel_id=1, source_target_pairs={{0,1},{1,0},{2,3},{3,2},{4,5},{5,4},{6,7},{7,6},{8,9},{9,8},{10,11... | collective-permute-start | bytes 393224 | tf_op jit(solution)/shard_map/ppermute | solution.py:419
  263.9 9.2 %collective-permute-start.26 = (bf16[64,1024]{1,0:T(8,128)(2,1)S(1)}, bf16[64,1024]{1,0:T(8,128)(2,1)S(1)}, u32[]{:S(2)}, u32[]{:S(2)}) collective-permute-start(bf16[64,1024]{1,0:T(8,128)(2,1)S(1)} %get-tuple-element.105.p0), channel_id=1, source_target_pairs={{0,2},{1,3},{2,0},{3,1},{4,6},{5,7},{6,4},{7,5},{8,10},{9,11},{10,... | collective-permute-start | bytes 393224 | tf_op jit(solution)/shard_map/ppermute | solution.py:419
  266.7 9.0 %collective-permute-start.27 = (bf16[64,1024]{1,0:T(8,128)(2,1)S(1)}, bf16[64,1024]{1,0:T(8,128)(2,1)S(1)}, u32[]{:S(2)}, u32[]{:S(2)}) collective-permute-start(bf16[64,1024]{1,0:T(8,128)(2,1)S(1)} %get-tuple-element.105.p0), channel_id=1, source_target_pairs={{0,3},{1,2},{2,1},{3,0},{4,7},{5,6},{6,5},{7,4},{8,11},{9,10},{10,... | collective-permute-start | bytes 393224 | tf_op jit(solution)/shard_map/ppermute | solution.py:419
  275.7 1.4 copy-start.39
  287.0 7.5 %copy-start.22 = (bf16[4,64,128]{2,1,0:T(8,128)(2,1)S(1)}, bf16[4,64,128]{2,1,0:T(8,128)(2,1)}, u32[]{:S(2)}) copy-start(bf16[4,64,128]{2,1,0:T(8,128)(2,1)} %copy-done.21) | copy-start | bytes 196612
  287.6 44.0 %all-to-all-start.5 = ((bf16[16,192,512]{2,1,0:T(8,128)(2,1)}), bf16[16,192,512]{2,1,0:T(8,128)(2,1)}, u32[]{:S(2)}, u32[]{:S(2)}) async-start(bf16[16,192,512]{2,1,0:T(8,128)(2,1)} %get-tuple-element.113), calls=%async_computation.5 | async-start | bytes 6291456 | tf_op jit(solution)/shard_map/all_to_all | solution.py:424
  293.4 7.3 %copy-start.30 = (f32[1,1024]{1,0:T(1,128)}, f32[1,1024]{1,0:T(1,128)S(1)}, u32[]{:S(2)}) copy-start(f32[1,1024]{1,0:T(1,128)S(1)} %get-tuple-element.131.o1) | copy-start | bytes 12292
  293.4 4.9 %collective-permute-start.36 = (bf16[8,2,128,512]{3,2,1,0:T(8,128)(2,1)S(1)}, bf16[8,2,128,512]{3,2,1,0:T(8,128)(2,1)S(1)}, u32[]{:S(2)}, u32[]{:S(2)}) collective-permute-start(bf16[8,2,128,512]{3,2,1,0:T(8,128)(2,1)S(1)} %get-tuple-element.143), channel_id=1, source_target_pairs={{0,64},{64,0},{1,65},{65,1},{2,66},{66,2},{3,67},{67,3},{4,68},{68... | collective-permute-start | bytes 6291464 | tf_op jit(solution)/shard_map/ppermute | solution.py:415
  295.5 4.2 %collective-permute-start.35 = (bf16[8,2,128,256]{3,2,1,0:T(8,128)(2,1)S(1)}, bf16[8,2,128,256]{3,2,1,0:T(8,128)(2,1)S(1)}, u32[]{:S(2)}, u32[]{:S(2)}) collective-permute-start(bf16[8,2,128,256]{3,2,1,0:T(8,128)(2,1)S(1)} %get-tuple-element.141), channel_id=1, source_target_pairs={{0,64},{64,0},{1,65},{65,1},{2,66},{66,2},{3,67},{67,3},{4,68},{68... | collective-permute-start | bytes 3145736 | tf_op jit(solution)/shard_map/ppermute | solution.py:415
  300.7 1.7 copy-start.5
  302.4 36.1 %copy-start.4 = (bf16[32,144,256]{2,1,0:T(8,128)(2,1)S(1)}, bf16[32,144,256]{2,1,0:T(8,128)(2,1)}, u32[]{:S(2)}) copy-start(bf16[32,144,256]{2,1,0:T(8,128)(2,1)} %copy-done.2) | copy-start | bytes 7077892
  331.6 45.9 %all-to-all-start.7 = ((bf16[16,128,768]{2,1,0:T(8,128)(2,1)}), bf16[16,128,768]{2,1,0:T(8,128)(2,1)}, u32[]{:S(2)}, u32[]{:S(2)}) async-start(bf16[16,128,768]{2,1,0:T(8,128)(2,1)} %copy-done.5), calls=%async_computation.7 | async-start | bytes 6291456 | tf_op jit(solution)/shard_map/all_to_all | solution.py:424
  338.5 0.8 copy-start.18
  339.4 3.1 copy-start.11
  339.4 3.1 copy-start.15
  339.4 3.1 copy-start.20
  339.4 25.9 %copy-start.7 = (f32[64,1024]{1,0:T(8,128)S(1)}, f32[64,1024]{1,0:T(8,128)}, u32[]{:S(2)}) copy-start(f32[64,1024]{1,0:T(8,128)} %copy-done.6) | copy-start | bytes 786436
  342.4 2.0 copy-start.32
  344.5 20.8 %collective-permute-start.32 = (bf16[8,2,128,256]{3,2,1,0:T(8,128)(2,1)}, bf16[8,2,128,256]{3,2,1,0:T(8,128)(2,1)S(1)}, u32[]{:S(2)}, u32[]{:S(2)}) collective-permute-start(bf16[8,2,128,256]{3,2,1,0:T(8,128)(2,1)} %get-tuple-element.121), channel_id=1, source_target_pairs={{0,64},{64,0},{1,65},{65,1},{2,66},{66,2},{3,67},{67,3},{4,68},{68... | collective-permute-start | bytes 3145736 | tf_op jit(solution)/shard_map/ppermute | solution.py:415
  346.4 9.5 %collective-permute-start.16 = (bf16[64,1024]{1,0:T(8,128)(2,1)}, bf16[64,1024]{1,0:T(8,128)(2,1)S(1)}, u32[]{:S(2)}, u32[]{:S(2)}) collective-permute-start(bf16[64,1024]{1,0:T(8,128)(2,1)} %get-tuple-element.96), channel_id=1, source_target_pairs={{0,3},{1,2},{2,1},{3,0},{4,7},{5,6},{6,5},{7,4},{8,11},{9,10},{10,... | collective-permute-start | bytes 393224 | tf_op jit(solution)/shard_map/ppermute | solution.py:419
  347.5 8.4 %collective-permute-start.15 = (bf16[64,1024]{1,0:T(8,128)(2,1)}, bf16[64,1024]{1,0:T(8,128)(2,1)S(1)}, u32[]{:S(2)}, u32[]{:S(2)}) collective-permute-start(bf16[64,1024]{1,0:T(8,128)(2,1)} %get-tuple-element.96), channel_id=1, source_target_pairs={{0,2},{1,3},{2,0},{3,1},{4,6},{5,7},{6,4},{7,5},{8,10},{9,11},{10,... | collective-permute-start | bytes 393224 | tf_op jit(solution)/shard_map/ppermute | solution.py:419
  347.5 9.2 %collective-permute-start.14 = (bf16[64,1024]{1,0:T(8,128)(2,1)}, bf16[64,1024]{1,0:T(8,128)(2,1)}, u32[]{:S(2)}, u32[]{:S(2)}) collective-permute-start(bf16[64,1024]{1,0:T(8,128)(2,1)} %get-tuple-element.96), channel_id=1, source_target_pairs={{0,1},{1,0},{2,3},{3,2},{4,5},{5,4},{6,7},{7,6},{8,9},{9,8},{10,11... | collective-permute-start | bytes 393224 | tf_op jit(solution)/shard_map/ppermute | solution.py:419
  349.7 9.5 %collective-permute-start.29 = (bf16[64,1024]{1,0:T(8,128)(2,1)}, bf16[64,1024]{1,0:T(8,128)(2,1)S(1)}, u32[]{:S(2)}, u32[]{:S(2)}) collective-permute-start(bf16[64,1024]{1,0:T(8,128)(2,1)} %copy-done.12), channel_id=1, source_target_pairs={{0,1},{1,0},{2,3},{3,2},{4,5},{5,4},{6,7},{7,6},{8,9},{9,8},{10,11... | collective-permute-start | bytes 393224 | tf_op jit(solution)/shard_map/ppermute | solution.py:419
  355.9 6.4 %collective-permute-start.30 = (bf16[64,1024]{1,0:T(8,128)(2,1)}, bf16[64,1024]{1,0:T(8,128)(2,1)S(1)}, u32[]{:S(2)}, u32[]{:S(2)}) collective-permute-start(bf16[64,1024]{1,0:T(8,128)(2,1)} %copy-done.12), channel_id=1, source_target_pairs={{0,2},{1,3},{2,0},{3,1},{4,6},{5,7},{6,4},{7,5},{8,10},{9,11},{10,... | collective-permute-start | bytes 393224 | tf_op jit(solution)/shard_map/ppermute | solution.py:419
  355.9 9.4 %collective-permute-start.31 = (bf16[64,1024]{1,0:T(8,128)(2,1)}, bf16[64,1024]{1,0:T(8,128)(2,1)S(1)}, u32[]{:S(2)}, u32[]{:S(2)}) collective-permute-start(bf16[64,1024]{1,0:T(8,128)(2,1)} %copy-done.12), channel_id=1, source_target_pairs={{0,3},{1,2},{2,1},{3,0},{4,7},{5,6},{6,5},{7,4},{8,11},{9,10},{10,... | collective-permute-start | bytes 393224 | tf_op jit(solution)/shard_map/ppermute | solution.py:419
  357.8 14.5 %collective-permute-start.17 = (bf16[64,1024]{1,0:T(8,128)(2,1)S(1)}, bf16[64,1024]{1,0:T(8,128)(2,1)S(1)}, u32[]{:S(2)}, u32[]{:S(2)}) collective-permute-start(bf16[64,1024]{1,0:T(8,128)(2,1)S(1)} %get-tuple-element.164), channel_id=1, source_target_pairs={{0,64},{64,0},{1,65},{65,1},{2,66},{66,2},{3,67},{67,3},{4,68},{68... | collective-permute-start | bytes 393224 | tf_op jit(solution)/shard_map/ppermute | solution.py:415
  365.2 0.9 copy-start.13
  371.5 15.1 %collective-permute-start.33 = (bf16[64,1024]{1,0:T(8,128)(2,1)S(1)}, bf16[64,1024]{1,0:T(8,128)(2,1)S(1)}, u32[]{:S(2)}, u32[]{:S(2)}) collective-permute-start(bf16[64,1024]{1,0:T(8,128)(2,1)S(1)} %broadcast_select_fusion.4), channel_id=1, source_target_pairs={{0,64},{64,0},{1,65},{65,1},{2,66},{66,2},{3,67},{67,3},{4,68},{68... | collective-permute-start | bytes 393224 | tf_op jit(solution)/shard_map/ppermute | solution.py:415
  377.4 32.8 %all-to-all-start.6 = ((bf16[16,144,256]{2,1,0:T(8,128)(2,1)}), bf16[16,144,256]{2,1,0:T(8,128)(2,1)S(1)}, u32[]{:S(2)}, u32[]{:S(2)}) async-start(bf16[16,144,256]{2,1,0:T(8,128)(2,1)} %get-tuple-element.135), calls=%async_computation.6 | async-start | bytes 2359296 | tf_op jit(solution)/shard_map/all_to_all | solution.py:424
  383.6 20.2 %collective-permute-start.18 = (bf16[2,64,1024]{2,1,0:T(8,128)(2,1)S(1)}, bf16[2,64,1024]{2,1,0:T(8,128)(2,1)S(1)}, u32[]{:S(2)}, u32[]{:S(2)}) collective-permute-start(bf16[2,64,1024]{2,1,0:T(8,128)(2,1)S(1)} %pad_maximum_fusion), channel_id=1, source_target_pairs={{0,4},{4,0},{1,5},{5,1},{2,6},{6,2},{3,7},{7,3},{8,12},{12,8},{9,1... | collective-permute-start | bytes 786440 | tf_op jit(solution)/shard_map/ppermute | solution.py:435
  386.6 22.8 %collective-permute-start.34 = (bf16[2,64,1024]{2,1,0:T(8,128)(2,1)S(1)}, bf16[2,64,1024]{2,1,0:T(8,128)(2,1)S(1)}, u32[]{:S(2)}, u32[]{:S(2)}) collective-permute-start(bf16[2,64,1024]{2,1,0:T(8,128)(2,1)S(1)} %pad_maximum_fusion.1), channel_id=1, source_target_pairs={{0,4},{4,0},{1,5},{5,1},{2,6},{6,2},{3,7},{7,3},{8,12},{12,8},{9,1... | collective-permute-start | bytes 786440 | tf_op jit(solution)/shard_map/ppermute | solution.py:435
  410.3 12.0 %copy-start.1 = (bf16[2,1,128,1024]{3,2,1,0:T(8,128)(2,1)S(1)}, bf16[2,1,128,1024]{3,2,1,0:T(8,128)(2,1)}, u32[]{:S(2)}) copy-start(bf16[2,1,128,1024]{3,2,1,0:T(8,128)(2,1)} %param.11) | copy-start | bytes 1572868
  (17 other events, 11.6 us)

commit v3 on v2

--- a/solution.py
+++ b/solution.py
@@ -73,8 +73,6 @@
 
 
 def attn_tile(ref, yh):
-    if len(ref.shape) == 5:
-        return ref[0, :, yh, 0:128, :].reshape(D, 256)
     return ref[:, yh, 0:128, :].reshape(D, 256)
 
 
@@ -149,7 +147,7 @@
             kv[g, kv.shape[1] - ROWS :, k * 128 : k * 128 + 128] = pair
 
 
-def pack_kernel(qkv, out, up, down, gain, shift, inb, outb, upb, msg, ffn):
+def pack_kernel(core, qkv, out, up, down, gain, shift, inb, outb, upb, keep, send):
     wt = out[...].astype(F32).T
     dt = down[...].astype(F32).T
     inb_, gain_, shift_, outb_ = [r[...].astype(F32) for r in (inb, gain, shift, outb)]
@@ -162,36 +160,53 @@
         cols = slice(j * 64, j * 64 + 64)
         rows.append(jnp.concatenate([zero, inb_[1:2, cols], inb_[0:1, cols], zero], axis=1))
     ups = [upb_[:, :256], upb_[:, 256:]]
-    tail = [flat(gain_), flat(shift_), flat(outb_), jnp.zeros((9, 256), F32)]
+    rest = [flat(gain_), flat(shift_), flat(outb_), jnp.zeros((9, 256), F32)]
+    halves = []
     for j in range(2):
         cols = slice(j * 64, j * 64 + 64)
-        tile = jnp.concatenate(
-            [
-                qkv[1, :, cols].astype(F32),
-                qkv[2, :, cols].astype(F32),
-                qkv[0, :, cols].astype(F32),
-                wt[:, cols],
-            ],
-            axis=1,
-        ).astype(BF)
-        small = jnp.concatenate([rows[j], rows[1 - j], ups[j], ups[1 - j], *tail]).astype(BF)
-        for g in range(16):
-            msg[j, g, 0:128, :] = tile
-            msg[j, g, 128:144, :] = small
-        ffn[j, :, 0:256] = up[:, j * 256 : j * 256 + 256]
-        ffn[j, :, 256:512] = dt[:, j * 256 : j * 256 + 256].astype(BF)
+        wide = slice(j * 256, j * 256 + 256)
+        halves.append(
+            (
+                up[:, wide].astype(F32),
+                dt[:, wide],
+                jnp.concatenate([qkv[i, :, cols].astype(F32) for i in (1, 2, 0)] + [wt[:, cols]], axis=1),
+                jnp.concatenate([rows[j], rows[1 - j], ups[j], ups[1 - j], *rest]),
+            )
+        )
+    first = core[0] == 0
+    for ref, pair in ((keep, halves), (send, halves[::-1])):
+        values = [jnp.where(first, a, b).astype(BF) for a, b in zip(*pair)]
+        ref[0:128, 0:256] = values[0]
+        ref[0:128, 256:512] = values[1]
+        ref[0:128, 512:768] = values[2]
+        ref[128:144, 512:768] = values[3]
+
+
+def spread_kernel(core, keep, got, msg, ffn0, ffn1, attn1):
+    first = core[0] == 0
+    k, o = keep[...], got[...]
+    lower, upper = jnp.where(first, k, o), jnp.where(first, o, k)
+    small = jnp.concatenate(
+        [v[128:144, 512:768].astype(F32)[0:8] for v in (lower, upper)]
+    ).astype(BF)
+    tile = lower[0:128, 512:768]
+    for g in range(16):
+        msg[g, 0:128, :] = tile
+        msg[g, 128:144, :] = small
+    ffn0[...] = lower[0:128, 0:512]
+    ffn1[...] = upper[0:128, 0:512]
+    attn1[...] = upper[0:128, 512:768]
 
 
 def first_kernel(x, params, wm, wo, piece, n1, q, msg, lnp, bias):
     for layer in range(2):
-        blocks = [params[layer, d, 0].astype(F32) for d in range(8)]
+        part = slice(layer * 8, layer * 8 + 8)
+        blocks = [params[d, 0].astype(F32)[part] for d in range(8)]
         for half in range(2):
             cols = slice(half * 128, half * 128 + 128)
-            lnp[half, layer * 8 : layer * 8 + 8, :] = jnp.concatenate(
-                [b[0:8, cols] for b in blocks], axis=1
-            )
+            lnp[half, part, :] = jnp.concatenate([b[:, cols] for b in blocks], axis=1)
         for yh in range(2):
-            bias[yh, layer * 8 : layer * 8 + 8, :] = params[layer, 0, yh].astype(F32)[0:8]
+            bias[yh, part, :] = params[0, yh].astype(F32)[part]
     project(x[...].astype(F32), lnp, bias, wm, wo, 0, n1, q, msg)
     rest = piece[...]
     for g in range(16):
@@ -374,33 +389,32 @@
 
 
 def combine_kernel(am, ar, fm, fr, msg):
-    msg[0, :, 0:256] = (am[0].astype(F32) + ar[0].astype(F32)).astype(BF)
-    msg[0, :, 256:768] = (fm[0].astype(F32) + fr[0].astype(F32)).astype(BF)
+    msg[0, :, 0:512] = (fm[0].astype(F32) + fr[0].astype(F32)).astype(BF)
+    msg[0, :, 512:768] = (am[0].astype(F32) + ar[0].astype(F32)).astype(BF)
 
 
 def settle_kernel(tail, l0, l1, out):
     t = jnp.sum(tail[...].astype(F32), axis=0)
-    out[0, 0:128, 0:256] = t[0:128]
-    out[1, 0:128, 0:256] = jnp.sum(l1[:, :, 0:256].astype(F32), axis=0)
+    out[0, 0:128, 512:768] = t[0:128]
     for j in range(2):
-        cols = slice(256 + j * 256, 512 + j * 256)
-        out[0, 0:128, cols] = jnp.sum(l0[:, 0:128, j * 256 : j * 256 + 256].astype(F32), axis=0)
-        out[1, 0:128, cols] = jnp.sum(l1[:, :, cols].astype(F32), axis=0)
+        cols = slice(j * 256, j * 256 + 256)
+        out[0, 0:128, cols] = jnp.sum(l0[:, 0:128, cols].astype(F32), axis=0)
+    out[1, 0:128, :] = l1[...].astype(F32)
     small = t[128:144]
     pad = jnp.zeros((1, 256), F32)
-    out[0, 128:136, 0:256] = jnp.concatenate([small[0:7], pad])
-    out[1, 128:136, 0:256] = jnp.concatenate([small[7:14], pad])
+    out[0, 128:136, 512:768] = jnp.concatenate([small[0:7], pad])
+    out[1, 128:136, 512:768] = jnp.concatenate([small[7:14], pad])
 
 
 def unpack_kernel(r, qkv, out, up, down, gain, shift, inb, outb, upb):
-    a = [r[j, 0:128, 0:256] for j in range(2)]
+    a = [r[j, 0:128, 512:768] for j in range(2)]
     for i, at in enumerate((128, 0, 64)):
         qkv[i] = jnp.concatenate([t[:, at : at + 64] for t in a], axis=1)
     out[...] = jnp.concatenate([t[:, 192:256] for t in a], axis=1).T
     for j in range(2):
-        up[:, j * 256 : j * 256 + 256] = r[j, 0:128, 256:512]
-        down[j * 256 : j * 256 + 256, :] = r[j, 0:128, 512:768].T
-    s0, s1 = r[0, 128:136, 0:256], r[1, 128:136, 0:256]
+        up[:, j * 256 : j * 256 + 256] = r[j, 0:128, 0:256]
+        down[j * 256 : j * 256 + 256, :] = r[j, 0:128, 256:512].T
+    s0, s1 = r[0, 128:136, 512:768], r[1, 128:136, 512:768]
     for row, ref in ((4, gain), (5, shift), (6, outb)):
         t = s0[row : row + 1] + s1[row : row + 1]
         ref[0:1, :] = t[:, 0:128]
@@ -446,25 +460,30 @@
         return lax.dynamic_slice(v, (s, 0, yh * ROWS, 0), (1, 1, ROWS, D)).reshape(ROWS, D)
 
     x, cot = own_rows(inputs), own_rows(cotangent)
-    msg, ffn = call(
+    core = (s.astype(jnp.int32).reshape(1), None, None)
+    keep, send = call(
         pack_kernel,
-        [sds(2, 16, 144, 256), sds(2, 128, 512)],
+        [sds(144, 768), sds(144, 768)],
         [
-            jnp.moveaxis(wqkv[0], 1, 0), wout[0], wup[0], wdown[0],
+            core, jnp.moveaxis(wqkv[0], 1, 0), wout[0], wup[0], wdown[0],
             gain[0], shift[0], inb[0], outb[0], upb,
         ],
     )
-    u = exchange(msg.reshape(32, 144, 256), ("s", *CHIPS)).reshape(2, 16, 144, 256)
-    got = swap_cores(by_layer(s, ffn[1], ffn[0]))
-    piece0, piece1 = by_layer(s, ffn[0], got), by_layer(s, got, ffn[1])
-    u = u.reshape(2, 8, 2, 144, 256)
-    am = [(u, (1, 8, 2, 144, 256), (l, 0, 0, 0, 0)) for l in range(2)]
-    ao = [swap_cores(u[l]) for l in range(2)]
+    msg, piece0, ffn1, attn1 = call(
+        spread_kernel,
+        [sds(16, 144, 256), sds(128, 512), sds(128, 512), sds(128, 256)],
+        [core, keep, swap_cores(send)],
+    )
+    a0 = exchange(msg).reshape(8, 2, 144, 256)
+    a1 = lax.all_gather(attn1, CHIPS, axis=0, tiled=True).reshape(8, 2, 128, 256)
+    f1 = lax.all_gather(ffn1, CHIPS, axis=0, tiled=True).reshape(8, 2, 128, 512)
+    am, ao = [a0, a1], [swap_cores(a0), swap_cores(a1)]
+    f1o = swap_cores(f1)
     kinds = dict(n1=sds(ROWS, D), q=sds(4, ROWS, 128))
     n10, q0, msg, lnp, bias = call(
         first_kernel,
         [kinds["n1"], kinds["q"], sds(16, 192, 512), sds(2, 16, D, dtype=F32), sds(2, 16, 256, dtype=F32)],
-        [x, (u, (2, 8, 2, 16, 256), (0, 0, 0, 8, 0)), am[0], ao[0], piece0],
+        [x, (a0, (8, 2, 16, 256), (0, 0, 8, 0)), am[0], ao[0], piece0],
     )
     got0 = exchange(msg)
     kv0 = (got0, (16, ROWS, 512), (0, 2, 0))
@@ -476,8 +495,6 @@
         sds(4, ROWS, 256, dtype=F32), sds(4, ROWS, 256),
     ]
     part, prob0, att0 = call(attend_kernel, attend_outs, [(first, None, None), q0, kv0, am[0], ao[0]])
-    f1 = exchange(jnp.broadcast_to(piece1, (16, 128, 512))).reshape(8, 2, 128, 512)
-    f1o = swap_cores(f1)
     part, mid0, n20, pre0, act0 = call(
         feed_kernel, feed_outs, [x, *all_parts(part), lnp, bias, f0, f0o]
     )
@@ -534,7 +551,7 @@
         compiler_params=pltpu.CompilerParams(vmem_limit_bytes=32 * 1024 * 1024),
         cost_estimate=pl.CostEstimate(flops=0, bytes_accessed=9_000_000, transcendentals=0),
     )(flat(gam1), flat(gar1), flat(gfm1), flat(gfr1))
-    l1 = exchange(msg1)
+    l1 = lax.psum_scatter(msg1.reshape(2048, 768), CHIPS, scatter_dimension=0, tiled=True)
     dmid0, bg0, dq0, msg, rows0 = call(
         attend_back_first_kernel,
         back_outs + [sds(16, 192, 512), rows_out],

time: 424 us -> 560 us (1.32)
  waiting for transfers between devices: 134 us -> 228 us
  local copies, waits for them, and re-layouts: 23.5 us -> 45.7 us
  starting transfers between devices: 70.5 us -> 84.6 us
  between operations: 1.14 us -> 14.4 us
  blocking collectives: 134 us -> 124 us
    all_gather x0 -> x2, waiting for transfers between devices: none -> 101 us  [the longest x1 75.5 us: local(): f1 = lax.all_gather(ffn1, CHIPS, axis=0, tiled=True).reshape(8, 2, 128, 512)]
    unnamed x80 -> x184, local copies, waits for them, and re-layouts: 19.3 us -> 44.8 us
    ppermute x11, starting transfers between devices: 14.1 us -> 33.5 us  [swap_cores(): return lax.ppermute(v, 's', [(0, 1), (1, 0)])]
    all_to_all x4 -> x3, waiting for transfers between devices: 62.4 us -> 51.5 us  [exchange(): return lax.all_to_all(v, axes, 0, 0, tiled=True)]
    all_to_all x5 -> x4, blocking collectives: 134 us -> 124 us  [exchange(): return lax.all_to_all(v, axes, 0, 0, tiled=True)]
    pallas_call x1, Pallas kernels: 0.91 us -> 7.83 us  [local(): pl.pallas_call(combine_kernel, grid=(16,), out_shape=sds(16, 128, 768), i...]
    pallas_call x19 -> x20, Pallas kernels: 55.8 us -> 49.9 us  [call(): pl.pallas_call(kernel, grid=(1,), out_shape=outs, in_specs=specs, out_spe...]
    all_to_all x4 -> x3, starting transfers between devices: 22 us -> 19.8 us  [exchange(): return lax.all_to_all(v, axes, 0, 0, tiled=True)]
  transfers between devices with their start and end apart: 41 -> 43, of which waited for: 27 -> 28; matrix products, arithmetic and copies ran while one was open for 1% -> 1% of each run, Pallas kernels for 5% -> 8%
where the time goes in v3:
time: 560 us; the launch traced here: 558 us
  waiting for transfers between devices  228 us (41%)
  blocking collectives  124 us (22%)
  starting transfers between devices  84.6 us (15%)
  Pallas kernels  57.7 us (10%)
  local copies, waits for them, and re-layouts  45.7 us (8%)
  between operations  14.4 us (3%)
    all_to_all x4, blocking collectives, exchange(): return lax.all_to_all(v, axes, 0, 0, tiled=True)  124 us
    all_gather x1, waiting for transfers between devices, local(): f1 = lax.all_gather(ffn1, CHIPS, axis=0, tiled=True).reshape(8, 2, 128, 512)  75.5 us
    all_to_all x3, waiting for transfers between devices, exchange(): return lax.all_to_all(v, axes, 0, 0, tiled=True)  51.5 us
    pallas_call x20, Pallas kernels, call(): pl.pallas_call(kernel, grid=(1,), out_shape=outs, in_specs=specs, out_spe...  49.9 us
    unnamed x184, local copies, waits for them, and re-layouts  44.8 us
    ppermute x24, waiting for transfers between devices, all_parts(): lax.ppermute(part, 'x', [(i, i ^ k) for i in range(4)])  44.1 us
    ppermute x11, starting transfers between devices, swap_cores(): return lax.ppermute(v, 's', [(0, 1), (1, 0)])  33.5 us
    ppermute x24, starting transfers between devices, all_parts(): lax.ppermute(part, 'x', [(i, i ^ k) for i in range(4)])  28.1 us
  transfers between devices with their start and end apart: 43, of which 28 were waited for; matrix products, arithmetic and copies ran while one was open for 1% of the time, Pallas kernels for 8%

profile of v3, /device:TPU:1, one launch (start us, length us, event | category | flops | bytes accessed | tf_op | source)
XLA Modules:
  0.0 557.8 jit_solution(10634985722844272031)
XLA Ops:
  14.3 1.5 collective-permute-start
  17.6 25.1 %all_to_all.35 = bf16[16,144,256]{2,1,0:T(8,128)(2,1)S(1)} all-to-all(bf16[16,144,256]{2,1,0:T(8,128)(2,1)S(1)} %get-tuple-element.88), channel_id=1, replica_groups=mesh['s'=2,'z'=4,'yl'=2,'yh'=2,'x'=4] {'z','yl','yh'}, dimensions={0} | all-to-all | bytes 2359296 | tf_op jit(solution)/shard_map/all_to_all | solution.py:438
  42.7 2.0 collective-permute-start.1
  44.8 2.4 collective-permute-done.1.wo
  48.1 1.7 copy-done.17
  50.4 3.8 all-to-all-start.1
  55.0 46.8 %all-to-all-done.1.kv = bf16[16,192,512]{2,1,0:T(8,128)(2,1)S(1)} async-done(((bf16[16,192,512]{2,1,0:T(8,128)(2,1)}), bf16[16,192,512]{2,1,0:T(8,128)(2,1)S(1)}, u32[]{:S(2)}, u32[]{:S(2)}) %all-to-all-start.1) | async-done | bytes 3145760 | tf_op jit(solution)/shard_map/all_to_all | solution.py:438
  101.7 1.9 collective-permute-start.5
  103.6 25.3 %all-gather.3.cloned.1.call-done = bf16[2048,256]{1,0:T(8,128)(2,1)} async-done(((bf16[128,256]{1,0:T(8,128)(2,1)}), bf16[2048,256]{1,0:T(8,128)(2,1)}) %all-gather.3.cloned.1.call-update) | async-done | bytes 1048592 | tf_op jit(solution)/shard_map/all_gather | solution.py:478
  128.9 6.5 %collective-permute-start.9 = (bf16[8,2,128,256]{3,2,1,0:T(8,128)(2,1)}, bf16[8,2,128,256]{3,2,1,0:T(8,128)(2,1)}, u32[]{:S(2)}, u32[]{:S(2)}) collective-permute-start(bf16[8,2,128,256]{3,2,1,0:T(8,128)(2,1)} %bitcast.61), channel_id=1, source_target_pairs={{0,64},{64,0},{1,65},{65,1},{2,66},{66,2},{3,67},{67,3},{4,68},{68... | collective-permute-start | bytes 3145736 | tf_op jit(solution)/shard_map/ppermute | solution.py:429
  135.4 75.5 %all-gather.5.cloned.1.call-done = bf16[2048,512]{1,0:T(8,128)(2,1)} async-done(((bf16[128,512]{1,0:T(8,128)(2,1)}), bf16[2048,512]{1,0:T(8,128)(2,1)}) %all-gather.5.cloned.1.call-update) | async-done | bytes 2097168 | tf_op jit(solution)/shard_map/all_gather | solution.py:479
  210.8 9.5 %collective-permute-start.13 = (bf16[8,2,128,512]{3,2,1,0:T(8,128)(2,1)}, bf16[8,2,128,512]{3,2,1,0:T(8,128)(2,1)}, u32[]{:S(2)}, u32[]{:S(2)}) collective-permute-start(bf16[8,2,128,512]{3,2,1,0:T(8,128)(2,1)} %bitcast.67), channel_id=1, source_target_pairs={{0,64},{64,0},{1,65},{65,1},{2,66},{66,2},{3,67},{67,3},{4,68},{68... | collective-permute-start | bytes 6291464 | tf_op jit(solution)/shard_map/ppermute | solution.py:429
  222.8 3.7 shard_map.197
  228.2 1.6 collective-permute-start.3
  229.8 3.5 collective-permute-done.2.p1
  233.7 2.5 collective-permute-done.3.p2
  236.2 2.1 collective-permute-done.4.p3
  238.3 1.9 copy-done.3
  240.2 3.4 shard_map.198
  244.9 1.4 collective-permute-start.6
  246.4 2.7 collective-permute-start.7
  249.1 5.5 collective-permute-done.7.p2
  254.6 2.5 collective-permute-done.8.p3
  257.9 2.0 shard_map.199
  259.9 21.7 %all_to_all.36.kv = bf16[16,64,512]{2,1,0:T(8,128)(2,1)S(1)} all-to-all(bf16[16,64,512]{2,1,0:T(8,128)(2,1)S(1)} %get-tuple-element.100), channel_id=1, replica_groups=mesh['s'=2,'z'=4,'yl'=2,'yh'=2,'x'=4] {'z','yl','yh'}, dimensions={0} | all-to-all | bytes 2097152 | tf_op jit(solution)/shard_map/all_to_all | solution.py:438
  281.6 4.1 shard_map.200
  286.4 3.9 collective-permute-start.12
  293.1 4.5 shard_map.201
  299.3 3.0 collective-permute-start.20
  302.8 3.4 collective-permute-done.20.p2
  306.1 1.4 collective-permute-done.21.p3
  307.5 5.4 shard_map.202
  315.6 8.9 %all-to-all-start.3 = ((bf16[16,64,512]{2,1,0:T(8,128)(2,1)}), bf16[16,64,512]{2,1,0:T(8,128)(2,1)}, u32[]{:S(2)}, u32[]{:S(2)}) async-start(bf16[16,64,512]{2,1,0:T(8,128)(2,1)} %get-tuple-element.108), calls=%async_computation.3 | async-start | bytes 2097152 | tf_op jit(solution)/shard_map/all_to_all | solution.py:438
  327.4 2.7 shard_map.209
  331.4 2.1 collective-permute-start.36
  333.5 4.7 all-to-all-done.3.dkv
  340.3 2.3 shard_map.203
  342.7 3.0 collective-permute-start.23
  346.6 2.9 collective-permute-done.23.p2
  351.8 3.6 shard_map.204
  356.7 2.6 shard_map.205
  360.8 4.5 collective-permute-start.28
  367.0 3.6 collective-permute-done.35
  370.6 7.8 %shard_map.212 = bf16[16,128,768]{2,1,0:T(8,128)(2,1)S(1)} custom-call(bf16[16,128,256]{2,1,0:T(8,128)(2,1)S(1)} %bitcast.70, bf16[16,128,256]{2,1,0:T(8,128)(2,1)S(1)} %bitcast.71, bf16[16,128,512]{2,1,0:T(8,128)(2,1)S(1)} %bitcast.69, bf16[16,128,512]{2,1,0:T(8,128)(2,1)} %bitcast.30.fr), custom_call_target="tpu_custom_call" | custom-call | bytes 9000000 | tf_op jit(solution)/shard_map/pallas_call | solution.py:545
  378.4 1.7 copy-done.15
  381.0 2.4 collective-permute-start.26
  383.4 1.5 collective-permute-start.27
  385.7 3.8 collective-permute-done.26.p2
  389.5 2.6 collective-permute-done.27.p3
  393.4 7.7 %shard_map.206 = (f32[64,1024]{1,0:T(8,128)S(1)}, bf16[64,1024]{1,0:T(8,128)(2,1)S(1)}, bf16[4,64,128]{2,1,0:T(8,128)(2,1)S(1)}, bf16[16,192,512]{2,1,0:T(8,128)(2,1)}, f32[8,1024]{1,0:T(8,128)S(1)}) custom-call(bf16[64,1024]{1,0:T(8,128)(2,1)S(1)} %get-tuple-element.112.g, f32[64,1024]{1,0:T(8,128)S(1)} %copy-done.31, bf16[64,1024]{1,0:T(8,128)(2,1)S(1)} %copy-done.45, ...), custom_call_target="tpu_custom_call" | custom-call | bytes 9000000 | tf_op jit(solution)/shard_map/pallas_call | solution.py:46
  401.1 72.1 %all_to_all.37.dkv.l0 = bf16[16,192,512]{2,1,0:T(8,128)(2,1)S(1)} all-to-all(bf16[16,192,512]{2,1,0:T(8,128)(2,1)} %get-tuple-element.121), channel_id=1, replica_groups=mesh['s'=2,'z'=4,'yl'=2,'yh'=2,'x'=4] {'z','yl','yh'}, dimensions={0} | all-to-all | bytes 6291456 | tf_op jit(solution)/shard_map/all_to_all | solution.py:438
  474.9 2.1 shard_map.208
  477.0 3.4 collective-permute-start.32
  480.4 2.9 collective-permute-start.15
  485.6 1.7 collective-permute-start.30
  487.3 2.6 collective-permute-done.15
  490.8 1.6 collective-permute-done.16
  495.5 3.0 collective-permute-done.31.p3
  505.4 7.1 %all-to-all-start.5 = ((bf16[16,144,256]{2,1,0:T(8,128)(2,1)}), bf16[16,144,256]{2,1,0:T(8,128)(2,1)S(1)}, u32[]{:S(2)}, u32[]{:S(2)}) async-start(bf16[16,144,256]{2,1,0:T(8,128)(2,1)} %copy-done.27), calls=%async_computation.5 | async-start | bytes 2359296 | tf_op jit(solution)/shard_map/all_to_all | solution.py:438
  512.6 2.9 collective-permute-start.18
  515.8 19.5 %collective-permute-done.18 = bf16[2,64,1024]{2,1,0:T(8,128)(2,1)S(1)} collective-permute-done((bf16[2,64,1024]{2,1,0:T(8,128)(2,1)S(1)}, bf16[2,64,1024]{2,1,0:T(8,128)(2,1)S(1)}, u32[]{:S(2)}, u32[]{:S(2)}) %collective-permute-start.18) | collective-permute-done | bytes 262176 | tf_op jit(solution)/shard_map/ppermute | solution.py:449
  536.2 4.7 collective-permute-done.34
  541.8 1.9 copy-done.9
  545.0 5.2 all_to_all.38.r
  (247 shorter events, 62.2 us)
Async XLA Ops:
  7.2 37.6 %copy-start = (bf16[2,1,128,1024]{3,2,1,0:T(8,128)(2,1)S(1)}, bf16[2,1,128,1024]{3,2,1,0:T(8,128)(2,1)}, u32[]{:S(2)}) copy-start(bf16[2,1,128,1024]{3,2,1,0:T(8,128)(2,1)} %param.11) | copy-start | bytes 1572868
  7.2 121.7 %all-gather.3.cloned.1.call-start = ((), (), s32[]{:S(2)}) async-start(), calls=%async_computation.8 | async-start | bytes 1114112 | tf_op jit(solution)/shard_map/all_gather | solution.py:478
  14.3 2.6 collective-permute-start
  17.6 25.1 %copy-start.58 = (bf16[128,512]{1,0:T(8,128)(2,1)}, bf16[128,512]{1,0:T(8,128)(2,1)S(1)}, u32[]{:S(2)}) copy-start(bf16[128,512]{1,0:T(8,128)(2,1)S(1)} %get-tuple-element.102) | copy-start | bytes 393220
  42.7 4.5 collective-permute-start.1
  50.4 169.9 %copy-start.37 = (bf16[4,64,128]{2,1,0:T(8,128)(2,1)}, bf16[4,64,128]{2,1,0:T(8,128)(2,1)S(1)}, u32[]{:S(2)}) copy-start(bf16[4,64,128]{2,1,0:T(8,128)(2,1)S(1)} %get-tuple-element.90.q) | copy-start | bytes 196612
  50.4 187.9 %copy-start.34 = (f32[2,16,256]{2,1,0:T(8,128)}, f32[2,16,256]{2,1,0:T(8,128)S(1)}, u32[]{:S(2)}) copy-start(f32[2,16,256]{2,1,0:T(8,128)S(1)} %get-tuple-element.94.bias) | copy-start | bytes 98308
  50.4 51.3 %all-to-all-start.1 = ((bf16[16,192,512]{2,1,0:T(8,128)(2,1)}), bf16[16,192,512]{2,1,0:T(8,128)(2,1)S(1)}, u32[]{:S(2)}, u32[]{:S(2)}) async-start(bf16[16,192,512]{2,1,0:T(8,128)(2,1)} %copy-done.17), calls=%async_computation.1 | async-start | bytes 6291456 | tf_op jit(solution)/shard_map/all_to_all | solution.py:438
  54.2 156.6 %all-gather.5.cloned.1.call-start = ((), (), s32[]{:S(2)}) async-start(), calls=%async_computation.9 | async-start | bytes 2228224 | tf_op jit(solution)/shard_map/all_gather | solution.py:479
  101.7 118.6 %copy-start.2 = (bf16[16,192,512]{2,1,0:T(8,128)(2,1)}, bf16[16,192,512]{2,1,0:T(8,128)(2,1)S(1)}, u32[]{:S(2)}) copy-start(bf16[16,192,512]{2,1,0:T(8,128)(2,1)S(1)} %all-to-all-done.1.kv) | copy-start | bytes 9437188
  101.7 136.6 %collective-permute-start.5 = (bf16[16,192,512]{2,1,0:T(8,128)(2,1)S(1)}, bf16[16,192,512]{2,1,0:T(8,128)(2,1)}, u32[]{:S(2)}, u32[]{:S(2)}) collective-permute-start(bf16[16,192,512]{2,1,0:T(8,128)(2,1)S(1)} %all-to-all-done.1.kv), channel_id=1, source_target_pairs={{0,64},{64,0},{1,65},{65,1},{2,66},{66,2},{3,67},{67,3},{4,68},{68... | collective-permute-start | bytes 9437192 | tf_op jit(solution)/shard_map/ppermute | solution.py:429
  128.9 120.2 %collective-permute-start.9 = (bf16[8,2,128,256]{3,2,1,0:T(8,128)(2,1)}, bf16[8,2,128,256]{3,2,1,0:T(8,128)(2,1)}, u32[]{:S(2)}, u32[]{:S(2)}) collective-permute-start(bf16[8,2,128,256]{3,2,1,0:T(8,128)(2,1)} %bitcast.61), channel_id=1, source_target_pairs={{0,64},{64,0},{1,65},{65,1},{2,66},{66,2},{3,67},{67,3},{4,68},{68... | collective-permute-start | bytes 3145736 | tf_op jit(solution)/shard_map/ppermute | solution.py:429
  210.8 80.3 %collective-permute-start.13 = (bf16[8,2,128,512]{3,2,1,0:T(8,128)(2,1)}, bf16[8,2,128,512]{3,2,1,0:T(8,128)(2,1)}, u32[]{:S(2)}, u32[]{:S(2)}) collective-permute-start(bf16[8,2,128,512]{3,2,1,0:T(8,128)(2,1)} %bitcast.67), channel_id=1, source_target_pairs={{0,64},{64,0},{1,65},{65,1},{2,66},{66,2},{3,67},{67,3},{4,68},{68... | collective-permute-start | bytes 6291464 | tf_op jit(solution)/shard_map/ppermute | solution.py:429
  228.2 5.1 collective-permute-start.2
  228.2 8.1 %collective-permute-start.3 = (bf16[64,1024]{1,0:T(8,128)(2,1)S(1)}, bf16[64,1024]{1,0:T(8,128)(2,1)S(1)}, u32[]{:S(2)}, u32[]{:S(2)}) collective-permute-start(bf16[64,1024]{1,0:T(8,128)(2,1)S(1)} %get-tuple-element.92.p0), channel_id=1, source_target_pairs={{0,2},{1,3},{2,0},{3,1},{4,6},{5,7},{6,4},{7,5},{8,10},{9,11},{10,... | collective-permute-start | bytes 393224 | tf_op jit(solution)/shard_map/ppermute | solution.py:433
  233.3 5.0 collective-permute-start.4
  240.2 16.9 %copy-start.13 = (bf16[2048,256]{1,0:T(8,128)(2,1)S(1)}, bf16[2048,256]{1,0:T(8,128)(2,1)}, u32[]{:S(2)}) copy-start(bf16[2048,256]{1,0:T(8,128)(2,1)} %all-gather.3.cloned.1.call-done) | copy-start | bytes 3145732
  244.9 36.7 %copy-start.30 = (f32[64,1024]{1,0:T(8,128)}, f32[64,1024]{1,0:T(8,128)S(1)}, u32[]{:S(2)}) copy-start(f32[64,1024]{1,0:T(8,128)S(1)} %get-tuple-element.95.mid) | copy-start | bytes 786436
  244.9 36.7 %copy-start.39 = (f32[4,64,256]{2,1,0:T(8,128)}, f32[4,64,256]{2,1,0:T(8,128)S(1)}, u32[]{:S(2)}) copy-start(f32[4,64,256]{2,1,0:T(8,128)S(1)} %get-tuple-element.111.pre) | copy-start | bytes 786436
  244.9 4.1 collective-permute-start.6
  246.4 8.2 %collective-permute-start.7 = (bf16[64,1024]{1,0:T(8,128)(2,1)S(1)}, bf16[64,1024]{1,0:T(8,128)(2,1)S(1)}, u32[]{:S(2)}, u32[]{:S(2)}) collective-permute-start(bf16[64,1024]{1,0:T(8,128)(2,1)S(1)} %get-tuple-element.96.p0), channel_id=1, source_target_pairs={{0,2},{1,3},{2,0},{3,1},{4,6},{5,7},{6,4},{7,5},{8,10},{9,11},{10,... | collective-permute-start | bytes 393224 | tf_op jit(solution)/shard_map/ppermute | solution.py:433
  249.1 8.0 %collective-permute-start.8 = (bf16[64,1024]{1,0:T(8,128)(2,1)S(1)}, bf16[64,1024]{1,0:T(8,128)(2,1)S(1)}, u32[]{:S(2)}, u32[]{:S(2)}) collective-permute-start(bf16[64,1024]{1,0:T(8,128)(2,1)S(1)} %get-tuple-element.96.p0), channel_id=1, source_target_pairs={{0,3},{1,2},{2,1},{3,0},{4,7},{5,6},{6,5},{7,4},{8,11},{9,10},{10,... | collective-permute-start | bytes 393224 | tf_op jit(solution)/shard_map/ppermute | solution.py:433
  259.9 21.7 %copy-start.50 = (bf16[64,1024]{1,0:T(8,128)(2,1)}, bf16[64,1024]{1,0:T(8,128)(2,1)S(1)}, u32[]{:S(2)}) copy-start(bf16[64,1024]{1,0:T(8,128)(2,1)S(1)} %get-tuple-element.144.n1) | copy-start | bytes 393220
  259.9 33.2 %copy-start.22 = (bf16[64,1024]{1,0:T(8,128)(2,1)}, bf16[64,1024]{1,0:T(8,128)(2,1)S(1)}, u32[]{:S(2)}) copy-start(bf16[64,1024]{1,0:T(8,128)(2,1)S(1)} %get-tuple-element.98.x) | copy-start | bytes 393220
  281.6 16.0 %copy-start.16 = (bf16[16,64,512]{2,1,0:T(8,128)(2,1)}, bf16[16,64,512]{2,1,0:T(8,128)(2,1)S(1)}, u32[]{:S(2)}) copy-start(bf16[16,64,512]{2,1,0:T(8,128)(2,1)S(1)} %all_to_all.36.kv) | copy-start | bytes 3145732
  286.3 4.8 collective-permute-start.10
  286.3 5.4 collective-permute-start.11
  286.4 6.7 %collective-permute-start.12 = (bf16[64,1024]{1,0:T(8,128)(2,1)S(1)}, bf16[64,1024]{1,0:T(8,128)(2,1)S(1)}, u32[]{:S(2)}, u32[]{:S(2)}) collective-permute-start(bf16[64,1024]{1,0:T(8,128)(2,1)S(1)} %get-tuple-element.101.p0), channel_id=1, source_target_pairs={{0,3},{1,2},{2,1},{3,0},{4,7},{5,6},{6,5},{7,4},{8,11},{9,10},{10,... | collective-permute-start | bytes 393224 | tf_op jit(solution)/shard_map/ppermute | solution.py:433
  291.1 16.4 %copy-start.25 = (bf16[64,1024]{1,0:T(8,128)(2,1)}, bf16[64,1024]{1,0:T(8,128)(2,1)S(1)}, u32[]{:S(2)}) copy-start(bf16[64,1024]{1,0:T(8,128)(2,1)S(1)} %dynamic-slice_bitcast_fusion.g) | copy-start | bytes 393220
  298.9 14.1 %copy-start.32 = (f32[64,1024]{1,0:T(8,128)}, f32[64,1024]{1,0:T(8,128)S(1)}, u32[]{:S(2)}) copy-start(f32[64,1024]{1,0:T(8,128)S(1)} %get-tuple-element.103.mid) | copy-start | bytes 786436
  298.9 14.1 %copy-start.48 = (bf16[64,1024]{1,0:T(8,128)(2,1)}, bf16[64,1024]{1,0:T(8,128)(2,1)S(1)}, u32[]{:S(2)}) copy-start(bf16[64,1024]{1,0:T(8,128)(2,1)S(1)} %get-tuple-element.104) | copy-start | bytes 393220
  298.9 14.1 %copy-start.63 = (bf16[64,1024]{1,0:T(8,128)(2,1)}, bf16[64,1024]{1,0:T(8,128)(2,1)S(1)}, u32[]{:S(2)}) copy-start(bf16[64,1024]{1,0:T(8,128)(2,1)S(1)} %get-tuple-element.136.n2) | copy-start | bytes 393220
  298.9 3.9 collective-permute-start.19
  299.3 6.8 %collective-permute-start.20 = (bf16[64,1024]{1,0:T(8,128)(2,1)S(1)}, bf16[64,1024]{1,0:T(8,128)(2,1)S(1)}, u32[]{:S(2)}, u32[]{:S(2)}) collective-permute-start(bf16[64,1024]{1,0:T(8,128)(2,1)S(1)} %get-tuple-element.105.p0), channel_id=1, source_target_pairs={{0,2},{1,3},{2,0},{3,1},{4,6},{5,7},{6,4},{7,5},{8,10},{9,11},{10,... | collective-permute-start | bytes 393224 | tf_op jit(solution)/shard_map/ppermute | solution.py:433
  302.4 5.2 collective-permute-start.21
  315.6 22.6 %all-to-all-start.3 = ((bf16[16,64,512]{2,1,0:T(8,128)(2,1)}), bf16[16,64,512]{2,1,0:T(8,128)(2,1)}, u32[]{:S(2)}, u32[]{:S(2)}) async-start(bf16[16,64,512]{2,1,0:T(8,128)(2,1)} %get-tuple-element.108), calls=%async_computation.3 | async-start | bytes 2097152 | tf_op jit(solution)/shard_map/all_to_all | solution.py:438
  324.5 26.4 %copy-start.4 = (bf16[16,192,512]{2,1,0:T(8,128)(2,1)S(1)}, bf16[16,192,512]{2,1,0:T(8,128)(2,1)}, u32[]{:S(2)}) copy-start(bf16[16,192,512]{2,1,0:T(8,128)(2,1)} %copy-done.2) | copy-start | bytes 9437188
  324.5 217.3 %reduce-scatter.2.cloned.1.call-start = ((), (), s32[]{:S(2)}) async-start(), calls=%async_computation.10 | async-start | bytes 3342336 | tf_op jit(solution)/shard_map/reduce_scatter | solution.py:554
  331.4 35.6 %collective-permute-start.36 = (bf16[8,2,128,512]{3,2,1,0:T(8,128)(2,1)}, bf16[8,2,128,512]{3,2,1,0:T(8,128)(2,1)}, u32[]{:S(2)}, u32[]{:S(2)}) collective-permute-start(bf16[8,2,128,512]{3,2,1,0:T(8,128)(2,1)} %get-tuple-element.151), channel_id=1, source_target_pairs={{0,64},{64,0},{1,65},{65,1},{2,66},{66,2},{3,67},{67,3},{4,68},{68... | collective-permute-start | bytes 6291464 | tf_op jit(solution)/shard_map/ppermute | solution.py:429
  342.6 3.9 collective-permute-start.22
  342.7 6.8 %collective-permute-start.23 = (bf16[64,1024]{1,0:T(8,128)(2,1)S(1)}, bf16[64,1024]{1,0:T(8,128)(2,1)S(1)}, u32[]{:S(2)}, u32[]{:S(2)}) collective-permute-start(bf16[64,1024]{1,0:T(8,128)(2,1)S(1)} %get-tuple-element.110.p0), channel_id=1, source_target_pairs={{0,2},{1,3},{2,0},{3,1},{4,6},{5,7},{6,4},{7,5},{8,10},{9,11},{10,... | collective-permute-start | bytes 393224 | tf_op jit(solution)/shard_map/ppermute | solution.py:433
  345.7 5.2 collective-permute-start.24
  351.8 13.5 %copy-start.55 = (bf16[64,1024]{1,0:T(8,128)(2,1)S(1)}, bf16[64,1024]{1,0:T(8,128)(2,1)}, u32[]{:S(2)}) copy-start(bf16[64,1024]{1,0:T(8,128)(2,1)} %copy-done.54) | copy-start | bytes 393220
  351.8 18.7 %copy-start.20 = (bf16[8,2,128,512]{3,2,1,0:T(8,128)(2,1)S(1)}, bf16[8,2,128,512]{3,2,1,0:T(8,128)(2,1)}, u32[]{:S(2)}) copy-start(bf16[8,2,128,512]{3,2,1,0:T(8,128)(2,1)} %copy-done.19) | copy-start | bytes 6291460
  360.8 31.4 %collective-permute-start.28 = (bf16[8,2,128,512]{3,2,1,0:T(8,128)(2,1)}, bf16[8,2,128,512]{3,2,1,0:T(8,128)(2,1)}, u32[]{:S(2)}, u32[]{:S(2)}) collective-permute-start(bf16[8,2,128,512]{3,2,1,0:T(8,128)(2,1)} %get-tuple-element.119), channel_id=1, source_target_pairs={{0,64},{64,0},{1,65},{65,1},{2,66},{66,2},{3,67},{67,3},{4,68},{68... | collective-permute-start | bytes 6291464 | tf_op jit(solution)/shard_map/ppermute | solution.py:429
  366.3 4.2 collective-permute-start.35
  381.0 4.7 collective-permute-start.25
  381.0 8.5 %collective-permute-start.26 = (bf16[64,1024]{1,0:T(8,128)(2,1)S(1)}, bf16[64,1024]{1,0:T(8,128)(2,1)S(1)}, u32[]{:S(2)}, u32[]{:S(2)}) collective-permute-start(bf16[64,1024]{1,0:T(8,128)(2,1)S(1)} %copy-done.45), channel_id=1, source_target_pairs={{0,2},{1,3},{2,0},{3,1},{4,6},{5,7},{6,4},{7,5},{8,10},{9,11},{10,... | collective-permute-start | bytes 393224 | tf_op jit(solution)/shard_map/ppermute | solution.py:433
  383.4 8.7 %collective-permute-start.27 = (bf16[64,1024]{1,0:T(8,128)(2,1)S(1)}, bf16[64,1024]{1,0:T(8,128)(2,1)S(1)}, u32[]{:S(2)}, u32[]{:S(2)}) collective-permute-start(bf16[64,1024]{1,0:T(8,128)(2,1)S(1)} %copy-done.45), channel_id=1, source_target_pairs={{0,3},{1,2},{2,1},{3,0},{4,7},{5,6},{6,5},{7,4},{8,11},{9,10},{10,... | collective-permute-start | bytes 393224 | tf_op jit(solution)/shard_map/ppermute | solution.py:433
  401.1 72.1 %copy-start.80 = (f32[8,1024]{1,0:T(8,128)}, f32[8,1024]{1,0:T(8,128)S(1)}, u32[]{:S(2)}) copy-start(f32[8,1024]{1,0:T(8,128)S(1)} %get-tuple-element.130.r0) | copy-start | bytes 98308
  473.2 19.2 %copy-start.24 = (bf16[64,1024]{1,0:T(8,128)(2,1)S(1)}, bf16[64,1024]{1,0:T(8,128)(2,1)}, u32[]{:S(2)}) copy-start(bf16[64,1024]{1,0:T(8,128)(2,1)} %copy-done.22) | copy-start | bytes 393220
  473.2 19.2 %copy-start.33 = (f32[64,1024]{1,0:T(8,128)S(1)}, f32[64,1024]{1,0:T(8,128)}, u32[]{:S(2)}) copy-start(f32[64,1024]{1,0:T(8,128)} %copy-done.32) | copy-start | bytes 786436
  477.0 21.6 %collective-permute-start.32 = (bf16[8,2,128,256]{3,2,1,0:T(8,128)(2,1)}, bf16[8,2,128,256]{3,2,1,0:T(8,128)(2,1)S(1)}, u32[]{:S(2)}, u32[]{:S(2)}) collective-permute-start(bf16[8,2,128,256]{3,2,1,0:T(8,128)(2,1)} %get-tuple-element.129), channel_id=1, source_target_pairs={{0,64},{64,0},{1,65},{65,1},{2,66},{66,2},{3,67},{67,3},{4,68},{68... | collective-permute-start | bytes 3145736 | tf_op jit(solution)/shard_map/ppermute | solution.py:429
  480.4 5.2 collective-permute-start.14
  480.4 9.6 %collective-permute-start.15 = (bf16[64,1024]{1,0:T(8,128)(2,1)S(1)}, bf16[64,1024]{1,0:T(8,128)(2,1)}, u32[]{:S(2)}, u32[]{:S(2)}) collective-permute-start(bf16[64,1024]{1,0:T(8,128)(2,1)S(1)} %copy-done.49), channel_id=1, source_target_pairs={{0,2},{1,3},{2,0},{3,1},{4,6},{5,7},{6,4},{7,5},{8,10},{9,11},{10,... | collective-permute-start | bytes 393224 | tf_op jit(solution)/shard_map/ppermute | solution.py:433
  483.3 9.2 %collective-permute-start.16 = (bf16[64,1024]{1,0:T(8,128)(2,1)S(1)}, bf16[64,1024]{1,0:T(8,128)(2,1)}, u32[]{:S(2)}, u32[]{:S(2)}) collective-permute-start(bf16[64,1024]{1,0:T(8,128)(2,1)S(1)} %copy-done.49), channel_id=1, source_target_pairs={{0,3},{1,2},{2,1},{3,0},{4,7},{5,6},{6,5},{7,4},{8,11},{9,10},{10,... | collective-permute-start | bytes 393224 | tf_op jit(solution)/shard_map/ppermute | solution.py:433
  484.2 10.2 %collective-permute-start.29 = (bf16[64,1024]{1,0:T(8,128)(2,1)}, bf16[64,1024]{1,0:T(8,128)(2,1)S(1)}, u32[]{:S(2)}, u32[]{:S(2)}) collective-permute-start(bf16[64,1024]{1,0:T(8,128)(2,1)} %copy-done.52), channel_id=1, source_target_pairs={{0,1},{1,0},{2,3},{3,2},{4,5},{5,4},{6,7},{7,6},{8,9},{9,8},{10,11... | collective-permute-start | bytes 393224 | tf_op jit(solution)/shard_map/ppermute | solution.py:433
  485.6 10.0 %collective-permute-start.30 = (bf16[64,1024]{1,0:T(8,128)(2,1)}, bf16[64,1024]{1,0:T(8,128)(2,1)S(1)}, u32[]{:S(2)}, u32[]{:S(2)}) collective-permute-start(bf16[64,1024]{1,0:T(8,128)(2,1)} %copy-done.52), channel_id=1, source_target_pairs={{0,2},{1,3},{2,0},{3,1},{4,6},{5,7},{6,4},{7,5},{8,10},{9,11},{10,... | collective-permute-start | bytes 393224 | tf_op jit(solution)/shard_map/ppermute | solution.py:433
  489.9 8.6 %collective-permute-start.31 = (bf16[64,1024]{1,0:T(8,128)(2,1)}, bf16[64,1024]{1,0:T(8,128)(2,1)S(1)}, u32[]{:S(2)}, u32[]{:S(2)}) collective-permute-start(bf16[64,1024]{1,0:T(8,128)(2,1)} %copy-done.52), channel_id=1, source_target_pairs={{0,3},{1,2},{2,1},{3,0},{4,7},{5,6},{6,5},{7,4},{8,11},{9,10},{10,... | collective-permute-start | bytes 393224 | tf_op jit(solution)/shard_map/ppermute | solution.py:433
  493.6 11.8 %collective-permute-start.17 = (bf16[64,1024]{1,0:T(8,128)(2,1)S(1)}, bf16[64,1024]{1,0:T(8,128)(2,1)S(1)}, u32[]{:S(2)}, u32[]{:S(2)}) collective-permute-start(bf16[64,1024]{1,0:T(8,128)(2,1)S(1)} %get-tuple-element.172), channel_id=1, source_target_pairs={{0,64},{64,0},{1,65},{65,1},{2,66},{66,2},{3,67},{67,3},{4,68},{68... | collective-permute-start | bytes 393224 | tf_op jit(solution)/shard_map/ppermute | solution.py:429
  504.8 10.7 %collective-permute-start.33 = (bf16[64,1024]{1,0:T(8,128)(2,1)S(1)}, bf16[64,1024]{1,0:T(8,128)(2,1)S(1)}, u32[]{:S(2)}, u32[]{:S(2)}) collective-permute-start(bf16[64,1024]{1,0:T(8,128)(2,1)S(1)} %broadcast_select_fusion.4), channel_id=1, source_target_pairs={{0,64},{64,0},{1,65},{65,1},{2,66},{66,2},{3,67},{67,3},{4,68},{68... | collective-permute-start | bytes 393224 | tf_op jit(solution)/shard_map/ppermute | solution.py:429
  505.4 36.4 %all-to-all-start.5 = ((bf16[16,144,256]{2,1,0:T(8,128)(2,1)}), bf16[16,144,256]{2,1,0:T(8,128)(2,1)S(1)}, u32[]{:S(2)}, u32[]{:S(2)}) async-start(bf16[16,144,256]{2,1,0:T(8,128)(2,1)} %copy-done.27), calls=%async_computation.5 | async-start | bytes 2359296 | tf_op jit(solution)/shard_map/all_to_all | solution.py:438
  512.6 22.7 %collective-permute-start.18 = (bf16[2,64,1024]{2,1,0:T(8,128)(2,1)S(1)}, bf16[2,64,1024]{2,1,0:T(8,128)(2,1)S(1)}, u32[]{:S(2)}, u32[]{:S(2)}) collective-permute-start(bf16[2,64,1024]{2,1,0:T(8,128)(2,1)S(1)} %pad_maximum_fusion), channel_id=1, source_target_pairs={{0,4},{4,0},{1,5},{5,1},{2,6},{6,2},{3,7},{7,3},{8,12},{12,8},{9,1... | collective-permute-start | bytes 786440 | tf_op jit(solution)/shard_map/ppermute | solution.py:449
  515.6 25.3 %collective-permute-start.34 = (bf16[2,64,1024]{2,1,0:T(8,128)(2,1)S(1)}, bf16[2,64,1024]{2,1,0:T(8,128)(2,1)S(1)}, u32[]{:S(2)}, u32[]{:S(2)}) collective-permute-start(bf16[2,64,1024]{2,1,0:T(8,128)(2,1)S(1)} %pad_maximum_fusion.1), channel_id=1, source_target_pairs={{0,4},{4,0},{1,5},{5,1},{2,6},{6,2},{3,7},{7,3},{8,12},{12,8},{9,1... | collective-permute-start | bytes 786440 | tf_op jit(solution)/shard_map/ppermute | solution.py:449
  (71 other events, 230.0 us)
Sparse Core Ops, SparseCore 0:
  44.9 83.9 all-gather.2
  131.1 79.6 all-gather.4
  380.3 112.0 reduce-scatter.1

commit v4 on v2

--- a/solution.py
+++ b/solution.py
@@ -22,7 +22,7 @@
     return jax.ShapeDtypeStruct(shape, dtype)
 
 
-def call(kernel, outs, ins, us=3):
+def call(kernel, outs, ins, us=3, through=()):
     specs, arrays = [], []
     for item in ins:
         if isinstance(item, tuple):
@@ -43,17 +43,23 @@
         pl.BlockSpec(o.shape, functools.partial(lambda n, i: (0,) * n, len(o.shape)))
         for o in outs
     ]
+    n, m, k = len(ins), len(outs), len(through)
+
+    def body(*refs):
+        kernel(*refs[:n], *refs[n + k : n + k + m])
+
     return pl.pallas_call(
-        kernel,
+        body,
         grid=(1,),
-        out_shape=outs,
-        in_specs=specs,
-        out_specs=out_specs,
+        out_shape=list(outs) + [sds(*t.shape, dtype=t.dtype) for t in through],
+        in_specs=specs + [pl.BlockSpec(memory_space=pl.ANY)] * k,
+        out_specs=out_specs + [pl.BlockSpec(memory_space=pl.ANY)] * k,
+        input_output_aliases={n + i: m + i for i in range(k)},
         compiler_params=pltpu.CompilerParams(vmem_limit_bytes=48 * 1024 * 1024),
         cost_estimate=pl.CostEstimate(
             flops=0, bytes_accessed=us * 3_000_000, transcendentals=0
         ),
-    )(*arrays)
+    )(*arrays, *through)
 
 
 def nn(a, b):
@@ -149,7 +155,19 @@
             kv[g, kv.shape[1] - ROWS :, k * 128 : k * 128 + 128] = pair
 
 
-def pack_kernel(qkv, out, up, down, gain, shift, inb, outb, upb, msg, ffn):
+def pack_kernel(*refs):
+    sources, (msg, ffn), held, sem = refs[:9], refs[9:11], refs[11:20], refs[20]
+    copies = [
+        pltpu.make_async_copy(a, b, sem.at[i]) for i, (a, b) in enumerate(zip(sources, held))
+    ]
+    for c in copies:
+        c.start()
+    for c in copies:
+        c.wait()
+    pack(*held, msg, ffn)
+
+
+def pack(qkv, out, up, down, gain, shift, inb, outb, upb, msg, ffn):
     wt = out[...].astype(F32).T
     dt = down[...].astype(F32).T
     inb_, gain_, shift_, outb_ = [r[...].astype(F32) for r in (inb, gain, shift, outb)]
@@ -204,6 +222,13 @@
     project(out.astype(F32), lnp, bias, wm, wo, 1, n1, q, msg)
 
 
+def attend_spread_kernel(first, q, kv, wm, wo, piece, part, prob, att, copies):
+    attend_kernel(first, q, kv, wm, wo, part, prob, att)
+    rest = piece[...]
+    for g in range(16):
+        copies[g] = rest
+
+
 def attend_kernel(first, q, kv, wm, wo, part, prob, att):
     length = 16 * ROWS
     qpos = first[0] + lax.broadcasted_iota(jnp.int32, (ROWS, length), 0)
@@ -291,17 +316,24 @@
         dkv[:, at:, k * 128 : k * 128 + 128] = both.astype(BF).reshape(16, ROWS, 128)
 
 
-def attend_back_kernel(g, mid, p0, p1, p2, p3, lnp, wm, wo, prob, q, kv, dmid, bg, dq, dkv, rows):
+def add_into(msg, gm, gr):
+    for i in range(8):
+        for j in range(2):
+            msg[2 * i + j, 0:128, :] = (gm[i, j].astype(F32) + gr[i, j].astype(F32)).astype(BF)
+
+
+def attend_back_kernel(
+    g, mid, p0, p1, p2, p3, lnp, wm, wo, prob, q, kv, gm, gr, dmid, bg, dq, dkv, rows, msg
+):
     attend_back(1, g, mid, (p0, p1, p2, p3), lnp, wm, wo, prob, q, kv, dmid, bg, dq, dkv, rows)
+    add_into(msg, gm, gr)
 
 
 def attend_back_first_kernel(
     g, mid, p0, p1, p2, p3, lnp, wm, wo, prob, q, kv, gm, gr, dmid, bg, dq, msg, rows
 ):
     attend_back(0, g, mid, (p0, p1, p2, p3), lnp, wm, wo, prob, q, kv, dmid, bg, dq, msg, rows)
-    for i in range(8):
-        for j in range(2):
-            msg[2 * i + j, 0:128, :] = (gm[i, j].astype(F32) + gr[i, j].astype(F32)).astype(BF)
+    add_into(msg, gm, gr)
 
 
 def project_back_kernel(dkv, dq, wm, wo, dproj, part, sums):
@@ -337,7 +369,7 @@
 
 
 def last_kernel(
-    x, dmid, p0, p1, p2, p3, lnp, gm, gr,
+    x, dmid, p0, p1, p2, p3, lnp, gm0, gr0, gm1, gr1,
     r0, o0, a0, u0, h1, r1, o1, a1, u1, dx, msg,
 ):
     back, gg, gs = layer_norm_back(
@@ -369,38 +401,54 @@
                 block += [jnp.concatenate([f[:, cols], s[:, cols]], axis=1) for f, s in pairs]
             block.append(jnp.zeros((2, 256), F32))
             g = 2 * d + yh
-            msg[g, 0:128, :] = (gm[d, yh].astype(F32) + gr[d, yh].astype(F32)).astype(BF)
-            msg[g, 128:144, :] = jnp.concatenate(block).astype(BF)
-
-
-def combine_kernel(am, ar, fm, fr, msg):
-    msg[0, :, 0:256] = (am[0].astype(F32) + ar[0].astype(F32)).astype(BF)
-    msg[0, :, 256:768] = (fm[0].astype(F32) + fr[0].astype(F32)).astype(BF)
-
-
-def settle_kernel(tail, l0, l1, out):
+            for at, gm, gr in ((0, gm0, gr0), (256, gm1, gr1)):
+                both = gm[d, yh].astype(F32) + gr[d, yh].astype(F32)
+                msg[g, 0:128, at : at + 256] = both.astype(BF)
+            msg[g, 128:144, 0:256] = jnp.concatenate(block).astype(BF)
+            msg[g, 128:144, 256:512] = jnp.zeros((16, 256), BF)
+
+
+def settle_kernel(core, l0, l1, keep, send):
+    first = core[0] == 0
+    for j in range(2):
+        cols = slice(j * 256, j * 256 + 256)
+        a = jnp.sum(l0[:, 0:128, cols].astype(F32), axis=0)
+        b = jnp.sum(l1[:, 0:128, cols].astype(F32), axis=0)
+        keep[:, cols] = jnp.where(first, a, b)
+        send[:, cols] = jnp.where(first, b, a)
+
+
+def settle_tail_kernel(core, tail, keep, send):
+    first = core[0] == 0
     t = jnp.sum(tail[...].astype(F32), axis=0)
-    out[0, 0:128, 0:256] = t[0:128]
-    out[1, 0:128, 0:256] = jnp.sum(l1[:, :, 0:256].astype(F32), axis=0)
-    for j in range(2):
-        cols = slice(256 + j * 256, 512 + j * 256)
-        out[0, 0:128, cols] = jnp.sum(l0[:, 0:128, j * 256 : j * 256 + 256].astype(F32), axis=0)
-        out[1, 0:128, cols] = jnp.sum(l1[:, :, cols].astype(F32), axis=0)
-    small = t[128:144]
+    a, b = t[0:128, 0:256], t[0:128, 256:512]
+    small = t[128:144, 0:256]
     pad = jnp.zeros((1, 256), F32)
-    out[0, 128:136, 0:256] = jnp.concatenate([small[0:7], pad])
-    out[1, 128:136, 0:256] = jnp.concatenate([small[7:14], pad])
-
-
-def unpack_kernel(r, qkv, out, up, down, gain, shift, inb, outb, upb):
-    a = [r[j, 0:128, 0:256] for j in range(2)]
+    c, d = jnp.concatenate([small[0:7], pad]), jnp.concatenate([small[7:14], pad])
+    keep[0:128, :] = jnp.where(first, a, b)
+    send[0:128, :] = jnp.where(first, b, a)
+    keep[128:136, :] = jnp.where(first, c, d)
+    send[128:136, :] = jnp.where(first, d, c)
+
+
+def unpack_kernel(
+    core, fk, fg, ak, ag, qkv, out, up, down, gain, shift, inb, outb, upb
+):
+    first = core[0] == 0
+
+    def ordered(k, g):
+        return jnp.where(first, k, g), jnp.where(first, g, k)
+
+    a = ordered(ak[0:128, :], ag[0:128, :])
     for i, at in enumerate((128, 0, 64)):
         qkv[i] = jnp.concatenate([t[:, at : at + 64] for t in a], axis=1)
     out[...] = jnp.concatenate([t[:, 192:256] for t in a], axis=1).T
+    ups = ordered(fk[:, 0:256], fg[:, 0:256])
+    downs = ordered(fk[:, 256:512], fg[:, 256:512])
     for j in range(2):
-        up[:, j * 256 : j * 256 + 256] = r[j, 0:128, 256:512]
-        down[j * 256 : j * 256 + 256, :] = r[j, 0:128, 512:768].T
-    s0, s1 = r[0, 128:136, 0:256], r[1, 128:136, 0:256]
+        up[:, j * 256 : j * 256 + 256] = ups[j]
+        down[j * 256 : j * 256 + 256, :] = downs[j].T
+    s0, s1 = ordered(ak[128:136, :], ag[128:136, :])
     for row, ref in ((4, gain), (5, shift), (6, outb)):
         t = s0[row : row + 1] + s1[row : row + 1]
         ref[0:1, :] = t[:, 0:128]
@@ -446,14 +494,20 @@
         return lax.dynamic_slice(v, (s, 0, yh * ROWS, 0), (1, 1, ROWS, D)).reshape(ROWS, D)
 
     x, cot = own_rows(inputs), own_rows(cotangent)
-    msg, ffn = call(
+    core = (s.astype(jnp.int32).reshape(1), None, None)
+    weights = [
+        jnp.moveaxis(wqkv[0], 1, 0), wout[0], wup[0], wdown[0],
+        gain[0], shift[0], inb[0], outb[0], upb,
+    ]
+    msg, ffn = pl.pallas_call(
         pack_kernel,
-        [sds(2, 16, 144, 256), sds(2, 128, 512)],
-        [
-            jnp.moveaxis(wqkv[0], 1, 0), wout[0], wup[0], wdown[0],
-            gain[0], shift[0], inb[0], outb[0], upb,
-        ],
-    )
+        out_shape=[sds(2, 16, 144, 256), sds(2, 128, 512)],
+        in_specs=[pl.BlockSpec(memory_space=pl.ANY)] * 9,
+        out_specs=[pl.BlockSpec(memory_space=pltpu.VMEM)] * 2,
+        scratch_shapes=[pltpu.VMEM(w.shape, BF) for w in weights]
+        + [pltpu.SemaphoreType.DMA((9,))],
+        compiler_params=pltpu.CompilerParams(vmem_limit_bytes=48 * 1024 * 1024),
+    )(*weights)
     u = exchange(msg.reshape(32, 144, 256), ("s", *CHIPS)).reshape(2, 16, 144, 256)
     got = swap_cores(by_layer(s, ffn[1], ffn[0]))
     piece0, piece1 = by_layer(s, ffn[0], got), by_layer(s, got, ffn[1])
@@ -475,17 +529,23 @@
         sds(ROWS, D), sds(ROWS, D, dtype=F32), sds(ROWS, D),
         sds(4, ROWS, 256, dtype=F32), sds(4, ROWS, 256),
     ]
-    part, prob0, att0 = call(attend_kernel, attend_outs, [(first, None, None), q0, kv0, am[0], ao[0]])
-    f1 = exchange(jnp.broadcast_to(piece1, (16, 128, 512))).reshape(8, 2, 128, 512)
-    f1o = swap_cores(f1)
+    part, prob0, att0, copies = call(
+        attend_spread_kernel,
+        attend_outs + [sds(16, 128, 512)],
+        [(first, None, None), q0, kv0, am[0], ao[0], piece1],
+    )
+    f1 = exchange(copies)
     part, mid0, n20, pre0, act0 = call(
         feed_kernel, feed_outs, [x, *all_parts(part), lnp, bias, f0, f0o]
     )
-    y0, n11, q1, msg = call(
+    y0, n11, q1, msg, f1 = call(
         next_kernel,
         [sds(ROWS, D), kinds["n1"], kinds["q"], sds(16, ROWS, 512)],
         [mid0, *all_parts(part), lnp, bias, am[1], ao[1]],
-    )
+        through=[f1],
+    )
+    f1 = f1.reshape(8, 2, 128, 512)
+    f1o = swap_cores(f1)
     kv1 = exchange(msg)
     part, prob1, att1 = call(attend_kernel, attend_outs, [(first, None, None), q1, kv1, am[1], ao[1]])
     part, mid1, n21, pre1, act1, dpre1, back = call(
@@ -503,14 +563,17 @@
     gfr1 = swap_cores(gfo1)
     back_outs = [sds(ROWS, D, dtype=F32), sds(ROWS, D), sds(4, ROWS, 128)]
     rows_out = sds(8, D, dtype=F32)
-    dmid1, bg1, dq1, dkv, rows1 = call(
+    dmid1, bg1, dq1, dkv, rows1, l1 = call(
         attend_back_kernel,
-        back_outs + [sds(16, ROWS, 512), rows_out],
-        [cot, mid1, *backs, lnp, am[1], ao[1], prob1, q1, kv1],
+        back_outs + [sds(16, ROWS, 512), rows_out, sds(16, 128, 512)],
+        [cot, mid1, *backs, lnp, am[1], ao[1], prob1, q1, kv1, gfm1, gfr1],
     )
     dkv = exchange(dkv)
     project_outs = [sds(4, ROWS, 256), sds(ROWS, D), sds(4, 256, dtype=F32)]
-    dproj1, part, gib1 = call(project_back_kernel, project_outs, [dkv, dq1, am[1], ao[1]])
+    dproj1, part, gib1, l1 = call(
+        project_back_kernel, project_outs, [dkv, dq1, am[1], ao[1]], through=[l1]
+    )
+    l1 = exchange(l1)
     backs = all_parts(part)
     grad_attn_outs = [sds(8, 2, 128, 256), sds(8, 2, 128, 256)]
     gam1, gao1 = call(grad_attn_kernel, grad_attn_outs, [n11, bg1, att1, dproj1])
@@ -523,22 +586,11 @@
     backs = all_parts(part)
     gfm0, gfo0, gub0, ob10 = call(grad_ffn_kernel, grad_ffn_outs, [n20, dx1, dpre0, act0])
     gfr0 = swap_cores(gfo0)
-    def flat(v):
-        return v.reshape(16, 128, v.shape[-1])
-    msg1 = pl.pallas_call(
-        combine_kernel,
-        grid=(16,),
-        out_shape=sds(16, 128, 768),
-        in_specs=[pl.BlockSpec((1, 128, w), lambda i: (i, 0, 0)) for w in (256, 256, 512, 512)],
-        out_specs=pl.BlockSpec((1, 128, 768), lambda i: (i, 0, 0)),
-        compiler_params=pltpu.CompilerParams(vmem_limit_bytes=32 * 1024 * 1024),
-        cost_estimate=pl.CostEstimate(flops=0, bytes_accessed=9_000_000, transcendentals=0),
-    )(flat(gam1), flat(gar1), flat(gfm1), flat(gfr1))
-    l1 = exchange(msg1)
-    dmid0, bg0, dq0, msg, rows0 = call(
+    dmid0, bg0, dq0, msg, rows0, l1 = call(
         attend_back_first_kernel,
         back_outs + [sds(16, 192, 512), rows_out],
         [dx1, mid0, *backs, lnp, am[0], ao[0], prob0, q0, kv0, gfm0, gfr0],
+        through=[l1],
     )
     l0 = exchange(msg)
     dproj0, part, gib0 = call(
@@ -549,19 +601,24 @@
     gar0 = swap_cores(gao0)
     dx0, msg = call(
         last_kernel,
-        [sds(ROWS, D), sds(16, 144, 256)],
-        [x, dmid0, *backs, lnp, gam0, gar0, rows0, ob10, gib0, gub0, head1, rows1, ob11, gib1, gub1],
+        [sds(ROWS, D), sds(16, 144, 512)],
+        [x, dmid0, *backs, lnp, gam0, gar0, gam1, gar1, rows0, ob10, gib0, gub0, head1, rows1, ob11, gib1, gub1],
     )
     tail = exchange(msg)
     acts = whole_rows(s, yh, y0, y1)
     grads = whole_rows(s, yh, dx0, dx1)
-    (settled,) = call(settle_kernel, [sds(2, 144, 768, dtype=F32)], [tail, l0, l1])
-    settled = exchange(settled, "s")
     f = functools.partial(sds, dtype=F32)
+    fk, send = call(
+        settle_kernel,
+        [f(128, 512), f(128, 512)],
+        [core, (l0, (16, 128, 512), (0, 0, 0)), l1],
+    )
+    fg = swap_cores(send)
+    ak, send = call(settle_tail_kernel, [f(136, 256), f(136, 256)], [core, tail])
     gq, go, gu, gd, gg, gs, gi, gb, gub = call(
         unpack_kernel,
         [f(3, 128, 128), f(128, 128), f(128, 512), f(512, 128), f(2, 128), f(2, 128), f(2, 128), f(2, 128), f(1, 512)],
-        [settled],
+        [core, fk, fg, ak, swap_cores(send)],
     )
     return (
         acts, grads, jnp.moveaxis(gq, 0, 1)[None], go[None], gu[None], gd[None],

time: 424 us -> 429 us (1.012)
  local copies, waits for them, and re-layouts: 23.5 us -> 38.6 us
  waiting for transfers between devices: 134 us -> 122 us
  blocking collectives: 134 us -> 123 us
  Pallas kernels: 56.7 us -> 63.3 us
    unnamed x80 -> x156, local copies, waits for them, and re-layouts: 19.3 us -> 36 us
    all_to_all x5 -> x4, blocking collectives: 134 us -> 123 us  [exchange(): return lax.all_to_all(v, axes, 0, 0, tiled=True)]
    all_to_all x4, waiting for transfers between devices: 62.4 us -> 54.7 us  [exchange(): return lax.all_to_all(v, axes, 0, 0, tiled=True)]
    pallas_call x20, Pallas kernels: 56.7 us -> 63.3 us  [the longest x19 62.4 us: call(): pl.pallas_call(body, grid=(1,), out_shape=list(outs) + [sds(*t.shape, dty...]
    ppermute x11 -> x13, starting transfers between devices: 14.1 us -> 19.4 us  [swap_cores(): return lax.ppermute(v, 's', [(0, 1), (1, 0)])]
  transfers between devices with their start and end apart: 41 -> 43, of which waited for: 27 -> 25; matrix products, arithmetic and copies ran while one was open for 1% -> 1% of each run, Pallas kernels for 5% -> 5%
where the time goes in v4:
time: 429 us; the launch traced here: 427 us
  blocking collectives  123 us (29%)
  waiting for transfers between devices  122 us (28%)
  starting transfers between devices  74 us (17%)
  Pallas kernels  63.3 us (15%)
  local copies, waits for them, and re-layouts  38.6 us (9%)
  other arithmetic  4.59 us (1%)
    all_to_all x4, blocking collectives, exchange(): return lax.all_to_all(v, axes, 0, 0, tiled=True)  123 us
    pallas_call x19, Pallas kernels, call(): pl.pallas_call(body, grid=(1,), out_shape=list(outs) + [sds(*t.shape, dty...  62.4 us
    all_to_all x4, waiting for transfers between devices, exchange(): return lax.all_to_all(v, axes, 0, 0, tiled=True)  54.7 us
    ppermute x24, waiting for transfers between devices, all_parts(): lax.ppermute(part, 'x', [(i, i ^ k) for i in range(4)])  46 us
    unnamed x156, local copies, waits for them, and re-layouts  36 us
    ppermute x24, starting transfers between devices, all_parts(): lax.ppermute(part, 'x', [(i, i ^ k) for i in range(4)])  31.2 us
    all_to_all x4, starting transfers between devices, exchange(): return lax.all_to_all(v, axes, 0, 0, tiled=True)  20.3 us
    ppermute x13, starting transfers between devices, swap_cores(): return lax.ppermute(v, 's', [(0, 1), (1, 0)])  19.4 us
  transfers between devices with their start and end apart: 43, of which 25 were waited for; matrix products, arithmetic and copies ran while one was open for 1% of the time, Pallas kernels for 5%

profile of v4, /device:TPU:1, one launch (start us, length us, event | category | flops | bytes accessed | tf_op | source)
XLA Modules:
  0.0 427.4 jit_solution(13059650459886063602)
XLA Ops:
  8.4 41.0 %all_to_all.40 = bf16[32,144,256]{2,1,0:T(8,128)(2,1)S(1)} all-to-all(bf16[32,144,256]{2,1,0:T(8,128)(2,1)S(1)} %bitcast.65), channel_id=1, replica_groups=mesh['s'=2,'z'=4,'yl'=2,'yh'=2,'x'=4] {'s','z','yl','yh'}, dimensions={0} | all-to-all | bytes 4718592 | tf_op jit(solution)/shard_map/all_to_all | solution.py:472
  49.3 1.7 fusion
  51.6 2.4 collective-permute-done.1
  54.2 3.8 shard_map.195
  58.0 42.5 %all_to_all.41.refs_2_.refs_11_ = bf16[16,192,512]{2,1,0:T(8,128)(2,1)} all-to-all(bf16[16,192,512]{2,1,0:T(8,128)(2,1)} %get-tuple-element.94), channel_id=1, replica_groups=mesh['s'=2,'z'=4,'yl'=2,'yh'=2,'x'=4] {'z','yl','yh'}, dimensions={0} | all-to-all | bytes 6291456 | tf_op jit(solution)/shard_map/all_to_all | solution.py:472
  100.6 1.8 collective-permute-start.5
  102.4 5.7 %shard_map.196 = (bf16[64,1024]{1,0:T(8,128)(2,1)S(1)}, f32[4,64,1024]{2,1,0:T(8,128)S(1)}, bf16[4,64,128]{2,1,0:T(8,128)(2,1)S(1)}, bf16[16,128,512]{2,1,0:T(8,128)(2,1)}) custom-call(s32[1]{0:T(128)} %bitcast.1.refs_0_, bf16[4,64,128]{2,1,0:T(8,128)(2,1)S(1)} %get-tuple-element.93.refs_1_.refs_10_, bf16[16,192,512]{2,1,0:T(8,128)(2,1)} %all_to_all.41.refs_2_.refs_11_, ...), custom_call_target="tpu_custom_call" | custom-call | bytes 9000000 | tf_op jit(solution)/shard_map/pallas_call | solution.py:51
  109.6 4.4 %all-to-all-start.2 = ((bf16[16,128,512]{2,1,0:T(8,128)(2,1)}), bf16[16,128,512]{2,1,0:T(8,128)(2,1)}, u32[]{:S(2)}, u32[]{:S(2)}) async-start(bf16[16,128,512]{2,1,0:T(8,128)(2,1)} %get-tuple-element.100), calls=%async_computation.2 | async-start | bytes 4194304 | tf_op jit(solution)/shard_map/all_to_all | solution.py:472
  115.5 2.4 collective-permute-start.3
  119.0 4.9 %collective-permute-done.3.refs_3_ = bf16[64,1024]{1,0:T(8,128)(2,1)S(1)} collective-permute-done((bf16[64,1024]{1,0:T(8,128)(2,1)S(1)}, bf16[64,1024]{1,0:T(8,128)(2,1)S(1)}, u32[]{:S(2)}, u32[]{:S(2)}) %collective-permute-start.3) | collective-permute-done | bytes 131104 | tf_op jit(solution)/shard_map/ppermute | solution.py:467
  124.0 2.6 collective-permute-done.4.refs_4_
  126.6 3.9 shard_map.197
  132.4 1.6 collective-permute-start.7
  134.0 2.2 collective-permute-start.8
  136.9 5.5 %all-to-all-done.2.refs_9_ = bf16[16,128,512]{2,1,0:T(8,128)(2,1)} async-done(((bf16[16,128,512]{2,1,0:T(8,128)(2,1)}), bf16[16,128,512]{2,1,0:T(8,128)(2,1)}, u32[]{:S(2)}, u32[]{:S(2)}) %all-to-all-start.2) | async-done | bytes 2097184 | tf_op jit(solution)/shard_map/all_to_all | solution.py:472
  148.0 2.2 shard_map.198
  151.2 21.3 %all_to_all.42.refs_2_.refs_11_ = bf16[16,64,512]{2,1,0:T(8,128)(2,1)S(1)} all-to-all(bf16[16,64,512]{2,1,0:T(8,128)(2,1)S(1)} %get-tuple-element.103), channel_id=1, replica_groups=mesh['s'=2,'z'=4,'yl'=2,'yh'=2,'x'=4] {'z','yl','yh'}, dimensions={0} | all-to-all | bytes 2097152 | tf_op jit(solution)/shard_map/all_to_all | solution.py:472
  172.4 2.5 shard_map.199
  176.3 2.4 collective-permute-start.11
  179.8 3.2 collective-permute-done.11.refs_3_
  183.0 2.8 collective-permute-done.12.refs_4_
  187.1 5.1 %shard_map.200 = (bf16[64,1024]{1,0:T(8,128)(2,1)S(1)}, f32[64,1024]{1,0:T(8,128)S(1)}, bf16[64,1024]{1,0:T(8,128)(2,1)S(1)}, f32[4,64,256]{2,1,0:T(8,128)}, bf1...) custom-call(bf16[64,1024]{1,0:T(8,128)(2,1)S(1)} %get-tuple-element.101.refs_0_, ...), custom_call_target="tpu_custom_call" | custom-call | bytes 9000000 | tf_op jit(solution)/shard_map/pallas_call | solution.py:51
  195.5 1.8 collective-permute-start.22
  197.2 2.2 collective-permute-start.20
  199.4 1.6 collective-permute-start.21
  202.3 3.6 collective-permute-done.20.refs_4_
  205.9 2.5 collective-permute-done.21.refs_5_
  209.8 7.5 %shard_map.202 = (f32[64,1024]{1,0:T(8,128)S(1)}, bf16[64,1024]{1,0:T(8,128)(2,1)S(1)}, bf16[4,64,128]{2,1,0:T(8,128)(2,1)S(1)}, bf16[16,64,512]{2,1,0:T(8,128)(...) custom-call(bf16[64,1024]{1,0:T(8,128)(2,1)S(1)} %dynamic-slice_bitcast_fusion.refs_9_.refs_1_.refs_0_, ...), custom_call_target="tpu_custom_call" | custom-call | bytes 9000000 | tf_op jit(solution)/shard_map/pallas_call | solution.py:51
  217.3 18.6 %all_to_all.43.refs_0_ = bf16[16,64,512]{2,1,0:T(8,128)(2,1)S(1)} all-to-all(bf16[16,64,512]{2,1,0:T(8,128)(2,1)S(1)} %get-tuple-element.116), channel_id=1, replica_groups=mesh['s'=2,'z'=4,'yl'=2,'yh'=2,'x'=4] {'z','yl','yh'}, dimensions={0} | all-to-all | bytes 2097152 | tf_op jit(solution)/shard_map/all_to_all | solution.py:472
  235.9 2.1 shard_map.203
  239.3 3.2 collective-permute-start.24
  243.2 3.1 collective-permute-done.24.refs_4_
  246.3 1.4 collective-permute-done.25.refs_5_
  247.7 3.9 shard_map.204
  252.2 2.6 shard_map.205
  256.1 4.5 %collective-permute-start.29 = (bf16[8,2,128,512]{3,2,1,0:T(8,128)(2,1)}, bf16[8,2,128,512]{3,2,1,0:T(8,128)(2,1)}, u32[]{:S(2)}, u32[]{:S(2)}) collective-permute-start(bf16[8,2,128,512]{3,2,1,0:T(8,128)(2,1)} %get-tuple-element.128), channel_id=1, source_target_pairs={{0,64},{64,0},{1,65},{65,1},{2,66},{66,2},{3,67},{67,3},{4,68},{68... | collective-permute-start | bytes 6291464 | tf_op jit(solution)/shard_map/ppermute | solution.py:463
  260.6 3.9 all-to-all-start.5
  264.6 1.9 collective-permute-start.27
  266.5 2.0 collective-permute-start.28
  268.9 3.2 collective-permute-done.27.refs_4_
  272.8 1.9 collective-permute-done.28.refs_5_
  275.3 15.9 %all-to-all-done.5.refs_14_ = bf16[16,128,512]{2,1,0:T(8,128)(2,1)S(1)} async-done(((bf16[16,128,512]{2,1,0:T(8,128)(2,1)}), bf16[16,128,512]{2,1,0:T(8,128)(2,1)S(1)}, u32[]{:S(2)}, u32[]{:S(2)}) %all-to-all-start.5) | async-done | bytes 2097184 | tf_op jit(solution)/shard_map/all_to_all | solution.py:472
  294.3 8.5 %shard_map.206 = (f32[64,1024]{1,0:T(8,128)S(1)}, bf16[64,1024]{1,0:T(8,128)(2,1)S(1)}, bf16[4,64,128]{2,1,0:T(8,128)(2,1)S(1)}, bf16[16,192,512]{2,1,0:T(8,128)...) custom-call(bf16[64,1024]{1,0:T(8,128)(2,1)S(1)} %get-tuple-element.121.refs_1_., ...), custom_call_target="tpu_custom_call", output_to_operand_aliasing={{5}: (14, {})} | custom-call | bytes 9000000 | tf_op jit(solution)/shard_map/pallas_call | solution.py:51
  302.8 1.4 copy-done.5
  306.7 6.1 %all-to-all-start.6 = ((bf16[16,192,512]{2,1,0:T(8,128)(2,1)}), bf16[16,192,512]{2,1,0:T(8,128)(2,1)}, u32[]{:S(2)}, u32[]{:S(2)}) async-start(bf16[16,192,512]{2,1,0:T(8,128)(2,1)} %get-tuple-element.131), calls=%async_computation.6 | async-start | bytes 6291456 | tf_op jit(solution)/shard_map/all_to_all | solution.py:472
  313.7 2.0 shard_map.209
  316.7 1.8 collective-permute-start.34
  318.5 33.3 %all-to-all-done.6.refs_0_.refs_1_ = bf16[16,192,512]{2,1,0:T(8,128)(2,1)} async-done(((bf16[16,192,512]{2,1,0:T(8,128)(2,1)}), bf16[16,192,512]{2,1,0:T(8,128)(2,1)}, u32[]{:S(2)}, u32[]{:S(2)}) %all-to-all-start.6) | async-done | bytes 3145760 | tf_op jit(solution)/shard_map/all_to_all | solution.py:472
  352.7 2.5 shard_map.207
  356.3 2.8 collective-permute-start.33
  359.0 1.9 collective-permute-start.31
  360.9 2.0 collective-permute-start.32
  364.1 3.3 collective-permute-done.31.refs_4_
  367.3 2.5 collective-permute-done.32.refs_5_
  369.9 3.5 shard_map.210
  373.5 5.9 %all-to-all-start.7 = ((bf16[16,144,512]{2,1,0:T(8,128)(2,1)}), bf16[16,144,512]{2,1,0:T(8,128)(2,1)S(1)}, u32[]{:S(2)}, u32[]{:S(2)}) async-start(bf16[16,144,512]{2,1,0:T(8,128)(2,1)} %get-tuple-element.159), calls=%async_computation.7 | async-start | bytes 4718592 | tf_op jit(solution)/shard_map/all_to_all | solution.py:472
  379.5 3.2 collective-permute-start.15
  383.4 4.5 %collective-permute-done.15 = bf16[64,1024]{1,0:T(8,128)(2,1)S(1)} collective-permute-done((bf16[64,1024]{1,0:T(8,128)(2,1)S(1)}, bf16[64,1024]{1,0:T(8,128)(2,1)S(1)}, u32[]{:S(2)}, u32[]{:S(2)}) %collective-permute-start.15) | collective-permute-done | bytes 131104 | tf_op jit(solution)/shard_map/ppermute | solution.py:467
  387.9 2.6 collective-permute-done.16
  391.5 1.5 collective-permute-start.17
  394.1 2.8 collective-permute-start.18
  398.0 18.1 %collective-permute-done.18 = bf16[2,64,1024]{2,1,0:T(8,128)(2,1)S(1)} collective-permute-done((bf16[2,64,1024]{2,1,0:T(8,128)(2,1)S(1)}, bf16[2,64,1024]{2,1,0:T(8,128)(2,1)S(1)}, u32[]{:S(2)}, u32[]{:S(2)}) %collective-permute-start.18) | collective-permute-done | bytes 262176 | tf_op jit(solution)/shard_map/ppermute | solution.py:483
  417.0 2.9 shard_map.211
  419.9 3.5 collective-permute-start.37
  (218 shorter events, 56.3 us)
Async XLA Ops:
  0.6 51.0 %copy-start = (bf16[2,1,128,1024]{3,2,1,0:T(8,128)(2,1)S(1)}, bf16[2,1,128,1024]{3,2,1,0:T(8,128)(2,1)}, u32[]{:S(2)}) copy-start(bf16[2,1,128,1024]{3,2,1,0:T(8,128)(2,1)} %param.11) | copy-start | bytes 1572868
  51.0 3.2 collective-permute-start
  51.4 2.6 collective-permute-start.1
  58.0 42.5 %copy-start.25 = (bf16[64,1024]{1,0:T(8,128)(2,1)}, bf16[64,1024]{1,0:T(8,128)(2,1)S(1)}, u32[]{:S(2)}) copy-start(bf16[64,1024]{1,0:T(8,128)(2,1)S(1)} %get-tuple-element.134.refs_0_) | copy-start | bytes 393220
  100.6 26.0 %collective-permute-start.5 = (bf16[16,192,512]{2,1,0:T(8,128)(2,1)}, bf16[16,192,512]{2,1,0:T(8,128)(2,1)}, u32[]{:S(2)}, u32[]{:S(2)}) collective-permute-start(bf16[16,192,512]{2,1,0:T(8,128)(2,1)} %all_to_all.41.refs_2_.refs_11_), channel_id=1, source_target_pairs={{0,64},{64,0},{1,65},{65,1},{2,66},{66,2},{3,67},{67,3},{4,68},{68... | collective-permute-start | bytes 9437192 | tf_op jit(solution)/shard_map/ppermute | solution.py:463
  109.6 32.8 %all-to-all-start.2 = ((bf16[16,128,512]{2,1,0:T(8,128)(2,1)}), bf16[16,128,512]{2,1,0:T(8,128)(2,1)}, u32[]{:S(2)}, u32[]{:S(2)}) async-start(bf16[16,128,512]{2,1,0:T(8,128)(2,1)} %get-tuple-element.100), calls=%async_computation.2 | async-start | bytes 4194304 | tf_op jit(solution)/shard_map/all_to_all | solution.py:472
  114.1 22.8 %collective-permute-start.9 = (bf16[8,2,144,256]{3,2,1,0:T(8,128)(2,1)}, bf16[8,2,144,256]{3,2,1,0:T(8,128)(2,1)S(1)}, u32[]{:S(2)}, u32[]{:S(2)}) collective-permute-start(bf16[8,2,144,256]{3,2,1,0:T(8,128)(2,1)} %bitcast.18), channel_id=1, source_target_pairs={{0,64},{64,0},{1,65},{65,1},{2,66},{66,2},{3,67},{67,3},{4,68},{68... | collective-permute-start | bytes 3538952 | tf_op jit(solution)/shard_map/ppermute | solution.py:463
  114.2 4.8 %collective-permute-start.2 = (bf16[64,1024]{1,0:T(8,128)(2,1)S(1)}, bf16[64,1024]{1,0:T(8,128)(2,1)S(1)}, u32[]{:S(2)}, u32[]{:S(2)}) collective-permute-start(bf16[64,1024]{1,0:T(8,128)(2,1)S(1)} %get-tuple-element.95.refs_1_), channel_id=1, source_target_pairs={{0,1},{1,0},{2,3},{3,2},{4,5},{5,4},{6,7},{7,6},{8,9},{9,8},{10,11... | collective-permute-start | bytes 393224 | tf_op jit(solution)/shard_map/ppermute | solution.py:467
  115.5 8.5 %collective-permute-start.3 = (bf16[64,1024]{1,0:T(8,128)(2,1)S(1)}, bf16[64,1024]{1,0:T(8,128)(2,1)S(1)}, u32[]{:S(2)}, u32[]{:S(2)}) collective-permute-start(bf16[64,1024]{1,0:T(8,128)(2,1)S(1)} %get-tuple-element.95.refs_1_), channel_id=1, source_target_pairs={{0,2},{1,3},{2,0},{3,1},{4,6},{5,7},{6,4},{7,5},{8,10},{9,11},{10,... | collective-permute-start | bytes 393224 | tf_op jit(solution)/shard_map/ppermute | solution.py:467
  117.9 8.6 %collective-permute-start.4 = (bf16[64,1024]{1,0:T(8,128)(2,1)S(1)}, bf16[64,1024]{1,0:T(8,128)(2,1)S(1)}, u32[]{:S(2)}, u32[]{:S(2)}) collective-permute-start(bf16[64,1024]{1,0:T(8,128)(2,1)S(1)} %get-tuple-element.95.refs_1_), channel_id=1, source_target_pairs={{0,3},{1,2},{2,1},{3,0},{4,7},{5,6},{6,5},{7,4},{8,11},{9,10},{10,... | collective-permute-start | bytes 393224 | tf_op jit(solution)/shard_map/ppermute | solution.py:467
  132.4 17.9 %copy-start.17 = (f32[64,1024]{1,0:T(8,128)}, f32[64,1024]{1,0:T(8,128)S(1)}, u32[]{:S(2)}) copy-start(f32[64,1024]{1,0:T(8,128)S(1)} %get-tuple-element.98.refs_0_.refs_1_) | copy-start | bytes 786436
  132.4 10.0 %collective-permute-start.6 = (bf16[64,1024]{1,0:T(8,128)(2,1)S(1)}, bf16[64,1024]{1,0:T(8,128)(2,1)S(1)}, u32[]{:S(2)}, u32[]{:S(2)}) collective-permute-start(bf16[64,1024]{1,0:T(8,128)(2,1)S(1)} %get-tuple-element.99.refs_1_), channel_id=1, source_target_pairs={{0,1},{1,0},{2,3},{3,2},{4,5},{5,4},{6,7},{7,6},{8,9},{9,8},{10,11... | collective-permute-start | bytes 393224 | tf_op jit(solution)/shard_map/ppermute | solution.py:467
  132.4 10.7 %collective-permute-start.7 = (bf16[64,1024]{1,0:T(8,128)(2,1)S(1)}, bf16[64,1024]{1,0:T(8,128)(2,1)S(1)}, u32[]{:S(2)}, u32[]{:S(2)}) collective-permute-start(bf16[64,1024]{1,0:T(8,128)(2,1)S(1)} %get-tuple-element.99.refs_1_), channel_id=1, source_target_pairs={{0,2},{1,3},{2,0},{3,1},{4,6},{5,7},{6,4},{7,5},{8,10},{9,11},{10,... | collective-permute-start | bytes 393224 | tf_op jit(solution)/shard_map/ppermute | solution.py:467
  134.0 9.7 %collective-permute-start.8 = (bf16[64,1024]{1,0:T(8,128)(2,1)S(1)}, bf16[64,1024]{1,0:T(8,128)(2,1)S(1)}, u32[]{:S(2)}, u32[]{:S(2)}) collective-permute-start(bf16[64,1024]{1,0:T(8,128)(2,1)S(1)} %get-tuple-element.99.refs_1_), channel_id=1, source_target_pairs={{0,3},{1,2},{2,1},{3,0},{4,7},{5,6},{6,5},{7,4},{8,11},{9,10},{10,... | collective-permute-start | bytes 393224 | tf_op jit(solution)/shard_map/ppermute | solution.py:467
  148.0 24.4 %copy-start.3 = (bf16[32,144,256]{2,1,0:T(8,128)(2,1)S(1)}, bf16[32,144,256]{2,1,0:T(8,128)(2,1)}, u32[]{:S(2)}) copy-start(bf16[32,144,256]{2,1,0:T(8,128)(2,1)} %copy-done.2) | copy-start | bytes 7077892
  150.3 22.2 %copy-start.29 = (bf16[64,1024]{1,0:T(8,128)(2,1)}, bf16[64,1024]{1,0:T(8,128)(2,1)S(1)}, u32[]{:S(2)}) copy-start(bf16[64,1024]{1,0:T(8,128)(2,1)S(1)} %get-tuple-element.140.refs_0_) | copy-start | bytes 393220
  150.3 35.5 %collective-permute-start.13 = (bf16[8,2,128,512]{3,2,1,0:T(8,128)(2,1)}, bf16[8,2,128,512]{3,2,1,0:T(8,128)(2,1)S(1)}, u32[]{:S(2)}, u32[]{:S(2)}) collective-permute-start(bf16[8,2,128,512]{3,2,1,0:T(8,128)(2,1)} %bitcast.19.refs_7_), channel_id=1, source_target_pairs={{0,64},{64,0},{1,65},{65,1},{2,66},{66,2},{3,67},{67,3},{4,68},{68... | collective-permute-start | bytes 6291464 | tf_op jit(solution)/shard_map/ppermute | solution.py:463
  174.9 17.3 %copy-start.58 = (bf16[4,64,128]{2,1,0:T(8,128)(2,1)}, bf16[4,64,128]{2,1,0:T(8,128)(2,1)S(1)}, u32[]{:S(2)}) copy-start(bf16[4,64,128]{2,1,0:T(8,128)(2,1)S(1)} %get-tuple-element.142.refs_2_) | copy-start | bytes 196612
  174.9 4.9 %collective-permute-start.10 = (bf16[64,1024]{1,0:T(8,128)(2,1)S(1)}, bf16[64,1024]{1,0:T(8,128)(2,1)S(1)}, u32[]{:S(2)}, u32[]{:S(2)}) collective-permute-start(bf16[64,1024]{1,0:T(8,128)(2,1)S(1)} %get-tuple-element.104.refs_1_), channel_id=1, source_target_pairs={{0,1},{1,0},{2,3},{3,2},{4,5},{5,4},{6,7},{7,6},{8,9},{9,8},{10,11... | collective-permute-start | bytes 393224 | tf_op jit(solution)/shard_map/ppermute | solution.py:467
  176.3 6.7 %collective-permute-start.11 = (bf16[64,1024]{1,0:T(8,128)(2,1)S(1)}, bf16[64,1024]{1,0:T(8,128)(2,1)S(1)}, u32[]{:S(2)}, u32[]{:S(2)}) collective-permute-start(bf16[64,1024]{1,0:T(8,128)(2,1)S(1)} %get-tuple-element.104.refs_1_), channel_id=1, source_target_pairs={{0,2},{1,3},{2,0},{3,1},{4,6},{5,7},{6,4},{7,5},{8,10},{9,11},{10,... | collective-permute-start | bytes 393224 | tf_op jit(solution)/shard_map/ppermute | solution.py:467
  178.7 7.1 %collective-permute-start.12 = (bf16[64,1024]{1,0:T(8,128)(2,1)S(1)}, bf16[64,1024]{1,0:T(8,128)(2,1)S(1)}, u32[]{:S(2)}, u32[]{:S(2)}) collective-permute-start(bf16[64,1024]{1,0:T(8,128)(2,1)S(1)} %get-tuple-element.104.refs_1_), channel_id=1, source_target_pairs={{0,3},{1,2},{2,1},{3,0},{4,7},{5,6},{6,5},{7,4},{8,11},{9,10},{10,... | collective-permute-start | bytes 393224 | tf_op jit(solution)/shard_map/ppermute | solution.py:467
  192.9 24.4 %copy-start.11 = (f32[64,1024]{1,0:T(8,128)}, f32[64,1024]{1,0:T(8,128)S(1)}, u32[]{:S(2)}) copy-start(f32[64,1024]{1,0:T(8,128)S(1)} %get-tuple-element.106.refs_1_) | copy-start | bytes 786436
  195.5 13.0 %collective-permute-start.22 = (bf16[8,2,128,512]{3,2,1,0:T(8,128)(2,1)S(1)}, bf16[8,2,128,512]{3,2,1,0:T(8,128)(2,1)S(1)}, u32[]{:S(2)}, u32[]{:S(2)}) collective-permute-start(bf16[8,2,128,512]{3,2,1,0:T(8,128)(2,1)S(1)} %get-tuple-element.114), channel_id=1, source_target_pairs={{0,64},{64,0},{1,65},{65,1},{2,66},{66,2},{3,67},{67,3},{4,68},{68... | collective-permute-start | bytes 6291464 | tf_op jit(solution)/shard_map/ppermute | solution.py:463
  197.2 5.1 %collective-permute-start.19 = (bf16[64,1024]{1,0:T(8,128)(2,1)S(1)}, bf16[64,1024]{1,0:T(8,128)(2,1)S(1)}, u32[]{:S(2)}, u32[]{:S(2)}) collective-permute-start(bf16[64,1024]{1,0:T(8,128)(2,1)S(1)} %get-tuple-element.108.refs_2_), channel_id=1, source_target_pairs={{0,1},{1,0},{2,3},{3,2},{4,5},{5,4},{6,7},{7,6},{8,9},{9,8},{10,11... | collective-permute-start | bytes 393224 | tf_op jit(solution)/shard_map/ppermute | solution.py:467
  197.2 8.7 %collective-permute-start.20 = (bf16[64,1024]{1,0:T(8,128)(2,1)S(1)}, bf16[64,1024]{1,0:T(8,128)(2,1)S(1)}, u32[]{:S(2)}, u32[]{:S(2)}) collective-permute-start(bf16[64,1024]{1,0:T(8,128)(2,1)S(1)} %get-tuple-element.108.refs_2_), channel_id=1, source_target_pairs={{0,2},{1,3},{2,0},{3,1},{4,6},{5,7},{6,4},{7,5},{8,10},{9,11},{10,... | collective-permute-start | bytes 393224 | tf_op jit(solution)/shard_map/ppermute | solution.py:467
  199.4 9.1 %collective-permute-start.21 = (bf16[64,1024]{1,0:T(8,128)(2,1)S(1)}, bf16[64,1024]{1,0:T(8,128)(2,1)S(1)}, u32[]{:S(2)}, u32[]{:S(2)}) collective-permute-start(bf16[64,1024]{1,0:T(8,128)(2,1)S(1)} %get-tuple-element.108.refs_2_), channel_id=1, source_target_pairs={{0,3},{1,2},{2,1},{3,0},{4,7},{5,6},{6,5},{7,4},{8,11},{9,10},{10,... | collective-permute-start | bytes 393224 | tf_op jit(solution)/shard_map/ppermute | solution.py:467
  217.3 18.6 %copy-start.31 = (bf16[64,1024]{1,0:T(8,128)(2,1)}, bf16[64,1024]{1,0:T(8,128)(2,1)S(1)}, u32[]{:S(2)}) copy-start(bf16[64,1024]{1,0:T(8,128)(2,1)S(1)} %get-tuple-element.141.refs_1_) | copy-start | bytes 393220
  217.3 20.7 %copy-start.60 = (f32[8,1024]{1,0:T(8,128)}, f32[8,1024]{1,0:T(8,128)S(1)}, u32[]{:S(2)}) copy-start(f32[8,1024]{1,0:T(8,128)S(1)} %get-tuple-element.151.refs_16_) | copy-start | bytes 98308
  217.3 18.6 %copy-start.7 = (bf16[16,128,512]{2,1,0:T(8,128)(2,1)S(1)}, bf16[16,128,512]{2,1,0:T(8,128)(2,1)}, u32[]{:S(2)}) copy-start(bf16[16,128,512]{2,1,0:T(8,128)(2,1)} %get-tuple-element.118.refs_4_) | copy-start | bytes 6291460
  239.3 3.9 collective-permute-start.23
  239.3 6.9 %collective-permute-start.24 = (bf16[64,1024]{1,0:T(8,128)(2,1)S(1)}, bf16[64,1024]{1,0:T(8,128)(2,1)S(1)}, u32[]{:S(2)}, u32[]{:S(2)}) collective-permute-start(bf16[64,1024]{1,0:T(8,128)(2,1)S(1)} %get-tuple-element.119.refs_2_), channel_id=1, source_target_pairs={{0,2},{1,3},{2,0},{3,1},{4,6},{5,7},{6,4},{7,5},{8,10},{9,11},{10,... | collective-permute-start | bytes 393224 | tf_op jit(solution)/shard_map/ppermute | solution.py:467
  242.5 5.2 %collective-permute-start.25 = (bf16[64,1024]{1,0:T(8,128)(2,1)S(1)}, bf16[64,1024]{1,0:T(8,128)(2,1)S(1)}, u32[]{:S(2)}, u32[]{:S(2)}) collective-permute-start(bf16[64,1024]{1,0:T(8,128)(2,1)S(1)} %get-tuple-element.119.refs_2_), channel_id=1, source_target_pairs={{0,3},{1,2},{2,1},{3,0},{4,7},{5,6},{6,5},{7,4},{8,11},{9,10},{10,... | collective-permute-start | bytes 393224 | tf_op jit(solution)/shard_map/ppermute | solution.py:467
  256.1 35.1 %collective-permute-start.29 = (bf16[8,2,128,512]{3,2,1,0:T(8,128)(2,1)}, bf16[8,2,128,512]{3,2,1,0:T(8,128)(2,1)}, u32[]{:S(2)}, u32[]{:S(2)}) collective-permute-start(bf16[8,2,128,512]{3,2,1,0:T(8,128)(2,1)} %get-tuple-element.128), channel_id=1, source_target_pairs={{0,64},{64,0},{1,65},{65,1},{2,66},{66,2},{3,67},{67,3},{4,68},{68... | collective-permute-start | bytes 6291464 | tf_op jit(solution)/shard_map/ppermute | solution.py:463
  260.6 30.6 %copy-start.18 = (f32[64,1024]{1,0:T(8,128)S(1)}, f32[64,1024]{1,0:T(8,128)}, u32[]{:S(2)}) copy-start(f32[64,1024]{1,0:T(8,128)} %copy-done.17) | copy-start | bytes 786436
  260.6 30.6 %all-to-all-start.5 = ((bf16[16,128,512]{2,1,0:T(8,128)(2,1)}), bf16[16,128,512]{2,1,0:T(8,128)(2,1)S(1)}, u32[]{:S(2)}, u32[]{:S(2)}) async-start(bf16[16,128,512]{2,1,0:T(8,128)(2,1)} %copy-done.8), calls=%async_computation.5 | async-start | bytes 4194304 | tf_op jit(solution)/shard_map/all_to_all | solution.py:472
  264.5 4.4 %collective-permute-start.26 = (bf16[64,1024]{1,0:T(8,128)(2,1)S(1)}, bf16[64,1024]{1,0:T(8,128)(2,1)S(1)}, u32[]{:S(2)}, u32[]{:S(2)}) collective-permute-start(bf16[64,1024]{1,0:T(8,128)(2,1)S(1)} %get-tuple-element.122.refs_2_), channel_id=1, source_target_pairs={{0,1},{1,0},{2,3},{3,2},{4,5},{5,4},{6,7},{7,6},{8,9},{9,8},{10,11... | collective-permute-start | bytes 393224 | tf_op jit(solution)/shard_map/ppermute | solution.py:467
  264.6 7.5 %collective-permute-start.27 = (bf16[64,1024]{1,0:T(8,128)(2,1)S(1)}, bf16[64,1024]{1,0:T(8,128)(2,1)S(1)}, u32[]{:S(2)}, u32[]{:S(2)}) collective-permute-start(bf16[64,1024]{1,0:T(8,128)(2,1)S(1)} %get-tuple-element.122.refs_2_), channel_id=1, source_target_pairs={{0,2},{1,3},{2,0},{3,1},{4,6},{5,7},{6,4},{7,5},{8,10},{9,11},{10,... | collective-permute-start | bytes 393224 | tf_op jit(solution)/shard_map/ppermute | solution.py:467
  266.5 8.2 %collective-permute-start.28 = (bf16[64,1024]{1,0:T(8,128)(2,1)S(1)}, bf16[64,1024]{1,0:T(8,128)(2,1)S(1)}, u32[]{:S(2)}, u32[]{:S(2)}) collective-permute-start(bf16[64,1024]{1,0:T(8,128)(2,1)S(1)} %get-tuple-element.122.refs_2_), channel_id=1, source_target_pairs={{0,3},{1,2},{2,1},{3,0},{4,7},{5,6},{6,5},{7,4},{8,11},{9,10},{10,... | collective-permute-start | bytes 393224 | tf_op jit(solution)/shard_map/ppermute | solution.py:467
  306.0 45.8 %copy-start.4 = (bf16[32,144,256]{2,1,0:T(8,128)(2,1)S(1)}, bf16[32,144,256]{2,1,0:T(8,128)(2,1)}, u32[]{:S(2)}) copy-start(bf16[32,144,256]{2,1,0:T(8,128)(2,1)} %copy-done.2) | copy-start | bytes 7077892
  306.7 45.1 %all-to-all-start.6 = ((bf16[16,192,512]{2,1,0:T(8,128)(2,1)}), bf16[16,192,512]{2,1,0:T(8,128)(2,1)}, u32[]{:S(2)}, u32[]{:S(2)}) async-start(bf16[16,192,512]{2,1,0:T(8,128)(2,1)} %get-tuple-element.131), calls=%async_computation.6 | async-start | bytes 6291456 | tf_op jit(solution)/shard_map/all_to_all | solution.py:472
  316.7 46.2 %collective-permute-start.34 = (bf16[8,2,128,256]{3,2,1,0:T(8,128)(2,1)}, bf16[8,2,128,256]{3,2,1,0:T(8,128)(2,1)}, u32[]{:S(2)}, u32[]{:S(2)}) collective-permute-start(bf16[8,2,128,256]{3,2,1,0:T(8,128)(2,1)} %get-tuple-element.145), channel_id=1, source_target_pairs={{0,64},{64,0},{1,65},{65,1},{2,66},{66,2},{3,67},{67,3},{4,68},{68... | collective-permute-start | bytes 3145736 | tf_op jit(solution)/shard_map/ppermute | solution.py:463
  352.7 17.2 %copy-start.14 = (bf16[8,2,128,256]{3,2,1,0:T(8,128)(2,1)S(1)}, bf16[8,2,128,256]{3,2,1,0:T(8,128)(2,1)}, u32[]{:S(2)}) copy-start(bf16[8,2,128,256]{3,2,1,0:T(8,128)(2,1)} %copy-done.13) | copy-start | bytes 3145732
  352.7 17.2 %copy-start.20 = (f32[64,1024]{1,0:T(8,128)S(1)}, f32[64,1024]{1,0:T(8,128)}, u32[]{:S(2)}) copy-start(f32[64,1024]{1,0:T(8,128)} %copy-done.19) | copy-start | bytes 786436
  352.7 17.2 %copy-start.61 = (f32[8,1024]{1,0:T(8,128)S(1)}, f32[8,1024]{1,0:T(8,128)}, u32[]{:S(2)}) copy-start(f32[8,1024]{1,0:T(8,128)} %copy-done.60) | copy-start | bytes 98308
  352.7 17.2 %copy-start.63 = (f32[8,1024]{1,0:T(8,128)S(1)}, f32[8,1024]{1,0:T(8,128)}, u32[]{:S(2)}) copy-start(f32[8,1024]{1,0:T(8,128)} %copy-done.62) | copy-start | bytes 98308
  352.7 17.2 %copy-start.65 = (f32[8,1024]{1,0:T(8,128)S(1)}, f32[8,1024]{1,0:T(8,128)}, u32[]{:S(2)}) copy-start(f32[8,1024]{1,0:T(8,128)} %copy-done.64) | copy-start | bytes 98308
  352.7 17.2 %copy-start.68 = (f32[1,1024]{1,0:T(1,128)S(1)}, f32[1,1024]{1,0:T(1,128)}, u32[]{:S(2)}) copy-start(f32[1,1024]{1,0:T(1,128)} %copy-done.67) | copy-start | bytes 12292
  356.3 13.6 %collective-permute-start.33 = (bf16[8,2,128,256]{3,2,1,0:T(8,128)(2,1)S(1)}, bf16[8,2,128,256]{3,2,1,0:T(8,128)(2,1)S(1)}, u32[]{:S(2)}, u32[]{:S(2)}) collective-permute-start(bf16[8,2,128,256]{3,2,1,0:T(8,128)(2,1)S(1)} %get-tuple-element.139), channel_id=1, source_target_pairs={{0,64},{64,0},{1,65},{65,1},{2,66},{66,2},{3,67},{67,3},{4,68},{68... | collective-permute-start | bytes 3145736 | tf_op jit(solution)/shard_map/ppermute | solution.py:463
  359.0 5.1 %collective-permute-start.30 = (bf16[64,1024]{1,0:T(8,128)(2,1)S(1)}, bf16[64,1024]{1,0:T(8,128)(2,1)S(1)}, u32[]{:S(2)}, u32[]{:S(2)}) collective-permute-start(bf16[64,1024]{1,0:T(8,128)(2,1)S(1)} %get-tuple-element.133.refs_2_), channel_id=1, source_target_pairs={{0,1},{1,0},{2,3},{3,2},{4,5},{5,4},{6,7},{7,6},{8,9},{9,8},{10,11... | collective-permute-start | bytes 393224 | tf_op jit(solution)/shard_map/ppermute | solution.py:467
  359.0 8.3 %collective-permute-start.31 = (bf16[64,1024]{1,0:T(8,128)(2,1)S(1)}, bf16[64,1024]{1,0:T(8,128)(2,1)S(1)}, u32[]{:S(2)}, u32[]{:S(2)}) collective-permute-start(bf16[64,1024]{1,0:T(8,128)(2,1)S(1)} %get-tuple-element.133.refs_2_), channel_id=1, source_target_pairs={{0,2},{1,3},{2,0},{3,1},{4,6},{5,7},{6,4},{7,5},{8,10},{9,11},{10,... | collective-permute-start | bytes 393224 | tf_op jit(solution)/shard_map/ppermute | solution.py:467
  360.9 9.0 %collective-permute-start.32 = (bf16[64,1024]{1,0:T(8,128)(2,1)S(1)}, bf16[64,1024]{1,0:T(8,128)(2,1)S(1)}, u32[]{:S(2)}, u32[]{:S(2)}) collective-permute-start(bf16[64,1024]{1,0:T(8,128)(2,1)S(1)} %get-tuple-element.133.refs_2_), channel_id=1, source_target_pairs={{0,3},{1,2},{2,1},{3,0},{4,7},{5,6},{6,5},{7,4},{8,11},{9,10},{10,... | collective-permute-start | bytes 393224 | tf_op jit(solution)/shard_map/ppermute | solution.py:467
  373.5 17.1 %copy-start.12 = (f32[64,1024]{1,0:T(8,128)S(1)}, f32[64,1024]{1,0:T(8,128)}, u32[]{:S(2)}) copy-start(f32[64,1024]{1,0:T(8,128)} %copy-done.11) | copy-start | bytes 786436
  373.5 50.0 %all-to-all-start.7 = ((bf16[16,144,512]{2,1,0:T(8,128)(2,1)}), bf16[16,144,512]{2,1,0:T(8,128)(2,1)S(1)}, u32[]{:S(2)}, u32[]{:S(2)}) async-start(bf16[16,144,512]{2,1,0:T(8,128)(2,1)} %get-tuple-element.159), calls=%async_computation.7 | async-start | bytes 4718592 | tf_op jit(solution)/shard_map/all_to_all | solution.py:472
  379.4 3.9 collective-permute-start.14
  379.5 8.4 %collective-permute-start.15 = (bf16[64,1024]{1,0:T(8,128)(2,1)S(1)}, bf16[64,1024]{1,0:T(8,128)(2,1)S(1)}, u32[]{:S(2)}, u32[]{:S(2)}) collective-permute-start(bf16[64,1024]{1,0:T(8,128)(2,1)S(1)} %copy-done.28), channel_id=1, source_target_pairs={{0,2},{1,3},{2,0},{3,1},{4,6},{5,7},{6,4},{7,5},{8,10},{9,11},{10,... | collective-permute-start | bytes 393224 | tf_op jit(solution)/shard_map/ppermute | solution.py:467
  382.7 7.9 %collective-permute-start.16 = (bf16[64,1024]{1,0:T(8,128)(2,1)S(1)}, bf16[64,1024]{1,0:T(8,128)(2,1)}, u32[]{:S(2)}, u32[]{:S(2)}) collective-permute-start(bf16[64,1024]{1,0:T(8,128)(2,1)S(1)} %copy-done.28), channel_id=1, source_target_pairs={{0,3},{1,2},{2,1},{3,0},{4,7},{5,6},{6,5},{7,4},{8,11},{9,10},{10,... | collective-permute-start | bytes 393224 | tf_op jit(solution)/shard_map/ppermute | solution.py:467
  391.5 2.5 collective-permute-start.17
  393.1 3.8 collective-permute-start.35
  394.0 22.9 %copy-start.6 = (bf16[16,128,512]{2,1,0:T(8,128)(2,1)S(1)}, bf16[16,128,512]{2,1,0:T(8,128)(2,1)}, u32[]{:S(2)}) copy-start(bf16[16,128,512]{2,1,0:T(8,128)(2,1)} %copy-done.5) | copy-start | bytes 6291460
  394.1 22.0 %collective-permute-start.18 = (bf16[2,64,1024]{2,1,0:T(8,128)(2,1)S(1)}, bf16[2,64,1024]{2,1,0:T(8,128)(2,1)S(1)}, u32[]{:S(2)}, u32[]{:S(2)}) collective-permute-start(bf16[2,64,1024]{2,1,0:T(8,128)(2,1)S(1)} %pad_maximum_fusion), channel_id=1, source_target_pairs={{0,4},{4,0},{1,5},{5,1},{2,6},{6,2},{3,7},{7,3},{8,12},{12,8},{9,1... | collective-permute-start | bytes 786440 | tf_op jit(solution)/shard_map/ppermute | solution.py:483
  397.0 20.0 %copy-start.76 = (bf16[1,64,1024]{2,1,0:T(8,128)(2,1)}, bf16[1,64,1024]{2,1,0:T(8,128)(2,1)S(1)}, u32[]{:S(2)}) copy-start(bf16[1,64,1024]{2,1,0:T(8,128)(2,1)S(1)} %get-tuple-element.191) | copy-start | bytes 393220
  397.7 26.1 %collective-permute-start.36 = (bf16[2,64,1024]{2,1,0:T(8,128)(2,1)}, bf16[2,64,1024]{2,1,0:T(8,128)(2,1)}, u32[]{:S(2)}, u32[]{:S(2)}) collective-permute-start(bf16[2,64,1024]{2,1,0:T(8,128)(2,1)} %pad_maximum_fusion.1), channel_id=1, source_target_pairs={{0,4},{4,0},{1,5},{5,1},{2,6},{6,2},{3,7},{7,3},{8,12},{12,8},{9,1... | collective-permute-start | bytes 786440 | tf_op jit(solution)/shard_map/ppermute | solution.py:483
  419.9 6.3 %collective-permute-start.37 = (f32[128,512]{1,0:T(8,128)}, f32[128,512]{1,0:T(8,128)S(1)}, u32[]{:S(2)}, u32[]{:S(2)}) collective-permute-start(f32[128,512]{1,0:T(8,128)} %get-tuple-element.158), channel_id=1, source_target_pairs={{0,64},{64,0},{1,65},{65,1},{2,66},{66,2},{3,67},{67,3},{4,68},{68... | collective-permute-start | bytes 786440 | tf_op jit(solution)/shard_map/ppermute | solution.py:463
  423.7 2.4 collective-permute-start.38
  (57 other events, 120.3 us)

commit v5 on v3

--- a/solution.py
+++ b/solution.py
@@ -22,7 +22,18 @@
     return jax.ShapeDtypeStruct(shape, dtype)
 
 
-def call(kernel, outs, ins, us=3):
+def kept(*shape, dtype=BF):
+    return ("kept", pltpu.HBM(shape, dtype))
+
+
+def message(*shape):
+    return pltpu.HBM(shape, BF)
+
+
+def call(kernel, outs, ins, us=3, through=()):
+    n, m, k = len(ins), len(outs), len(through)
+    held = [i for i, o in enumerate(outs) if isinstance(o, tuple)]
+    outs = [o[1] if isinstance(o, tuple) else o for o in outs]
     specs, arrays = [], []
     for item in ins:
         if isinstance(item, tuple):
@@ -30,12 +41,20 @@
             if block is None:
                 specs.append(pl.BlockSpec(memory_space=pltpu.SMEM))
             else:
-                specs.append(pl.BlockSpec(block, functools.partial(lambda at, i: at, index)))
+                specs.append(
+                    pl.BlockSpec(
+                        block,
+                        functools.partial(lambda at, i: at, index),
+                        pipeline_mode=pl.Buffered(1),
+                    )
+                )
         else:
             array = item
             specs.append(
                 pl.BlockSpec(
-                    array.shape, functools.partial(lambda n, i: (0,) * n, array.ndim)
+                    array.shape,
+                    functools.partial(lambda n, i: (0,) * n, array.ndim),
+                    pipeline_mode=pl.Buffered(1),
                 )
             )
         arrays.append(array)
@@ -43,17 +62,26 @@
         pl.BlockSpec(o.shape, functools.partial(lambda n, i: (0,) * n, len(o.shape)))
         for o in outs
     ]
-    return pl.pallas_call(
-        kernel,
+
+    def body(*refs):
+        kernel(*refs[:n], *refs[n + k : n + k + m])
+
+    results = pl.pallas_call(
+        body,
         grid=(1,),
-        out_shape=outs,
-        in_specs=specs,
-        out_specs=out_specs,
+        out_shape=list(outs) + [pltpu.HBM(t.shape, t.dtype) for t in through],
+        in_specs=specs + [pl.BlockSpec(memory_space=pl.ANY)] * k,
+        out_specs=out_specs + [pl.BlockSpec(memory_space=pl.ANY)] * k,
+        input_output_aliases={n + i: m + i for i in range(k)},
         compiler_params=pltpu.CompilerParams(vmem_limit_bytes=48 * 1024 * 1024),
         cost_estimate=pl.CostEstimate(
             flops=0, bytes_accessed=us * 3_000_000, transcendentals=0
         ),
-    )(*arrays)
+    )(*arrays, *[pltpu.with_memory_space_constraint(t, pltpu.HBM) for t in through])
+    return [
+        pltpu.with_memory_space_constraint(r, pltpu.HBM) if i in held else r
+        for i, r in enumerate(results)
+    ]
 
 
 def nn(a, b):
@@ -147,7 +175,19 @@
             kv[g, kv.shape[1] - ROWS :, k * 128 : k * 128 + 128] = pair
 
 
-def pack_kernel(core, qkv, out, up, down, gain, shift, inb, outb, upb, keep, send):
+def pack_kernel(core, *refs):
+    sources, (keep, send), held, sem = refs[:9], refs[9:11], refs[11:20], refs[20]
+    copies = [
+        pltpu.make_async_copy(a, b, sem.at[i]) for i, (a, b) in enumerate(zip(sources, held))
+    ]
+    for c in copies:
+        c.start()
+    for c in copies:
+        c.wait()
+    pack(core, *held, keep, send)
+
+
+def pack(core, qkv, out, up, down, gain, shift, inb, outb, upb, keep, send):
     wt = out[...].astype(F32).T
     dt = down[...].astype(F32).T
     inb_, gain_, shift_, outb_ = [r[...].astype(F32) for r in (inb, gain, shift, outb)]
@@ -182,20 +222,20 @@
         ref[128:144, 512:768] = values[3]
 
 
-def spread_kernel(core, keep, got, msg, ffn0, ffn1, attn1):
+def spread_kernel(core, keep, got, msg, ffn0, ffn1):
     first = core[0] == 0
     k, o = keep[...], got[...]
     lower, upper = jnp.where(first, k, o), jnp.where(first, o, k)
     small = jnp.concatenate(
         [v[128:144, 512:768].astype(F32)[0:8] for v in (lower, upper)]
     ).astype(BF)
-    tile = lower[0:128, 512:768]
+    tiles = lower[0:128, 512:768], upper[0:128, 512:768]
     for g in range(16):
-        msg[g, 0:128, :] = tile
-        msg[g, 128:144, :] = small
+        msg[g, 0:128, :] = tiles[0]
+        msg[g, 128:256, :] = tiles[1]
+        msg[g, 256:272, :] = small
     ffn0[...] = lower[0:128, 0:512]
     ffn1[...] = upper[0:128, 0:512]
-    attn1[...] = upper[0:128, 512:768]
 
 
 def first_kernel(x, params, wm, wo, piece, n1, q, msg, lnp, bias):
@@ -217,6 +257,13 @@
     out = (mid[...] + (total((p0, p1, p2, p3)) + ln_row(lnp, 0, 1, 2))).astype(BF)
     y[...] = out
     project(out.astype(F32), lnp, bias, wm, wo, 1, n1, q, msg)
+
+
+def attend_spread_kernel(first, q, kv, wm, wo, piece, part, prob, att, copies):
+    attend_kernel(first, q, kv, wm, wo, part, prob, att)
+    rest = piece[...]
+    for g in range(16):
+        copies[g] = rest
 
 
 def attend_kernel(first, q, kv, wm, wo, part, prob, att):
@@ -274,6 +321,10 @@
 def turn_kernel(x, p0, p1, p2, p3, lnp, bias, wm, wo, g, part, mid, n2, pre, act, dpre, back):
     feed(x, (p0, p1, p2, p3), lnp, bias, wm, wo, 1, part, mid, n2, pre, act)
     feed_back(g[...], pre, wm, wo, dpre, back)
+
+
+def finish_kernel(mid, p0, p1, p2, p3, lnp, y):
+    y[...] = (mid[...] + (total((p0, p1, p2, p3)) + ln_row(lnp, 1, 1, 2))).astype(BF)
 
 
 def grad_ffn_kernel(n2, g, dpre, act, mine, other, sums, row):
@@ -311,12 +362,29 @@
 
 
 def attend_back_first_kernel(
-    g, mid, p0, p1, p2, p3, lnp, wm, wo, prob, q, kv, gm, gr, dmid, bg, dq, msg, rows
+    g, mid, p0, p1, p2, p3, lnp, wm, wo, prob, q, kv, dmid, bg, dq, dkv, rows
 ):
-    attend_back(0, g, mid, (p0, p1, p2, p3), lnp, wm, wo, prob, q, kv, dmid, bg, dq, msg, rows)
+    attend_back(0, g, mid, (p0, p1, p2, p3), lnp, wm, wo, prob, q, kv, dmid, bg, dq, dkv, rows)
+
+
+def add_into(msg, at, gm, gr):
     for i in range(8):
         for j in range(2):
-            msg[2 * i + j, 0:128, :] = (gm[i, j].astype(F32) + gr[i, j].astype(F32)).astype(BF)
+            both = gm[i, j].astype(F32) + gr[i, j].astype(F32)
+            msg[2 * i + j, 0:128, at : at + gm.shape[3]] = both.astype(BF)
+
+
+def add_kernel(gm, gr, msg):
+    add_into(msg, 0, gm, gr)
+
+
+def join_kernel(fm, fr, am, ar, msg):
+    add_into(msg, 0, fm, fr)
+    add_into(msg, 512, am, ar)
+
+
+def mark_kernel(rows, out):
+    out[...] = rows[0:1, 0:128]
 
 
 def project_back_kernel(dkv, dq, wm, wo, dproj, part, sums):
@@ -388,33 +456,48 @@
             msg[g, 128:144, :] = jnp.concatenate(block).astype(BF)
 
 
-def combine_kernel(am, ar, fm, fr, msg):
-    msg[0, :, 0:512] = (fm[0].astype(F32) + fr[0].astype(F32)).astype(BF)
-    msg[0, :, 512:768] = (am[0].astype(F32) + ar[0].astype(F32)).astype(BF)
-
-
-def settle_kernel(tail, l0, l1, out):
-    t = jnp.sum(tail[...].astype(F32), axis=0)
-    out[0, 0:128, 512:768] = t[0:128]
+def settle_kernel(core, l0, l1, keep, send, attn):
+    first = core[0] == 0
     for j in range(2):
         cols = slice(j * 256, j * 256 + 256)
-        out[0, 0:128, cols] = jnp.sum(l0[:, 0:128, cols].astype(F32), axis=0)
-    out[1, 0:128, :] = l1[...].astype(F32)
+        a = jnp.sum(l0[:, :, cols].astype(F32), axis=0)
+        b = jnp.sum(l1[:, :, cols].astype(F32), axis=0)
+        keep[:, cols] = jnp.where(first, a, b)
+        send[:, cols] = jnp.where(first, b, a)
+    attn[...] = jnp.sum(l1[:, :, 512:768].astype(F32), axis=0)
+
+
+def settle_tail_kernel(core, tail, attn, keep, send):
+    first = core[0] == 0
+    t = jnp.sum(tail[...].astype(F32), axis=0)
+    a, b = t[0:128], attn[...]
     small = t[128:144]
     pad = jnp.zeros((1, 256), F32)
-    out[0, 128:136, 512:768] = jnp.concatenate([small[0:7], pad])
-    out[1, 128:136, 512:768] = jnp.concatenate([small[7:14], pad])
-
-
-def unpack_kernel(r, qkv, out, up, down, gain, shift, inb, outb, upb):
-    a = [r[j, 0:128, 512:768] for j in range(2)]
+    c, d = jnp.concatenate([small[0:7], pad]), jnp.concatenate([small[7:14], pad])
+    keep[0:128, :] = jnp.where(first, a, b)
+    send[0:128, :] = jnp.where(first, b, a)
+    keep[128:136, :] = jnp.where(first, c, d)
+    send[128:136, :] = jnp.where(first, d, c)
+
+
+def unpack_kernel(
+    core, fk, fg, ak, ag, qkv, out, up, down, gain, shift, inb, outb, upb
+):
+    first = core[0] == 0
+
+    def ordered(k, g):
+        return jnp.where(first, k, g), jnp.where(first, g, k)
+
+    a = ordered(ak[0:128, :], ag[0:128, :])
     for i, at in enumerate((128, 0, 64)):
         qkv[i] = jnp.concatenate([t[:, at : at + 64] for t in a], axis=1)
     out[...] = jnp.concatenate([t[:, 192:256] for t in a], axis=1).T
+    ups = ordered(fk[:, 0:256], fg[:, 0:256])
+    downs = ordered(fk[:, 256:512], fg[:, 256:512])
     for j in range(2):
-        up[:, j * 256 : j * 256 + 256] = r[j, 0:128, 0:256]
-        down[j * 256 : j * 256 + 256, :] = r[j, 0:128, 256:512].T
-    s0, s1 = r[0, 128:136, 512:768], r[1, 128:136, 512:768]
+        up[:, j * 256 : j * 256 + 256] = ups[j]
+        down[j * 256 : j * 256 + 256, :] = downs[j].T
+    s0, s1 = ordered(ak[128:136, :], ag[128:136, :])
     for row, ref in ((4, gain), (5, shift), (6, outb)):
         t = s0[row : row + 1] + s1[row : row + 1]
         ref[0:1, :] = t[:, 0:128]
@@ -461,124 +544,134 @@
 
     x, cot = own_rows(inputs), own_rows(cotangent)
     core = (s.astype(jnp.int32).reshape(1), None, None)
-    keep, send = call(
+    weights = [
+        jnp.moveaxis(wqkv[0], 1, 0), wout[0], wup[0], wdown[0],
+        gain[0], shift[0], inb[0], outb[0], upb,
+    ]
+    keep, send = pl.pallas_call(
         pack_kernel,
-        [sds(144, 768), sds(144, 768)],
-        [
-            core, jnp.moveaxis(wqkv[0], 1, 0), wout[0], wup[0], wdown[0],
-            gain[0], shift[0], inb[0], outb[0], upb,
-        ],
-    )
-    msg, piece0, ffn1, attn1 = call(
+        out_shape=[sds(144, 768), sds(144, 768)],
+        in_specs=[pl.BlockSpec(memory_space=pltpu.SMEM)]
+        + [pl.BlockSpec(memory_space=pl.ANY)] * 9,
+        out_specs=[pl.BlockSpec(memory_space=pltpu.VMEM)] * 2,
+        scratch_shapes=[pltpu.VMEM(w.shape, BF) for w in weights]
+        + [pltpu.SemaphoreType.DMA((9,))],
+        compiler_params=pltpu.CompilerParams(vmem_limit_bytes=48 * 1024 * 1024),
+    )(core[0], *[pltpu.with_memory_space_constraint(w, pltpu.HBM) for w in weights])
+    msg, piece0, piece1 = call(
         spread_kernel,
-        [sds(16, 144, 256), sds(128, 512), sds(128, 512), sds(128, 256)],
+        [message(16, 272, 256), sds(128, 512), sds(128, 512)],
         [core, keep, swap_cores(send)],
     )
-    a0 = exchange(msg).reshape(8, 2, 144, 256)
-    a1 = lax.all_gather(attn1, CHIPS, axis=0, tiled=True).reshape(8, 2, 128, 256)
-    f1 = lax.all_gather(ffn1, CHIPS, axis=0, tiled=True).reshape(8, 2, 128, 512)
-    am, ao = [a0, a1], [swap_cores(a0), swap_cores(a1)]
-    f1o = swap_cores(f1)
-    kinds = dict(n1=sds(ROWS, D), q=sds(4, ROWS, 128))
+    u = exchange(msg).reshape(8, 2, 272, 256)
+    uo = swap_cores(u)
+    am = [(u, (8, 2, 128, 256), (0, 0, l, 0)) for l in range(2)]
+    ao = [(uo, (8, 2, 128, 256), (0, 0, l, 0)) for l in range(2)]
+    kinds = dict(n1=kept(ROWS, D), q=kept(4, ROWS, 128))
     n10, q0, msg, lnp, bias = call(
         first_kernel,
-        [kinds["n1"], kinds["q"], sds(16, 192, 512), sds(2, 16, D, dtype=F32), sds(2, 16, 256, dtype=F32)],
-        [x, (a0, (8, 2, 16, 256), (0, 0, 8, 0)), am[0], ao[0], piece0],
+        [kinds["n1"], kinds["q"], message(16, 192, 512), kept(2, 16, D, dtype=F32), kept(2, 16, 256, dtype=F32)],
+        [x, (u, (8, 2, 16, 256), (0, 0, 16, 0)), am[0], ao[0], piece0],
     )
     got0 = exchange(msg)
     kv0 = (got0, (16, ROWS, 512), (0, 2, 0))
     f0 = (got0.reshape(8, 2, 192, 512), (8, 2, 128, 512), (0, 0, 0, 0))
     f0o = (swap_cores(got0).reshape(8, 2, 192, 512), (8, 2, 128, 512), (0, 0, 0, 0))
-    attend_outs = [sds(ROWS, D), sds(4, ROWS, D, dtype=F32), sds(4, ROWS, 128)]
+    attend_outs = [sds(ROWS, D), kept(4, ROWS, D, dtype=F32), kept(4, ROWS, 128)]
     feed_outs = [
-        sds(ROWS, D), sds(ROWS, D, dtype=F32), sds(ROWS, D),
-        sds(4, ROWS, 256, dtype=F32), sds(4, ROWS, 256),
+        sds(ROWS, D), kept(ROWS, D, dtype=F32), kept(ROWS, D),
+        kept(4, ROWS, 256, dtype=F32), kept(4, ROWS, 256),
     ]
-    part, prob0, att0 = call(attend_kernel, attend_outs, [(first, None, None), q0, kv0, am[0], ao[0]])
+    part, prob0, att0, copies = call(
+        attend_spread_kernel,
+        attend_outs + [message(16, 128, 512)],
+        [(first, None, None), q0, kv0, am[0], ao[0], piece1],
+    )
+    f1 = exchange(copies)
     part, mid0, n20, pre0, act0 = call(
         feed_kernel, feed_outs, [x, *all_parts(part), lnp, bias, f0, f0o]
     )
-    y0, n11, q1, msg = call(
+    y0, n11, q1, msg, f1 = call(
         next_kernel,
-        [sds(ROWS, D), kinds["n1"], kinds["q"], sds(16, ROWS, 512)],
+        [sds(ROWS, D), kinds["n1"], kinds["q"], message(16, ROWS, 512)],
         [mid0, *all_parts(part), lnp, bias, am[1], ao[1]],
-    )
+        through=[f1],
+    )
+    f1 = f1.reshape(8, 2, 128, 512)
+    f1o = swap_cores(f1)
     kv1 = exchange(msg)
     part, prob1, att1 = call(attend_kernel, attend_outs, [(first, None, None), q1, kv1, am[1], ao[1]])
-    part, mid1, n21, pre1, act1, dpre1, back = call(
+    last_part, mid1, n21, pre1, act1, dpre1, back = call(
         turn_kernel,
-        feed_outs + [sds(4, ROWS, 256), sds(ROWS, D)],
+        feed_outs + [kept(4, ROWS, 256), sds(ROWS, D)],
         [y0, *all_parts(part), lnp, bias, f1, f1o, cot],
     )
     backs = all_parts(back)
-    a, b, c, d = [p.astype(F32) for p in all_parts(part)]
-    y1 = (mid1 + (((a + b) + (c + d)) + lnp[1, 14:15])).astype(BF)
     grad_ffn_outs = [
-        sds(8, 2, 128, 512), sds(8, 2, 128, 512), sds(4, 256, dtype=F32), sds(1, D, dtype=F32)
+        kept(8, 2, 128, 512), sds(8, 2, 128, 512), kept(4, 256, dtype=F32), kept(1, D, dtype=F32)
     ]
     gfm1, gfo1, gub1, ob11 = call(grad_ffn_kernel, grad_ffn_outs, [n21, cot, dpre1, act1])
     gfr1 = swap_cores(gfo1)
-    back_outs = [sds(ROWS, D, dtype=F32), sds(ROWS, D), sds(4, ROWS, 128)]
-    rows_out = sds(8, D, dtype=F32)
+    back_outs = [kept(ROWS, D, dtype=F32), kept(ROWS, D), kept(4, ROWS, 128)]
+    rows_out = kept(8, D, dtype=F32)
     dmid1, bg1, dq1, dkv, rows1 = call(
         attend_back_kernel,
-        back_outs + [sds(16, ROWS, 512), rows_out],
+        back_outs + [message(16, ROWS, 512), rows_out],
         [cot, mid1, *backs, lnp, am[1], ao[1], prob1, q1, kv1],
     )
     dkv = exchange(dkv)
-    project_outs = [sds(4, ROWS, 256), sds(ROWS, D), sds(4, 256, dtype=F32)]
+    project_outs = [kept(4, ROWS, 256), sds(ROWS, D), kept(4, 256, dtype=F32)]
     dproj1, part, gib1 = call(project_back_kernel, project_outs, [dkv, dq1, am[1], ao[1]])
     backs = all_parts(part)
-    grad_attn_outs = [sds(8, 2, 128, 256), sds(8, 2, 128, 256)]
+    grad_attn_outs = [kept(8, 2, 128, 256), sds(8, 2, 128, 256)]
     gam1, gao1 = call(grad_attn_kernel, grad_attn_outs, [n11, bg1, att1, dproj1])
-    gar1 = swap_cores(gao1)
-    dx1, dpre0, part, head1 = call(
+    (l1,) = call(join_kernel, [message(16, 128, 768)], [gfm1, gfr1, gam1, swap_cores(gao1)])
+    dx1, dpre0, part, head1, l1 = call(
         hand_down_kernel,
-        [sds(ROWS, D), sds(4, ROWS, 256), sds(ROWS, D), rows_out],
+        [sds(ROWS, D), kept(4, ROWS, 256), sds(ROWS, D), rows_out],
         [y0, dmid1, *backs, lnp, pre0, f0, f0o],
-    )
+        through=[l1],
+    )
+    l1 = exchange(l1)
     backs = all_parts(part)
     gfm0, gfo0, gub0, ob10 = call(grad_ffn_kernel, grad_ffn_outs, [n20, dx1, dpre0, act0])
     gfr0 = swap_cores(gfo0)
-    def flat(v):
-        return v.reshape(16, 128, v.shape[-1])
-    msg1 = pl.pallas_call(
-        combine_kernel,
-        grid=(16,),
-        out_shape=sds(16, 128, 768),
-        in_specs=[pl.BlockSpec((1, 128, w), lambda i: (i, 0, 0)) for w in (256, 256, 512, 512)],
-        out_specs=pl.BlockSpec((1, 128, 768), lambda i: (i, 0, 0)),
-        compiler_params=pltpu.CompilerParams(vmem_limit_bytes=32 * 1024 * 1024),
-        cost_estimate=pl.CostEstimate(flops=0, bytes_accessed=9_000_000, transcendentals=0),
-    )(flat(gam1), flat(gar1), flat(gfm1), flat(gfr1))
-    l1 = lax.psum_scatter(msg1.reshape(2048, 768), CHIPS, scatter_dimension=0, tiled=True)
-    dmid0, bg0, dq0, msg, rows0 = call(
+    dmid0, bg0, dq0, dkv, rows0, last_part = call(
         attend_back_first_kernel,
-        back_outs + [sds(16, 192, 512), rows_out],
-        [dx1, mid0, *backs, lnp, am[0], ao[0], prob0, q0, kv0, gfm0, gfr0],
-    )
-    l0 = exchange(msg)
-    dproj0, part, gib0 = call(
-        project_back_kernel, project_outs, [(l0, (16, ROWS, 512), (0, 2, 0)), dq0, am[0], ao[0]]
-    )
+        back_outs + [message(16, ROWS, 512), rows_out],
+        [dx1, mid0, *backs, lnp, am[0], ao[0], prob0, q0, kv0],
+        through=[last_part],
+    )
+    (y1,) = call(finish_kernel, [sds(ROWS, D)], [mid1, *all_parts(last_part), lnp])
+    _, dkv, l1, y1 = call(
+        mark_kernel, [sds(1, 128, dtype=F32)], [rows0], through=[dkv, l1, y1]
+    )
+    dkv = exchange(dkv)
+    (l0,) = call(add_kernel, [message(16, 128, 512)], [gfm0, gfr0])
+    acts = whole_rows(s, yh, y0, y1)
+    dproj0, part, gib0, l0, acts = call(
+        project_back_kernel, project_outs, [dkv, dq0, am[0], ao[0]], through=[l0, acts]
+    )
+    l0 = exchange(l0)
     backs = all_parts(part)
     gam0, gao0 = call(grad_attn_kernel, grad_attn_outs, [n10, bg0, att0, dproj0])
     gar0 = swap_cores(gao0)
-    dx0, msg = call(
+    dx0, msg, l0 = call(
         last_kernel,
-        [sds(ROWS, D), sds(16, 144, 256)],
+        [sds(ROWS, D), message(16, 144, 256)],
         [x, dmid0, *backs, lnp, gam0, gar0, rows0, ob10, gib0, gub0, head1, rows1, ob11, gib1, gub1],
+        through=[l0],
     )
     tail = exchange(msg)
-    acts = whole_rows(s, yh, y0, y1)
     grads = whole_rows(s, yh, dx0, dx1)
-    (settled,) = call(settle_kernel, [sds(2, 144, 768, dtype=F32)], [tail, l0, l1])
-    settled = exchange(settled, "s")
     f = functools.partial(sds, dtype=F32)
+    fk, send, at1 = call(settle_kernel, [f(128, 512), f(128, 512), f(128, 256)], [core, l0, l1])
+    fg = swap_cores(send)
+    ak, send = call(settle_tail_kernel, [f(136, 256), f(136, 256)], [core, tail, at1])
     gq, go, gu, gd, gg, gs, gi, gb, gub = call(
         unpack_kernel,
         [f(3, 128, 128), f(128, 128), f(128, 512), f(512, 128), f(2, 128), f(2, 128), f(2, 128), f(2, 128), f(1, 512)],
-        [settled],
+        [core, fk, fg, ak, swap_cores(send)],
     )
     return (
         acts, grads, jnp.moveaxis(gq, 0, 1)[None], go[None], gu[None], gd[None],

time: 560 us -> 388 us (0.69)
  waiting for transfers between devices: 228 us -> 81.4 us
  local copies, waits for them, and re-layouts: 45.7 us -> 8.36 us
  Pallas kernels: 57.7 us -> 81.6 us
  between operations: 14.4 us -> 0.94 us
    all_gather x2 -> x0, waiting for transfers between devices: 101 us -> none  [the longest x1 75.5 us: local(): f1 = lax.all_gather(ffn1, CHIPS, axis=0, tiled=True).reshape(8, 2, 128, 512)]
    unnamed x184 -> x28, local copies, waits for them, and re-layouts: 44.8 us -> 7.44 us
    all_to_all x3 -> x5, waiting for transfers between devices: 51.5 us -> 21.2 us  [exchange(): return lax.all_to_all(v, axes, 0, 0, tiled=True)]
    pallas_call x21 -> x25, Pallas kernels: 57.7 us -> 81.6 us  [the longest x24 80.2 us: call(): pl.pallas_call(body, grid=(1,), out_shape=list(outs) + [pltpu.HBM(t.shape...]
    ppermute x2, waiting for transfers between devices: 24.2 us -> 14.1 us  [whole_rows(): far = lax.ppermute(rows, 'yh', [(0, 1), (1, 0)])]
    ppermute x11 -> x12, starting transfers between devices: 33.5 us -> 27.3 us  [swap_cores(): return lax.ppermute(v, 's', [(0, 1), (1, 0)])]
    all_to_all x3 -> x5, starting transfers between devices: 19.8 us -> 25.1 us  [exchange(): return lax.all_to_all(v, axes, 0, 0, tiled=True)]
  transfers between devices with their start and end apart: 43 -> 43, of which waited for: 28 -> 23; matrix products, arithmetic and copies ran while one was open for 1% -> 1% of each run, Pallas kernels for 8% -> 14%
where the time goes in v5:
time: 388 us; the launch traced here: 387 us
  blocking collectives  121 us (31%)
  starting transfers between devices  89.1 us (23%)
  Pallas kernels  81.6 us (21%)
  waiting for transfers between devices  81.4 us (21%)
  local copies, waits for them, and re-layouts  8.36 us (2%)
  other arithmetic  4.62 us (1%)
    all_to_all x4, blocking collectives, exchange(): return lax.all_to_all(v, axes, 0, 0, tiled=True)  121 us
    pallas_call x24, Pallas kernels, call(): pl.pallas_call(body, grid=(1,), out_shape=list(outs) + [pltpu.HBM(t.shape...  80.2 us
    ppermute x24, waiting for transfers between devices, all_parts(): lax.ppermute(part, 'x', [(i, i ^ k) for i in range(4)])  40 us
    ppermute x24, starting transfers between devices, all_parts(): lax.ppermute(part, 'x', [(i, i ^ k) for i in range(4)])  30.7 us
    ppermute x12, starting transfers between devices, swap_cores(): return lax.ppermute(v, 's', [(0, 1), (1, 0)])  27.3 us
    all_to_all x5, starting transfers between devices, exchange(): return lax.all_to_all(v, axes, 0, 0, tiled=True)  25.1 us
    all_to_all x5, waiting for transfers between devices, exchange(): return lax.all_to_all(v, axes, 0, 0, tiled=True)  21.2 us
    ppermute x2, waiting for transfers between devices, whole_rows(): far = lax.ppermute(rows, 'yh', [(0, 1), (1, 0)])  14.1 us
  transfers between devices with their start and end apart: 43, of which 23 were waited for; matrix products, arithmetic and copies ran while one was open for 1% of the time, Pallas kernels for 14%

profile of v5, /device:TPU:1, one launch (start us, length us, event | category | flops | bytes accessed | tf_op | source)
XLA Modules:
  0.0 386.8 jit_solution(6017200883976564431)
XLA Ops:
  2.1 1.5 collective-permute-start
  4.7 1.5 shard_map.195
  6.2 36.5 %all_to_all.45 = bf16[16,272,256]{2,1,0:T(8,128)(2,1)S(1)} all-to-all(bf16[16,272,256]{2,1,0:T(8,128)(2,1)} %get-tuple-element.102), channel_id=1, replica_groups=mesh['s'=2,'z'=4,'yl'=2,'yh'=2,'x'=4] {'z','yl','yh'}, dimensions={0} | all-to-all | bytes 4456448 | tf_op jit(solution)/shard_map/all_to_all | solution.py:521
  42.7 2.0 collective-permute-start.1
  44.8 4.1 %collective-permute-done.1.refs_3_.refs_4_.refs_8_ = bf16[8,2,272,256]{3,2,1,0:T(8,128)(2,1)} collective-permute-done((bf16[8,2,272,256]{3,2,1,0:T(8,128)(2,1)S(1)}, bf16[8,2,272,256]{3,2,1,0:T(8,128)(2,1)}, u32[]{:S(2)}, u32[]{:S(2)}) %collective-permute-start.1) | collective-permute-done | bytes 2228256 | tf_op jit(solution)/shard_map/ppermute | solution.py:512
  48.9 3.9 shard_map.196
  52.7 42.5 %all_to_all.46.refs_2_.refs_11_ = bf16[16,192,512]{2,1,0:T(8,128)(2,1)} all-to-all(bf16[16,192,512]{2,1,0:T(8,128)(2,1)} %get-tuple-element.105), channel_id=1, replica_groups=mesh['s'=2,'z'=4,'yl'=2,'yh'=2,'x'=4] {'z','yl','yh'}, dimensions={0} | all-to-all | bytes 6291456 | tf_op jit(solution)/shard_map/all_to_all | solution.py:521
  95.3 1.8 collective-permute-start.5
  97.1 5.4 %shard_map.197 = (bf16[64,1024]{1,0:T(8,128)(2,1)S(1)}, f32[4,64,1024]{2,1,0:T(8,128)}, bf16[4,64,128]{2,1,0:T(8,128)(2,1)}, bf16[16,128,512]{2,1,0:T(8,128)(2,1)}) custom-call(s32[1]{0:T(128)} %bitcast.1.refs_0_, bf16[4,64,128]{2,1,0:T(8,128)(2,1)} %get-tuple-element.104.refs_1_.refs_10_, bf16[16,192,512]{2,1,0:T(8,128)(2,1)} %all_to_all.46.refs_2_.refs_11_, ...), custom_call_target="tpu_custom_call" | custom-call | bytes 9000000 | tf_op jit(solution)/shard_map/pallas_call | solution.py:69
  102.4 4.4 %all-to-all-start.2 = ((bf16[16,128,512]{2,1,0:T(8,128)(2,1)}), bf16[16,128,512]{2,1,0:T(8,128)(2,1)}, u32[]{:S(2)}, u32[]{:S(2)}) async-start(bf16[16,128,512]{2,1,0:T(8,128)(2,1)} %get-tuple-element.112), calls=%async_computation.2 | async-start | bytes 4194304 | tf_op jit(solution)/shard_map/all_to_all | solution.py:521
  108.2 2.5 collective-permute-start.3
  112.2 4.9 %collective-permute-done.3.refs_3_ = bf16[64,1024]{1,0:T(8,128)(2,1)S(1)} collective-permute-done((bf16[64,1024]{1,0:T(8,128)(2,1)S(1)}, bf16[64,1024]{1,0:T(8,128)(2,1)S(1)}, u32[]{:S(2)}, u32[]{:S(2)}) %collective-permute-start.3) | collective-permute-done | bytes 131104 | tf_op jit(solution)/shard_map/ppermute | solution.py:516
  117.2 2.6 collective-permute-done.4.refs_4_
  119.8 4.5 %shard_map.198 = (bf16[64,1024]{1,0:T(8,128)(2,1)S(1)}, f32[64,1024]{1,0:T(8,128)}, bf16[64,1024]{1,0:T(8,128)(2,1)}, f32[4,64,256]{2,1,0:T(8,128)}, bf16[4,64,256]{2,1,0:T(8,128)(2,1)}) custom-call(bf16[64,1024]{1,0:T(8,128)(2,1)S(1)} %dynamic-slice_bitcast_fusion.1.refs_0_, bf16[64,1024]{1,0:T(8,128)(2,1)S(1)} %get-tuple-element.107.refs_1_, ...), custom_call_target="tpu_custom_call" | custom-call | bytes 9000000 | tf_op jit(solution)/shard_map/pallas_call | solution.py:69
  125.7 2.5 collective-permute-start.8
  128.1 7.1 %all-to-all-done.2.refs_9_ = bf16[16,128,512]{2,1,0:T(8,128)(2,1)} async-done(((bf16[16,128,512]{2,1,0:T(8,128)(2,1)}), bf16[16,128,512]{2,1,0:T(8,128)(2,1)}, u32[]{:S(2)}, u32[]{:S(2)}) %all-to-all-start.2) | async-done | bytes 2097184 | tf_op jit(solution)/shard_map/all_to_all | solution.py:521
  135.3 3.3 shard_map.199
  139.3 21.5 %all_to_all.47.refs_2_.refs_11_ = bf16[16,64,512]{2,1,0:T(8,128)(2,1)S(1)} all-to-all(bf16[16,64,512]{2,1,0:T(8,128)(2,1)} %get-tuple-element.115), channel_id=1, replica_groups=mesh['s'=2,'z'=4,'yl'=2,'yh'=2,'x'=4] {'z','yl','yh'}, dimensions={0} | all-to-all | bytes 2097152 | tf_op jit(solution)/shard_map/all_to_all | solution.py:521
  160.9 4.5 %shard_map.200 = (bf16[64,1024]{1,0:T(8,128)(2,1)S(1)}, f32[4,64,1024]{2,1,0:T(8,128)}, bf16[4,64,128]{2,1,0:T(8,128)(2,1)}) custom-call(s32[1]{0:T(128)} %bitcast.1.refs_0_, bf16[4,64,128]{2,1,0:T(8,128)(2,1)} %get-tuple-element.114.refs_1_.refs_10_, bf16[16,64,512]{2,1,0:T(8,128)(2,1)S(1)} %all_to_all.47.refs_2_.refs_11_, ...), custom_call_target="tpu_custom_call" | custom-call | bytes 9000000 | tf_op jit(solution)/shard_map/pallas_call | solution.py:69
  165.3 2.7 collective-permute-start.10
  170.7 3.9 %collective-permute-done.11.refs_4_ = bf16[64,1024]{1,0:T(8,128)(2,1)S(1)} collective-permute-done((bf16[64,1024]{1,0:T(8,128)(2,1)S(1)}, bf16[64,1024]{1,0:T(8,128)(2,1)S(1)}, u32[]{:S(2)}, u32[]{:S(2)}) %collective-permute-start.11) | collective-permute-done | bytes 131104 | tf_op jit(solution)/shard_map/ppermute | solution.py:516
  174.6 5.0 %shard_map.201 = (bf16[64,1024]{1,0:T(8,128)(2,1)S(1)}, f32[64,1024]{1,0:T(8,128)}, bf16[64,1024]{1,0:T(8,128)(2,1)}, f32[4,64,256]{2,1,0:T(8,128)}, bf16[4,64,2...) custom-call(bf16[64,1024]{1,0:T(8,128)(2,1)S(1)} %get-tuple-element.113.refs_0_, ...), custom_call_target="tpu_custom_call" | custom-call | bytes 9000000 | tf_op jit(solution)/shard_map/pallas_call | solution.py:69
  180.5 2.1 collective-permute-start.14
  182.5 1.6 collective-permute-start.15
  184.2 3.1 shard_map.204
  187.2 2.5 collective-permute-start.19
  189.8 5.7 %shard_map.202 = (f32[64,1024]{1,0:T(8,128)}, bf16[64,1024]{1,0:T(8,128)(2,1)}, bf16[4,64,128]{2,1,0:T(8,128)(2,1)}, bf16[16,64,512]{2,1,0:T(8,128)(2,1)}, f32[8,1024]{1,0:T(8,128)}) custom-call(bf16[64,1024]{1,0:T(8,128)(2,1)S(1)} %dynamic-slice_bitcast_fusion.refs_9_.refs_0_.refs_1_, f32[64,1024]{1,0:T(8,128)} %get-tuple-element.118.refs_1_.refs_0_, ...), custom_call_target="tpu_custom_call" | custom-call | bytes 9000000 | tf_op jit(solution)/shard_map/pallas_call | solution.py:69
  195.5 20.2 %all_to_all.48.refs_0_ = bf16[16,64,512]{2,1,0:T(8,128)(2,1)S(1)} all-to-all(bf16[16,64,512]{2,1,0:T(8,128)(2,1)} %get-tuple-element.122), channel_id=1, replica_groups=mesh['s'=2,'z'=4,'yl'=2,'yh'=2,'x'=4] {'z','yl','yh'}, dimensions={0} | all-to-all | bytes 2097152 | tf_op jit(solution)/shard_map/all_to_all | solution.py:521
  215.7 2.6 shard_map.203
  218.3 2.7 shard_map.205
  221.0 3.5 collective-permute-start.20
  225.7 2.6 collective-permute-start.18
  228.4 4.3 %shard_map.206.refs_10_ = bf16[16,128,768]{2,1,0:T(8,128)(2,1)} custom-call(bf16[8,2,128,512]{3,2,1,0:T(8,128)(2,1)} %get-tuple-element.129.refs_0_, bf16[8,2,128,512]{3,2,1,0:T(8,128)(2,1)S(1)} %collective-permute-done.19.refs_1_, bf16[8,2,128,256]{3,2,1,0:T(8,128)(2,1)} %get-tuple-element.135.refs_2_, ...), custom_call_target="tpu_custom_call" | custom-call | bytes 9000000 | tf_op jit(solution)/shard_map/pallas_call | solution.py:69
  232.7 2.1 collective-permute-done.18.refs_5_
  234.8 4.7 %shard_map.207 = (bf16[64,1024]{1,0:T(8,128)(2,1)S(1)}, bf16[4,64,256]{2,1,0:T(8,128)(2,1)}, bf16[64,1024]{1,0:T(8,128)(2,1)S(1)}, f32[8,1024]{1,0:T(8,128)}, bf16[16,128,768]{2,1,0:T(8,128)(2,1)}) custom-call(bf16[64,1024]{1,0:T(8,128)(2,1)S(1)} %get-tuple-element.113.refs_0_, ...), custom_call_target="tpu_custom_call", output_to_operand_aliasing={{4}: (10, {})} | custom-call | bytes 9000000 | tf_op jit(solution)/shard_map/pallas_call | solution.py:69
  239.4 4.5 %all-to-all-start.5 = ((bf16[16,128,768]{2,1,0:T(8,128)(2,1)}), bf16[16,128,768]{2,1,0:T(8,128)(2,1)}, u32[]{:S(2)}, u32[]{:S(2)}) async-start(bf16[16,128,768]{2,1,0:T(8,128)(2,1)} %get-tuple-element.143), calls=%async_computation.5 | async-start | bytes 6291456 | tf_op jit(solution)/shard_map/all_to_all | solution.py:521
  243.9 3.7 shard_map.211
  248.4 3.8 collective-permute-start.22
  253.7 5.2 %collective-permute-done.22.refs_4_ = bf16[64,1024]{1,0:T(8,128)(2,1)S(1)} collective-permute-done((bf16[64,1024]{1,0:T(8,128)(2,1)S(1)}, bf16[64,1024]{1,0:T(8,128)(2,1)S(1)}, u32[]{:S(2)}, u32[]{:S(2)}) %collective-permute-start.22) | collective-permute-done | bytes 131104 | tf_op jit(solution)/shard_map/ppermute | solution.py:516
  258.8 2.5 collective-permute-done.23.refs_5_
  261.4 5.9 %shard_map.208 = (f32[64,1024]{1,0:T(8,128)}, bf16[64,1024]{1,0:T(8,128)(2,1)}, bf16[4,64,128]{2,1,0:T(8,128)(2,1)}, bf16[16,64,512]{2,1,0:T(8,128)(2,1)}, f32[8,1024]{1,0:T(8,128)}, /*index=5*/bf16[64,1024]{1,0:T(8,128)(2,1)}) custom-call(bf16[64,1024]{1,0:T(8,128)(2,1)S(1)} %get-tuple-element.137.refs_0_.refs_1_, ...), custom_call_target="tpu_custom_call", output_to_operand_aliasing={{5}: (12, {})} | custom-call | bytes 9000000 | tf_op jit(solution)/shard_map/pallas_call | solution.py:69
  268.6 2.6 collective-permute-start.26
  272.0 2.6 collective-permute-done.25.refs_3_
  274.7 2.5 collective-permute-done.26.refs_4_
  279.8 3.9 %all-to-all-done.5.refs_2_ = bf16[16,128,768]{2,1,0:T(8,128)(2,1)} async-done(((bf16[16,128,768]{2,1,0:T(8,128)(2,1)}), bf16[16,128,768]{2,1,0:T(8,128)(2,1)}, u32[]{:S(2)}, u32[]{:S(2)}) %all-to-all-start.5) | async-done | bytes 3145760 | tf_op jit(solution)/shard_map/all_to_all | solution.py:521
  285.0 3.1 collective-permute-start.28
  288.1 6.3 %all-to-all-start.6 = ((bf16[16,64,512]{2,1,0:T(8,128)(2,1)}), bf16[16,64,512]{2,1,0:T(8,128)(2,1)}, u32[]{:S(2)}, u32[]{:S(2)}) async-start(bf16[16,64,512]{2,1,0:T(8,128)(2,1)} %get-tuple-element.145), calls=%async_computation.6 | async-start | bytes 2097152 | tf_op jit(solution)/shard_map/all_to_all | solution.py:521
  294.5 2.9 collective-permute-start.29
  297.4 4.0 %shard_map.212.refs_4_ = bf16[16,128,512]{2,1,0:T(8,128)(2,1)} custom-call(bf16[8,2,128,512]{3,2,1,0:T(8,128)(2,1)} %get-tuple-element.150.refs_0_, bf16[8,2,128,512]{3,2,1,0:T(8,128)(2,1)} %collective-permute-done.27.refs_1_), custom_call_target="tpu_custom_call" | custom-call | bytes 9000000 | tf_op jit(solution)/shard_map/pallas_call | solution.py:69
  301.4 14.1 %collective-permute-done.29 = bf16[2,64,1024]{2,1,0:T(8,128)(2,1)} collective-permute-done((bf16[2,64,1024]{2,1,0:T(8,128)(2,1)S(1)}, bf16[2,64,1024]{2,1,0:T(8,128)(2,1)}, u32[]{:S(2)}, u32[]{:S(2)}) %collective-permute-start.29) | collective-permute-done | bytes 262176 | tf_op jit(solution)/shard_map/ppermute | solution.py:532
  317.3 2.9 shard_map.213
  320.2 4.1 %all-to-all-start.7 = ((bf16[16,128,512]{2,1,0:T(8,128)(2,1)}), bf16[16,128,512]{2,1,0:T(8,128)(2,1)S(1)}, u32[]{:S(2)}, u32[]{:S(2)}) async-start(bf16[16,128,512]{2,1,0:T(8,128)(2,1)} %get-tuple-element.170), calls=%async_computation.7 | async-start | bytes 4194304 | tf_op jit(solution)/shard_map/all_to_all | solution.py:521
  324.3 2.6 shard_map.214
  328.4 3.8 collective-permute-start.31
  333.5 5.2 %collective-permute-done.31.refs_4_ = bf16[64,1024]{1,0:T(8,128)(2,1)S(1)} collective-permute-done((bf16[64,1024]{1,0:T(8,128)(2,1)S(1)}, bf16[64,1024]{1,0:T(8,128)(2,1)S(1)}, u32[]{:S(2)}, u32[]{:S(2)}) %collective-permute-start.31) | collective-permute-done | bytes 131104 | tf_op jit(solution)/shard_map/ppermute | solution.py:516
  338.7 2.5 collective-permute-done.32.refs_5_
  342.3 8.0 %all-to-all-done.7.refs_18_ = bf16[16,128,512]{2,1,0:T(8,128)(2,1)S(1)} async-done(((bf16[16,128,512]{2,1,0:T(8,128)(2,1)}), bf16[16,128,512]{2,1,0:T(8,128)(2,1)S(1)}, u32[]{:S(2)}, u32[]{:S(2)}) %all-to-all-start.7) | async-done | bytes 2097184 | tf_op jit(solution)/shard_map/all_to_all | solution.py:521
  352.8 3.2 shard_map.215
  356.0 5.7 %all-to-all-start.8 = ((bf16[16,144,256]{2,1,0:T(8,128)(2,1)}), bf16[16,144,256]{2,1,0:T(8,128)(2,1)S(1)}, u32[]{:S(2)}, u32[]{:S(2)}) async-start(bf16[16,144,256]{2,1,0:T(8,128)(2,1)} %get-tuple-element.176), calls=%async_computation.8 | async-start | bytes 2359296 | tf_op jit(solution)/shard_map/all_to_all | solution.py:521
  361.7 2.8 collective-permute-start.34
  366.3 3.1 collective-permute-start.35
  369.5 3.2 shard_map.216
  373.9 2.2 all-to-all-done.8.refs_1_
  377.3 6.5 %collective-permute-start.37 = (f32[136,256]{1,0:T(8,128)S(1)}, f32[136,256]{1,0:T(8,128)S(1)}, u32[]{:S(2)}, u32[]{:S(2)}) collective-permute-start(f32[136,256]{1,0:T(8,128)S(1)} %get-tuple-element.179), channel_id=1, source_target_pairs={{0,64},{64,0},{1,65},{65,1},{2,66},{66,2},{3,67},{67,3},{4,68},{68... | collective-permute-start | bytes 417800 | tf_op jit(solution)/shard_map/ppermute | solution.py:512
  (91 shorter events, 36.0 us)
Async XLA Ops:
  0.6 44.1 %copy-start = (bf16[2,1,128,1024]{3,2,1,0:T(8,128)(2,1)S(1)}, bf16[2,1,128,1024]{3,2,1,0:T(8,128)(2,1)}, u32[]{:S(2)}) copy-start(bf16[2,1,128,1024]{3,2,1,0:T(8,128)(2,1)} %param.11) | copy-start | bytes 1572868
  2.1 2.6 collective-permute-start
  42.7 6.1 %collective-permute-start.1 = (bf16[8,2,272,256]{3,2,1,0:T(8,128)(2,1)S(1)}, bf16[8,2,272,256]{3,2,1,0:T(8,128)(2,1)}, u32[]{:S(2)}, u32[]{:S(2)}) collective-permute-start(bf16[8,2,272,256]{3,2,1,0:T(8,128)(2,1)S(1)} %bitcast.46), channel_id=1, source_target_pairs={{0,64},{64,0},{1,65},{65,1},{2,66},{66,2},{3,67},{67,3},{4,68},{68... | collective-permute-start | bytes 6684680 | tf_op jit(solution)/shard_map/ppermute | solution.py:512
  95.3 24.5 %collective-permute-start.5 = (bf16[16,192,512]{2,1,0:T(8,128)(2,1)}, bf16[16,192,512]{2,1,0:T(8,128)(2,1)}, u32[]{:S(2)}, u32[]{:S(2)}) collective-permute-start(bf16[16,192,512]{2,1,0:T(8,128)(2,1)} %all_to_all.46.refs_2_.refs_11_), channel_id=1, source_target_pairs={{0,64},{64,0},{1,65},{65,1},{2,66},{66,2},{3,67},{67,3},{4,68},{68... | collective-permute-start | bytes 9437192 | tf_op jit(solution)/shard_map/ppermute | solution.py:512
  102.4 32.8 %all-to-all-start.2 = ((bf16[16,128,512]{2,1,0:T(8,128)(2,1)}), bf16[16,128,512]{2,1,0:T(8,128)(2,1)}, u32[]{:S(2)}, u32[]{:S(2)}) async-start(bf16[16,128,512]{2,1,0:T(8,128)(2,1)} %get-tuple-element.112), calls=%async_computation.2 | async-start | bytes 4194304 | tf_op jit(solution)/shard_map/all_to_all | solution.py:521
  106.9 5.3 %collective-permute-start.2 = (bf16[64,1024]{1,0:T(8,128)(2,1)S(1)}, bf16[64,1024]{1,0:T(8,128)(2,1)S(1)}, u32[]{:S(2)}, u32[]{:S(2)}) collective-permute-start(bf16[64,1024]{1,0:T(8,128)(2,1)S(1)} %get-tuple-element.107.refs_1_), channel_id=1, source_target_pairs={{0,1},{1,0},{2,3},{3,2},{4,5},{5,4},{6,7},{7,6},{8,9},{9,8},{10,11... | collective-permute-start | bytes 393224 | tf_op jit(solution)/shard_map/ppermute | solution.py:516
  108.2 9.0 %collective-permute-start.3 = (bf16[64,1024]{1,0:T(8,128)(2,1)S(1)}, bf16[64,1024]{1,0:T(8,128)(2,1)S(1)}, u32[]{:S(2)}, u32[]{:S(2)}) collective-permute-start(bf16[64,1024]{1,0:T(8,128)(2,1)S(1)} %get-tuple-element.107.refs_1_), channel_id=1, source_target_pairs={{0,2},{1,3},{2,0},{3,1},{4,6},{5,7},{6,4},{7,5},{8,10},{9,11},{10,... | collective-permute-start | bytes 393224 | tf_op jit(solution)/shard_map/ppermute | solution.py:516
  110.6 9.2 %collective-permute-start.4 = (bf16[64,1024]{1,0:T(8,128)(2,1)S(1)}, bf16[64,1024]{1,0:T(8,128)(2,1)S(1)}, u32[]{:S(2)}, u32[]{:S(2)}) collective-permute-start(bf16[64,1024]{1,0:T(8,128)(2,1)S(1)} %get-tuple-element.107.refs_1_), channel_id=1, source_target_pairs={{0,3},{1,2},{2,1},{3,0},{4,7},{5,6},{6,5},{7,4},{8,11},{9,10},{10,... | collective-permute-start | bytes 393224 | tf_op jit(solution)/shard_map/ppermute | solution.py:516
  124.3 11.0 %collective-permute-start.6 = (bf16[64,1024]{1,0:T(8,128)(2,1)S(1)}, bf16[64,1024]{1,0:T(8,128)(2,1)S(1)}, u32[]{:S(2)}, u32[]{:S(2)}) collective-permute-start(bf16[64,1024]{1,0:T(8,128)(2,1)S(1)} %get-tuple-element.111.refs_1_), channel_id=1, source_target_pairs={{0,1},{1,0},{2,3},{3,2},{4,5},{5,4},{6,7},{7,6},{8,9},{9,8},{10,11... | collective-permute-start | bytes 393224 | tf_op jit(solution)/shard_map/ppermute | solution.py:516
  124.3 11.0 %collective-permute-start.7 = (bf16[64,1024]{1,0:T(8,128)(2,1)S(1)}, bf16[64,1024]{1,0:T(8,128)(2,1)S(1)}, u32[]{:S(2)}, u32[]{:S(2)}) collective-permute-start(bf16[64,1024]{1,0:T(8,128)(2,1)S(1)} %get-tuple-element.111.refs_1_), channel_id=1, source_target_pairs={{0,2},{1,3},{2,0},{3,1},{4,6},{5,7},{6,4},{7,5},{8,10},{9,11},{10,... | collective-permute-start | bytes 393224 | tf_op jit(solution)/shard_map/ppermute | solution.py:516
  125.7 9.6 %collective-permute-start.8 = (bf16[64,1024]{1,0:T(8,128)(2,1)S(1)}, bf16[64,1024]{1,0:T(8,128)(2,1)S(1)}, u32[]{:S(2)}, u32[]{:S(2)}) collective-permute-start(bf16[64,1024]{1,0:T(8,128)(2,1)S(1)} %get-tuple-element.111.refs_1_), channel_id=1, source_target_pairs={{0,3},{1,2},{2,1},{3,0},{4,7},{5,6},{6,5},{7,4},{8,11},{9,10},{10,... | collective-permute-start | bytes 393224 | tf_op jit(solution)/shard_map/ppermute | solution.py:516
  138.5 36.1 %collective-permute-start.12 = (bf16[8,2,128,512]{3,2,1,0:T(8,128)(2,1)}, bf16[8,2,128,512]{3,2,1,0:T(8,128)(2,1)S(1)}, u32[]{:S(2)}, u32[]{:S(2)}) collective-permute-start(bf16[8,2,128,512]{3,2,1,0:T(8,128)(2,1)} %bitcast.16.refs_7_), channel_id=1, source_target_pairs={{0,64},{64,0},{1,65},{65,1},{2,66},{66,2},{3,67},{67,3},{4,68},{68... | collective-permute-start | bytes 6291464 | tf_op jit(solution)/shard_map/ppermute | solution.py:512
  165.3 5.3 %collective-permute-start.10 = (bf16[64,1024]{1,0:T(8,128)(2,1)S(1)}, bf16[64,1024]{1,0:T(8,128)(2,1)S(1)}, u32[]{:S(2)}, u32[]{:S(2)}) collective-permute-start(bf16[64,1024]{1,0:T(8,128)(2,1)S(1)} %get-tuple-element.116.refs_1_), channel_id=1, source_target_pairs={{0,2},{1,3},{2,0},{3,1},{4,6},{5,7},{6,4},{7,5},{8,10},{9,11},{10,... | collective-permute-start | bytes 393224 | tf_op jit(solution)/shard_map/ppermute | solution.py:516
  168.0 6.6 %collective-permute-start.11 = (bf16[64,1024]{1,0:T(8,128)(2,1)S(1)}, bf16[64,1024]{1,0:T(8,128)(2,1)S(1)}, u32[]{:S(2)}, u32[]{:S(2)}) collective-permute-start(bf16[64,1024]{1,0:T(8,128)(2,1)S(1)} %get-tuple-element.116.refs_1_), channel_id=1, source_target_pairs={{0,3},{1,2},{2,1},{3,0},{4,7},{5,6},{6,5},{7,4},{8,11},{9,10},{10,... | collective-permute-start | bytes 393224 | tf_op jit(solution)/shard_map/ppermute | solution.py:516
  168.9 5.7 %collective-permute-start.9 = (bf16[64,1024]{1,0:T(8,128)(2,1)S(1)}, bf16[64,1024]{1,0:T(8,128)(2,1)S(1)}, u32[]{:S(2)}, u32[]{:S(2)}) collective-permute-start(bf16[64,1024]{1,0:T(8,128)(2,1)S(1)} %get-tuple-element.116.refs_1_), channel_id=1, source_target_pairs={{0,1},{1,0},{2,3},{3,2},{4,5},{5,4},{6,7},{7,6},{8,9},{9,8},{10,11... | collective-permute-start | bytes 393224 | tf_op jit(solution)/shard_map/ppermute | solution.py:516
  179.6 0.7 copy-start.8
  180.3 9.5 %collective-permute-start.13 = (bf16[64,1024]{1,0:T(8,128)(2,1)S(1)}, bf16[64,1024]{1,0:T(8,128)(2,1)S(1)}, u32[]{:S(2)}, u32[]{:S(2)}) collective-permute-start(bf16[64,1024]{1,0:T(8,128)(2,1)S(1)} %get-tuple-element.119.refs_2_), channel_id=1, source_target_pairs={{0,1},{1,0},{2,3},{3,2},{4,5},{5,4},{6,7},{7,6},{8,9},{9,8},{10,11... | collective-permute-start | bytes 393224 | tf_op jit(solution)/shard_map/ppermute | solution.py:516
  180.5 9.3 %collective-permute-start.14 = (bf16[64,1024]{1,0:T(8,128)(2,1)S(1)}, bf16[64,1024]{1,0:T(8,128)(2,1)S(1)}, u32[]{:S(2)}, u32[]{:S(2)}) collective-permute-start(bf16[64,1024]{1,0:T(8,128)(2,1)S(1)} %get-tuple-element.119.refs_2_), channel_id=1, source_target_pairs={{0,2},{1,3},{2,0},{3,1},{4,6},{5,7},{6,4},{7,5},{8,10},{9,11},{10,... | collective-permute-start | bytes 393224 | tf_op jit(solution)/shard_map/ppermute | solution.py:516
  182.5 7.3 %collective-permute-start.15 = (bf16[64,1024]{1,0:T(8,128)(2,1)S(1)}, bf16[64,1024]{1,0:T(8,128)(2,1)S(1)}, u32[]{:S(2)}, u32[]{:S(2)}) collective-permute-start(bf16[64,1024]{1,0:T(8,128)(2,1)S(1)} %get-tuple-element.119.refs_2_), channel_id=1, source_target_pairs={{0,3},{1,2},{2,1},{3,0},{4,7},{5,6},{6,5},{7,4},{8,11},{9,10},{10,... | collective-permute-start | bytes 393224 | tf_op jit(solution)/shard_map/ppermute | solution.py:516
  187.2 41.1 %collective-permute-start.19 = (bf16[8,2,128,512]{3,2,1,0:T(8,128)(2,1)S(1)}, bf16[8,2,128,512]{3,2,1,0:T(8,128)(2,1)S(1)}, u32[]{:S(2)}, u32[]{:S(2)}) collective-permute-start(bf16[8,2,128,512]{3,2,1,0:T(8,128)(2,1)S(1)} %get-tuple-element.130), channel_id=1, source_target_pairs={{0,64},{64,0},{1,65},{65,1},{2,66},{66,2},{3,67},{67,3},{4,68},{68... | collective-permute-start | bytes 6291464 | tf_op jit(solution)/shard_map/ppermute | solution.py:512
  221.0 7.4 %collective-permute-start.20 = (bf16[8,2,128,256]{3,2,1,0:T(8,128)(2,1)S(1)}, bf16[8,2,128,256]{3,2,1,0:T(8,128)(2,1)S(1)}, u32[]{:S(2)}, u32[]{:S(2)}) collective-permute-start(bf16[8,2,128,256]{3,2,1,0:T(8,128)(2,1)S(1)} %get-tuple-element.136), channel_id=1, source_target_pairs={{0,64},{64,0},{1,65},{65,1},{2,66},{66,2},{3,67},{67,3},{4,68},{68... | collective-permute-start | bytes 3145736 | tf_op jit(solution)/shard_map/ppermute | solution.py:512
  224.5 8.2 %collective-permute-start.16 = (bf16[64,1024]{1,0:T(8,128)(2,1)S(1)}, bf16[64,1024]{1,0:T(8,128)(2,1)S(1)}, u32[]{:S(2)}, u32[]{:S(2)}) collective-permute-start(bf16[64,1024]{1,0:T(8,128)(2,1)S(1)} %get-tuple-element.124.refs_2_), channel_id=1, source_target_pairs={{0,1},{1,0},{2,3},{3,2},{4,5},{5,4},{6,7},{7,6},{8,9},{9,8},{10,11... | collective-permute-start | bytes 393224 | tf_op jit(solution)/shard_map/ppermute | solution.py:516
  224.5 8.2 %collective-permute-start.17 = (bf16[64,1024]{1,0:T(8,128)(2,1)S(1)}, bf16[64,1024]{1,0:T(8,128)(2,1)S(1)}, u32[]{:S(2)}, u32[]{:S(2)}) collective-permute-start(bf16[64,1024]{1,0:T(8,128)(2,1)S(1)} %get-tuple-element.124.refs_2_), channel_id=1, source_target_pairs={{0,2},{1,3},{2,0},{3,1},{4,6},{5,7},{6,4},{7,5},{8,10},{9,11},{10,... | collective-permute-start | bytes 393224 | tf_op jit(solution)/shard_map/ppermute | solution.py:516
  225.7 9.1 %collective-permute-start.18 = (bf16[64,1024]{1,0:T(8,128)(2,1)S(1)}, bf16[64,1024]{1,0:T(8,128)(2,1)S(1)}, u32[]{:S(2)}, u32[]{:S(2)}) collective-permute-start(bf16[64,1024]{1,0:T(8,128)(2,1)S(1)} %get-tuple-element.124.refs_2_), channel_id=1, source_target_pairs={{0,3},{1,2},{2,1},{3,0},{4,7},{5,6},{6,5},{7,4},{8,11},{9,10},{10,... | collective-permute-start | bytes 393224 | tf_op jit(solution)/shard_map/ppermute | solution.py:516
  239.4 44.3 %all-to-all-start.5 = ((bf16[16,128,768]{2,1,0:T(8,128)(2,1)}), bf16[16,128,768]{2,1,0:T(8,128)(2,1)}, u32[]{:S(2)}, u32[]{:S(2)}) async-start(bf16[16,128,768]{2,1,0:T(8,128)(2,1)} %get-tuple-element.143), calls=%async_computation.5 | async-start | bytes 6291456 | tf_op jit(solution)/shard_map/all_to_all | solution.py:521
  247.7 49.7 %collective-permute-start.27 = (bf16[8,2,128,512]{3,2,1,0:T(8,128)(2,1)}, bf16[8,2,128,512]{3,2,1,0:T(8,128)(2,1)}, u32[]{:S(2)}, u32[]{:S(2)}) collective-permute-start(bf16[8,2,128,512]{3,2,1,0:T(8,128)(2,1)} %get-tuple-element.151), channel_id=1, source_target_pairs={{0,64},{64,0},{1,65},{65,1},{2,66},{66,2},{3,67},{67,3},{4,68},{68... | collective-permute-start | bytes 6291464 | tf_op jit(solution)/shard_map/ppermute | solution.py:512
  248.4 5.2 %collective-permute-start.21 = (bf16[64,1024]{1,0:T(8,128)(2,1)S(1)}, bf16[64,1024]{1,0:T(8,128)(2,1)S(1)}, u32[]{:S(2)}, u32[]{:S(2)}) collective-permute-start(bf16[64,1024]{1,0:T(8,128)(2,1)S(1)} %get-tuple-element.138.refs_2_), channel_id=1, source_target_pairs={{0,1},{1,0},{2,3},{3,2},{4,5},{5,4},{6,7},{7,6},{8,9},{9,8},{10,11... | collective-permute-start | bytes 393224 | tf_op jit(solution)/shard_map/ppermute | solution.py:516
  248.4 10.4 %collective-permute-start.22 = (bf16[64,1024]{1,0:T(8,128)(2,1)S(1)}, bf16[64,1024]{1,0:T(8,128)(2,1)S(1)}, u32[]{:S(2)}, u32[]{:S(2)}) collective-permute-start(bf16[64,1024]{1,0:T(8,128)(2,1)S(1)} %get-tuple-element.138.refs_2_), channel_id=1, source_target_pairs={{0,2},{1,3},{2,0},{3,1},{4,6},{5,7},{6,4},{7,5},{8,10},{9,11},{10,... | collective-permute-start | bytes 393224 | tf_op jit(solution)/shard_map/ppermute | solution.py:516
  252.2 9.2 %collective-permute-start.23 = (bf16[64,1024]{1,0:T(8,128)(2,1)S(1)}, bf16[64,1024]{1,0:T(8,128)(2,1)S(1)}, u32[]{:S(2)}, u32[]{:S(2)}) collective-permute-start(bf16[64,1024]{1,0:T(8,128)(2,1)S(1)} %get-tuple-element.138.refs_2_), channel_id=1, source_target_pairs={{0,3},{1,2},{2,1},{3,0},{4,7},{5,6},{6,5},{7,4},{8,11},{9,10},{10,... | collective-permute-start | bytes 393224 | tf_op jit(solution)/shard_map/ppermute | solution.py:516
  267.3 4.7 %collective-permute-start.24 = (bf16[64,1024]{1,0:T(8,128)(2,1)}, bf16[64,1024]{1,0:T(8,128)(2,1)S(1)}, u32[]{:S(2)}, u32[]{:S(2)}) collective-permute-start(bf16[64,1024]{1,0:T(8,128)(2,1)} %get-tuple-element.144.refs_1_), channel_id=1, source_target_pairs={{0,1},{1,0},{2,3},{3,2},{4,5},{5,4},{6,7},{7,6},{8,9},{9,8},{10,11... | collective-permute-start | bytes 393224 | tf_op jit(solution)/shard_map/ppermute | solution.py:516
  267.3 7.3 %collective-permute-start.25 = (bf16[64,1024]{1,0:T(8,128)(2,1)}, bf16[64,1024]{1,0:T(8,128)(2,1)S(1)}, u32[]{:S(2)}, u32[]{:S(2)}) collective-permute-start(bf16[64,1024]{1,0:T(8,128)(2,1)} %get-tuple-element.144.refs_1_), channel_id=1, source_target_pairs={{0,2},{1,3},{2,0},{3,1},{4,6},{5,7},{6,4},{7,5},{8,10},{9,11},{10,... | collective-permute-start | bytes 393224 | tf_op jit(solution)/shard_map/ppermute | solution.py:516
  268.6 8.6 %collective-permute-start.26 = (bf16[64,1024]{1,0:T(8,128)(2,1)}, bf16[64,1024]{1,0:T(8,128)(2,1)S(1)}, u32[]{:S(2)}, u32[]{:S(2)}) collective-permute-start(bf16[64,1024]{1,0:T(8,128)(2,1)} %get-tuple-element.144.refs_1_), channel_id=1, source_target_pairs={{0,3},{1,2},{2,1},{3,0},{4,7},{5,6},{6,5},{7,4},{8,11},{9,10},{10,... | collective-permute-start | bytes 393224 | tf_op jit(solution)/shard_map/ppermute | solution.py:516
  277.2 0.9 copy-start.9
  279.2 0.7 copy-start.4
  285.0 9.4 %copy-start.5 = (bf16[64,1024]{1,0:T(8,128)(2,1)S(1)}, bf16[64,1024]{1,0:T(8,128)(2,1)}, u32[]{:S(2)}) copy-start(bf16[64,1024]{1,0:T(8,128)(2,1)} %get-tuple-element.152) | copy-start | bytes 393220
  285.0 9.4 %collective-permute-start.28 = (bf16[64,1024]{1,0:T(8,128)(2,1)S(1)}, bf16[64,1024]{1,0:T(8,128)(2,1)S(1)}, u32[]{:S(2)}, u32[]{:S(2)}) collective-permute-start(bf16[64,1024]{1,0:T(8,128)(2,1)S(1)} %broadcast_select_fusion.6), channel_id=1, source_target_pairs={{0,64},{64,0},{1,65},{65,1},{2,66},{66,2},{3,67},{67,3},{4,68},{68... | collective-permute-start | bytes 393224 | tf_op jit(solution)/shard_map/ppermute | solution.py:512
  288.1 29.2 %all-to-all-start.6 = ((bf16[16,64,512]{2,1,0:T(8,128)(2,1)}), bf16[16,64,512]{2,1,0:T(8,128)(2,1)}, u32[]{:S(2)}, u32[]{:S(2)}) async-start(bf16[16,64,512]{2,1,0:T(8,128)(2,1)} %get-tuple-element.145), calls=%async_computation.6 | async-start | bytes 2097152 | tf_op jit(solution)/shard_map/all_to_all | solution.py:521
  294.5 21.0 %collective-permute-start.29 = (bf16[2,64,1024]{2,1,0:T(8,128)(2,1)S(1)}, bf16[2,64,1024]{2,1,0:T(8,128)(2,1)}, u32[]{:S(2)}, u32[]{:S(2)}) collective-permute-start(bf16[2,64,1024]{2,1,0:T(8,128)(2,1)S(1)} %pad_maximum_fusion), channel_id=1, source_target_pairs={{0,4},{4,0},{1,5},{5,1},{2,6},{6,2},{3,7},{7,3},{8,12},{12,8},{9,1... | collective-permute-start | bytes 786440 | tf_op jit(solution)/shard_map/ppermute | solution.py:532
  320.2 30.1 %all-to-all-start.7 = ((bf16[16,128,512]{2,1,0:T(8,128)(2,1)}), bf16[16,128,512]{2,1,0:T(8,128)(2,1)S(1)}, u32[]{:S(2)}, u32[]{:S(2)}) async-start(bf16[16,128,512]{2,1,0:T(8,128)(2,1)} %get-tuple-element.170), calls=%async_computation.7 | async-start | bytes 4194304 | tf_op jit(solution)/shard_map/all_to_all | solution.py:521
  327.0 14.3 %collective-permute-start.33 = (bf16[8,2,128,256]{3,2,1,0:T(8,128)(2,1)S(1)}, bf16[8,2,128,256]{3,2,1,0:T(8,128)(2,1)S(1)}, u32[]{:S(2)}, u32[]{:S(2)}) collective-permute-start(bf16[8,2,128,256]{3,2,1,0:T(8,128)(2,1)S(1)} %get-tuple-element.161), channel_id=1, source_target_pairs={{0,64},{64,0},{1,65},{65,1},{2,66},{66,2},{3,67},{67,3},{4,68},{68... | collective-permute-start | bytes 3145736 | tf_op jit(solution)/shard_map/ppermute | solution.py:512
  328.4 5.1 %collective-permute-start.30 = (bf16[64,1024]{1,0:T(8,128)(2,1)S(1)}, bf16[64,1024]{1,0:T(8,128)(2,1)S(1)}, u32[]{:S(2)}, u32[]{:S(2)}) collective-permute-start(bf16[64,1024]{1,0:T(8,128)(2,1)S(1)} %get-tuple-element.155.refs_2_), channel_id=1, source_target_pairs={{0,1},{1,0},{2,3},{3,2},{4,5},{5,4},{6,7},{7,6},{8,9},{9,8},{10,11... | collective-permute-start | bytes 393224 | tf_op jit(solution)/shard_map/ppermute | solution.py:516
  328.4 10.3 %collective-permute-start.31 = (bf16[64,1024]{1,0:T(8,128)(2,1)S(1)}, bf16[64,1024]{1,0:T(8,128)(2,1)S(1)}, u32[]{:S(2)}, u32[]{:S(2)}) collective-permute-start(bf16[64,1024]{1,0:T(8,128)(2,1)S(1)} %get-tuple-element.155.refs_2_), channel_id=1, source_target_pairs={{0,2},{1,3},{2,0},{3,1},{4,6},{5,7},{6,4},{7,5},{8,10},{9,11},{10,... | collective-permute-start | bytes 393224 | tf_op jit(solution)/shard_map/ppermute | solution.py:516
  332.2 9.1 %collective-permute-start.32 = (bf16[64,1024]{1,0:T(8,128)(2,1)S(1)}, bf16[64,1024]{1,0:T(8,128)(2,1)S(1)}, u32[]{:S(2)}, u32[]{:S(2)}) collective-permute-start(bf16[64,1024]{1,0:T(8,128)(2,1)S(1)} %get-tuple-element.155.refs_2_), channel_id=1, source_target_pairs={{0,3},{1,2},{2,1},{3,0},{4,7},{5,6},{6,5},{7,4},{8,11},{9,10},{10,... | collective-permute-start | bytes 393224 | tf_op jit(solution)/shard_map/ppermute | solution.py:516
  341.2 1.1 copy-start.6
  350.3 1.3 copy-start.2
  351.6 1.2 copy-start.7
  356.0 13.4 %copy-start.3 = (bf16[16,128,512]{2,1,0:T(8,128)(2,1)S(1)}, bf16[16,128,512]{2,1,0:T(8,128)(2,1)}, u32[]{:S(2)}) copy-start(bf16[16,128,512]{2,1,0:T(8,128)(2,1)} %get-tuple-element.172.refs_1_) | copy-start | bytes 6291460
  356.0 20.1 %all-to-all-start.8 = ((bf16[16,144,256]{2,1,0:T(8,128)(2,1)}), bf16[16,144,256]{2,1,0:T(8,128)(2,1)S(1)}, u32[]{:S(2)}, u32[]{:S(2)}) async-start(bf16[16,144,256]{2,1,0:T(8,128)(2,1)} %get-tuple-element.176), calls=%async_computation.8 | async-start | bytes 2359296 | tf_op jit(solution)/shard_map/all_to_all | solution.py:521
  361.7 3.8 collective-permute-start.34
  365.5 3.9 %copy-start.12 = (bf16[1,64,1024]{2,1,0:T(8,128)(2,1)}, bf16[1,64,1024]{2,1,0:T(8,128)(2,1)S(1)}, u32[]{:S(2)}) copy-start(bf16[1,64,1024]{2,1,0:T(8,128)(2,1)S(1)} %get-tuple-element.204) | copy-start | bytes 393220
  365.5 3.9 %copy-start.13 = (bf16[1,64,1024]{2,1,0:T(8,128)(2,1)}, bf16[1,64,1024]{2,1,0:T(8,128)(2,1)S(1)}, u32[]{:S(2)}) copy-start(bf16[1,64,1024]{2,1,0:T(8,128)(2,1)S(1)} %get-tuple-element.205) | copy-start | bytes 393220
  366.3 17.4 %collective-permute-start.35 = (bf16[2,64,1024]{2,1,0:T(8,128)(2,1)}, bf16[2,64,1024]{2,1,0:T(8,128)(2,1)}, u32[]{:S(2)}, u32[]{:S(2)}) collective-permute-start(bf16[2,64,1024]{2,1,0:T(8,128)(2,1)} %pad_maximum_fusion.1), channel_id=1, source_target_pairs={{0,4},{4,0},{1,5},{5,1},{2,6},{6,2},{3,7},{7,3},{8,12},{12,8},{9,1... | collective-permute-start | bytes 786440 | tf_op jit(solution)/shard_map/ppermute | solution.py:532
  372.6 0.7 copy-start.10
  373.3 12.4 %collective-permute-start.36 = (f32[128,512]{1,0:T(8,128)}, f32[128,512]{1,0:T(8,128)S(1)}, u32[]{:S(2)}, u32[]{:S(2)}) collective-permute-start(f32[128,512]{1,0:T(8,128)} %get-tuple-element.175), channel_id=1, source_target_pairs={{0,64},{64,0},{1,65},{65,1},{2,66},{66,2},{3,67},{67,3},{4,68},{68... | collective-permute-start | bytes 786440 | tf_op jit(solution)/shard_map/ppermute | solution.py:512
  376.1 10.7 %copy-start.1 = (bf16[2,1,128,1024]{3,2,1,0:T(8,128)(2,1)S(1)}, bf16[2,1,128,1024]{3,2,1,0:T(8,128)(2,1)}, u32[]{:S(2)}) copy-start(bf16[2,1,128,1024]{3,2,1,0:T(8,128)(2,1)} %param.11) | copy-start | bytes 1572868
  376.1 1.0 copy-start.11
  377.3 8.4 %collective-permute-start.37 = (f32[136,256]{1,0:T(8,128)S(1)}, f32[136,256]{1,0:T(8,128)S(1)}, u32[]{:S(2)}, u32[]{:S(2)}) collective-permute-start(f32[136,256]{1,0:T(8,128)S(1)} %get-tuple-element.179), channel_id=1, source_target_pairs={{0,64},{64,0},{1,65},{65,1},{2,66},{66,2},{3,67},{67,3},{4,68},{68... | collective-permute-start | bytes 417800 | tf_op jit(solution)/shard_map/ppermute | solution.py:512

commit v6 on v5

--- a/solution.py
+++ b/solution.py
@@ -30,8 +30,11 @@
     return pltpu.HBM(shape, BF)
 
 
-def call(kernel, outs, ins, us=3, through=()):
+def call(kernel, outs, ins, us=3, through=(), after=None):
     n, m, k = len(ins), len(outs), len(through)
+    if after is not None:
+        ins = [*ins, (after, (16 if after.dtype == BF else 8, 128), (0, 0))]
+    e = len(ins)
     held = [i for i, o in enumerate(outs) if isinstance(o, tuple)]
     outs = [o[1] if isinstance(o, tuple) else o for o in outs]
     specs, arrays = [], []
@@ -64,7 +67,7 @@
     ]
 
     def body(*refs):
-        kernel(*refs[:n], *refs[n + k : n + k + m])
+        kernel(*refs[:n], *refs[e + k : e + k + m])
 
     results = pl.pallas_call(
         body,
@@ -72,7 +75,7 @@
         out_shape=list(outs) + [pltpu.HBM(t.shape, t.dtype) for t in through],
         in_specs=specs + [pl.BlockSpec(memory_space=pl.ANY)] * k,
         out_specs=out_specs + [pl.BlockSpec(memory_space=pl.ANY)] * k,
-        input_output_aliases={n + i: m + i for i in range(k)},
+        input_output_aliases={e + i: m + i for i in range(k)},
         compiler_params=pltpu.CompilerParams(vmem_limit_bytes=48 * 1024 * 1024),
         cost_estimate=pl.CostEstimate(
             flops=0, bytes_accessed=us * 3_000_000, transcendentals=0
@@ -323,8 +326,29 @@
     feed_back(g[...], pre, wm, wo, dpre, back)
 
 
-def finish_kernel(mid, p0, p1, p2, p3, lnp, y):
-    y[...] = (mid[...] + (total((p0, p1, p2, p3)) + ln_row(lnp, 1, 1, 2))).astype(BF)
+def by_section(core, a, b, keep, send):
+    first = core[0] == 0
+    keep[...] = jnp.where(first, a, b)
+    send[...] = jnp.where(first, b, a)
+
+
+def finish_kernel(core, y0, mid, p0, p1, p2, p3, lnp, keep, send):
+    y1 = (mid[...] + (total((p0, p1, p2, p3)) + ln_row(lnp, 1, 1, 2))).astype(BF)
+    by_section(core, y0[...], y1, keep, send)
+
+
+def pair_kernel(core, keep, got, rows):
+    first = core[0] == 0
+    k, g = keep[...], got[...]
+    rows[0] = jnp.where(first, k, g)
+    rows[1] = jnp.where(first, g, k)
+
+
+def line_up_kernel(half, rows, far, out):
+    first = half[0] == 0
+    k, g = rows[...], far[...]
+    out[:, 0:ROWS, :] = jnp.where(first, k, g)
+    out[:, ROWS:, :] = jnp.where(first, g, k)
 
 
 def grad_ffn_kernel(n2, g, dpre, act, mine, other, sums, row):
@@ -420,13 +444,13 @@
 
 
 def last_kernel(
-    x, dmid, p0, p1, p2, p3, lnp, gm, gr,
-    r0, o0, a0, u0, h1, r1, o1, a1, u1, dx, msg,
+    core, dx1, x, dmid, p0, p1, p2, p3, lnp, gm, gr,
+    r0, o0, a0, u0, h1, r1, o1, a1, u1, keep, send, msg,
 ):
     back, gg, gs = layer_norm_back(
         x[...].astype(F32), ln_row(lnp, 0, 0, 0), total((p0, p1, p2, p3))
     )
-    dx[...] = (dmid[...] + back).astype(BF)
+    by_section(core, (dmid[...] + back).astype(BF), dx1[...], keep, send)
     lines = []
     for first, rows, ob, a, u in (
         ((gg, gs), r0, o0, a0, u0),
@@ -464,7 +488,7 @@
         b = jnp.sum(l1[:, :, cols].astype(F32), axis=0)
         keep[:, cols] = jnp.where(first, a, b)
         send[:, cols] = jnp.where(first, b, a)
-    attn[...] = jnp.sum(l1[:, :, 512:768].astype(F32), axis=0)
+    attn[...] = jnp.sum(l0[:, :, 512:768].astype(F32), axis=0)
 
 
 def settle_tail_kernel(core, tail, attn, keep, send):
@@ -514,7 +538,7 @@
 
 def all_parts(part):
     got = [lax.ppermute(part, "x", [(i, i ^ k) for i in range(4)]) for k in (1, 3, 2)]
-    return part, got[0], got[2], got[1]
+    return [part, got[0], got[2], got[1]]
 
 
 def exchange(v, axes=CHIPS):
@@ -525,14 +549,8 @@
     return jnp.where(mine == 0, first, second)
 
 
-def whole_rows(s, yh, a, b):
-    keep, send = by_layer(s, a, b), by_layer(s, b, a)
-    got = swap_cores(send)
-    rows = jnp.stack([by_layer(s, keep, got), by_layer(s, got, keep)])
-    far = lax.ppermute(rows, "yh", [(0, 1), (1, 0)])
-    return jnp.concatenate([by_layer(yh, rows, far), by_layer(yh, far, rows)], axis=1).reshape(
-        1, 2, 1, 128, D
-    )
+def other_half(v):
+    return lax.ppermute(v, "yh", [(0, 1), (1, 0)])
 
 
 def local(inputs, cotangent, wqkv, wout, wup, wdown, gain, shift, inb, outb, upb):
@@ -610,60 +628,75 @@
     grad_ffn_outs = [
         kept(8, 2, 128, 512), sds(8, 2, 128, 512), kept(4, 256, dtype=F32), kept(1, D, dtype=F32)
     ]
-    gfm1, gfo1, gub1, ob11 = call(grad_ffn_kernel, grad_ffn_outs, [n21, cot, dpre1, act1])
-    gfr1 = swap_cores(gfo1)
     back_outs = [kept(ROWS, D, dtype=F32), kept(ROWS, D), kept(4, ROWS, 128)]
     rows_out = kept(8, D, dtype=F32)
-    dmid1, bg1, dq1, dkv, rows1 = call(
+    dmid1, bg1, dq1, dkv, rows1, last_part = call(
         attend_back_kernel,
         back_outs + [message(16, ROWS, 512), rows_out],
         [cot, mid1, *backs, lnp, am[1], ao[1], prob1, q1, kv1],
+        through=[last_part],
     )
     dkv = exchange(dkv)
+    gfm1, gfo1, gub1, ob11 = call(
+        grad_ffn_kernel, grad_ffn_outs, [n21, cot, dpre1, act1], after=rows1
+    )
+    gfr1 = swap_cores(gfo1)
+    keep, send = call(
+        finish_kernel,
+        [sds(ROWS, D), sds(ROWS, D)],
+        [core, y0, mid1, *all_parts(last_part), lnp],
+    )
+    (acts,) = call(pair_kernel, [sds(2, ROWS, D)], [core, keep, swap_cores(send)], us=1)
     project_outs = [kept(4, ROWS, 256), sds(ROWS, D), kept(4, 256, dtype=F32)]
-    dproj1, part, gib1 = call(project_back_kernel, project_outs, [dkv, dq1, am[1], ao[1]])
+    dproj1, part, gib1, acts = call(
+        project_back_kernel, project_outs, [dkv, dq1, am[1], ao[1]], through=[acts]
+    )
+    far = other_half(acts)
     backs = all_parts(part)
     grad_attn_outs = [kept(8, 2, 128, 256), sds(8, 2, 128, 256)]
-    gam1, gao1 = call(grad_attn_kernel, grad_attn_outs, [n11, bg1, att1, dproj1])
-    (l1,) = call(join_kernel, [message(16, 128, 768)], [gfm1, gfr1, gam1, swap_cores(gao1)])
-    dx1, dpre0, part, head1, l1 = call(
+    (l1,) = call(add_kernel, [message(16, 128, 512)], [gfm1, gfr1])
+    dx1, dpre0, part, head1, l1, far = call(
         hand_down_kernel,
         [sds(ROWS, D), kept(4, ROWS, 256), sds(ROWS, D), rows_out],
         [y0, dmid1, *backs, lnp, pre0, f0, f0o],
-        through=[l1],
+        through=[l1, far],
     )
     l1 = exchange(l1)
     backs = all_parts(part)
-    gfm0, gfo0, gub0, ob10 = call(grad_ffn_kernel, grad_ffn_outs, [n20, dx1, dpre0, act0])
-    gfr0 = swap_cores(gfo0)
-    dmid0, bg0, dq0, dkv, rows0, last_part = call(
+    dmid0, bg0, dq0, dkv, rows0 = call(
         attend_back_first_kernel,
         back_outs + [message(16, ROWS, 512), rows_out],
         [dx1, mid0, *backs, lnp, am[0], ao[0], prob0, q0, kv0],
-        through=[last_part],
-    )
-    (y1,) = call(finish_kernel, [sds(ROWS, D)], [mid1, *all_parts(last_part), lnp])
-    _, dkv, l1, y1 = call(
-        mark_kernel, [sds(1, 128, dtype=F32)], [rows0], through=[dkv, l1, y1]
-    )
+    )
+    _, dkv, l1 = call(mark_kernel, [sds(1, 128, dtype=F32)], [rows0], through=[dkv, l1])
     dkv = exchange(dkv)
-    (l0,) = call(add_kernel, [message(16, 128, 512)], [gfm0, gfr0])
-    acts = whole_rows(s, yh, y0, y1)
-    dproj0, part, gib0, l0, acts = call(
-        project_back_kernel, project_outs, [dkv, dq0, am[0], ao[0]], through=[l0, acts]
+    gfm0, gfo0, gub0, ob10 = call(
+        grad_ffn_kernel, grad_ffn_outs, [n20, dx1, dpre0, act0], after=rows0
+    )
+    gfr0 = swap_cores(gfo0)
+    gam1, gao1 = call(
+        grad_attn_kernel, grad_attn_outs, [n11, bg1, att1, dproj1], after=rows0
+    )
+    gar1 = swap_cores(gao1)
+    (l0,) = call(join_kernel, [message(16, 128, 768)], [gfm0, gfr0, gam1, gar1])
+    dproj0, part, gib0, l0 = call(
+        project_back_kernel, project_outs, [dkv, dq0, am[0], ao[0]], through=[l0]
     )
     l0 = exchange(l0)
     backs = all_parts(part)
     gam0, gao0 = call(grad_attn_kernel, grad_attn_outs, [n10, bg0, att0, dproj0])
     gar0 = swap_cores(gao0)
-    dx0, msg, l0 = call(
+    half = (yh.astype(jnp.int32).reshape(1), None, None)
+    (acts,) = call(line_up_kernel, [sds(2, 2 * ROWS, D)], [half, acts, far], us=1)
+    keep, send, msg, acts = call(
         last_kernel,
-        [sds(ROWS, D), message(16, 144, 256)],
-        [x, dmid0, *backs, lnp, gam0, gar0, rows0, ob10, gib0, gub0, head1, rows1, ob11, gib1, gub1],
-        through=[l0],
+        [sds(ROWS, D), sds(ROWS, D), message(16, 144, 256)],
+        [core, dx1, x, dmid0, *backs, lnp, gam0, gar0, rows0, ob10, gib0, gub0, head1, rows1, ob11, gib1, gub1],
+        through=[acts],
     )
     tail = exchange(msg)
-    grads = whole_rows(s, yh, dx0, dx1)
+    (grads,) = call(pair_kernel, [sds(2, ROWS, D)], [core, keep, swap_cores(send)], us=1)
+    (grads,) = call(line_up_kernel, [sds(2, 2 * ROWS, D)], [half, grads, other_half(grads)], us=1)
     f = functools.partial(sds, dtype=F32)
     fk, send, at1 = call(settle_kernel, [f(128, 512), f(128, 512), f(128, 256)], [core, l0, l1])
     fg = swap_cores(send)
@@ -674,7 +707,7 @@
         [core, fk, fg, ak, swap_cores(send)],
     )
     return (
-        acts, grads, jnp.moveaxis(gq, 0, 1)[None], go[None], gu[None], gd[None],
+        acts[None, :, None], grads[None, :, None], jnp.moveaxis(gq, 0, 1)[None], go[None], gu[None], gd[None],
         gg[None], gs[None], gi[None], gb[None], gub,
     )
 

time: 388 us -> 369 us (0.951)
  blocking collectives: 121 us -> 101 us
  waiting for transfers between devices: 81.4 us -> 75.1 us
  starting transfers between devices: 89.1 us -> 94.4 us
  other arithmetic: 4.62 us -> 0 us
    all_to_all x4 -> x3, blocking collectives: 121 us -> 101 us  [exchange(): return lax.all_to_all(v, axes, 0, 0, tiled=True)]
    all_to_all x5 -> x6, waiting for transfers between devices: 21.2 us -> 37.8 us  [exchange(): return lax.all_to_all(v, axes, 0, 0, tiled=True)]
    ppermute x2, waiting for transfers between devices: 14.1 us -> 0.01 us  [other_half(): return lax.ppermute(v, 'yh', [(0, 1), (1, 0)])]
    ppermute x24, waiting for transfers between devices: 40 us -> 30 us  [all_parts(): lax.ppermute(part, 'x', [(i, i ^ k) for i in range(4)])]
    all_to_all x5 -> x6, starting transfers between devices: 25.1 us -> 31 us  [exchange(): return lax.all_to_all(v, axes, 0, 0, tiled=True)]
    ppermute x24, starting transfers between devices: 30.7 us -> 26.3 us  [all_parts(): lax.ppermute(part, 'x', [(i, i ^ k) for i in range(4)])]
    pallas_call x24 -> x28, Pallas kernels: 80.2 us -> 83.6 us  [call(): pl.pallas_call(body, grid=(1,), out_shape=list(outs) + [pltpu.HBM(t.shape...]
  transfers between devices with their start and end apart: 43 -> 44, of which waited for: 23 -> 26; matrix products, arithmetic and copies ran while one was open for 1% -> 0% of each run, Pallas kernels for 14% -> 14%
where the time goes in v6:
time: 369 us; the launch traced here: 366 us
  blocking collectives  101 us (27%)
  starting transfers between devices  94.4 us (26%)
  Pallas kernels  85 us (23%)
  waiting for transfers between devices  75.1 us (20%)
  local copies, waits for them, and re-layouts  9.94 us (3%)
    all_to_all x3, blocking collectives, exchange(): return lax.all_to_all(v, axes, 0, 0, tiled=True)  101 us
    pallas_call x28, Pallas kernels, call(): pl.pallas_call(body, grid=(1,), out_shape=list(outs) + [pltpu.HBM(t.shape...  83.6 us
    all_to_all x6, waiting for transfers between devices, exchange(): return lax.all_to_all(v, axes, 0, 0, tiled=True)  37.8 us
    all_to_all x6, starting transfers between devices, exchange(): return lax.all_to_all(v, axes, 0, 0, tiled=True)  31 us
    ppermute x12, starting transfers between devices, swap_cores(): return lax.ppermute(v, 's', [(0, 1), (1, 0)])  30.9 us
    ppermute x24, waiting for transfers between devices, all_parts(): lax.ppermute(part, 'x', [(i, i ^ k) for i in range(4)])  30 us
    ppermute x24, starting transfers between devices, all_parts(): lax.ppermute(part, 'x', [(i, i ^ k) for i in range(4)])  26.3 us
    unnamed x28, local copies, waits for them, and re-layouts  9.01 us
  transfers between devices with their start and end apart: 44, of which 26 were waited for; matrix products, arithmetic and copies ran while one was open for 0% of the time, Pallas kernels for 14%

profile of v6, /device:TPU:1, one launch (start us, length us, event | category | flops | bytes accessed | tf_op | source)
XLA Modules:
  0.0 365.9 jit_solution(16696164776627667239)
XLA Ops:
  2.1 1.5 collective-permute-start
  4.7 1.5 shard_map.195
  6.2 36.5 %all_to_all.45 = bf16[16,272,256]{2,1,0:T(8,128)(2,1)S(1)} all-to-all(bf16[16,272,256]{2,1,0:T(8,128)(2,1)} %get-tuple-element.105), channel_id=1, replica_groups=mesh['s'=2,'z'=4,'yl'=2,'yh'=2,'x'=4] {'z','yl','yh'}, dimensions={0} | all-to-all | bytes 4456448 | tf_op jit(solution)/shard_map/all_to_all | solution.py:545
  42.7 2.0 collective-permute-start.1
  44.8 4.1 %collective-permute-done.1.refs_3_.refs_4_.refs_8_ = bf16[8,2,272,256]{3,2,1,0:T(8,128)(2,1)} collective-permute-done((bf16[8,2,272,256]{3,2,1,0:T(8,128)(2,1)S(1)}, bf16[8,2,272,256]{3,2,1,0:T(8,128)(2,1)}, u32[]{:S(2)}, u32[]{:S(2)}) %collective-permute-start.1) | collective-permute-done | bytes 2228256 | tf_op jit(solution)/shard_map/ppermute | solution.py:536
  48.8 3.9 %shard_map.196 = (bf16[64,1024]{1,0:T(8,128)(2,1)}, bf16[4,64,128]{2,1,0:T(8,128)(2,1)}, bf16[16,192,512]{2,1,0:T(8,128)(2,1)}, f32[2,16,1024]{2,1,0:T(8,128)}, f32[2,16,256]{2,1,0:T(8,128)}) custom-call(bf16[64,1024]{1,0:T(8,128)(2,1)S(1)} %dynamic-slice_bitcast_fusion.1.refs_0_.refs_2_, bf16[8,2,272,256]{3,2,1,0:T(8,128)(2,1)S(1)} %bitcast.38, ...), custom_call_target="tpu_custom_call" | custom-call | bytes 9000000 | tf_op jit(solution)/shard_map/pallas_call | solution.py:72
  52.7 42.5 %all_to_all.46.refs_2_.refs_11_ = bf16[16,192,512]{2,1,0:T(8,128)(2,1)} all-to-all(bf16[16,192,512]{2,1,0:T(8,128)(2,1)} %get-tuple-element.108), channel_id=1, replica_groups=mesh['s'=2,'z'=4,'yl'=2,'yh'=2,'x'=4] {'z','yl','yh'}, dimensions={0} | all-to-all | bytes 6291456 | tf_op jit(solution)/shard_map/all_to_all | solution.py:545
  95.2 1.8 collective-permute-start.5
  97.0 5.5 %shard_map.197 = (bf16[64,1024]{1,0:T(8,128)(2,1)S(1)}, f32[4,64,1024]{2,1,0:T(8,128)}, bf16[4,64,128]{2,1,0:T(8,128)(2,1)}, bf16[16,128,512]{2,1,0:T(8,128)(2,1)}) custom-call(s32[1]{0:T(128)} %bitcast.2.refs_0_, bf16[4,64,128]{2,1,0:T(8,128)(2,1)} %get-tuple-element.107.refs_1_.refs_10_, bf16[16,192,512]{2,1,0:T(8,128)(2,1)} %all_to_all.46.refs_2_.refs_11_, ...), custom_call_target="tpu_custom_call" | custom-call | bytes 9000000 | tf_op jit(solution)/shard_map/pallas_call | solution.py:72
  102.5 4.4 %all-to-all-start.2 = ((bf16[16,128,512]{2,1,0:T(8,128)(2,1)}), bf16[16,128,512]{2,1,0:T(8,128)(2,1)}, u32[]{:S(2)}, u32[]{:S(2)}) async-start(bf16[16,128,512]{2,1,0:T(8,128)(2,1)} %get-tuple-element.115), calls=%async_computation.2 | async-start | bytes 4194304 | tf_op jit(solution)/shard_map/all_to_all | solution.py:545
  107.0 2.6 collective-permute-start.4
  110.3 4.8 %collective-permute-done.4.refs_4_ = bf16[64,1024]{1,0:T(8,128)(2,1)S(1)} collective-permute-done((bf16[64,1024]{1,0:T(8,128)(2,1)S(1)}, bf16[64,1024]{1,0:T(8,128)(2,1)S(1)}, u32[]{:S(2)}, u32[]{:S(2)}) %collective-permute-start.4) | collective-permute-done | bytes 131104 | tf_op jit(solution)/shard_map/ppermute | solution.py:540
  116.6 4.5 %shard_map.198 = (bf16[64,1024]{1,0:T(8,128)(2,1)S(1)}, f32[64,1024]{1,0:T(8,128)}, bf16[64,1024]{1,0:T(8,128)(2,1)}, f32[4,64,256]{2,1,0:T(8,128)}, bf16[4,64,256]{2,1,0:T(8,128)(2,1)}) custom-call(bf16[64,1024]{1,0:T(8,128)(2,1)S(1)} %dynamic-slice_bitcast_fusion.1.refs_0_.refs_2_, bf16[64,1024]{1,0:T(8,128)(2,1)S(1)} %get-tuple-element.110.refs_1_, ...), custom_call_target="tpu_custom_call" | custom-call | bytes 9000000 | tf_op jit(solution)/shard_map/pallas_call | solution.py:72
  121.1 2.4 collective-permute-start.8
  124.4 11.0 %all-to-all-done.2.refs_9_ = bf16[16,128,512]{2,1,0:T(8,128)(2,1)} async-done(((bf16[16,128,512]{2,1,0:T(8,128)(2,1)}), bf16[16,128,512]{2,1,0:T(8,128)(2,1)}, u32[]{:S(2)}, u32[]{:S(2)}) %all-to-all-start.2) | async-done | bytes 2097184 | tf_op jit(solution)/shard_map/all_to_all | solution.py:545
  135.4 3.3 shard_map.199
  139.4 21.6 %all_to_all.47.refs_2_.refs_11_ = bf16[16,64,512]{2,1,0:T(8,128)(2,1)S(1)} all-to-all(bf16[16,64,512]{2,1,0:T(8,128)(2,1)} %get-tuple-element.118), channel_id=1, replica_groups=mesh['s'=2,'z'=4,'yl'=2,'yh'=2,'x'=4] {'z','yl','yh'}, dimensions={0} | all-to-all | bytes 2097152 | tf_op jit(solution)/shard_map/all_to_all | solution.py:545
  161.0 4.5 %shard_map.200 = (bf16[64,1024]{1,0:T(8,128)(2,1)S(1)}, f32[4,64,1024]{2,1,0:T(8,128)}, bf16[4,64,128]{2,1,0:T(8,128)(2,1)}) custom-call(s32[1]{0:T(128)} %bitcast.2.refs_0_, bf16[4,64,128]{2,1,0:T(8,128)(2,1)} %get-tuple-element.117.refs_1_.refs_10_, bf16[16,64,512]{2,1,0:T(8,128)(2,1)S(1)} %all_to_all.47.refs_2_.refs_11_, ...), custom_call_target="tpu_custom_call" | custom-call | bytes 9000000 | tf_op jit(solution)/shard_map/pallas_call | solution.py:72
  165.5 2.5 collective-permute-start.11
  169.7 2.1 collective-permute-done.11.refs_4_
  171.8 1.6 collective-permute-done.10.refs_3_
  173.4 5.0 %shard_map.201 = (bf16[64,1024]{1,0:T(8,128)(2,1)S(1)}, f32[64,1024]{1,0:T(8,128)}, bf16[64,1024]{1,0:T(8,128)(2,1)}, f32[4,64,256]{2,1,0:T(8,128)}, bf16[4,64,2...) custom-call(bf16[64,1024]{1,0:T(8,128)(2,1)S(1)} %get-tuple-element.116.refs_0_.refs_1_, ...), custom_call_target="tpu_custom_call" | custom-call | bytes 9000000 | tf_op jit(solution)/shard_map/pallas_call | solution.py:72
  179.1 2.7 collective-permute-start.15
  182.4 2.7 collective-permute-done.15.refs_5_
  185.1 2.1 collective-permute-done.14.refs_4_
  187.2 5.6 %shard_map.202 = (f32[64,1024]{1,0:T(8,128)}, bf16[64,1024]{1,0:T(8,128)(2,1)}, bf16[4,64,128]{2,1,0:T(8,128)(2,1)}, bf16[16,64,512]{2,1,0:T(8,128)(2,1)}, f32[8,1024]{1,0:T(8,128)}, /*index=5*/bf16[64,1024]{1,0:T(8,128)(2,1)}) custom-call(bf16[64,1024]{1,0:T(8,128)(2,1)S(1)} %dynamic-slice_bitcast_fusion.refs_9_.refs_0_.refs_1_, ...), custom_call_target="tpu_custom_call", output_to_operand_aliasing={{5}: (12, {})} | custom-call | bytes 9000000 | tf_op jit(solution)/shard_map/pallas_call | solution.py:72
  192.8 3.9 %shard_map.206 = (bf16[8,2,128,512]{3,2,1,0:T(8,128)(2,1)}, bf16[8,2,128,512]{3,2,1,0:T(8,128)(2,1)}, f32[4,256]{1,0:T(4,128)}, f32[1,1024]{1,0:T(1,128)}) custom-call(bf16[64,1024]{1,0:T(8,128)(2,1)} %get-tuple-element.133.refs_0_, bf16[64,1024]{1,0:T(8,128)(2,1)S(1)} %dynamic-slice_bitcast_fusion.refs_9_.refs_0_.refs_1_, ...), custom_call_target="tpu_custom_call" | custom-call | bytes 9000000 | tf_op jit(solution)/shard_map/pallas_call | solution.py:72
  196.7 3.8 %collective-permute-start.23 = (bf16[8,2,128,512]{3,2,1,0:T(8,128)(2,1)}, bf16[8,2,128,512]{3,2,1,0:T(8,128)(2,1)}, u32[]{:S(2)}, u32[]{:S(2)}) collective-permute-start(bf16[8,2,128,512]{3,2,1,0:T(8,128)(2,1)} %get-tuple-element.138), channel_id=1, source_target_pairs={{0,64},{64,0},{1,65},{65,1},{2,66},{66,2},{3,67},{67,3},{4,68},{68... | collective-permute-start | bytes 6291464 | tf_op jit(solution)/shard_map/ppermute | solution.py:536
  200.5 4.5 %all-to-all-start.4 = ((bf16[16,64,512]{2,1,0:T(8,128)(2,1)}), bf16[16,64,512]{2,1,0:T(8,128)(2,1)}, u32[]{:S(2)}, u32[]{:S(2)}) async-start(bf16[16,64,512]{2,1,0:T(8,128)(2,1)} %get-tuple-element.126), calls=%async_computation.4 | async-start | bytes 2097152 | tf_op jit(solution)/shard_map/all_to_all | solution.py:545
  205.0 1.8 collective-permute-start.18
  208.3 4.8 %collective-permute-done.18.refs_6_ = bf16[64,1024]{1,0:T(8,128)(2,1)S(1)} collective-permute-done((bf16[64,1024]{1,0:T(8,128)(2,1)S(1)}, bf16[64,1024]{1,0:T(8,128)(2,1)S(1)}, u32[]{:S(2)}, u32[]{:S(2)}) %collective-permute-start.18) | collective-permute-done | bytes 131104 | tf_op jit(solution)/shard_map/ppermute | solution.py:540
  218.5 2.0 all-to-all-done.4.refs_0_
  220.5 2.9 shard_map.205
  223.3 3.0 collective-permute-start.24
  226.3 1.7 collective-permute-start.22
  229.6 4.0 %shard_map.207.refs_10_ = bf16[16,128,512]{2,1,0:T(8,128)(2,1)} custom-call(bf16[8,2,128,512]{3,2,1,0:T(8,128)(2,1)} %get-tuple-element.137.refs_0_, bf16[8,2,128,512]{3,2,1,0:T(8,128)(2,1)} %collective-permute-done.23.refs_1_), custom_call_target="tpu_custom_call" | custom-call | bytes 9000000 | tf_op jit(solution)/shard_map/pallas_call | solution.py:72
  234.8 4.7 %shard_map.208 = (bf16[64,1024]{1,0:T(8,128)(2,1)S(1)}, bf16[4,64,256]{2,1,0:T(8,128)(2,1)}, bf16[64,1024]{1,0:T(8,128)(2,1)S(1)}, f32[8,1024]{1,0:T(8,128)}, bf...) custom-call(bf16[64,1024]{1,0:T(8,128)(2,1)S(1)} %get-tuple-element.116., ...), custom_call_target="tpu_custom_call", output_to_operand_aliasing={{4}: (10, {}), {5}: (11, {})} | custom-call | bytes 9000000 | tf_op jit(solution)/shard_map/pallas_call | solution.py:72
  239.5 4.5 %all-to-all-start.5 = ((bf16[16,128,512]{2,1,0:T(8,128)(2,1)}), bf16[16,128,512]{2,1,0:T(8,128)(2,1)}, u32[]{:S(2)}, u32[]{:S(2)}) async-start(bf16[16,128,512]{2,1,0:T(8,128)(2,1)} %get-tuple-element.146), calls=%async_computation.5 | async-start | bytes 4194304 | tf_op jit(solution)/shard_map/all_to_all | solution.py:545
  243.9 1.7 collective-permute-start.27
  245.6 1.6 collective-permute-start.26
  247.2 1.8 collective-permute-done.27.refs_5_
  249.0 1.9 collective-permute-done.26.refs_4_
  251.3 5.9 %shard_map.209 = (f32[64,1024]{1,0:T(8,128)}, bf16[64,1024]{1,0:T(8,128)(2,1)}, bf16[4,64,128]{2,1,0:T(8,128)(2,1)}, bf16[16,64,512]{2,1,0:T(8,128)(2,1)}, f32[8,1024]{1,0:T(8,128)}) custom-call(bf16[64,1024]{1,0:T(8,128)(2,1)S(1)} %get-tuple-element.140.refs_0_.refs_1_, f32[64,1024]{1,0:T(8,128)} %get-tuple-element.113.refs_0_.refs_1_, ...), custom_call_target="tpu_custom_call" | custom-call | bytes 9000000 | tf_op jit(solution)/shard_map/pallas_call | solution.py:72
  257.3 3.8 %shard_map.211 = (bf16[8,2,128,512]{3,2,1,0:T(8,128)(2,1)}, bf16[8,2,128,512]{3,2,1,0:T(8,128)(2,1)}, f32[4,256]{1,0:T(4,128)}, f32[1,1024]{1,0:T(1,128)}) custom-call(bf16[64,1024]{1,0:T(8,128)(2,1)} %get-tuple-element.149.refs_0_, bf16[64,1024]{1,0:T(8,128)(2,1)S(1)} %get-tuple-element.140.refs_0_.refs_1_, bf16[4,64,256]{2,1,0:T(8,128)(2,1)} %get-tuple-element.150.refs_2_, ...), custom_call_target="tpu_custom_call" | custom-call | bytes 9000000 | tf_op jit(solution)/shard_map/pallas_call | solution.py:72
  261.0 4.0 %collective-permute-start.28 = (bf16[8,2,128,512]{3,2,1,0:T(8,128)(2,1)}, bf16[8,2,128,512]{3,2,1,0:T(8,128)(2,1)}, u32[]{:S(2)}, u32[]{:S(2)}) collective-permute-start(bf16[8,2,128,512]{3,2,1,0:T(8,128)(2,1)} %get-tuple-element.153), channel_id=1, source_target_pairs={{0,64},{64,0},{1,65},{65,1},{2,66},{66,2},{3,67},{67,3},{4,68},{68... | collective-permute-start | bytes 6291464 | tf_op jit(solution)/shard_map/ppermute | solution.py:536
  265.0 3.0 shard_map.212
  270.4 5.7 %all-to-all-start.6 = ((bf16[16,64,512]{2,1,0:T(8,128)(2,1)}), bf16[16,64,512]{2,1,0:T(8,128)(2,1)}, u32[]{:S(2)}, u32[]{:S(2)}) async-start(bf16[16,64,512]{2,1,0:T(8,128)(2,1)} %get-tuple-element.147), calls=%async_computation.6 | async-start | bytes 2097152 | tf_op jit(solution)/shard_map/all_to_all | solution.py:545
  276.2 5.1 %shard_map.213.refs_4_ = bf16[16,128,768]{2,1,0:T(8,128)(2,1)} custom-call(bf16[8,2,128,512]{3,2,1,0:T(8,128)(2,1)} %get-tuple-element.152.refs_0_, bf16[8,2,128,512]{3,2,1,0:T(8,128)(2,1)} %collective-permute-done.28.refs_1_, bf16[8,2,128,256]{3,2,1,0:T(8,128)(2,1)} %get-tuple-element.158.refs_2_, bf16[8,2,128,256]{3,2,1,0:T(8,128)(2,1)} %collective-permute-done.29.refs_3_), custom_call_target="tpu_custom_call" | custom-call | bytes 9000000 | tf_op jit(solution)/shard_map/pallas_call | solution.py:72
  281.3 7.6 %all-to-all-done.6.refs_0_ = bf16[16,64,512]{2,1,0:T(8,128)(2,1)} async-done(((bf16[16,64,512]{2,1,0:T(8,128)(2,1)}), bf16[16,64,512]{2,1,0:T(8,128)(2,1)}, u32[]{:S(2)}, u32[]{:S(2)}) %all-to-all-start.6) | async-done | bytes 1048608 | tf_op jit(solution)/shard_map/all_to_all | solution.py:545
  289.0 2.9 shard_map.214
  292.5 5.2 %all-to-all-start.7 = ((bf16[16,128,768]{2,1,0:T(8,128)(2,1)}), bf16[16,128,768]{2,1,0:T(8,128)(2,1)S(1)}, u32[]{:S(2)}, u32[]{:S(2)}) async-start(bf16[16,128,768]{2,1,0:T(8,128)(2,1)} %get-tuple-element.178), calls=%async_computation.7 | async-start | bytes 6291456 | tf_op jit(solution)/shard_map/all_to_all | solution.py:545
  297.7 2.8 shard_map.215
  300.5 3.4 collective-permute-start.33
  303.9 1.7 collective-permute-start.32
  308.9 4.0 %collective-permute-done.32.refs_7_ = bf16[64,1024]{1,0:T(8,128)(2,1)S(1)} collective-permute-done((bf16[64,1024]{1,0:T(8,128)(2,1)}, bf16[64,1024]{1,0:T(8,128)(2,1)S(1)}, u32[]{:S(2)}, u32[]{:S(2)}) %collective-permute-start.32) | collective-permute-done | bytes 131104 | tf_op jit(solution)/shard_map/ppermute | solution.py:540
  315.3 3.1 shard_map.217
  318.5 15.9 %all-to-all-done.7.refs_1_ = bf16[16,128,768]{2,1,0:T(8,128)(2,1)S(1)} async-done(((bf16[16,128,768]{2,1,0:T(8,128)(2,1)}), bf16[16,128,768]{2,1,0:T(8,128)(2,1)S(1)}, u32[]{:S(2)}, u32[]{:S(2)}) %all-to-all-start.7) | async-done | bytes 3145760 | tf_op jit(solution)/shard_map/all_to_all | solution.py:545
  334.4 1.6 copy-done.2
  336.0 6.6 %all-to-all-start.8 = ((bf16[16,144,256]{2,1,0:T(8,128)(2,1)}), bf16[16,144,256]{2,1,0:T(8,128)(2,1)S(1)}, u32[]{:S(2)}, u32[]{:S(2)}) async-start(bf16[16,144,256]{2,1,0:T(8,128)(2,1)} %get-tuple-element.182), calls=%async_computation.8 | async-start | bytes 2359296 | tf_op jit(solution)/shard_map/all_to_all | solution.py:545
  342.7 3.9 %collective-permute-start.34 = (bf16[64,1024]{1,0:T(8,128)(2,1)S(1)}, bf16[64,1024]{1,0:T(8,128)(2,1)S(1)}, u32[]{:S(2)}, u32[]{:S(2)}) collective-permute-start(bf16[64,1024]{1,0:T(8,128)(2,1)S(1)} %get-tuple-element.177), channel_id=1, source_target_pairs={{0,64},{64,0},{1,65},{65,1},{2,66},{66,2},{3,67},{67,3},{4,68},{68... | collective-permute-start | bytes 393224 | tf_op jit(solution)/shard_map/ppermute | solution.py:536
  347.6 3.1 collective-permute-start.35
  350.8 1.9 copy-done.3
  352.7 2.4 shard_map.220
  356.1 7.6 %collective-permute-start.37 = (f32[136,256]{1,0:T(8,128)S(1)}, f32[136,256]{1,0:T(8,128)S(1)}, u32[]{:S(2)}, u32[]{:S(2)}) collective-permute-start(f32[136,256]{1,0:T(8,128)S(1)} %get-tuple-element.185), channel_id=1, source_target_pairs={{0,64},{64,0},{1,65},{65,1},{2,66},{66,2},{3,67},{67,3},{4,68},{68... | collective-permute-start | bytes 417800 | tf_op jit(solution)/shard_map/ppermute | solution.py:536
  (86 shorter events, 32.5 us)
Async XLA Ops:
  0.6 44.1 %copy-start = (bf16[2,1,128,1024]{3,2,1,0:T(8,128)(2,1)S(1)}, bf16[2,1,128,1024]{3,2,1,0:T(8,128)(2,1)}, u32[]{:S(2)}) copy-start(bf16[2,1,128,1024]{3,2,1,0:T(8,128)(2,1)} %param.11) | copy-start | bytes 1572868
  2.1 2.6 collective-permute-start
  42.7 6.1 %collective-permute-start.1 = (bf16[8,2,272,256]{3,2,1,0:T(8,128)(2,1)S(1)}, bf16[8,2,272,256]{3,2,1,0:T(8,128)(2,1)}, u32[]{:S(2)}, u32[]{:S(2)}) collective-permute-start(bf16[8,2,272,256]{3,2,1,0:T(8,128)(2,1)S(1)} %bitcast.37), channel_id=1, source_target_pairs={{0,64},{64,0},{1,65},{65,1},{2,66},{66,2},{3,67},{67,3},{4,68},{68... | collective-permute-start | bytes 6684680 | tf_op jit(solution)/shard_map/ppermute | solution.py:536
  95.2 21.4 %collective-permute-start.5 = (bf16[16,192,512]{2,1,0:T(8,128)(2,1)}, bf16[16,192,512]{2,1,0:T(8,128)(2,1)}, u32[]{:S(2)}, u32[]{:S(2)}) collective-permute-start(bf16[16,192,512]{2,1,0:T(8,128)(2,1)} %all_to_all.46.refs_2_.refs_11_), channel_id=1, source_target_pairs={{0,64},{64,0},{1,65},{65,1},{2,66},{66,2},{3,67},{67,3},{4,68},{68... | collective-permute-start | bytes 9437192 | tf_op jit(solution)/shard_map/ppermute | solution.py:536
  102.5 32.8 %all-to-all-start.2 = ((bf16[16,128,512]{2,1,0:T(8,128)(2,1)}), bf16[16,128,512]{2,1,0:T(8,128)(2,1)}, u32[]{:S(2)}, u32[]{:S(2)}) async-start(bf16[16,128,512]{2,1,0:T(8,128)(2,1)} %get-tuple-element.115), calls=%async_computation.2 | async-start | bytes 4194304 | tf_op jit(solution)/shard_map/all_to_all | solution.py:545
  107.0 8.2 %collective-permute-start.4 = (bf16[64,1024]{1,0:T(8,128)(2,1)S(1)}, bf16[64,1024]{1,0:T(8,128)(2,1)S(1)}, u32[]{:S(2)}, u32[]{:S(2)}) collective-permute-start(bf16[64,1024]{1,0:T(8,128)(2,1)S(1)} %get-tuple-element.110.refs_1_), channel_id=1, source_target_pairs={{0,3},{1,2},{2,1},{3,0},{4,7},{5,6},{6,5},{7,4},{8,11},{9,10},{10,... | collective-permute-start | bytes 393224 | tf_op jit(solution)/shard_map/ppermute | solution.py:540
  109.5 6.4 %collective-permute-start.3 = (bf16[64,1024]{1,0:T(8,128)(2,1)S(1)}, bf16[64,1024]{1,0:T(8,128)(2,1)S(1)}, u32[]{:S(2)}, u32[]{:S(2)}) collective-permute-start(bf16[64,1024]{1,0:T(8,128)(2,1)S(1)} %get-tuple-element.110.refs_1_), channel_id=1, source_target_pairs={{0,2},{1,3},{2,0},{3,1},{4,6},{5,7},{6,4},{7,5},{8,10},{9,11},{10,... | collective-permute-start | bytes 393224 | tf_op jit(solution)/shard_map/ppermute | solution.py:540
  110.0 6.6 %collective-permute-start.2 = (bf16[64,1024]{1,0:T(8,128)(2,1)S(1)}, bf16[64,1024]{1,0:T(8,128)(2,1)S(1)}, u32[]{:S(2)}, u32[]{:S(2)}) collective-permute-start(bf16[64,1024]{1,0:T(8,128)(2,1)S(1)} %get-tuple-element.110.refs_1_), channel_id=1, source_target_pairs={{0,1},{1,0},{2,3},{3,2},{4,5},{5,4},{6,7},{7,6},{8,9},{9,8},{10,11... | collective-permute-start | bytes 393224 | tf_op jit(solution)/shard_map/ppermute | solution.py:540
  121.1 14.2 %collective-permute-start.8 = (bf16[64,1024]{1,0:T(8,128)(2,1)S(1)}, bf16[64,1024]{1,0:T(8,128)(2,1)S(1)}, u32[]{:S(2)}, u32[]{:S(2)}) collective-permute-start(bf16[64,1024]{1,0:T(8,128)(2,1)S(1)} %get-tuple-element.114.refs_1_), channel_id=1, source_target_pairs={{0,3},{1,2},{2,1},{3,0},{4,7},{5,6},{6,5},{7,4},{8,11},{9,10},{10,... | collective-permute-start | bytes 393224 | tf_op jit(solution)/shard_map/ppermute | solution.py:540
  123.6 11.8 %collective-permute-start.7 = (bf16[64,1024]{1,0:T(8,128)(2,1)S(1)}, bf16[64,1024]{1,0:T(8,128)(2,1)S(1)}, u32[]{:S(2)}, u32[]{:S(2)}) collective-permute-start(bf16[64,1024]{1,0:T(8,128)(2,1)S(1)} %get-tuple-element.114.refs_1_), channel_id=1, source_target_pairs={{0,2},{1,3},{2,0},{3,1},{4,6},{5,7},{6,4},{7,5},{8,10},{9,11},{10,... | collective-permute-start | bytes 393224 | tf_op jit(solution)/shard_map/ppermute | solution.py:540
  124.1 11.3 %collective-permute-start.6 = (bf16[64,1024]{1,0:T(8,128)(2,1)S(1)}, bf16[64,1024]{1,0:T(8,128)(2,1)S(1)}, u32[]{:S(2)}, u32[]{:S(2)}) collective-permute-start(bf16[64,1024]{1,0:T(8,128)(2,1)S(1)} %get-tuple-element.114.refs_1_), channel_id=1, source_target_pairs={{0,1},{1,0},{2,3},{3,2},{4,5},{5,4},{6,7},{7,6},{8,9},{9,8},{10,11... | collective-permute-start | bytes 393224 | tf_op jit(solution)/shard_map/ppermute | solution.py:540
  138.7 34.7 %collective-permute-start.12 = (bf16[8,2,128,512]{3,2,1,0:T(8,128)(2,1)}, bf16[8,2,128,512]{3,2,1,0:T(8,128)(2,1)S(1)}, u32[]{:S(2)}, u32[]{:S(2)}) collective-permute-start(bf16[8,2,128,512]{3,2,1,0:T(8,128)(2,1)} %bitcast.16.refs_7_), channel_id=1, source_target_pairs={{0,64},{64,0},{1,65},{65,1},{2,66},{66,2},{3,67},{67,3},{4,68},{68... | collective-permute-start | bytes 6291464 | tf_op jit(solution)/shard_map/ppermute | solution.py:536
  165.5 6.3 %collective-permute-start.11 = (bf16[64,1024]{1,0:T(8,128)(2,1)S(1)}, bf16[64,1024]{1,0:T(8,128)(2,1)S(1)}, u32[]{:S(2)}, u32[]{:S(2)}) collective-permute-start(bf16[64,1024]{1,0:T(8,128)(2,1)S(1)} %get-tuple-element.119.refs_1_), channel_id=1, source_target_pairs={{0,3},{1,2},{2,1},{3,0},{4,7},{5,6},{6,5},{7,4},{8,11},{9,10},{10,... | collective-permute-start | bytes 393224 | tf_op jit(solution)/shard_map/ppermute | solution.py:540
  167.9 5.4 %collective-permute-start.10 = (bf16[64,1024]{1,0:T(8,128)(2,1)S(1)}, bf16[64,1024]{1,0:T(8,128)(2,1)S(1)}, u32[]{:S(2)}, u32[]{:S(2)}) collective-permute-start(bf16[64,1024]{1,0:T(8,128)(2,1)S(1)} %get-tuple-element.119.refs_1_), channel_id=1, source_target_pairs={{0,2},{1,3},{2,0},{3,1},{4,6},{5,7},{6,4},{7,5},{8,10},{9,11},{10,... | collective-permute-start | bytes 393224 | tf_op jit(solution)/shard_map/ppermute | solution.py:540
  168.4 5.0 %collective-permute-start.9 = (bf16[64,1024]{1,0:T(8,128)(2,1)S(1)}, bf16[64,1024]{1,0:T(8,128)(2,1)S(1)}, u32[]{:S(2)}, u32[]{:S(2)}) collective-permute-start(bf16[64,1024]{1,0:T(8,128)(2,1)S(1)} %get-tuple-element.119.refs_1_), channel_id=1, source_target_pairs={{0,1},{1,0},{2,3},{3,2},{4,5},{5,4},{6,7},{7,6},{8,9},{9,8},{10,11... | collective-permute-start | bytes 393224 | tf_op jit(solution)/shard_map/ppermute | solution.py:540
  178.4 0.6 copy-start.10
  179.1 6.1 %collective-permute-start.15 = (bf16[64,1024]{1,0:T(8,128)(2,1)S(1)}, bf16[64,1024]{1,0:T(8,128)(2,1)S(1)}, u32[]{:S(2)}, u32[]{:S(2)}) collective-permute-start(bf16[64,1024]{1,0:T(8,128)(2,1)S(1)} %get-tuple-element.122.refs_2_), channel_id=1, source_target_pairs={{0,3},{1,2},{2,1},{3,0},{4,7},{5,6},{6,5},{7,4},{8,11},{9,10},{10,... | collective-permute-start | bytes 393224 | tf_op jit(solution)/shard_map/ppermute | solution.py:540
  181.8 5.4 %collective-permute-start.14 = (bf16[64,1024]{1,0:T(8,128)(2,1)S(1)}, bf16[64,1024]{1,0:T(8,128)(2,1)S(1)}, u32[]{:S(2)}, u32[]{:S(2)}) collective-permute-start(bf16[64,1024]{1,0:T(8,128)(2,1)S(1)} %get-tuple-element.122.refs_2_), channel_id=1, source_target_pairs={{0,2},{1,3},{2,0},{3,1},{4,6},{5,7},{6,4},{7,5},{8,10},{9,11},{10,... | collective-permute-start | bytes 393224 | tf_op jit(solution)/shard_map/ppermute | solution.py:540
  181.8 5.4 %collective-permute-start.13 = (bf16[64,1024]{1,0:T(8,128)(2,1)S(1)}, bf16[64,1024]{1,0:T(8,128)(2,1)S(1)}, u32[]{:S(2)}, u32[]{:S(2)}) collective-permute-start(bf16[64,1024]{1,0:T(8,128)(2,1)S(1)} %get-tuple-element.122.refs_2_), channel_id=1, source_target_pairs={{0,1},{1,0},{2,3},{3,2},{4,5},{5,4},{6,7},{7,6},{8,9},{9,8},{10,11... | collective-permute-start | bytes 393224 | tf_op jit(solution)/shard_map/ppermute | solution.py:540
  192.8 12.2 %copy-start.11 = (bf16[64,1024]{1,0:T(8,128)(2,1)S(1)}, bf16[64,1024]{1,0:T(8,128)(2,1)}, u32[]{:S(2)}) copy-start(bf16[64,1024]{1,0:T(8,128)(2,1)} %get-tuple-element.128.refs_3_) | copy-start | bytes 393220
  196.7 32.9 %collective-permute-start.23 = (bf16[8,2,128,512]{3,2,1,0:T(8,128)(2,1)}, bf16[8,2,128,512]{3,2,1,0:T(8,128)(2,1)}, u32[]{:S(2)}, u32[]{:S(2)}) collective-permute-start(bf16[8,2,128,512]{3,2,1,0:T(8,128)(2,1)} %get-tuple-element.138), channel_id=1, source_target_pairs={{0,64},{64,0},{1,65},{65,1},{2,66},{66,2},{3,67},{67,3},{4,68},{68... | collective-permute-start | bytes 6291464 | tf_op jit(solution)/shard_map/ppermute | solution.py:536
  200.5 20.0 %all-to-all-start.4 = ((bf16[16,64,512]{2,1,0:T(8,128)(2,1)}), bf16[16,64,512]{2,1,0:T(8,128)(2,1)}, u32[]{:S(2)}, u32[]{:S(2)}) async-start(bf16[16,64,512]{2,1,0:T(8,128)(2,1)} %get-tuple-element.126), calls=%async_computation.4 | async-start | bytes 2097152 | tf_op jit(solution)/shard_map/all_to_all | solution.py:545
  205.0 8.1 %collective-permute-start.18 = (bf16[64,1024]{1,0:T(8,128)(2,1)S(1)}, bf16[64,1024]{1,0:T(8,128)(2,1)S(1)}, u32[]{:S(2)}, u32[]{:S(2)}) collective-permute-start(bf16[64,1024]{1,0:T(8,128)(2,1)S(1)} %copy-done.11), channel_id=1, source_target_pairs={{0,3},{1,2},{2,1},{3,0},{4,7},{5,6},{6,5},{7,4},{8,11},{9,10},{10,... | collective-permute-start | bytes 393224 | tf_op jit(solution)/shard_map/ppermute | solution.py:540
  206.8 6.4 %collective-permute-start.17 = (bf16[64,1024]{1,0:T(8,128)(2,1)S(1)}, bf16[64,1024]{1,0:T(8,128)(2,1)S(1)}, u32[]{:S(2)}, u32[]{:S(2)}) collective-permute-start(bf16[64,1024]{1,0:T(8,128)(2,1)S(1)} %copy-done.11), channel_id=1, source_target_pairs={{0,2},{1,3},{2,0},{3,1},{4,6},{5,7},{6,4},{7,5},{8,10},{9,11},{10,... | collective-permute-start | bytes 393224 | tf_op jit(solution)/shard_map/ppermute | solution.py:540
  207.1 7.3 %collective-permute-start.16 = (bf16[64,1024]{1,0:T(8,128)(2,1)S(1)}, bf16[64,1024]{1,0:T(8,128)(2,1)S(1)}, u32[]{:S(2)}, u32[]{:S(2)}) collective-permute-start(bf16[64,1024]{1,0:T(8,128)(2,1)S(1)} %copy-done.11), channel_id=1, source_target_pairs={{0,1},{1,0},{2,3},{3,2},{4,5},{5,4},{6,7},{7,6},{8,9},{9,8},{10,11... | collective-permute-start | bytes 393224 | tf_op jit(solution)/shard_map/ppermute | solution.py:540
  215.5 2.3 collective-permute-start.19
  217.8 0.7 copy-start.4
  223.3 10.7 %collective-permute-start.24 = (bf16[2,64,1024]{2,1,0:T(8,128)(2,1)}, bf16[2,64,1024]{2,1,0:T(8,128)(2,1)S(1)}, u32[]{:S(2)}, u32[]{:S(2)}) collective-permute-start(bf16[2,64,1024]{2,1,0:T(8,128)(2,1)} %get-tuple-element.139.refs_1_), channel_id=1, source_target_pairs={{0,4},{4,0},{1,5},{5,1},{2,6},{6,2},{3,7},{7,3},{8,12},{12,8},{9,1... | collective-permute-start | bytes 786440 | tf_op jit(solution)/shard_map/ppermute | solution.py:553
  226.3 7.3 %collective-permute-start.22 = (bf16[64,1024]{1,0:T(8,128)(2,1)S(1)}, bf16[64,1024]{1,0:T(8,128)(2,1)S(1)}, u32[]{:S(2)}, u32[]{:S(2)}) collective-permute-start(bf16[64,1024]{1,0:T(8,128)(2,1)S(1)} %get-tuple-element.131.refs_2_), channel_id=1, source_target_pairs={{0,3},{1,2},{2,1},{3,0},{4,7},{5,6},{6,5},{7,4},{8,11},{9,10},{10,... | collective-permute-start | bytes 393224 | tf_op jit(solution)/shard_map/ppermute | solution.py:540
  228.0 5.6 %collective-permute-start.21 = (bf16[64,1024]{1,0:T(8,128)(2,1)S(1)}, bf16[64,1024]{1,0:T(8,128)(2,1)S(1)}, u32[]{:S(2)}, u32[]{:S(2)}) collective-permute-start(bf16[64,1024]{1,0:T(8,128)(2,1)S(1)} %get-tuple-element.131.refs_2_), channel_id=1, source_target_pairs={{0,2},{1,3},{2,0},{3,1},{4,6},{5,7},{6,4},{7,5},{8,10},{9,11},{10,... | collective-permute-start | bytes 393224 | tf_op jit(solution)/shard_map/ppermute | solution.py:540
  229.0 5.1 %collective-permute-start.20 = (bf16[64,1024]{1,0:T(8,128)(2,1)S(1)}, bf16[64,1024]{1,0:T(8,128)(2,1)S(1)}, u32[]{:S(2)}, u32[]{:S(2)}) collective-permute-start(bf16[64,1024]{1,0:T(8,128)(2,1)S(1)} %get-tuple-element.131.refs_2_), channel_id=1, source_target_pairs={{0,1},{1,0},{2,3},{3,2},{4,5},{5,4},{6,7},{7,6},{8,9},{9,8},{10,11... | collective-permute-start | bytes 393224 | tf_op jit(solution)/shard_map/ppermute | solution.py:540
  234.1 0.7 copy-start.8
  239.5 17.8 %copy-start.6 = (bf16[64,1024]{1,0:T(8,128)(2,1)}, bf16[64,1024]{1,0:T(8,128)(2,1)S(1)}, u32[]{:S(2)}) copy-start(bf16[64,1024]{1,0:T(8,128)(2,1)S(1)} %get-tuple-element.140.refs_0_.refs_1_) | copy-start | bytes 393220
  239.5 29.7 %all-to-all-start.5 = ((bf16[16,128,512]{2,1,0:T(8,128)(2,1)}), bf16[16,128,512]{2,1,0:T(8,128)(2,1)}, u32[]{:S(2)}, u32[]{:S(2)}) async-start(bf16[16,128,512]{2,1,0:T(8,128)(2,1)} %get-tuple-element.146), calls=%async_computation.5 | async-start | bytes 4194304 | tf_op jit(solution)/shard_map/all_to_all | solution.py:545
  243.9 5.1 %collective-permute-start.27 = (bf16[64,1024]{1,0:T(8,128)(2,1)S(1)}, bf16[64,1024]{1,0:T(8,128)(2,1)S(1)}, u32[]{:S(2)}, u32[]{:S(2)}) collective-permute-start(bf16[64,1024]{1,0:T(8,128)(2,1)S(1)} %get-tuple-element.141.refs_2_), channel_id=1, source_target_pairs={{0,3},{1,2},{2,1},{3,0},{4,7},{5,6},{6,5},{7,4},{8,11},{9,10},{10,... | collective-permute-start | bytes 393224 | tf_op jit(solution)/shard_map/ppermute | solution.py:540
  245.6 5.3 %collective-permute-start.26 = (bf16[64,1024]{1,0:T(8,128)(2,1)S(1)}, bf16[64,1024]{1,0:T(8,128)(2,1)S(1)}, u32[]{:S(2)}, u32[]{:S(2)}) collective-permute-start(bf16[64,1024]{1,0:T(8,128)(2,1)S(1)} %get-tuple-element.141.refs_2_), channel_id=1, source_target_pairs={{0,2},{1,3},{2,0},{3,1},{4,6},{5,7},{6,4},{7,5},{8,10},{9,11},{10,... | collective-permute-start | bytes 393224 | tf_op jit(solution)/shard_map/ppermute | solution.py:540
  247.1 4.2 %collective-permute-start.25 = (bf16[64,1024]{1,0:T(8,128)(2,1)S(1)}, bf16[64,1024]{1,0:T(8,128)(2,1)S(1)}, u32[]{:S(2)}, u32[]{:S(2)}) collective-permute-start(bf16[64,1024]{1,0:T(8,128)(2,1)S(1)} %get-tuple-element.141.refs_2_), channel_id=1, source_target_pairs={{0,1},{1,0},{2,3},{3,2},{4,5},{5,4},{6,7},{7,6},{8,9},{9,8},{10,11... | collective-permute-start | bytes 393224 | tf_op jit(solution)/shard_map/ppermute | solution.py:540
  261.0 15.1 %collective-permute-start.28 = (bf16[8,2,128,512]{3,2,1,0:T(8,128)(2,1)}, bf16[8,2,128,512]{3,2,1,0:T(8,128)(2,1)}, u32[]{:S(2)}, u32[]{:S(2)}) collective-permute-start(bf16[8,2,128,512]{3,2,1,0:T(8,128)(2,1)} %get-tuple-element.153), channel_id=1, source_target_pairs={{0,64},{64,0},{1,65},{65,1},{2,66},{66,2},{3,67},{67,3},{4,68},{68... | collective-permute-start | bytes 6291464 | tf_op jit(solution)/shard_map/ppermute | solution.py:536
  268.0 8.1 %collective-permute-start.29 = (bf16[8,2,128,256]{3,2,1,0:T(8,128)(2,1)}, bf16[8,2,128,256]{3,2,1,0:T(8,128)(2,1)}, u32[]{:S(2)}, u32[]{:S(2)}) collective-permute-start(bf16[8,2,128,256]{3,2,1,0:T(8,128)(2,1)} %get-tuple-element.159), channel_id=1, source_target_pairs={{0,64},{64,0},{1,65},{65,1},{2,66},{66,2},{3,67},{67,3},{4,68},{68... | collective-permute-start | bytes 3145736 | tf_op jit(solution)/shard_map/ppermute | solution.py:536
  270.4 18.5 %all-to-all-start.6 = ((bf16[16,64,512]{2,1,0:T(8,128)(2,1)}), bf16[16,64,512]{2,1,0:T(8,128)(2,1)}, u32[]{:S(2)}, u32[]{:S(2)}) async-start(bf16[16,64,512]{2,1,0:T(8,128)(2,1)} %get-tuple-element.147), calls=%async_computation.6 | async-start | bytes 2097152 | tf_op jit(solution)/shard_map/all_to_all | solution.py:545
  291.8 0.7 copy-start.12
  291.8 15.3 %copy-start.5 = (bf16[2,64,1024]{2,1,0:T(8,128)(2,1)S(1)}, bf16[2,64,1024]{2,1,0:T(8,128)(2,1)}, u32[]{:S(2)}) copy-start(bf16[2,64,1024]{2,1,0:T(8,128)(2,1)} %get-tuple-element.139.refs_1_) | copy-start | bytes 786436
  292.5 41.9 %all-to-all-start.7 = ((bf16[16,128,768]{2,1,0:T(8,128)(2,1)}), bf16[16,128,768]{2,1,0:T(8,128)(2,1)S(1)}, u32[]{:S(2)}, u32[]{:S(2)}) async-start(bf16[16,128,768]{2,1,0:T(8,128)(2,1)} %get-tuple-element.178), calls=%async_computation.7 | async-start | bytes 6291456 | tf_op jit(solution)/shard_map/all_to_all | solution.py:545
  300.5 13.1 %collective-permute-start.33 = (bf16[8,2,128,256]{3,2,1,0:T(8,128)(2,1)S(1)}, bf16[8,2,128,256]{3,2,1,0:T(8,128)(2,1)S(1)}, u32[]{:S(2)}, u32[]{:S(2)}) collective-permute-start(bf16[8,2,128,256]{3,2,1,0:T(8,128)(2,1)S(1)} %get-tuple-element.166), channel_id=1, source_target_pairs={{0,64},{64,0},{1,65},{65,1},{2,66},{66,2},{3,67},{67,3},{4,68},{68... | collective-permute-start | bytes 3145736 | tf_op jit(solution)/shard_map/ppermute | solution.py:536
  303.9 9.1 %collective-permute-start.32 = (bf16[64,1024]{1,0:T(8,128)(2,1)}, bf16[64,1024]{1,0:T(8,128)(2,1)S(1)}, u32[]{:S(2)}, u32[]{:S(2)}) collective-permute-start(bf16[64,1024]{1,0:T(8,128)(2,1)} %copy-done.12), channel_id=1, source_target_pairs={{0,3},{1,2},{2,1},{3,0},{4,7},{5,6},{6,5},{7,4},{8,11},{9,10},{10,... | collective-permute-start | bytes 393224 | tf_op jit(solution)/shard_map/ppermute | solution.py:540
  305.5 7.4 %collective-permute-start.31 = (bf16[64,1024]{1,0:T(8,128)(2,1)}, bf16[64,1024]{1,0:T(8,128)(2,1)S(1)}, u32[]{:S(2)}, u32[]{:S(2)}) collective-permute-start(bf16[64,1024]{1,0:T(8,128)(2,1)} %copy-done.12), channel_id=1, source_target_pairs={{0,2},{1,3},{2,0},{3,1},{4,6},{5,7},{6,4},{7,5},{8,10},{9,11},{10,... | collective-permute-start | bytes 393224 | tf_op jit(solution)/shard_map/ppermute | solution.py:540
  306.8 6.7 %collective-permute-start.30 = (bf16[64,1024]{1,0:T(8,128)(2,1)}, bf16[64,1024]{1,0:T(8,128)(2,1)S(1)}, u32[]{:S(2)}, u32[]{:S(2)}) collective-permute-start(bf16[64,1024]{1,0:T(8,128)(2,1)} %copy-done.12), channel_id=1, source_target_pairs={{0,1},{1,0},{2,3},{3,2},{4,5},{5,4},{6,7},{7,6},{8,9},{9,8},{10,11... | collective-permute-start | bytes 393224 | tf_op jit(solution)/shard_map/ppermute | solution.py:540
  307.1 1.0 copy-start.9
  313.5 0.9 copy-start.7
  314.4 0.9 copy-start.13
  334.4 1.6 copy-start.2
  336.0 19.9 %all-to-all-start.8 = ((bf16[16,144,256]{2,1,0:T(8,128)(2,1)}), bf16[16,144,256]{2,1,0:T(8,128)(2,1)S(1)}, u32[]{:S(2)}, u32[]{:S(2)}) async-start(bf16[16,144,256]{2,1,0:T(8,128)(2,1)} %get-tuple-element.182), calls=%async_computation.8 | async-start | bytes 2359296 | tf_op jit(solution)/shard_map/all_to_all | solution.py:545
  342.7 4.9 %collective-permute-start.34 = (bf16[64,1024]{1,0:T(8,128)(2,1)S(1)}, bf16[64,1024]{1,0:T(8,128)(2,1)S(1)}, u32[]{:S(2)}, u32[]{:S(2)}) collective-permute-start(bf16[64,1024]{1,0:T(8,128)(2,1)S(1)} %get-tuple-element.177), channel_id=1, source_target_pairs={{0,64},{64,0},{1,65},{65,1},{2,66},{66,2},{3,67},{67,3},{4,68},{68... | collective-permute-start | bytes 393224 | tf_op jit(solution)/shard_map/ppermute | solution.py:536
  347.6 16.1 %collective-permute-start.35 = (bf16[2,64,1024]{2,1,0:T(8,128)(2,1)S(1)}, bf16[2,64,1024]{2,1,0:T(8,128)(2,1)S(1)}, u32[]{:S(2)}, u32[]{:S(2)}) collective-permute-start(bf16[2,64,1024]{2,1,0:T(8,128)(2,1)S(1)} %shard_map.218.refs_1_), channel_id=1, source_target_pairs={{0,4},{4,0},{1,5},{5,1},{2,6},{6,2},{3,7},{7,3},{8,12},{12,8},{9,1... | collective-permute-start | bytes 786440 | tf_op jit(solution)/shard_map/ppermute | solution.py:553
  350.8 1.9 copy-start.3
  352.7 13.2 %copy-start.1 = (bf16[2,1,128,1024]{3,2,1,0:T(8,128)(2,1)S(1)}, bf16[2,1,128,1024]{3,2,1,0:T(8,128)(2,1)}, u32[]{:S(2)}) copy-start(bf16[2,1,128,1024]{3,2,1,0:T(8,128)(2,1)} %param.11) | copy-start | bytes 1572868
  355.1 9.7 %collective-permute-start.36 = (f32[128,512]{1,0:T(8,128)S(1)}, f32[128,512]{1,0:T(8,128)S(1)}, u32[]{:S(2)}, u32[]{:S(2)}) collective-permute-start(f32[128,512]{1,0:T(8,128)S(1)} %get-tuple-element.181), channel_id=1, source_target_pairs={{0,64},{64,0},{1,65},{65,1},{2,66},{66,2},{3,67},{67,3},{4,68},{68... | collective-permute-start | bytes 786440 | tf_op jit(solution)/shard_map/ppermute | solution.py:536
  356.1 8.6 %collective-permute-start.37 = (f32[136,256]{1,0:T(8,128)S(1)}, f32[136,256]{1,0:T(8,128)S(1)}, u32[]{:S(2)}, u32[]{:S(2)}) collective-permute-start(f32[136,256]{1,0:T(8,128)S(1)} %get-tuple-element.185), channel_id=1, source_target_pairs={{0,64},{64,0},{1,65},{65,1},{2,66},{66,2},{3,67},{67,3},{4,68},{68... | collective-permute-start | bytes 417800 | tf_op jit(solution)/shard_map/ppermute | solution.py:536

commit v7 on v6

--- a/solution.py
+++ b/solution.py
@@ -32,9 +32,7 @@
 
 def call(kernel, outs, ins, us=3, through=(), after=None):
     n, m, k = len(ins), len(outs), len(through)
-    if after is not None:
-        ins = [*ins, (after, (16 if after.dtype == BF else 8, 128), (0, 0))]
-    e = len(ins)
+    e = n + (after is not None)
     held = [i for i, o in enumerate(outs) if isinstance(o, tuple)]
     outs = [o[1] if isinstance(o, tuple) else o for o in outs]
     specs, arrays = [], []
@@ -61,6 +59,9 @@
                 )
             )
         arrays.append(array)
+    if after is not None:
+        specs.append(pl.BlockSpec(memory_space=pl.ANY))
+        arrays.append(after)
     out_specs = [
         pl.BlockSpec(o.shape, functools.partial(lambda n, i: (0,) * n, len(o.shape)))
         for o in outs
@@ -394,8 +395,7 @@
 def add_into(msg, at, gm, gr):
     for i in range(8):
         for j in range(2):
-            both = gm[i, j].astype(F32) + gr[i, j].astype(F32)
-            msg[2 * i + j, 0:128, at : at + gm.shape[3]] = both.astype(BF)
+            msg[2 * i + j, 0:128, at : at + gm.shape[3]] = gm[i, j] + gr[i, j]
 
 
 def add_kernel(gm, gr, msg):
@@ -621,7 +621,7 @@
     part, prob1, att1 = call(attend_kernel, attend_outs, [(first, None, None), q1, kv1, am[1], ao[1]])
     last_part, mid1, n21, pre1, act1, dpre1, back = call(
         turn_kernel,
-        feed_outs + [kept(4, ROWS, 256), sds(ROWS, D)],
+        [message(ROWS, D), *feed_outs[1:], kept(4, ROWS, 256), sds(ROWS, D)],
         [y0, *all_parts(part), lnp, bias, f1, f1o, cot],
     )
     backs = all_parts(back)
@@ -646,7 +646,7 @@
         [sds(ROWS, D), sds(ROWS, D)],
         [core, y0, mid1, *all_parts(last_part), lnp],
     )
-    (acts,) = call(pair_kernel, [sds(2, ROWS, D)], [core, keep, swap_cores(send)], us=1)
+    (acts,) = call(pair_kernel, [message(2, ROWS, D)], [core, keep, swap_cores(send)], us=1)
     project_outs = [kept(4, ROWS, 256), sds(ROWS, D), kept(4, 256, dtype=F32)]
     dproj1, part, gib1, acts = call(
         project_back_kernel, project_outs, [dkv, dq1, am[1], ao[1]], through=[acts]
@@ -655,11 +655,12 @@
     backs = all_parts(part)
     grad_attn_outs = [kept(8, 2, 128, 256), sds(8, 2, 128, 256)]
     (l1,) = call(add_kernel, [message(16, 128, 512)], [gfm1, gfr1])
-    dx1, dpre0, part, head1, l1, far = call(
+    dx1, dpre0, part, head1, l1 = call(
         hand_down_kernel,
-        [sds(ROWS, D), kept(4, ROWS, 256), sds(ROWS, D), rows_out],
+        [kept(ROWS, D), kept(4, ROWS, 256), sds(ROWS, D), rows_out],
         [y0, dmid1, *backs, lnp, pre0, f0, f0o],
-        through=[l1, far],
+        through=[l1],
+        after=far,
     )
     l1 = exchange(l1)
     backs = all_parts(part)
@@ -698,7 +699,9 @@
     (grads,) = call(pair_kernel, [sds(2, ROWS, D)], [core, keep, swap_cores(send)], us=1)
     (grads,) = call(line_up_kernel, [sds(2, 2 * ROWS, D)], [half, grads, other_half(grads)], us=1)
     f = functools.partial(sds, dtype=F32)
-    fk, send, at1 = call(settle_kernel, [f(128, 512), f(128, 512), f(128, 256)], [core, l0, l1])
+    fk, send, at1 = call(
+        settle_kernel, [f(128, 512), f(128, 512), f(128, 256)], [core, *[pltpu.with_memory_space_constraint(v, pltpu.HBM) for v in (l0, l1)]],
+    )
     fg = swap_cores(send)
     ak, send = call(settle_tail_kernel, [f(136, 256), f(136, 256)], [core, tail, at1])
     gq, go, gu, gd, gg, gs, gi, gb, gub = call(

time: 369 us -> 365 us (0.989)
  local copies, waits for them, and re-layouts: 9.94 us -> 0.94 us
  waiting for transfers between devices: 75.1 us -> 78.9 us
    unnamed x28 -> x8, local copies, waits for them, and re-layouts: 9.01 us -> 0.02 us
  transfers between devices with their start and end apart: 44 -> 44, of which waited for: 26 -> 27; matrix products, arithmetic and copies ran while one was open for 0% -> 0% of each run, Pallas kernels for 14% -> 15%
where the time goes in v7:
time: 365 us; the launch traced here: 363 us
  blocking collectives  101 us (28%)
  starting transfers between devices  95 us (26%)
  Pallas kernels  86.4 us (24%)
  waiting for transfers between devices  78.9 us (22%)
    all_to_all x3, blocking collectives, exchange(): return lax.all_to_all(v, axes, 0, 0, tiled=True)  101 us
    pallas_call x28, Pallas kernels, call(): pl.pallas_call(body, grid=(1,), out_shape=list(outs) + [pltpu.HBM(t.shape...  85 us
    all_to_all x6, waiting for transfers between devices, exchange(): return lax.all_to_all(v, axes, 0, 0, tiled=True)  40.8 us
    ppermute x12, starting transfers between devices, swap_cores(): return lax.ppermute(v, 's', [(0, 1), (1, 0)])  31.3 us
    all_to_all x6, starting transfers between devices, exchange(): return lax.all_to_all(v, axes, 0, 0, tiled=True)  31.2 us
    ppermute x24, waiting for transfers between devices, all_parts(): lax.ppermute(part, 'x', [(i, i ^ k) for i in range(4)])  30.7 us
    ppermute x24, starting transfers between devices, all_parts(): lax.ppermute(part, 'x', [(i, i ^ k) for i in range(4)])  26.3 us
    ppermute x12, waiting for transfers between devices, swap_cores(): return lax.ppermute(v, 's', [(0, 1), (1, 0)])  7.35 us
  transfers between devices with their start and end apart: 44, of which 27 were waited for; matrix products, arithmetic and copies ran while one was open for 0% of the time, Pallas kernels for 15%

profile of v7, /device:TPU:1, one launch (start us, length us, event | category | flops | bytes accessed | tf_op | source)
XLA Modules:
  0.0 362.8 jit_solution(1800705108316677036)
XLA Ops:
  0.7 1.4 shard_map.194
  2.1 1.5 collective-permute-start
  4.7 1.5 shard_map.195
  6.2 36.5 %all_to_all.45 = bf16[16,272,256]{2,1,0:T(8,128)(2,1)S(1)} all-to-all(bf16[16,272,256]{2,1,0:T(8,128)(2,1)} %get-tuple-element.104), channel_id=1, replica_groups=mesh['s'=2,'z'=4,'yl'=2,'yh'=2,'x'=4] {'z','yl','yh'}, dimensions={0} | all-to-all | bytes 4456448 | tf_op jit(solution)/shard_map/all_to_all | solution.py:545
  42.7 2.0 collective-permute-start.1
  44.8 4.1 %collective-permute-done.1.refs_3_.refs_4_.refs_8_ = bf16[8,2,272,256]{3,2,1,0:T(8,128)(2,1)} collective-permute-done((bf16[8,2,272,256]{3,2,1,0:T(8,128)(2,1)S(1)}, bf16[8,2,272,256]{3,2,1,0:T(8,128)(2,1)}, u32[]{:S(2)}, u32[]{:S(2)}) %collective-permute-start.1) | collective-permute-done | bytes 2228256 | tf_op jit(solution)/shard_map/ppermute | solution.py:536
  48.9 3.9 %shard_map.196 = (bf16[64,1024]{1,0:T(8,128)(2,1)}, bf16[4,64,128]{2,1,0:T(8,128)(2,1)}, bf16[16,192,512]{2,1,0:T(8,128)(2,1)}, f32[2,16,1024]{2,1,0:T(8,128)}, f32[2,16,256]{2,1,0:T(8,128)}) custom-call(bf16[64,1024]{1,0:T(8,128)(2,1)S(1)} %dynamic-slice_bitcast_fusion.1.refs_0_.refs_2_, bf16[8,2,272,256]{3,2,1,0:T(8,128)(2,1)S(1)} %bitcast.38, ...), custom_call_target="tpu_custom_call" | custom-call | bytes 9000000 | tf_op jit(solution)/shard_map/pallas_call | solution.py:73
  52.7 42.5 %all_to_all.46.refs_2_.refs_11_ = bf16[16,192,512]{2,1,0:T(8,128)(2,1)} all-to-all(bf16[16,192,512]{2,1,0:T(8,128)(2,1)} %get-tuple-element.107), channel_id=1, replica_groups=mesh['s'=2,'z'=4,'yl'=2,'yh'=2,'x'=4] {'z','yl','yh'}, dimensions={0} | all-to-all | bytes 6291456 | tf_op jit(solution)/shard_map/all_to_all | solution.py:545
  95.3 1.8 collective-permute-start.5
  97.1 5.6 %shard_map.197 = (bf16[64,1024]{1,0:T(8,128)(2,1)S(1)}, f32[4,64,1024]{2,1,0:T(8,128)}, bf16[4,64,128]{2,1,0:T(8,128)(2,1)}, bf16[16,128,512]{2,1,0:T(8,128)(2,1)}) custom-call(s32[1]{0:T(128)} %bitcast.2.refs_0_, bf16[4,64,128]{2,1,0:T(8,128)(2,1)} %get-tuple-element.106.refs_1_.refs_10_, bf16[16,192,512]{2,1,0:T(8,128)(2,1)} %all_to_all.46.refs_2_.refs_11_, ...), custom_call_target="tpu_custom_call" | custom-call | bytes 9000000 | tf_op jit(solution)/shard_map/pallas_call | solution.py:73
  102.7 4.4 %all-to-all-start.2 = ((bf16[16,128,512]{2,1,0:T(8,128)(2,1)}), bf16[16,128,512]{2,1,0:T(8,128)(2,1)}, u32[]{:S(2)}, u32[]{:S(2)}) async-start(bf16[16,128,512]{2,1,0:T(8,128)(2,1)} %get-tuple-element.114), calls=%async_computation.2 | async-start | bytes 4194304 | tf_op jit(solution)/shard_map/all_to_all | solution.py:545
  107.1 2.5 collective-permute-start.4
  110.4 4.8 %collective-permute-done.4.refs_4_ = bf16[64,1024]{1,0:T(8,128)(2,1)S(1)} collective-permute-done((bf16[64,1024]{1,0:T(8,128)(2,1)S(1)}, bf16[64,1024]{1,0:T(8,128)(2,1)S(1)}, u32[]{:S(2)}, u32[]{:S(2)}) %collective-permute-start.4) | collective-permute-done | bytes 131104 | tf_op jit(solution)/shard_map/ppermute | solution.py:540
  116.7 4.5 %shard_map.198 = (bf16[64,1024]{1,0:T(8,128)(2,1)S(1)}, f32[64,1024]{1,0:T(8,128)}, bf16[64,1024]{1,0:T(8,128)(2,1)}, f32[4,64,256]{2,1,0:T(8,128)}, bf16[4,64,256]{2,1,0:T(8,128)(2,1)}) custom-call(bf16[64,1024]{1,0:T(8,128)(2,1)S(1)} %dynamic-slice_bitcast_fusion.1.refs_0_.refs_2_, bf16[64,1024]{1,0:T(8,128)(2,1)S(1)} %get-tuple-element.109.refs_1_, ...), custom_call_target="tpu_custom_call" | custom-call | bytes 9000000 | tf_op jit(solution)/shard_map/pallas_call | solution.py:73
  121.2 2.4 collective-permute-start.8
  124.5 11.0 %all-to-all-done.2.refs_9_ = bf16[16,128,512]{2,1,0:T(8,128)(2,1)} async-done(((bf16[16,128,512]{2,1,0:T(8,128)(2,1)}), bf16[16,128,512]{2,1,0:T(8,128)(2,1)}, u32[]{:S(2)}, u32[]{:S(2)}) %all-to-all-start.2) | async-done | bytes 2097184 | tf_op jit(solution)/shard_map/all_to_all | solution.py:545
  135.5 3.3 shard_map.199
  139.6 21.5 %all_to_all.47.refs_2_.refs_11_ = bf16[16,64,512]{2,1,0:T(8,128)(2,1)S(1)} all-to-all(bf16[16,64,512]{2,1,0:T(8,128)(2,1)} %get-tuple-element.117), channel_id=1, replica_groups=mesh['s'=2,'z'=4,'yl'=2,'yh'=2,'x'=4] {'z','yl','yh'}, dimensions={0} | all-to-all | bytes 2097152 | tf_op jit(solution)/shard_map/all_to_all | solution.py:545
  161.1 4.5 %shard_map.200 = (bf16[64,1024]{1,0:T(8,128)(2,1)S(1)}, f32[4,64,1024]{2,1,0:T(8,128)}, bf16[4,64,128]{2,1,0:T(8,128)(2,1)}) custom-call(s32[1]{0:T(128)} %bitcast.2.refs_0_, bf16[4,64,128]{2,1,0:T(8,128)(2,1)} %get-tuple-element.116.refs_1_.refs_10_, bf16[16,64,512]{2,1,0:T(8,128)(2,1)S(1)} %all_to_all.47.refs_2_.refs_11_, ...), custom_call_target="tpu_custom_call" | custom-call | bytes 9000000 | tf_op jit(solution)/shard_map/pallas_call | solution.py:73
  165.6 2.4 collective-permute-start.11
  169.8 2.1 collective-permute-done.11.refs_4_
  171.8 1.6 collective-permute-done.10.refs_3_
  173.4 5.1 %shard_map.201 = (bf16[64,1024]{1,0:T(8,128)(2,1)}, f32[64,1024]{1,0:T(8,128)}, bf16[64,1024]{1,0:T(8,128)(2,1)}, f32[4,64,256]{2,1,0:T(8,128)}, bf16[4,64,256]{...) custom-call(bf16[64,1024]{1,0:T(8,128)(2,1)S(1)} %get-tuple-element.115.refs_0_.refs_1_, ...), custom_call_target="tpu_custom_call" | custom-call | bytes 9000000 | tf_op jit(solution)/shard_map/pallas_call | solution.py:73
  178.6 2.4 collective-permute-start.15
  181.8 2.5 collective-permute-done.15.refs_5_
  184.3 2.0 collective-permute-done.14.refs_4_
  186.3 5.6 %shard_map.202 = (f32[64,1024]{1,0:T(8,128)}, bf16[64,1024]{1,0:T(8,128)(2,1)}, bf16[4,64,128]{2,1,0:T(8,128)(2,1)}, bf16[16,64,512]{2,1,0:T(8,128)(2,1)}, f32[8,1024]{1,0:T(8,128)}, /*index=5*/bf16[64,1024]{1,0:T(8,128)(2,1)}) custom-call(bf16[64,1024]{1,0:T(8,128)(2,1)S(1)} %dynamic-slice_bitcast_fusion.refs_9_.refs_0_.refs_1_, ...), custom_call_target="tpu_custom_call", output_to_operand_aliasing={{5}: (12, {})} | custom-call | bytes 9000000 | tf_op jit(solution)/shard_map/pallas_call | solution.py:73
  191.9 3.9 %shard_map.206 = (bf16[8,2,128,512]{3,2,1,0:T(8,128)(2,1)}, bf16[8,2,128,512]{3,2,1,0:T(8,128)(2,1)}, f32[4,256]{1,0:T(4,128)}, f32[1,1024]{1,0:T(1,128)}) custom-call(bf16[64,1024]{1,0:T(8,128)(2,1)} %get-tuple-element.133.refs_0_, bf16[64,1024]{1,0:T(8,128)(2,1)S(1)} %dynamic-slice_bitcast_fusion.refs_9_.refs_0_.refs_1_, ...), custom_call_target="tpu_custom_call" | custom-call | bytes 9000000 | tf_op jit(solution)/shard_map/pallas_call | solution.py:73
  195.8 4.1 %collective-permute-start.24 = (bf16[8,2,128,512]{3,2,1,0:T(8,128)(2,1)}, bf16[8,2,128,512]{3,2,1,0:T(8,128)(2,1)}, u32[]{:S(2)}, u32[]{:S(2)}) collective-permute-start(bf16[8,2,128,512]{3,2,1,0:T(8,128)(2,1)} %get-tuple-element.138), channel_id=1, source_target_pairs={{0,64},{64,0},{1,65},{65,1},{2,66},{66,2},{3,67},{67,3},{4,68},{68... | collective-permute-start | bytes 6291464 | tf_op jit(solution)/shard_map/ppermute | solution.py:536
  199.9 4.4 %all-to-all-start.4 = ((bf16[16,64,512]{2,1,0:T(8,128)(2,1)}), bf16[16,64,512]{2,1,0:T(8,128)(2,1)}, u32[]{:S(2)}, u32[]{:S(2)}) async-start(bf16[16,64,512]{2,1,0:T(8,128)(2,1)} %get-tuple-element.125), calls=%async_computation.4 | async-start | bytes 2097152 | tf_op jit(solution)/shard_map/all_to_all | solution.py:545
  204.4 1.8 collective-permute-start.18
  207.7 4.8 %collective-permute-done.18.refs_6_ = bf16[64,1024]{1,0:T(8,128)(2,1)S(1)} collective-permute-done((bf16[64,1024]{1,0:T(8,128)(2,1)S(1)}, bf16[64,1024]{1,0:T(8,128)(2,1)S(1)}, u32[]{:S(2)}, u32[]{:S(2)}) %collective-permute-start.18) | collective-permute-done | bytes 131104 | tf_op jit(solution)/shard_map/ppermute | solution.py:540
  214.9 1.3 collective-permute-start.19
  217.9 2.0 all-to-all-done.4.refs_0_
  219.9 2.9 shard_map.205
  222.7 3.0 collective-permute-start.23
  225.7 1.7 collective-permute-start.22
  229.0 3.8 %shard_map.207.refs_11_ = bf16[16,128,512]{2,1,0:T(8,128)(2,1)} custom-call(bf16[8,2,128,512]{3,2,1,0:T(8,128)(2,1)} %get-tuple-element.137.refs_0_, bf16[8,2,128,512]{3,2,1,0:T(8,128)(2,1)} %collective-permute-done.24.refs_1_), custom_call_target="tpu_custom_call" | custom-call | bytes 9000000 | tf_op jit(solution)/shard_map/pallas_call | solution.py:73
  233.5 4.7 %shard_map.208 = (bf16[64,1024]{1,0:T(8,128)(2,1)}, bf16[4,64,256]{2,1,0:T(8,128)(2,1)}, bf16[64,1024]{1,0:T(8,128)(2,1)S(1)}, f32[8,1024]{1,0:T(8,128)}, bf16[16,128,512]{2,1,0:T(8,128)(2,1)}) custom-call(bf16[64,1024]{1,0:T(8,128)(2,1)S(1)} %get-tuple-element.115.refs_0_.refs_1_, ...), custom_call_target="tpu_custom_call", output_to_operand_aliasing={{4}: (11, {})} | custom-call | bytes 9000000 | tf_op jit(solution)/shard_map/pallas_call | solution.py:73
  238.1 4.4 %all-to-all-start.5 = ((bf16[16,128,512]{2,1,0:T(8,128)(2,1)}), bf16[16,128,512]{2,1,0:T(8,128)(2,1)}, u32[]{:S(2)}, u32[]{:S(2)}) async-start(bf16[16,128,512]{2,1,0:T(8,128)(2,1)} %get-tuple-element.145), calls=%async_computation.5 | async-start | bytes 4194304 | tf_op jit(solution)/shard_map/all_to_all | solution.py:545
  242.6 1.7 collective-permute-start.27
  244.2 1.5 collective-permute-start.26
  245.9 1.8 collective-permute-done.27.refs_5_
  247.7 1.9 collective-permute-done.26.refs_4_
  250.0 6.0 %shard_map.209 = (f32[64,1024]{1,0:T(8,128)}, bf16[64,1024]{1,0:T(8,128)(2,1)}, bf16[4,64,128]{2,1,0:T(8,128)(2,1)}, bf16[16,64,512]{2,1,0:T(8,128)(2,1)}, f32[8,1024]{1,0:T(8,128)}) custom-call(bf16[64,1024]{1,0:T(8,128)(2,1)} %get-tuple-element.139.refs_0_.refs_1_, f32[64,1024]{1,0:T(8,128)} %get-tuple-element.112.refs_0_.refs_1_, ...), custom_call_target="tpu_custom_call" | custom-call | bytes 9000000 | tf_op jit(solution)/shard_map/pallas_call | solution.py:73
  256.0 3.8 %shard_map.211 = (bf16[8,2,128,512]{3,2,1,0:T(8,128)(2,1)}, bf16[8,2,128,512]{3,2,1,0:T(8,128)(2,1)}, f32[4,256]{1,0:T(4,128)}, f32[1,1024]{1,0:T(1,128)}) custom-call(bf16[64,1024]{1,0:T(8,128)(2,1)} %get-tuple-element.148.refs_0_, bf16[64,1024]{1,0:T(8,128)(2,1)} %get-tuple-element.139.refs_0_.refs_1_, bf16[4,64,256]{2,1,0:T(8,128)(2,1)} %get-tuple-element.149.refs_2_, ...), custom_call_target="tpu_custom_call" | custom-call | bytes 9000000 | tf_op jit(solution)/shard_map/pallas_call | solution.py:73
  259.8 4.0 %collective-permute-start.28 = (bf16[8,2,128,512]{3,2,1,0:T(8,128)(2,1)}, bf16[8,2,128,512]{3,2,1,0:T(8,128)(2,1)}, u32[]{:S(2)}, u32[]{:S(2)}) collective-permute-start(bf16[8,2,128,512]{3,2,1,0:T(8,128)(2,1)} %get-tuple-element.152), channel_id=1, source_target_pairs={{0,64},{64,0},{1,65},{65,1},{2,66},{66,2},{3,67},{67,3},{4,68},{68... | collective-permute-start | bytes 6291464 | tf_op jit(solution)/shard_map/ppermute | solution.py:536
  263.8 3.1 shard_map.212
  269.1 5.9 %all-to-all-start.6 = ((bf16[16,64,512]{2,1,0:T(8,128)(2,1)}), bf16[16,64,512]{2,1,0:T(8,128)(2,1)}, u32[]{:S(2)}, u32[]{:S(2)}) async-start(bf16[16,64,512]{2,1,0:T(8,128)(2,1)} %get-tuple-element.146), calls=%async_computation.6 | async-start | bytes 2097152 | tf_op jit(solution)/shard_map/all_to_all | solution.py:545
  275.0 4.8 %shard_map.213.refs_4_ = bf16[16,128,768]{2,1,0:T(8,128)(2,1)} custom-call(bf16[8,2,128,512]{3,2,1,0:T(8,128)(2,1)} %get-tuple-element.151.refs_0_, bf16[8,2,128,512]{3,2,1,0:T(8,128)(2,1)} %collective-permute-done.28.refs_1_, bf16[8,2,128,256]{3,2,1,0:T(8,128)(2,1)} %get-tuple-element.157.refs_2_, bf16[8,2,128,256]{3,2,1,0:T(8,128)(2,1)} %collective-permute-done.29.refs_3_), custom_call_target="tpu_custom_call" | custom-call | bytes 9000000 | tf_op jit(solution)/shard_map/pallas_call | solution.py:73
  279.8 8.1 %all-to-all-done.6.refs_0_ = bf16[16,64,512]{2,1,0:T(8,128)(2,1)} async-done(((bf16[16,64,512]{2,1,0:T(8,128)(2,1)}), bf16[16,64,512]{2,1,0:T(8,128)(2,1)}, u32[]{:S(2)}, u32[]{:S(2)}) %all-to-all-start.6) | async-done | bytes 1048608 | tf_op jit(solution)/shard_map/all_to_all | solution.py:545
  287.9 2.9 shard_map.214
  290.7 5.4 %all-to-all-start.7 = ((bf16[16,128,768]{2,1,0:T(8,128)(2,1)}), bf16[16,128,768]{2,1,0:T(8,128)(2,1)}, u32[]{:S(2)}, u32[]{:S(2)}) async-start(bf16[16,128,768]{2,1,0:T(8,128)(2,1)} %get-tuple-element.176), calls=%async_computation.7 | async-start | bytes 6291456 | tf_op jit(solution)/shard_map/all_to_all | solution.py:545
  296.1 2.8 shard_map.215
  298.9 3.5 collective-permute-start.33
  302.4 1.6 collective-permute-start.32
  306.5 4.8 %collective-permute-done.32.refs_7_ = bf16[64,1024]{1,0:T(8,128)(2,1)S(1)} collective-permute-done((bf16[64,1024]{1,0:T(8,128)(2,1)S(1)}, bf16[64,1024]{1,0:T(8,128)(2,1)S(1)}, u32[]{:S(2)}, u32[]{:S(2)}) %collective-permute-start.32) | collective-permute-done | bytes 131104 | tf_op jit(solution)/shard_map/ppermute | solution.py:540
  311.9 3.2 shard_map.217
  315.2 17.8 %all-to-all-done.7.refs_1_ = bf16[16,128,768]{2,1,0:T(8,128)(2,1)} async-done(((bf16[16,128,768]{2,1,0:T(8,128)(2,1)}), bf16[16,128,768]{2,1,0:T(8,128)(2,1)}, u32[]{:S(2)}, u32[]{:S(2)}) %all-to-all-start.7) | async-done | bytes 3145760 | tf_op jit(solution)/shard_map/all_to_all | solution.py:545
  332.9 6.6 %all-to-all-start.8 = ((bf16[16,144,256]{2,1,0:T(8,128)(2,1)}), bf16[16,144,256]{2,1,0:T(8,128)(2,1)S(1)}, u32[]{:S(2)}, u32[]{:S(2)}) async-start(bf16[16,144,256]{2,1,0:T(8,128)(2,1)} %get-tuple-element.180), calls=%async_computation.8 | async-start | bytes 2359296 | tf_op jit(solution)/shard_map/all_to_all | solution.py:545
  339.5 3.9 %collective-permute-start.34 = (bf16[64,1024]{1,0:T(8,128)(2,1)S(1)}, bf16[64,1024]{1,0:T(8,128)(2,1)S(1)}, u32[]{:S(2)}, u32[]{:S(2)}) collective-permute-start(bf16[64,1024]{1,0:T(8,128)(2,1)S(1)} %get-tuple-element.175), channel_id=1, source_target_pairs={{0,64},{64,0},{1,65},{65,1},{2,66},{66,2},{3,67},{67,3},{4,68},{68... | collective-permute-start | bytes 393224 | tf_op jit(solution)/shard_map/ppermute | solution.py:536
  344.5 3.1 collective-permute-start.35
  347.6 3.3 shard_map.220
  353.0 7.6 %collective-permute-start.37 = (f32[136,256]{1,0:T(8,128)S(1)}, f32[136,256]{1,0:T(8,128)S(1)}, u32[]{:S(2)}, u32[]{:S(2)}) collective-permute-start(f32[136,256]{1,0:T(8,128)S(1)} %get-tuple-element.183), channel_id=1, source_target_pairs={{0,64},{64,0},{1,65},{65,1},{2,66},{66,2},{3,67},{67,3},{4,68},{68... | collective-permute-start | bytes 417800 | tf_op jit(solution)/shard_map/ppermute | solution.py:536
  (66 shorter events, 26.7 us)
Async XLA Ops:
  0.6 44.1 %copy-start = (bf16[2,1,128,1024]{3,2,1,0:T(8,128)(2,1)S(1)}, bf16[2,1,128,1024]{3,2,1,0:T(8,128)(2,1)}, u32[]{:S(2)}) copy-start(bf16[2,1,128,1024]{3,2,1,0:T(8,128)(2,1)} %param.11) | copy-start | bytes 1572868
  2.1 2.6 collective-permute-start
  42.7 6.1 %collective-permute-start.1 = (bf16[8,2,272,256]{3,2,1,0:T(8,128)(2,1)S(1)}, bf16[8,2,272,256]{3,2,1,0:T(8,128)(2,1)}, u32[]{:S(2)}, u32[]{:S(2)}) collective-permute-start(bf16[8,2,272,256]{3,2,1,0:T(8,128)(2,1)S(1)} %bitcast.37), channel_id=1, source_target_pairs={{0,64},{64,0},{1,65},{65,1},{2,66},{66,2},{3,67},{67,3},{4,68},{68... | collective-permute-start | bytes 6684680 | tf_op jit(solution)/shard_map/ppermute | solution.py:536
  95.3 21.5 %collective-permute-start.5 = (bf16[16,192,512]{2,1,0:T(8,128)(2,1)}, bf16[16,192,512]{2,1,0:T(8,128)(2,1)}, u32[]{:S(2)}, u32[]{:S(2)}) collective-permute-start(bf16[16,192,512]{2,1,0:T(8,128)(2,1)} %all_to_all.46.refs_2_.refs_11_), channel_id=1, source_target_pairs={{0,64},{64,0},{1,65},{65,1},{2,66},{66,2},{3,67},{67,3},{4,68},{68... | collective-permute-start | bytes 9437192 | tf_op jit(solution)/shard_map/ppermute | solution.py:536
  102.7 32.8 %all-to-all-start.2 = ((bf16[16,128,512]{2,1,0:T(8,128)(2,1)}), bf16[16,128,512]{2,1,0:T(8,128)(2,1)}, u32[]{:S(2)}, u32[]{:S(2)}) async-start(bf16[16,128,512]{2,1,0:T(8,128)(2,1)} %get-tuple-element.114), calls=%async_computation.2 | async-start | bytes 4194304 | tf_op jit(solution)/shard_map/all_to_all | solution.py:545
  107.1 8.1 %collective-permute-start.4 = (bf16[64,1024]{1,0:T(8,128)(2,1)S(1)}, bf16[64,1024]{1,0:T(8,128)(2,1)S(1)}, u32[]{:S(2)}, u32[]{:S(2)}) collective-permute-start(bf16[64,1024]{1,0:T(8,128)(2,1)S(1)} %get-tuple-element.109.refs_1_), channel_id=1, source_target_pairs={{0,3},{1,2},{2,1},{3,0},{4,7},{5,6},{6,5},{7,4},{8,11},{9,10},{10,... | collective-permute-start | bytes 393224 | tf_op jit(solution)/shard_map/ppermute | solution.py:540
  109.6 6.4 %collective-permute-start.3 = (bf16[64,1024]{1,0:T(8,128)(2,1)S(1)}, bf16[64,1024]{1,0:T(8,128)(2,1)S(1)}, u32[]{:S(2)}, u32[]{:S(2)}) collective-permute-start(bf16[64,1024]{1,0:T(8,128)(2,1)S(1)} %get-tuple-element.109.refs_1_), channel_id=1, source_target_pairs={{0,2},{1,3},{2,0},{3,1},{4,6},{5,7},{6,4},{7,5},{8,10},{9,11},{10,... | collective-permute-start | bytes 393224 | tf_op jit(solution)/shard_map/ppermute | solution.py:540
  110.2 6.6 %collective-permute-start.2 = (bf16[64,1024]{1,0:T(8,128)(2,1)S(1)}, bf16[64,1024]{1,0:T(8,128)(2,1)S(1)}, u32[]{:S(2)}, u32[]{:S(2)}) collective-permute-start(bf16[64,1024]{1,0:T(8,128)(2,1)S(1)} %get-tuple-element.109.refs_1_), channel_id=1, source_target_pairs={{0,1},{1,0},{2,3},{3,2},{4,5},{5,4},{6,7},{7,6},{8,9},{9,8},{10,11... | collective-permute-start | bytes 393224 | tf_op jit(solution)/shard_map/ppermute | solution.py:540
  121.2 14.2 %collective-permute-start.8 = (bf16[64,1024]{1,0:T(8,128)(2,1)S(1)}, bf16[64,1024]{1,0:T(8,128)(2,1)S(1)}, u32[]{:S(2)}, u32[]{:S(2)}) collective-permute-start(bf16[64,1024]{1,0:T(8,128)(2,1)S(1)} %get-tuple-element.113.refs_1_), channel_id=1, source_target_pairs={{0,3},{1,2},{2,1},{3,0},{4,7},{5,6},{6,5},{7,4},{8,11},{9,10},{10,... | collective-permute-start | bytes 393224 | tf_op jit(solution)/shard_map/ppermute | solution.py:540
  123.6 11.8 %collective-permute-start.7 = (bf16[64,1024]{1,0:T(8,128)(2,1)S(1)}, bf16[64,1024]{1,0:T(8,128)(2,1)S(1)}, u32[]{:S(2)}, u32[]{:S(2)}) collective-permute-start(bf16[64,1024]{1,0:T(8,128)(2,1)S(1)} %get-tuple-element.113.refs_1_), channel_id=1, source_target_pairs={{0,2},{1,3},{2,0},{3,1},{4,6},{5,7},{6,4},{7,5},{8,10},{9,11},{10,... | collective-permute-start | bytes 393224 | tf_op jit(solution)/shard_map/ppermute | solution.py:540
  124.2 11.2 %collective-permute-start.6 = (bf16[64,1024]{1,0:T(8,128)(2,1)S(1)}, bf16[64,1024]{1,0:T(8,128)(2,1)S(1)}, u32[]{:S(2)}, u32[]{:S(2)}) collective-permute-start(bf16[64,1024]{1,0:T(8,128)(2,1)S(1)} %get-tuple-element.113.refs_1_), channel_id=1, source_target_pairs={{0,1},{1,0},{2,3},{3,2},{4,5},{5,4},{6,7},{7,6},{8,9},{9,8},{10,11... | collective-permute-start | bytes 393224 | tf_op jit(solution)/shard_map/ppermute | solution.py:540
  138.8 34.7 %collective-permute-start.12 = (bf16[8,2,128,512]{3,2,1,0:T(8,128)(2,1)}, bf16[8,2,128,512]{3,2,1,0:T(8,128)(2,1)S(1)}, u32[]{:S(2)}, u32[]{:S(2)}) collective-permute-start(bf16[8,2,128,512]{3,2,1,0:T(8,128)(2,1)} %bitcast.16.refs_7_), channel_id=1, source_target_pairs={{0,64},{64,0},{1,65},{65,1},{2,66},{66,2},{3,67},{67,3},{4,68},{68... | collective-permute-start | bytes 6291464 | tf_op jit(solution)/shard_map/ppermute | solution.py:536
  165.6 6.2 %collective-permute-start.11 = (bf16[64,1024]{1,0:T(8,128)(2,1)S(1)}, bf16[64,1024]{1,0:T(8,128)(2,1)S(1)}, u32[]{:S(2)}, u32[]{:S(2)}) collective-permute-start(bf16[64,1024]{1,0:T(8,128)(2,1)S(1)} %get-tuple-element.118.refs_1_), channel_id=1, source_target_pairs={{0,3},{1,2},{2,1},{3,0},{4,7},{5,6},{6,5},{7,4},{8,11},{9,10},{10,... | collective-permute-start | bytes 393224 | tf_op jit(solution)/shard_map/ppermute | solution.py:540
  168.0 5.4 %collective-permute-start.10 = (bf16[64,1024]{1,0:T(8,128)(2,1)S(1)}, bf16[64,1024]{1,0:T(8,128)(2,1)S(1)}, u32[]{:S(2)}, u32[]{:S(2)}) collective-permute-start(bf16[64,1024]{1,0:T(8,128)(2,1)S(1)} %get-tuple-element.118.refs_1_), channel_id=1, source_target_pairs={{0,2},{1,3},{2,0},{3,1},{4,6},{5,7},{6,4},{7,5},{8,10},{9,11},{10,... | collective-permute-start | bytes 393224 | tf_op jit(solution)/shard_map/ppermute | solution.py:540
  168.6 4.8 %collective-permute-start.9 = (bf16[64,1024]{1,0:T(8,128)(2,1)S(1)}, bf16[64,1024]{1,0:T(8,128)(2,1)S(1)}, u32[]{:S(2)}, u32[]{:S(2)}) collective-permute-start(bf16[64,1024]{1,0:T(8,128)(2,1)S(1)} %get-tuple-element.118.refs_1_), channel_id=1, source_target_pairs={{0,1},{1,0},{2,3},{3,2},{4,5},{5,4},{6,7},{7,6},{8,9},{9,8},{10,11... | collective-permute-start | bytes 393224 | tf_op jit(solution)/shard_map/ppermute | solution.py:540
  178.6 5.7 %collective-permute-start.15 = (bf16[64,1024]{1,0:T(8,128)(2,1)S(1)}, bf16[64,1024]{1,0:T(8,128)(2,1)S(1)}, u32[]{:S(2)}, u32[]{:S(2)}) collective-permute-start(bf16[64,1024]{1,0:T(8,128)(2,1)S(1)} %get-tuple-element.121.refs_2_), channel_id=1, source_target_pairs={{0,3},{1,2},{2,1},{3,0},{4,7},{5,6},{6,5},{7,4},{8,11},{9,10},{10,... | collective-permute-start | bytes 393224 | tf_op jit(solution)/shard_map/ppermute | solution.py:540
  180.9 5.3 %collective-permute-start.14 = (bf16[64,1024]{1,0:T(8,128)(2,1)S(1)}, bf16[64,1024]{1,0:T(8,128)(2,1)S(1)}, u32[]{:S(2)}, u32[]{:S(2)}) collective-permute-start(bf16[64,1024]{1,0:T(8,128)(2,1)S(1)} %get-tuple-element.121.refs_2_), channel_id=1, source_target_pairs={{0,2},{1,3},{2,0},{3,1},{4,6},{5,7},{6,4},{7,5},{8,10},{9,11},{10,... | collective-permute-start | bytes 393224 | tf_op jit(solution)/shard_map/ppermute | solution.py:540
  181.3 5.0 %collective-permute-start.13 = (bf16[64,1024]{1,0:T(8,128)(2,1)S(1)}, bf16[64,1024]{1,0:T(8,128)(2,1)S(1)}, u32[]{:S(2)}, u32[]{:S(2)}) collective-permute-start(bf16[64,1024]{1,0:T(8,128)(2,1)S(1)} %get-tuple-element.121.refs_2_), channel_id=1, source_target_pairs={{0,1},{1,0},{2,3},{3,2},{4,5},{5,4},{6,7},{7,6},{8,9},{9,8},{10,11... | collective-permute-start | bytes 393224 | tf_op jit(solution)/shard_map/ppermute | solution.py:540
  191.9 12.5 %copy-start.3 = (bf16[64,1024]{1,0:T(8,128)(2,1)S(1)}, bf16[64,1024]{1,0:T(8,128)(2,1)}, u32[]{:S(2)}) copy-start(bf16[64,1024]{1,0:T(8,128)(2,1)} %get-tuple-element.127.refs_3_) | copy-start | bytes 393220
  195.8 33.2 %collective-permute-start.24 = (bf16[8,2,128,512]{3,2,1,0:T(8,128)(2,1)}, bf16[8,2,128,512]{3,2,1,0:T(8,128)(2,1)}, u32[]{:S(2)}, u32[]{:S(2)}) collective-permute-start(bf16[8,2,128,512]{3,2,1,0:T(8,128)(2,1)} %get-tuple-element.138), channel_id=1, source_target_pairs={{0,64},{64,0},{1,65},{65,1},{2,66},{66,2},{3,67},{67,3},{4,68},{68... | collective-permute-start | bytes 6291464 | tf_op jit(solution)/shard_map/ppermute | solution.py:536
  199.9 19.9 %all-to-all-start.4 = ((bf16[16,64,512]{2,1,0:T(8,128)(2,1)}), bf16[16,64,512]{2,1,0:T(8,128)(2,1)}, u32[]{:S(2)}, u32[]{:S(2)}) async-start(bf16[16,64,512]{2,1,0:T(8,128)(2,1)} %get-tuple-element.125), calls=%async_computation.4 | async-start | bytes 2097152 | tf_op jit(solution)/shard_map/all_to_all | solution.py:545
  204.4 8.1 %collective-permute-start.18 = (bf16[64,1024]{1,0:T(8,128)(2,1)S(1)}, bf16[64,1024]{1,0:T(8,128)(2,1)S(1)}, u32[]{:S(2)}, u32[]{:S(2)}) collective-permute-start(bf16[64,1024]{1,0:T(8,128)(2,1)S(1)} %copy-done.3), channel_id=1, source_target_pairs={{0,3},{1,2},{2,1},{3,0},{4,7},{5,6},{6,5},{7,4},{8,11},{9,10},{10,... | collective-permute-start | bytes 393224 | tf_op jit(solution)/shard_map/ppermute | solution.py:540
  206.2 6.3 %collective-permute-start.17 = (bf16[64,1024]{1,0:T(8,128)(2,1)S(1)}, bf16[64,1024]{1,0:T(8,128)(2,1)S(1)}, u32[]{:S(2)}, u32[]{:S(2)}) collective-permute-start(bf16[64,1024]{1,0:T(8,128)(2,1)S(1)} %copy-done.3), channel_id=1, source_target_pairs={{0,2},{1,3},{2,0},{3,1},{4,6},{5,7},{6,4},{7,5},{8,10},{9,11},{10,... | collective-permute-start | bytes 393224 | tf_op jit(solution)/shard_map/ppermute | solution.py:540
  206.6 7.2 %collective-permute-start.16 = (bf16[64,1024]{1,0:T(8,128)(2,1)S(1)}, bf16[64,1024]{1,0:T(8,128)(2,1)S(1)}, u32[]{:S(2)}, u32[]{:S(2)}) collective-permute-start(bf16[64,1024]{1,0:T(8,128)(2,1)S(1)} %copy-done.3), channel_id=1, source_target_pairs={{0,1},{1,0},{2,3},{3,2},{4,5},{5,4},{6,7},{7,6},{8,9},{9,8},{10,11... | collective-permute-start | bytes 393224 | tf_op jit(solution)/shard_map/ppermute | solution.py:540
  214.9 2.3 collective-permute-start.19
  222.7 10.7 %collective-permute-start.23 = (bf16[2,64,1024]{2,1,0:T(8,128)(2,1)}, bf16[2,64,1024]{2,1,0:T(8,128)(2,1)S(1)}, u32[]{:S(2)}, u32[]{:S(2)}) collective-permute-start(bf16[2,64,1024]{2,1,0:T(8,128)(2,1)} %get-tuple-element.132.refs_1_), channel_id=1, source_target_pairs={{0,4},{4,0},{1,5},{5,1},{2,6},{6,2},{3,7},{7,3},{8,12},{12,8},{9,1... | collective-permute-start | bytes 786440 | tf_op jit(solution)/shard_map/ppermute | solution.py:553
  225.7 7.0 %collective-permute-start.22 = (bf16[64,1024]{1,0:T(8,128)(2,1)S(1)}, bf16[64,1024]{1,0:T(8,128)(2,1)S(1)}, u32[]{:S(2)}, u32[]{:S(2)}) collective-permute-start(bf16[64,1024]{1,0:T(8,128)(2,1)S(1)} %get-tuple-element.130.refs_2_), channel_id=1, source_target_pairs={{0,3},{1,2},{2,1},{3,0},{4,7},{5,6},{6,5},{7,4},{8,11},{9,10},{10,... | collective-permute-start | bytes 393224 | tf_op jit(solution)/shard_map/ppermute | solution.py:540
  227.4 5.4 %collective-permute-start.21 = (bf16[64,1024]{1,0:T(8,128)(2,1)S(1)}, bf16[64,1024]{1,0:T(8,128)(2,1)S(1)}, u32[]{:S(2)}, u32[]{:S(2)}) collective-permute-start(bf16[64,1024]{1,0:T(8,128)(2,1)S(1)} %get-tuple-element.130.refs_2_), channel_id=1, source_target_pairs={{0,2},{1,3},{2,0},{3,1},{4,6},{5,7},{6,4},{7,5},{8,10},{9,11},{10,... | collective-permute-start | bytes 393224 | tf_op jit(solution)/shard_map/ppermute | solution.py:540
  228.4 5.1 %collective-permute-start.20 = (bf16[64,1024]{1,0:T(8,128)(2,1)S(1)}, bf16[64,1024]{1,0:T(8,128)(2,1)S(1)}, u32[]{:S(2)}, u32[]{:S(2)}) collective-permute-start(bf16[64,1024]{1,0:T(8,128)(2,1)S(1)} %get-tuple-element.130.refs_2_), channel_id=1, source_target_pairs={{0,1},{1,0},{2,3},{3,2},{4,5},{5,4},{6,7},{7,6},{8,9},{9,8},{10,11... | collective-permute-start | bytes 393224 | tf_op jit(solution)/shard_map/ppermute | solution.py:540
  238.1 29.7 %all-to-all-start.5 = ((bf16[16,128,512]{2,1,0:T(8,128)(2,1)}), bf16[16,128,512]{2,1,0:T(8,128)(2,1)}, u32[]{:S(2)}, u32[]{:S(2)}) async-start(bf16[16,128,512]{2,1,0:T(8,128)(2,1)} %get-tuple-element.145), calls=%async_computation.5 | async-start | bytes 4194304 | tf_op jit(solution)/shard_map/all_to_all | solution.py:545
  242.6 5.1 %collective-permute-start.27 = (bf16[64,1024]{1,0:T(8,128)(2,1)S(1)}, bf16[64,1024]{1,0:T(8,128)(2,1)S(1)}, u32[]{:S(2)}, u32[]{:S(2)}) collective-permute-start(bf16[64,1024]{1,0:T(8,128)(2,1)S(1)} %get-tuple-element.140.refs_2_), channel_id=1, source_target_pairs={{0,3},{1,2},{2,1},{3,0},{4,7},{5,6},{6,5},{7,4},{8,11},{9,10},{10,... | collective-permute-start | bytes 393224 | tf_op jit(solution)/shard_map/ppermute | solution.py:540
  244.2 5.3 %collective-permute-start.26 = (bf16[64,1024]{1,0:T(8,128)(2,1)S(1)}, bf16[64,1024]{1,0:T(8,128)(2,1)S(1)}, u32[]{:S(2)}, u32[]{:S(2)}) collective-permute-start(bf16[64,1024]{1,0:T(8,128)(2,1)S(1)} %get-tuple-element.140.refs_2_), channel_id=1, source_target_pairs={{0,2},{1,3},{2,0},{3,1},{4,6},{5,7},{6,4},{7,5},{8,10},{9,11},{10,... | collective-permute-start | bytes 393224 | tf_op jit(solution)/shard_map/ppermute | solution.py:540
  245.8 4.2 %collective-permute-start.25 = (bf16[64,1024]{1,0:T(8,128)(2,1)S(1)}, bf16[64,1024]{1,0:T(8,128)(2,1)S(1)}, u32[]{:S(2)}, u32[]{:S(2)}) collective-permute-start(bf16[64,1024]{1,0:T(8,128)(2,1)S(1)} %get-tuple-element.140.refs_2_), channel_id=1, source_target_pairs={{0,1},{1,0},{2,3},{3,2},{4,5},{5,4},{6,7},{7,6},{8,9},{9,8},{10,11... | collective-permute-start | bytes 393224 | tf_op jit(solution)/shard_map/ppermute | solution.py:540
  259.8 15.1 %collective-permute-start.28 = (bf16[8,2,128,512]{3,2,1,0:T(8,128)(2,1)}, bf16[8,2,128,512]{3,2,1,0:T(8,128)(2,1)}, u32[]{:S(2)}, u32[]{:S(2)}) collective-permute-start(bf16[8,2,128,512]{3,2,1,0:T(8,128)(2,1)} %get-tuple-element.152), channel_id=1, source_target_pairs={{0,64},{64,0},{1,65},{65,1},{2,66},{66,2},{3,67},{67,3},{4,68},{68... | collective-permute-start | bytes 6291464 | tf_op jit(solution)/shard_map/ppermute | solution.py:536
  266.9 8.1 %collective-permute-start.29 = (bf16[8,2,128,256]{3,2,1,0:T(8,128)(2,1)}, bf16[8,2,128,256]{3,2,1,0:T(8,128)(2,1)}, u32[]{:S(2)}, u32[]{:S(2)}) collective-permute-start(bf16[8,2,128,256]{3,2,1,0:T(8,128)(2,1)} %get-tuple-element.158), channel_id=1, source_target_pairs={{0,64},{64,0},{1,65},{65,1},{2,66},{66,2},{3,67},{67,3},{4,68},{68... | collective-permute-start | bytes 3145736 | tf_op jit(solution)/shard_map/ppermute | solution.py:536
  269.1 18.8 %all-to-all-start.6 = ((bf16[16,64,512]{2,1,0:T(8,128)(2,1)}), bf16[16,64,512]{2,1,0:T(8,128)(2,1)}, u32[]{:S(2)}, u32[]{:S(2)}) async-start(bf16[16,64,512]{2,1,0:T(8,128)(2,1)} %get-tuple-element.146), calls=%async_computation.6 | async-start | bytes 2097152 | tf_op jit(solution)/shard_map/all_to_all | solution.py:545
  290.7 14.9 %copy-start.2 = (bf16[2,64,1024]{2,1,0:T(8,128)(2,1)S(1)}, bf16[2,64,1024]{2,1,0:T(8,128)(2,1)}, u32[]{:S(2)}) copy-start(bf16[2,64,1024]{2,1,0:T(8,128)(2,1)} %get-tuple-element.132.refs_1_) | copy-start | bytes 786436
  290.7 42.2 %all-to-all-start.7 = ((bf16[16,128,768]{2,1,0:T(8,128)(2,1)}), bf16[16,128,768]{2,1,0:T(8,128)(2,1)}, u32[]{:S(2)}, u32[]{:S(2)}) async-start(bf16[16,128,768]{2,1,0:T(8,128)(2,1)} %get-tuple-element.176), calls=%async_computation.7 | async-start | bytes 6291456 | tf_op jit(solution)/shard_map/all_to_all | solution.py:545
  298.9 13.0 %collective-permute-start.33 = (bf16[8,2,128,256]{3,2,1,0:T(8,128)(2,1)S(1)}, bf16[8,2,128,256]{3,2,1,0:T(8,128)(2,1)S(1)}, u32[]{:S(2)}, u32[]{:S(2)}) collective-permute-start(bf16[8,2,128,256]{3,2,1,0:T(8,128)(2,1)S(1)} %get-tuple-element.165), channel_id=1, source_target_pairs={{0,64},{64,0},{1,65},{65,1},{2,66},{66,2},{3,67},{67,3},{4,68},{68... | collective-permute-start | bytes 3145736 | tf_op jit(solution)/shard_map/ppermute | solution.py:536
  302.4 8.9 %collective-permute-start.32 = (bf16[64,1024]{1,0:T(8,128)(2,1)S(1)}, bf16[64,1024]{1,0:T(8,128)(2,1)S(1)}, u32[]{:S(2)}, u32[]{:S(2)}) collective-permute-start(bf16[64,1024]{1,0:T(8,128)(2,1)S(1)} %get-tuple-element.159.refs_4_), channel_id=1, source_target_pairs={{0,3},{1,2},{2,1},{3,0},{4,7},{5,6},{6,5},{7,4},{8,11},{9,10},{10,... | collective-permute-start | bytes 393224 | tf_op jit(solution)/shard_map/ppermute | solution.py:540
  304.0 7.3 %collective-permute-start.31 = (bf16[64,1024]{1,0:T(8,128)(2,1)S(1)}, bf16[64,1024]{1,0:T(8,128)(2,1)S(1)}, u32[]{:S(2)}, u32[]{:S(2)}) collective-permute-start(bf16[64,1024]{1,0:T(8,128)(2,1)S(1)} %get-tuple-element.159.refs_4_), channel_id=1, source_target_pairs={{0,2},{1,3},{2,0},{3,1},{4,6},{5,7},{6,4},{7,5},{8,10},{9,11},{10,... | collective-permute-start | bytes 393224 | tf_op jit(solution)/shard_map/ppermute | solution.py:540
  305.3 6.7 %collective-permute-start.30 = (bf16[64,1024]{1,0:T(8,128)(2,1)S(1)}, bf16[64,1024]{1,0:T(8,128)(2,1)S(1)}, u32[]{:S(2)}, u32[]{:S(2)}) collective-permute-start(bf16[64,1024]{1,0:T(8,128)(2,1)S(1)} %get-tuple-element.159.refs_4_), channel_id=1, source_target_pairs={{0,1},{1,0},{2,3},{3,2},{4,5},{5,4},{6,7},{7,6},{8,9},{9,8},{10,11... | collective-permute-start | bytes 393224 | tf_op jit(solution)/shard_map/ppermute | solution.py:540
  332.9 19.9 %all-to-all-start.8 = ((bf16[16,144,256]{2,1,0:T(8,128)(2,1)}), bf16[16,144,256]{2,1,0:T(8,128)(2,1)S(1)}, u32[]{:S(2)}, u32[]{:S(2)}) async-start(bf16[16,144,256]{2,1,0:T(8,128)(2,1)} %get-tuple-element.180), calls=%async_computation.8 | async-start | bytes 2359296 | tf_op jit(solution)/shard_map/all_to_all | solution.py:545
  339.5 4.9 %collective-permute-start.34 = (bf16[64,1024]{1,0:T(8,128)(2,1)S(1)}, bf16[64,1024]{1,0:T(8,128)(2,1)S(1)}, u32[]{:S(2)}, u32[]{:S(2)}) collective-permute-start(bf16[64,1024]{1,0:T(8,128)(2,1)S(1)} %get-tuple-element.175), channel_id=1, source_target_pairs={{0,64},{64,0},{1,65},{65,1},{2,66},{66,2},{3,67},{67,3},{4,68},{68... | collective-permute-start | bytes 393224 | tf_op jit(solution)/shard_map/ppermute | solution.py:536
  344.5 16.1 %collective-permute-start.35 = (bf16[2,64,1024]{2,1,0:T(8,128)(2,1)S(1)}, bf16[2,64,1024]{2,1,0:T(8,128)(2,1)S(1)}, u32[]{:S(2)}, u32[]{:S(2)}) collective-permute-start(bf16[2,64,1024]{2,1,0:T(8,128)(2,1)S(1)} %shard_map.218.refs_1_), channel_id=1, source_target_pairs={{0,4},{4,0},{1,5},{5,1},{2,6},{6,2},{3,7},{7,3},{8,12},{12,8},{9,1... | collective-permute-start | bytes 786440 | tf_op jit(solution)/shard_map/ppermute | solution.py:553
  347.6 15.1 %copy-start.1 = (bf16[2,1,128,1024]{3,2,1,0:T(8,128)(2,1)S(1)}, bf16[2,1,128,1024]{3,2,1,0:T(8,128)(2,1)}, u32[]{:S(2)}) copy-start(bf16[2,1,128,1024]{3,2,1,0:T(8,128)(2,1)} %param.11) | copy-start | bytes 1572868
  350.9 10.7 %collective-permute-start.36 = (f32[128,512]{1,0:T(8,128)S(1)}, f32[128,512]{1,0:T(8,128)S(1)}, u32[]{:S(2)}, u32[]{:S(2)}) collective-permute-start(f32[128,512]{1,0:T(8,128)S(1)} %get-tuple-element.179), channel_id=1, source_target_pairs={{0,64},{64,0},{1,65},{65,1},{2,66},{66,2},{3,67},{67,3},{4,68},{68... | collective-permute-start | bytes 786440 | tf_op jit(solution)/shard_map/ppermute | solution.py:536
  353.0 8.6 %collective-permute-start.37 = (f32[136,256]{1,0:T(8,128)S(1)}, f32[136,256]{1,0:T(8,128)S(1)}, u32[]{:S(2)}, u32[]{:S(2)}) collective-permute-start(f32[136,256]{1,0:T(8,128)S(1)} %get-tuple-element.183), channel_id=1, source_target_pairs={{0,64},{64,0},{1,65},{65,1},{2,66},{66,2},{3,67},{67,3},{4,68},{68... | collective-permute-start | bytes 417800 | tf_op jit(solution)/shard_map/ppermute | solution.py:536

commit v8 on v7

--- a/solution.py
+++ b/solution.py
@@ -28,6 +28,161 @@
 
 def message(*shape):
     return pltpu.HBM(shape, BF)
+
+
+def fan(rows, columns):
+    return ("fan", pltpu.HBM((16, rows, columns), BF))
+
+
+class Source:
+    def __init__(self, copies, held):
+        self.copies, self.held = copies, held
+        self.shape, self.dtype = held.shape, held.dtype
+
+    def __getitem__(self, at):
+        key = at[1] if isinstance(at, tuple) and len(at) > 1 else at
+        if isinstance(key, int) and key in self.copies:
+            self.copies.pop(key).wait()
+        elif not isinstance(key, int) or None in self.copies:
+            self.settle()
+        return self.held[at]
+
+    def settle(self):
+        for key in list(self.copies):
+            self.copies.pop(key).wait()
+
+
+class Sink:
+    def __init__(self, place, held, next_sem, copies):
+        self.place, self.held, self.next_sem = place, held, next_sem
+        self.copies, self.sent, self.shape = copies, [], held.shape
+
+    def __setitem__(self, at, value):
+        self.held[at] = value
+
+    def __getitem__(self, at):
+        return self.held[at]
+
+    def send(self, at=None):
+        source = self.held if at is None else self.held.at[at]
+        for g in range(self.copies):
+            if self.copies > 1:
+                place = self.place.at[g] if at is None else self.place.at[g, at]
+            else:
+                place = self.place if at is None else self.place.at[at]
+            copy = pltpu.make_async_copy(source, place, self.next_sem())
+            copy.start()
+            self.sent.append(copy)
+
+    def settle(self):
+        for copy in self.sent:
+            copy.wait()
+
+
+def call_early(kernel, outs, ins, us=3, through=(), after=None, more=0):
+    m, k = len(outs), len(through)
+    kinds = [o[0] if isinstance(o, tuple) else "" for o in outs]
+    outs = [o[1] if isinstance(o, tuple) else o for o in outs]
+    specs, arrays, scratch, windows = [], [], [], []
+    for item in ins:
+        array, block, index = item if isinstance(item, tuple) else (item, item.shape, None)
+        arrays.append(array)
+        if block is None:
+            specs.append(pl.BlockSpec(memory_space=pltpu.SMEM))
+            windows.append(None)
+            continue
+        if index is None and jax.typeof(array).memory_space is not pltpu.HBM:
+            specs.append(pl.BlockSpec(memory_space=pltpu.VMEM))
+            windows.append(None)
+            continue
+        specs.append(pl.BlockSpec(memory_space=pl.ANY))
+        index = index or (0,) * len(block)
+        windows.append(tuple(slice(i * b, i * b + b) for i, b in zip(index, block)))
+        scratch.append(pltpu.VMEM(block, array.dtype))
+    out_specs = []
+    for kind, o in zip(kinds, outs):
+        if isinstance(o, jax.ShapeDtypeStruct):
+            out_specs.append(pl.BlockSpec(memory_space=pltpu.VMEM))
+            continue
+        out_specs.append(pl.BlockSpec(memory_space=pl.ANY))
+        scratch.append(pltpu.VMEM(o.shape[1:] if kind == "fan" else o.shape, o.dtype))
+    sem_count = more + sum(16 if kind == "fan" else 1 for kind in kinds)
+    for window, array in zip(windows, arrays):
+        if window is not None:
+            sem_count += 2 if len(window) == 4 else 4 if array.shape == (4, ROWS, D) else 1
+    extra = list(through) + ([] if after is None else [after])
+    n, e = len(ins), len(ins) + len(extra)
+
+    def body(*refs):
+        held, sems = list(refs[e + m + k : -1]), refs[-1]
+        used = []
+
+        def next_sem():
+            used.append(None)
+            return sems.at[len(used) - 1]
+
+        operands = []
+        for ref, window in zip(refs[:n], windows):
+            if window is None:
+                operands.append(ref)
+                continue
+            place = held.pop(0)
+            if len(window) == 4:
+                keys = {i: (slice(None), i) for i in range(2)}
+            elif place.shape == (4, ROWS, D):
+                keys = {i: (i,) for i in range(4)}
+            else:
+                keys = {None: ()}
+            copies = {}
+            for key, at in keys.items():
+                if len(window) == 4:
+                    source = ref.at[window[0], key, window[2], window[3]]
+                elif key is None:
+                    source = ref.at[window]
+                else:
+                    source = ref.at[key]
+                copies[key] = pltpu.make_async_copy(
+                    source, place.at[at] if at else place, next_sem()
+                )
+                copies[key].start()
+            operands.append(Source(copies, place))
+        sinks = [
+            ref
+            if isinstance(o, jax.ShapeDtypeStruct)
+            else Sink(ref, held.pop(0), next_sem, 16 if kind == "fan" else 1)
+            for kind, o, ref in zip(kinds, outs, refs[e : e + m])
+        ]
+        kernel(*operands, *sinks)
+        sinks = [o for o in sinks if isinstance(o, Sink)]
+        for o in operands:
+            if isinstance(o, Source):
+                o.settle()
+        for o in sinks:
+            if not o.sent:
+                o.send()
+        for o in sinks:
+            o.settle()
+
+    results = pl.pallas_call(
+        body,
+        out_shape=list(outs) + [pltpu.HBM(t.shape, t.dtype) for t in through],
+        in_specs=specs + [pl.BlockSpec(memory_space=pl.ANY)] * len(extra),
+        out_specs=out_specs + [pl.BlockSpec(memory_space=pl.ANY)] * k,
+        input_output_aliases={n + i: m + i for i in range(k)},
+        scratch_shapes=scratch + [pltpu.SemaphoreType.DMA((sem_count,))],
+        compiler_params=pltpu.CompilerParams(vmem_limit_bytes=48 * 1024 * 1024),
+        cost_estimate=pl.CostEstimate(
+            flops=0, bytes_accessed=us * 3_000_000, transcendentals=0
+        ),
+    )(
+        *arrays,
+        *[pltpu.with_memory_space_constraint(t, pltpu.HBM) for t in through],
+        *([] if after is None else [after]),
+    )
+    return [
+        pltpu.with_memory_space_constraint(r, pltpu.HBM) if kind == "kept" else r
+        for kind, r in zip(kinds + [""] * k, results)
+    ]
 
 
 def call(kernel, outs, ins, us=3, through=(), after=None):
@@ -88,6 +243,19 @@
     ]
 
 
+def send(ref, at=None):
+    if isinstance(ref, Sink):
+        ref.send(at)
+
+
+def fill(msg, rows, columns, value):
+    if isinstance(msg, Sink):
+        msg[rows, columns] = value
+    else:
+        for g in range(16):
+            msg[g, rows, columns] = value
+
+
 def nn(a, b):
     return jnp.dot(a, b, preferred_element_type=F32)
 
@@ -106,6 +274,10 @@
 
 def attn_tile(ref, yh):
     return ref[:, yh, 0:128, :].reshape(D, 256)
+
+
+def out_tile(ref, yh):
+    return ref[:, yh, :, :].reshape(D, 128)
 
 
 def ffn_tile(ref, yh, part):
@@ -170,13 +342,14 @@
 def project(x, lnp, bias, wm, wo, layer, n1, q, kv):
     normed = layer_norm(x, ln_row(lnp, layer, 0, 0), ln_row(lnp, layer, 0, 1)).astype(BF)
     n1[...] = normed
+    send(n1)
+    at = kv.shape[-2] - ROWS
     for k, side, yh in heads():
         tile = nn(normed, attn_tile((wm, wo)[side], yh))
         tile = tile + bias[yh, layer * 8 + side : layer * 8 + side + 1, :]
         q[k] = low_half(tile[:, 128:]).astype(BF)
-        pair = tile[:, :128].astype(BF)
-        for g in range(16):
-            kv[g, kv.shape[1] - ROWS :, k * 128 : k * 128 + 128] = pair
+        fill(kv, slice(at, at + ROWS), slice(k * 128, k * 128 + 128), tile[:, :128].astype(BF))
+    send(kv, slice(at, at + ROWS))
 
 
 def pack_kernel(core, *refs):
@@ -234,10 +407,10 @@
         [v[128:144, 512:768].astype(F32)[0:8] for v in (lower, upper)]
     ).astype(BF)
     tiles = lower[0:128, 512:768], upper[0:128, 512:768]
-    for g in range(16):
-        msg[g, 0:128, :] = tiles[0]
-        msg[g, 128:256, :] = tiles[1]
-        msg[g, 256:272, :] = small
+    msg[0:128, :] = tiles[0]
+    msg[128:256, :] = tiles[1]
+    msg[256:272, :] = small
+    msg.send()
     ffn0[...] = lower[0:128, 0:512]
     ffn1[...] = upper[0:128, 0:512]
 
@@ -251,10 +424,9 @@
             lnp[half, part, :] = jnp.concatenate([b[:, cols] for b in blocks], axis=1)
         for yh in range(2):
             bias[yh, part, :] = params[0, yh].astype(F32)[part]
+    msg[0:128, :] = piece[...]
+    msg.send(slice(0, 128))
     project(x[...].astype(F32), lnp, bias, wm, wo, 0, n1, q, msg)
-    rest = piece[...]
-    for g in range(16):
-        msg[g, 0:128, :] = rest
 
 
 def next_kernel(mid, p0, p1, p2, p3, lnp, bias, wm, wo, y, n1, q, msg):
@@ -264,10 +436,9 @@
 
 
 def attend_spread_kernel(first, q, kv, wm, wo, piece, part, prob, att, copies):
+    copies[...] = piece[...]
+    copies.send()
     attend_kernel(first, q, kv, wm, wo, part, prob, att)
-    rest = piece[...]
-    for g in range(16):
-        copies[g] = rest
 
 
 def attend_kernel(first, q, kv, wm, wo, part, prob, att):
@@ -282,9 +453,10 @@
         e = jnp.exp(scores - jnp.max(scores, axis=-1, keepdims=True))
         p = e / jnp.sum(e, axis=-1, keepdims=True)
         prob[k] = p
+        send(prob, k)
         mixed = high_half(nn(p.astype(BF), pair)).astype(BF)
         att[k] = mixed
-        term = nt(mixed, attn_tile((wm, wo)[side], yh)[:, 128:])
+        term = nt(mixed, out_tile((wm, wo)[side], yh))
         acc = term if acc is None else acc + term
     part[...] = acc.astype(BF)
 
@@ -292,8 +464,10 @@
 def feed(x, parts, lnp, bias, wm, wo, layer, part, mid, n2, pre, act):
     middle = x[...].astype(F32) + (total(parts) + ln_row(lnp, layer, 0, 2))
     mid[...] = middle
+    send(mid)
     normed = layer_norm(middle, ln_row(lnp, layer, 1, 0), ln_row(lnp, layer, 1, 1)).astype(BF)
     n2[...] = normed
+    send(n2)
     acc = None
     for k, side, yh in heads():
         w = (wm, wo)[side]
@@ -353,10 +527,11 @@
 
 
 def grad_ffn_kernel(n2, g, dpre, act, mine, other, sums, row):
+    first, second = n2[...].T, g[...].T
     for k, side, yh in heads():
         out = (mine, other)[side]
-        out[:, yh, :, 0:256] = tn(n2[...], dpre[k]).astype(BF).reshape(8, 128, 256)
-        out[:, yh, :, 256:512] = tn(g[...], act[k]).astype(BF).reshape(8, 128, 256)
+        out[:, yh, :, 0:256] = nn(first, dpre[k]).astype(BF).reshape(8, 128, 256)
+        out[:, yh, :, 256:512] = nn(second, act[k]).astype(BF).reshape(8, 128, 256)
         sums[k : k + 1, :] = jnp.sum(dpre[k].astype(F32), axis=0, keepdims=True)
     row[...] = jnp.sum(g[...].astype(F32), axis=0, keepdims=True)
 
@@ -365,21 +540,22 @@
     back, gg, gs = layer_norm_back(mid[...], ln_row(lnp, layer, 1, 0), total(parts))
     dm = g[...].astype(F32) + back
     dmid[...] = dm
+    send(dmid)
     low = dm.astype(BF)
     bg[...] = low
+    send(bg)
     rows[0:1, :] = gg
     rows[1:2, :] = gs
     rows[2:3, :] = jnp.sum(low.astype(F32), axis=0, keepdims=True)
-    at = dkv.shape[1] - ROWS
     for k, side, yh in heads():
         pair = kv[:, :, k * 128 : k * 128 + 128].reshape(16 * ROWS, 128)
-        da = high_half(nn(low, attn_tile((wm, wo)[side], yh)[:, 128:])).astype(BF)
+        da = high_half(nn(low, out_tile((wm, wo)[side], yh))).astype(BF)
         p = prob[k]
         dp = nt(da, pair)
         ds = (p * (dp - jnp.sum(p * dp, axis=-1, keepdims=True))).astype(BF)
         dq[k] = low_half(nn(ds, pair) * SCALE).astype(BF)
         both = tn(ds, q[k]) * SCALE + tn(p.astype(BF), da)
-        dkv[:, at:, k * 128 : k * 128 + 128] = both.astype(BF).reshape(16, ROWS, 128)
+        dkv[:, :, k * 128 : k * 128 + 128] = both.astype(BF).reshape(16, ROWS, 128)
 
 
 def attend_back_kernel(g, mid, p0, p1, p2, p3, lnp, wm, wo, prob, q, kv, dmid, bg, dq, dkv, rows):
@@ -399,7 +575,20 @@
 
 
 def add_kernel(gm, gr, msg):
-    add_into(msg, 0, gm, gr)
+    msg[...] = (gm[...] + gr[...]).reshape(4, 128, 512)
+
+
+def add_in_steps(gm, gr):
+    block = pl.BlockSpec((2, 2, 128, 512), lambda i: (i, 0, 0, 0))
+    return pl.pallas_call(
+        add_kernel,
+        grid=(4,),
+        out_shape=message(16, 128, 512),
+        in_specs=[block, block],
+        out_specs=pl.BlockSpec((4, 128, 512), lambda i: (i, 0, 0)),
+        compiler_params=pltpu.CompilerParams(vmem_limit_bytes=16 * 1024 * 1024),
+        cost_estimate=pl.CostEstimate(flops=0, bytes_accessed=9_000_000, transcendentals=0),
+    )(gm, gr)
 
 
 def join_kernel(fm, fr, am, ar, msg):
@@ -424,10 +613,11 @@
 
 
 def grad_attn_kernel(n1, bg, att, dproj, mine, other):
+    left, right = n1[...].T, bg[...].T
     for k, side, yh in heads():
         out = (mine, other)[side]
-        first = tn(n1[...], dproj[k])
-        second = tn(bg[...], att[k])
+        first = nn(left, dproj[k])
+        second = nn(right, att[k])
         out[:, yh, :, 0:128] = first[:, :128].astype(BF).reshape(8, 128, 128)
         out[:, yh, :, 128:] = (first[:, 128:] + second).astype(BF).reshape(8, 128, 128)
 
@@ -576,20 +766,23 @@
         + [pltpu.SemaphoreType.DMA((9,))],
         compiler_params=pltpu.CompilerParams(vmem_limit_bytes=48 * 1024 * 1024),
     )(core[0], *[pltpu.with_memory_space_constraint(w, pltpu.HBM) for w in weights])
-    msg, piece0, piece1 = call(
+    msg, piece0, piece1 = call_early(
         spread_kernel,
-        [message(16, 272, 256), sds(128, 512), sds(128, 512)],
+        [fan(272, 256), sds(128, 512), sds(128, 512)],
         [core, keep, swap_cores(send)],
     )
     u = exchange(msg).reshape(8, 2, 272, 256)
     uo = swap_cores(u)
     am = [(u, (8, 2, 128, 256), (0, 0, l, 0)) for l in range(2)]
     ao = [(uo, (8, 2, 128, 256), (0, 0, l, 0)) for l in range(2)]
+    outm = [(u, (8, 2, 128, 128), (0, 0, l, 1)) for l in range(2)]
+    outo = [(uo, (8, 2, 128, 128), (0, 0, l, 1)) for l in range(2)]
     kinds = dict(n1=kept(ROWS, D), q=kept(4, ROWS, 128))
-    n10, q0, msg, lnp, bias = call(
+    n10, q0, msg, lnp, bias = call_early(
         first_kernel,
-        [kinds["n1"], kinds["q"], message(16, 192, 512), kept(2, 16, D, dtype=F32), kept(2, 16, 256, dtype=F32)],
+        [kinds["n1"], kinds["q"], fan(192, 512), kept(2, 16, D, dtype=F32), kept(2, 16, 256, dtype=F32)],
         [x, (u, (8, 2, 16, 256), (0, 0, 16, 0)), am[0], ao[0], piece0],
+        more=16,
     )
     got0 = exchange(msg)
     kv0 = (got0, (16, ROWS, 512), (0, 2, 0))
@@ -600,13 +793,14 @@
         sds(ROWS, D), kept(ROWS, D, dtype=F32), kept(ROWS, D),
         kept(4, ROWS, 256, dtype=F32), kept(4, ROWS, 256),
     ]
-    part, prob0, att0, copies = call(
+    part, prob0, att0, copies = call_early(
         attend_spread_kernel,
-        attend_outs + [message(16, 128, 512)],
-        [(first, None, None), q0, kv0, am[0], ao[0], piece1],
+        attend_outs + [fan(128, 512)],
+        [(first, None, None), q0, kv0, outm[0], outo[0], piece1],
+        more=3,
     )
     f1 = exchange(copies)
-    part, mid0, n20, pre0, act0 = call(
+    part, mid0, n20, pre0, act0 = call_early(
         feed_kernel, feed_outs, [x, *all_parts(part), lnp, bias, f0, f0o]
     )
     y0, n11, q1, msg, f1 = call(
@@ -618,7 +812,7 @@
     f1 = f1.reshape(8, 2, 128, 512)
     f1o = swap_cores(f1)
     kv1 = exchange(msg)
-    part, prob1, att1 = call(attend_kernel, attend_outs, [(first, None, None), q1, kv1, am[1], ao[1]])
+    part, prob1, att1 = call_early(attend_kernel, attend_outs, [(first, None, None), q1, kv1, outm[1], outo[1]], more=3)
     last_part, mid1, n21, pre1, act1, dpre1, back = call(
         turn_kernel,
         [message(ROWS, D), *feed_outs[1:], kept(4, ROWS, 256), sds(ROWS, D)],
@@ -633,7 +827,7 @@
     dmid1, bg1, dq1, dkv, rows1, last_part = call(
         attend_back_kernel,
         back_outs + [message(16, ROWS, 512), rows_out],
-        [cot, mid1, *backs, lnp, am[1], ao[1], prob1, q1, kv1],
+        [cot, mid1, *backs, lnp, outm[1], outo[1], prob1, q1, kv1],
         through=[last_part],
     )
     dkv = exchange(dkv)
@@ -654,8 +848,8 @@
     far = other_half(acts)
     backs = all_parts(part)
     grad_attn_outs = [kept(8, 2, 128, 256), sds(8, 2, 128, 256)]
-    (l1,) = call(add_kernel, [message(16, 128, 512)], [gfm1, gfr1])
-    dx1, dpre0, part, head1, l1 = call(
+    l1 = add_in_steps(gfm1, gfr1)
+    dx1, dpre0, part, head1, l1 = call_early(
         hand_down_kernel,
         [kept(ROWS, D), kept(4, ROWS, 256), sds(ROWS, D), rows_out],
         [y0, dmid1, *backs, lnp, pre0, f0, f0o],
@@ -667,7 +861,7 @@
     dmid0, bg0, dq0, dkv, rows0 = call(
         attend_back_first_kernel,
         back_outs + [message(16, ROWS, 512), rows_out],
-        [dx1, mid0, *backs, lnp, am[0], ao[0], prob0, q0, kv0],
+        [dx1, mid0, *backs, lnp, outm[0], outo[0], prob0, q0, kv0],
     )
     _, dkv, l1 = call(mark_kernel, [sds(1, 128, dtype=F32)], [rows0], through=[dkv, l1])
     dkv = exchange(dkv)

time: 365 us -> 363 us (level)
    pallas_call x28 -> x21, Pallas kernels: 85 us -> 56.4 us  [call(): pl.pallas_call(body, grid=(1,), out_shape=list(outs) + [pltpu.HBM(t.shape...]
    pallas_call x0 -> x7, Pallas kernels: none -> 25.9 us  [the longest x6 21.7 us: call_early(): pl.pallas_call(body, out_shape=list(outs) + [pltpu.HBM(t.shape, t.dtype)...]
  transfers between devices with their start and end apart: 44 -> 44, of which waited for: 27 -> 26; matrix products, arithmetic and copies ran while one was open for 0% -> 0% of each run, Pallas kernels for 15% -> 14%
where the time goes in v8:
time: 363 us; the launch traced here: 360 us
  blocking collectives  101 us (28%)
  starting transfers between devices  95.3 us (26%)
  Pallas kernels  83.6 us (23%)
  waiting for transfers between devices  78.7 us (22%)
    all_to_all x3, blocking collectives, exchange(): return lax.all_to_all(v, axes, 0, 0, tiled=True)  101 us
    pallas_call x21, Pallas kernels, call(): pl.pallas_call(body, grid=(1,), out_shape=list(outs) + [pltpu.HBM(t.shape...  56.4 us
    all_to_all x6, waiting for transfers between devices, exchange(): return lax.all_to_all(v, axes, 0, 0, tiled=True)  40.9 us
    ppermute x12, starting transfers between devices, swap_cores(): return lax.ppermute(v, 's', [(0, 1), (1, 0)])  32 us
    all_to_all x6, starting transfers between devices, exchange(): return lax.all_to_all(v, axes, 0, 0, tiled=True)  30.7 us
    ppermute x24, waiting for transfers between devices, all_parts(): lax.ppermute(part, 'x', [(i, i ^ k) for i in range(4)])  30.4 us
    ppermute x24, starting transfers between devices, all_parts(): lax.ppermute(part, 'x', [(i, i ^ k) for i in range(4)])  26.4 us
    pallas_call x6, Pallas kernels, call_early(): pl.pallas_call(body, out_shape=list(outs) + [pltpu.HBM(t.shape, t.dtype)...  21.7 us
  transfers between devices with their start and end apart: 44, of which 26 were waited for; matrix products, arithmetic and copies ran while one was open for 0% of the time, Pallas kernels for 14%

profile of v8, /device:TPU:1, one launch (start us, length us, event | category | flops | bytes accessed | tf_op | source)
XLA Modules:
  0.0 360.1 jit_solution(18116936006837240811)
XLA Ops:
  0.7 1.4 shard_map.194
  2.1 1.5 collective-permute-start
  4.7 1.5 shard_map.195
  6.2 36.5 %all_to_all.45 = bf16[16,272,256]{2,1,0:T(8,128)(2,1)S(1)} all-to-all(bf16[16,272,256]{2,1,0:T(8,128)(2,1)} %get-tuple-element.104), channel_id=1, replica_groups=mesh['s'=2,'z'=4,'yl'=2,'yh'=2,'x'=4] {'z','yl','yh'}, dimensions={0} | all-to-all | bytes 4456448 | tf_op jit(solution)/shard_map/all_to_all | solution.py:735
  42.8 2.0 collective-permute-start.1
  44.8 4.1 %collective-permute-done.1.refs_3_.refs_4_.refs_8_ = bf16[8,2,272,256]{3,2,1,0:T(8,128)(2,1)} collective-permute-done((bf16[8,2,272,256]{3,2,1,0:T(8,128)(2,1)S(1)}, bf16[8,2,272,256]{3,2,1,0:T(8,128)(2,1)}, u32[]{:S(2)}, u32[]{:S(2)}) %collective-permute-start.1) | collective-permute-done | bytes 2228256 | tf_op jit(solution)/shard_map/ppermute | solution.py:726
  48.9 3.4 shard_map.196
  52.3 42.5 %all_to_all.46.refs_2_.refs_11_ = bf16[16,192,512]{2,1,0:T(8,128)(2,1)} all-to-all(bf16[16,192,512]{2,1,0:T(8,128)(2,1)} %get-tuple-element.107), channel_id=1, replica_groups=mesh['s'=2,'z'=4,'yl'=2,'yh'=2,'x'=4] {'z','yl','yh'}, dimensions={0} | all-to-all | bytes 6291456 | tf_op jit(solution)/shard_map/all_to_all | solution.py:735
  94.8 1.8 collective-permute-start.5
  96.6 5.3 %shard_map.197 = (bf16[64,1024]{1,0:T(8,128)(2,1)S(1)}, f32[4,64,1024]{2,1,0:T(8,128)}, bf16[4,64,128]{2,1,0:T(8,128)(2,1)}, bf16[16,128,512]{2,1,0:T(8,128)(2,1)}) custom-call(s32[1]{0:T(128)} %bitcast.2.refs_0_, bf16[4,64,128]{2,1,0:T(8,128)(2,1)} %get-tuple-element.106.refs_1_.refs_10_, bf16[16,192,512]{2,1,0:T(8,128)(2,1)} %all_to_all.46.refs_2_.refs_11_, ...), custom_call_target="tpu_custom_call" | custom-call | bytes 9000000 | tf_op jit(solution)/shard_map/pallas_call | solution.py:166
  101.9 4.4 %all-to-all-start.2 = ((bf16[16,128,512]{2,1,0:T(8,128)(2,1)}), bf16[16,128,512]{2,1,0:T(8,128)(2,1)}, u32[]{:S(2)}, u32[]{:S(2)}) async-start(bf16[16,128,512]{2,1,0:T(8,128)(2,1)} %get-tuple-element.114), calls=%async_computation.2 | async-start | bytes 4194304 | tf_op jit(solution)/shard_map/all_to_all | solution.py:735
  106.4 2.5 collective-permute-start.4
  109.7 4.8 %collective-permute-done.4.refs_4_ = bf16[64,1024]{1,0:T(8,128)(2,1)S(1)} collective-permute-done((bf16[64,1024]{1,0:T(8,128)(2,1)S(1)}, bf16[64,1024]{1,0:T(8,128)(2,1)S(1)}, u32[]{:S(2)}, u32[]{:S(2)}) %collective-permute-start.4) | collective-permute-done | bytes 131104 | tf_op jit(solution)/shard_map/ppermute | solution.py:730
  116.0 3.7 %shard_map.198 = (bf16[64,1024]{1,0:T(8,128)(2,1)S(1)}, f32[64,1024]{1,0:T(8,128)}, bf16[64,1024]{1,0:T(8,128)(2,1)}, f32[4,64,256]{2,1,0:T(8,128)}, bf16[4,64,256]{2,1,0:T(8,128)(2,1)}) custom-call(bf16[64,1024]{1,0:T(8,128)(2,1)S(1)} %dynamic-slice_bitcast_fusion.1.refs_0_.refs_2_, bf16[64,1024]{1,0:T(8,128)(2,1)S(1)} %get-tuple-element.109.refs_1_, ...), custom_call_target="tpu_custom_call" | custom-call | bytes 9000000 | tf_op jit(solution)/shard_map/pallas_call | solution.py:166
  119.7 2.5 collective-permute-start.8
  123.0 11.7 %all-to-all-done.2.refs_9_ = bf16[16,128,512]{2,1,0:T(8,128)(2,1)} async-done(((bf16[16,128,512]{2,1,0:T(8,128)(2,1)}), bf16[16,128,512]{2,1,0:T(8,128)(2,1)}, u32[]{:S(2)}, u32[]{:S(2)}) %all-to-all-start.2) | async-done | bytes 2097184 | tf_op jit(solution)/shard_map/all_to_all | solution.py:735
  134.7 3.3 shard_map.199
  138.8 21.5 %all_to_all.47.refs_2_.refs_11_ = bf16[16,64,512]{2,1,0:T(8,128)(2,1)S(1)} all-to-all(bf16[16,64,512]{2,1,0:T(8,128)(2,1)} %get-tuple-element.117), channel_id=1, replica_groups=mesh['s'=2,'z'=4,'yl'=2,'yh'=2,'x'=4] {'z','yl','yh'}, dimensions={0} | all-to-all | bytes 2097152 | tf_op jit(solution)/shard_map/all_to_all | solution.py:735
  160.4 4.1 %shard_map.200 = (bf16[64,1024]{1,0:T(8,128)(2,1)S(1)}, f32[4,64,1024]{2,1,0:T(8,128)}, bf16[4,64,128]{2,1,0:T(8,128)(2,1)}) custom-call(s32[1]{0:T(128)} %bitcast.2.refs_0_, bf16[4,64,128]{2,1,0:T(8,128)(2,1)} %get-tuple-element.116.refs_1_.refs_10_, bf16[16,64,512]{2,1,0:T(8,128)(2,1)S(1)} %all_to_all.47.refs_2_.refs_11_, ...), custom_call_target="tpu_custom_call" | custom-call | bytes 9000000 | tf_op jit(solution)/shard_map/pallas_call | solution.py:166
  164.5 2.5 collective-permute-start.11
  168.7 2.1 collective-permute-done.11.refs_4_
  170.8 1.6 collective-permute-done.10.refs_3_
  172.4 5.1 %shard_map.201 = (bf16[64,1024]{1,0:T(8,128)(2,1)}, f32[64,1024]{1,0:T(8,128)}, bf16[64,1024]{1,0:T(8,128)(2,1)}, f32[4,64,256]{2,1,0:T(8,128)}, bf16[4,64,256]{...) custom-call(bf16[64,1024]{1,0:T(8,128)(2,1)S(1)} %get-tuple-element.115.refs_0_.refs_1_, ...), custom_call_target="tpu_custom_call" | custom-call | bytes 9000000 | tf_op jit(solution)/shard_map/pallas_call | solution.py:228
  177.5 2.5 collective-permute-start.15
  180.8 2.5 collective-permute-done.15.refs_5_
  183.3 2.0 collective-permute-done.14.refs_4_
  185.3 5.5 %shard_map.202 = (f32[64,1024]{1,0:T(8,128)}, bf16[64,1024]{1,0:T(8,128)(2,1)}, bf16[4,64,128]{2,1,0:T(8,128)(2,1)}, bf16[16,64,512]{2,1,0:T(8,128)(2,1)}, f32[8,1024]{1,0:T(8,128)}, /*index=5*/bf16[64,1024]{1,0:T(8,128)(2,1)}) custom-call(bf16[64,1024]{1,0:T(8,128)(2,1)S(1)} %dynamic-slice_bitcast_fusion.refs_9_.refs_0_.refs_1_, ...), custom_call_target="tpu_custom_call", output_to_operand_aliasing={{5}: (12, {})} | custom-call | bytes 9000000 | tf_op jit(solution)/shard_map/pallas_call | solution.py:228
  190.8 3.9 %shard_map.206 = (bf16[8,2,128,512]{3,2,1,0:T(8,128)(2,1)}, bf16[8,2,128,512]{3,2,1,0:T(8,128)(2,1)}, f32[4,256]{1,0:T(4,128)}, f32[1,1024]{1,0:T(1,128)}) custom-call(bf16[64,1024]{1,0:T(8,128)(2,1)} %get-tuple-element.132.refs_0_, bf16[64,1024]{1,0:T(8,128)(2,1)S(1)} %dynamic-slice_bitcast_fusion.refs_9_.refs_0_.refs_1_, ...), custom_call_target="tpu_custom_call" | custom-call | bytes 9000000 | tf_op jit(solution)/shard_map/pallas_call | solution.py:228
  194.7 4.1 %collective-permute-start.23 = (bf16[8,2,128,512]{3,2,1,0:T(8,128)(2,1)}, bf16[8,2,128,512]{3,2,1,0:T(8,128)(2,1)}, u32[]{:S(2)}, u32[]{:S(2)}) collective-permute-start(bf16[8,2,128,512]{3,2,1,0:T(8,128)(2,1)} %get-tuple-element.137), channel_id=1, source_target_pairs={{0,64},{64,0},{1,65},{65,1},{2,66},{66,2},{3,67},{67,3},{4,68},{68... | collective-permute-start | bytes 6291464 | tf_op jit(solution)/shard_map/ppermute | solution.py:726
  198.8 4.5 %all-to-all-start.4 = ((bf16[16,64,512]{2,1,0:T(8,128)(2,1)}), bf16[16,64,512]{2,1,0:T(8,128)(2,1)}, u32[]{:S(2)}, u32[]{:S(2)}) async-start(bf16[16,64,512]{2,1,0:T(8,128)(2,1)} %get-tuple-element.125), calls=%async_computation.4 | async-start | bytes 2097152 | tf_op jit(solution)/shard_map/all_to_all | solution.py:735
  203.3 1.8 collective-permute-start.18
  206.6 4.8 %collective-permute-done.18.refs_6_ = bf16[64,1024]{1,0:T(8,128)(2,1)S(1)} collective-permute-done((bf16[64,1024]{1,0:T(8,128)(2,1)S(1)}, bf16[64,1024]{1,0:T(8,128)(2,1)S(1)}, u32[]{:S(2)}, u32[]{:S(2)}) %collective-permute-start.18) | collective-permute-done | bytes 131104 | tf_op jit(solution)/shard_map/ppermute | solution.py:730
  213.7 1.4 collective-permute-start.19
  216.8 2.0 all-to-all-done.4.refs_0_
  218.7 2.9 shard_map.205
  221.6 3.0 collective-permute-start.24
  224.6 1.7 collective-permute-start.22
  227.9 4.2 %shard_map.207.refs_10_ = bf16[16,128,512]{2,1,0:T(8,128)(2,1)} custom-call(bf16[8,2,128,512]{3,2,1,0:T(8,128)(2,1)} %get-tuple-element.136.gm, bf16[8,2,128,512]{3,2,1,0:T(8,128)(2,1)} %collective-permute-done.23.gr), custom_call_target="tpu_custom_call" | custom-call | bytes 9000000 | tf_op jit(solution)/shard_map/pallas_call | solution.py:583
  232.3 3.8 %shard_map.208 = (bf16[64,1024]{1,0:T(8,128)(2,1)}, bf16[4,64,256]{2,1,0:T(8,128)(2,1)}, bf16[64,1024]{1,0:T(8,128)(2,1)S(1)}, f32[8,1024]{1,0:T(8,128)}, bf16[16,128,512]{2,1,0:T(8,128)(2,1)}) custom-call(bf16[64,1024]{1,0:T(8,128)(2,1)S(1)} %get-tuple-element.115.refs_0_.refs_1_, ...), custom_call_target="tpu_custom_call", output_to_operand_aliasing={{4}: (10, {})} | custom-call | bytes 9000000 | tf_op jit(solution)/shard_map/pallas_call | solution.py:166
  236.1 4.4 %all-to-all-start.5 = ((bf16[16,128,512]{2,1,0:T(8,128)(2,1)}), bf16[16,128,512]{2,1,0:T(8,128)(2,1)}, u32[]{:S(2)}, u32[]{:S(2)}) async-start(bf16[16,128,512]{2,1,0:T(8,128)(2,1)} %get-tuple-element.145), calls=%async_computation.5 | async-start | bytes 4194304 | tf_op jit(solution)/shard_map/all_to_all | solution.py:735
  240.6 1.7 collective-permute-start.27
  242.2 1.4 collective-permute-start.26
  243.9 1.8 collective-permute-done.27.refs_5_
  245.7 1.9 collective-permute-done.26.refs_4_
  247.9 5.9 %shard_map.209 = (f32[64,1024]{1,0:T(8,128)}, bf16[64,1024]{1,0:T(8,128)(2,1)}, bf16[4,64,128]{2,1,0:T(8,128)(2,1)}, bf16[16,64,512]{2,1,0:T(8,128)(2,1)}, f32[8,1024]{1,0:T(8,128)}) custom-call(bf16[64,1024]{1,0:T(8,128)(2,1)} %get-tuple-element.139.refs_0_.refs_1_, f32[64,1024]{1,0:T(8,128)} %get-tuple-element.112.refs_0_.refs_1_, ...), custom_call_target="tpu_custom_call" | custom-call | bytes 9000000 | tf_op jit(solution)/shard_map/pallas_call | solution.py:228
  253.8 3.8 %shard_map.211 = (bf16[8,2,128,512]{3,2,1,0:T(8,128)(2,1)}, bf16[8,2,128,512]{3,2,1,0:T(8,128)(2,1)}, f32[4,256]{1,0:T(4,128)}, f32[1,1024]{1,0:T(1,128)}) custom-call(bf16[64,1024]{1,0:T(8,128)(2,1)} %get-tuple-element.148.refs_0_, bf16[64,1024]{1,0:T(8,128)(2,1)} %get-tuple-element.139.refs_0_.refs_1_, bf16[4,64,256]{2,1,0:T(8,128)(2,1)} %get-tuple-element.149.refs_2_, ...), custom_call_target="tpu_custom_call" | custom-call | bytes 9000000 | tf_op jit(solution)/shard_map/pallas_call | solution.py:228
  257.7 4.0 %collective-permute-start.28 = (bf16[8,2,128,512]{3,2,1,0:T(8,128)(2,1)}, bf16[8,2,128,512]{3,2,1,0:T(8,128)(2,1)}, u32[]{:S(2)}, u32[]{:S(2)}) collective-permute-start(bf16[8,2,128,512]{3,2,1,0:T(8,128)(2,1)} %get-tuple-element.152), channel_id=1, source_target_pairs={{0,64},{64,0},{1,65},{65,1},{2,66},{66,2},{3,67},{67,3},{4,68},{68... | collective-permute-start | bytes 6291464 | tf_op jit(solution)/shard_map/ppermute | solution.py:726
  261.6 3.1 shard_map.212
  267.0 5.8 %all-to-all-start.6 = ((bf16[16,64,512]{2,1,0:T(8,128)(2,1)}), bf16[16,64,512]{2,1,0:T(8,128)(2,1)}, u32[]{:S(2)}, u32[]{:S(2)}) async-start(bf16[16,64,512]{2,1,0:T(8,128)(2,1)} %get-tuple-element.146), calls=%async_computation.6 | async-start | bytes 2097152 | tf_op jit(solution)/shard_map/all_to_all | solution.py:735
  272.8 4.8 %shard_map.213.refs_4_ = bf16[16,128,768]{2,1,0:T(8,128)(2,1)} custom-call(bf16[8,2,128,512]{3,2,1,0:T(8,128)(2,1)} %get-tuple-element.151.refs_0_, bf16[8,2,128,512]{3,2,1,0:T(8,128)(2,1)} %collective-permute-done.28.refs_1_, bf16[8,2,128,256]{3,2,1,0:T(8,128)(2,1)} %get-tuple-element.157.refs_2_, bf16[8,2,128,256]{3,2,1,0:T(8,128)(2,1)} %collective-permute-done.29.refs_3_), custom_call_target="tpu_custom_call" | custom-call | bytes 9000000 | tf_op jit(solution)/shard_map/pallas_call | solution.py:228
  277.6 8.0 %all-to-all-done.6.refs_0_ = bf16[16,64,512]{2,1,0:T(8,128)(2,1)} async-done(((bf16[16,64,512]{2,1,0:T(8,128)(2,1)}), bf16[16,64,512]{2,1,0:T(8,128)(2,1)}, u32[]{:S(2)}, u32[]{:S(2)}) %all-to-all-start.6) | async-done | bytes 1048608 | tf_op jit(solution)/shard_map/all_to_all | solution.py:735
  285.6 2.9 shard_map.214
  288.5 5.4 %all-to-all-start.7 = ((bf16[16,128,768]{2,1,0:T(8,128)(2,1)}), bf16[16,128,768]{2,1,0:T(8,128)(2,1)}, u32[]{:S(2)}, u32[]{:S(2)}) async-start(bf16[16,128,768]{2,1,0:T(8,128)(2,1)} %get-tuple-element.176), calls=%async_computation.7 | async-start | bytes 6291456 | tf_op jit(solution)/shard_map/all_to_all | solution.py:735
  293.9 2.8 shard_map.215
  296.6 3.7 %collective-permute-start.33 = (bf16[8,2,128,256]{3,2,1,0:T(8,128)(2,1)S(1)}, bf16[8,2,128,256]{3,2,1,0:T(8,128)(2,1)S(1)}, u32[]{:S(2)}, u32[]{:S(2)}) collective-permute-start(bf16[8,2,128,256]{3,2,1,0:T(8,128)(2,1)S(1)} %get-tuple-element.165), channel_id=1, source_target_pairs={{0,64},{64,0},{1,65},{65,1},{2,66},{66,2},{3,67},{67,3},{4,68},{68... | collective-permute-start | bytes 3145736 | tf_op jit(solution)/shard_map/ppermute | solution.py:726
  300.3 1.6 collective-permute-start.32
  304.4 4.9 %collective-permute-done.32.refs_7_ = bf16[64,1024]{1,0:T(8,128)(2,1)S(1)} collective-permute-done((bf16[64,1024]{1,0:T(8,128)(2,1)S(1)}, bf16[64,1024]{1,0:T(8,128)(2,1)S(1)}, u32[]{:S(2)}, u32[]{:S(2)}) %collective-permute-start.32) | collective-permute-done | bytes 131104 | tf_op jit(solution)/shard_map/ppermute | solution.py:730
  309.8 3.2 shard_map.217
  313.0 17.6 %all-to-all-done.7.refs_1_ = bf16[16,128,768]{2,1,0:T(8,128)(2,1)} async-done(((bf16[16,128,768]{2,1,0:T(8,128)(2,1)}), bf16[16,128,768]{2,1,0:T(8,128)(2,1)}, u32[]{:S(2)}, u32[]{:S(2)}) %all-to-all-start.7) | async-done | bytes 3145760 | tf_op jit(solution)/shard_map/all_to_all | solution.py:735
  330.7 6.2 %all-to-all-start.8 = ((bf16[16,144,256]{2,1,0:T(8,128)(2,1)}), bf16[16,144,256]{2,1,0:T(8,128)(2,1)S(1)}, u32[]{:S(2)}, u32[]{:S(2)}) async-start(bf16[16,144,256]{2,1,0:T(8,128)(2,1)} %get-tuple-element.180), calls=%async_computation.8 | async-start | bytes 2359296 | tf_op jit(solution)/shard_map/all_to_all | solution.py:735
  336.9 4.2 %collective-permute-start.34 = (bf16[64,1024]{1,0:T(8,128)(2,1)S(1)}, bf16[64,1024]{1,0:T(8,128)(2,1)S(1)}, u32[]{:S(2)}, u32[]{:S(2)}) collective-permute-start(bf16[64,1024]{1,0:T(8,128)(2,1)S(1)} %get-tuple-element.175), channel_id=1, source_target_pairs={{0,64},{64,0},{1,65},{65,1},{2,66},{66,2},{3,67},{67,3},{4,68},{68... | collective-permute-start | bytes 393224 | tf_op jit(solution)/shard_map/ppermute | solution.py:726
  342.1 3.1 collective-permute-start.35
  345.3 3.3 shard_map.220
  350.0 7.9 %collective-permute-start.37 = (f32[136,256]{1,0:T(8,128)S(1)}, f32[136,256]{1,0:T(8,128)S(1)}, u32[]{:S(2)}, u32[]{:S(2)}) collective-permute-start(f32[136,256]{1,0:T(8,128)S(1)} %get-tuple-element.183), channel_id=1, source_target_pairs={{0,64},{64,0},{1,65},{65,1},{2,66},{66,2},{3,67},{67,3},{4,68},{68... | collective-permute-start | bytes 417800 | tf_op jit(solution)/shard_map/ppermute | solution.py:726
  (66 shorter events, 25.6 us)
Async XLA Ops:
  0.6 44.2 %copy-start = (bf16[2,1,128,1024]{3,2,1,0:T(8,128)(2,1)S(1)}, bf16[2,1,128,1024]{3,2,1,0:T(8,128)(2,1)}, u32[]{:S(2)}) copy-start(bf16[2,1,128,1024]{3,2,1,0:T(8,128)(2,1)} %param.11) | copy-start | bytes 1572868
  2.1 2.6 collective-permute-start
  42.8 6.1 %collective-permute-start.1 = (bf16[8,2,272,256]{3,2,1,0:T(8,128)(2,1)S(1)}, bf16[8,2,272,256]{3,2,1,0:T(8,128)(2,1)}, u32[]{:S(2)}, u32[]{:S(2)}) collective-permute-start(bf16[8,2,272,256]{3,2,1,0:T(8,128)(2,1)S(1)} %bitcast.37), channel_id=1, source_target_pairs={{0,64},{64,0},{1,65},{65,1},{2,66},{66,2},{3,67},{67,3},{4,68},{68... | collective-permute-start | bytes 6684680 | tf_op jit(solution)/shard_map/ppermute | solution.py:726
  94.8 21.2 %collective-permute-start.5 = (bf16[16,192,512]{2,1,0:T(8,128)(2,1)}, bf16[16,192,512]{2,1,0:T(8,128)(2,1)}, u32[]{:S(2)}, u32[]{:S(2)}) collective-permute-start(bf16[16,192,512]{2,1,0:T(8,128)(2,1)} %all_to_all.46.refs_2_.refs_11_), channel_id=1, source_target_pairs={{0,64},{64,0},{1,65},{65,1},{2,66},{66,2},{3,67},{67,3},{4,68},{68... | collective-permute-start | bytes 9437192 | tf_op jit(solution)/shard_map/ppermute | solution.py:726
  101.9 32.8 %all-to-all-start.2 = ((bf16[16,128,512]{2,1,0:T(8,128)(2,1)}), bf16[16,128,512]{2,1,0:T(8,128)(2,1)}, u32[]{:S(2)}, u32[]{:S(2)}) async-start(bf16[16,128,512]{2,1,0:T(8,128)(2,1)} %get-tuple-element.114), calls=%async_computation.2 | async-start | bytes 4194304 | tf_op jit(solution)/shard_map/all_to_all | solution.py:735
  106.4 8.1 %collective-permute-start.4 = (bf16[64,1024]{1,0:T(8,128)(2,1)S(1)}, bf16[64,1024]{1,0:T(8,128)(2,1)S(1)}, u32[]{:S(2)}, u32[]{:S(2)}) collective-permute-start(bf16[64,1024]{1,0:T(8,128)(2,1)S(1)} %get-tuple-element.109.refs_1_), channel_id=1, source_target_pairs={{0,3},{1,2},{2,1},{3,0},{4,7},{5,6},{6,5},{7,4},{8,11},{9,10},{10,... | collective-permute-start | bytes 393224 | tf_op jit(solution)/shard_map/ppermute | solution.py:730
  108.9 6.4 %collective-permute-start.3 = (bf16[64,1024]{1,0:T(8,128)(2,1)S(1)}, bf16[64,1024]{1,0:T(8,128)(2,1)S(1)}, u32[]{:S(2)}, u32[]{:S(2)}) collective-permute-start(bf16[64,1024]{1,0:T(8,128)(2,1)S(1)} %get-tuple-element.109.refs_1_), channel_id=1, source_target_pairs={{0,2},{1,3},{2,0},{3,1},{4,6},{5,7},{6,4},{7,5},{8,10},{9,11},{10,... | collective-permute-start | bytes 393224 | tf_op jit(solution)/shard_map/ppermute | solution.py:730
  109.4 6.6 %collective-permute-start.2 = (bf16[64,1024]{1,0:T(8,128)(2,1)S(1)}, bf16[64,1024]{1,0:T(8,128)(2,1)S(1)}, u32[]{:S(2)}, u32[]{:S(2)}) collective-permute-start(bf16[64,1024]{1,0:T(8,128)(2,1)S(1)} %get-tuple-element.109.refs_1_), channel_id=1, source_target_pairs={{0,1},{1,0},{2,3},{3,2},{4,5},{5,4},{6,7},{7,6},{8,9},{9,8},{10,11... | collective-permute-start | bytes 393224 | tf_op jit(solution)/shard_map/ppermute | solution.py:730
  119.7 15.0 %collective-permute-start.8 = (bf16[64,1024]{1,0:T(8,128)(2,1)S(1)}, bf16[64,1024]{1,0:T(8,128)(2,1)S(1)}, u32[]{:S(2)}, u32[]{:S(2)}) collective-permute-start(bf16[64,1024]{1,0:T(8,128)(2,1)S(1)} %get-tuple-element.113.refs_1_), channel_id=1, source_target_pairs={{0,3},{1,2},{2,1},{3,0},{4,7},{5,6},{6,5},{7,4},{8,11},{9,10},{10,... | collective-permute-start | bytes 393224 | tf_op jit(solution)/shard_map/ppermute | solution.py:730
  122.2 12.5 %collective-permute-start.7 = (bf16[64,1024]{1,0:T(8,128)(2,1)S(1)}, bf16[64,1024]{1,0:T(8,128)(2,1)S(1)}, u32[]{:S(2)}, u32[]{:S(2)}) collective-permute-start(bf16[64,1024]{1,0:T(8,128)(2,1)S(1)} %get-tuple-element.113.refs_1_), channel_id=1, source_target_pairs={{0,2},{1,3},{2,0},{3,1},{4,6},{5,7},{6,4},{7,5},{8,10},{9,11},{10,... | collective-permute-start | bytes 393224 | tf_op jit(solution)/shard_map/ppermute | solution.py:730
  122.8 12.0 %collective-permute-start.6 = (bf16[64,1024]{1,0:T(8,128)(2,1)S(1)}, bf16[64,1024]{1,0:T(8,128)(2,1)S(1)}, u32[]{:S(2)}, u32[]{:S(2)}) collective-permute-start(bf16[64,1024]{1,0:T(8,128)(2,1)S(1)} %get-tuple-element.113.refs_1_), channel_id=1, source_target_pairs={{0,1},{1,0},{2,3},{3,2},{4,5},{5,4},{6,7},{7,6},{8,9},{9,8},{10,11... | collective-permute-start | bytes 393224 | tf_op jit(solution)/shard_map/ppermute | solution.py:730
  138.0 34.4 %collective-permute-start.12 = (bf16[8,2,128,512]{3,2,1,0:T(8,128)(2,1)}, bf16[8,2,128,512]{3,2,1,0:T(8,128)(2,1)S(1)}, u32[]{:S(2)}, u32[]{:S(2)}) collective-permute-start(bf16[8,2,128,512]{3,2,1,0:T(8,128)(2,1)} %bitcast.16.refs_7_), channel_id=1, source_target_pairs={{0,64},{64,0},{1,65},{65,1},{2,66},{66,2},{3,67},{67,3},{4,68},{68... | collective-permute-start | bytes 6291464 | tf_op jit(solution)/shard_map/ppermute | solution.py:726
  164.5 6.3 %collective-permute-start.11 = (bf16[64,1024]{1,0:T(8,128)(2,1)S(1)}, bf16[64,1024]{1,0:T(8,128)(2,1)S(1)}, u32[]{:S(2)}, u32[]{:S(2)}) collective-permute-start(bf16[64,1024]{1,0:T(8,128)(2,1)S(1)} %get-tuple-element.118.refs_1_), channel_id=1, source_target_pairs={{0,3},{1,2},{2,1},{3,0},{4,7},{5,6},{6,5},{7,4},{8,11},{9,10},{10,... | collective-permute-start | bytes 393224 | tf_op jit(solution)/shard_map/ppermute | solution.py:730
  167.0 5.4 %collective-permute-start.10 = (bf16[64,1024]{1,0:T(8,128)(2,1)S(1)}, bf16[64,1024]{1,0:T(8,128)(2,1)S(1)}, u32[]{:S(2)}, u32[]{:S(2)}) collective-permute-start(bf16[64,1024]{1,0:T(8,128)(2,1)S(1)} %get-tuple-element.118.refs_1_), channel_id=1, source_target_pairs={{0,2},{1,3},{2,0},{3,1},{4,6},{5,7},{6,4},{7,5},{8,10},{9,11},{10,... | collective-permute-start | bytes 393224 | tf_op jit(solution)/shard_map/ppermute | solution.py:730
  167.5 4.9 %collective-permute-start.9 = (bf16[64,1024]{1,0:T(8,128)(2,1)S(1)}, bf16[64,1024]{1,0:T(8,128)(2,1)S(1)}, u32[]{:S(2)}, u32[]{:S(2)}) collective-permute-start(bf16[64,1024]{1,0:T(8,128)(2,1)S(1)} %get-tuple-element.118.refs_1_), channel_id=1, source_target_pairs={{0,1},{1,0},{2,3},{3,2},{4,5},{5,4},{6,7},{7,6},{8,9},{9,8},{10,11... | collective-permute-start | bytes 393224 | tf_op jit(solution)/shard_map/ppermute | solution.py:730
  177.5 5.8 %collective-permute-start.15 = (bf16[64,1024]{1,0:T(8,128)(2,1)S(1)}, bf16[64,1024]{1,0:T(8,128)(2,1)S(1)}, u32[]{:S(2)}, u32[]{:S(2)}) collective-permute-start(bf16[64,1024]{1,0:T(8,128)(2,1)S(1)} %get-tuple-element.121.refs_2_), channel_id=1, source_target_pairs={{0,3},{1,2},{2,1},{3,0},{4,7},{5,6},{6,5},{7,4},{8,11},{9,10},{10,... | collective-permute-start | bytes 393224 | tf_op jit(solution)/shard_map/ppermute | solution.py:730
  180.0 5.3 %collective-permute-start.14 = (bf16[64,1024]{1,0:T(8,128)(2,1)S(1)}, bf16[64,1024]{1,0:T(8,128)(2,1)S(1)}, u32[]{:S(2)}, u32[]{:S(2)}) collective-permute-start(bf16[64,1024]{1,0:T(8,128)(2,1)S(1)} %get-tuple-element.121.refs_2_), channel_id=1, source_target_pairs={{0,2},{1,3},{2,0},{3,1},{4,6},{5,7},{6,4},{7,5},{8,10},{9,11},{10,... | collective-permute-start | bytes 393224 | tf_op jit(solution)/shard_map/ppermute | solution.py:730
  180.3 5.1 %collective-permute-start.13 = (bf16[64,1024]{1,0:T(8,128)(2,1)S(1)}, bf16[64,1024]{1,0:T(8,128)(2,1)S(1)}, u32[]{:S(2)}, u32[]{:S(2)}) collective-permute-start(bf16[64,1024]{1,0:T(8,128)(2,1)S(1)} %get-tuple-element.121.refs_2_), channel_id=1, source_target_pairs={{0,1},{1,0},{2,3},{3,2},{4,5},{5,4},{6,7},{7,6},{8,9},{9,8},{10,11... | collective-permute-start | bytes 393224 | tf_op jit(solution)/shard_map/ppermute | solution.py:730
  190.8 12.4 %copy-start.3 = (bf16[64,1024]{1,0:T(8,128)(2,1)S(1)}, bf16[64,1024]{1,0:T(8,128)(2,1)}, u32[]{:S(2)}) copy-start(bf16[64,1024]{1,0:T(8,128)(2,1)} %get-tuple-element.127.refs_3_) | copy-start | bytes 393220
  194.7 33.1 %collective-permute-start.23 = (bf16[8,2,128,512]{3,2,1,0:T(8,128)(2,1)}, bf16[8,2,128,512]{3,2,1,0:T(8,128)(2,1)}, u32[]{:S(2)}, u32[]{:S(2)}) collective-permute-start(bf16[8,2,128,512]{3,2,1,0:T(8,128)(2,1)} %get-tuple-element.137), channel_id=1, source_target_pairs={{0,64},{64,0},{1,65},{65,1},{2,66},{66,2},{3,67},{67,3},{4,68},{68... | collective-permute-start | bytes 6291464 | tf_op jit(solution)/shard_map/ppermute | solution.py:726
  198.8 20.0 %all-to-all-start.4 = ((bf16[16,64,512]{2,1,0:T(8,128)(2,1)}), bf16[16,64,512]{2,1,0:T(8,128)(2,1)}, u32[]{:S(2)}, u32[]{:S(2)}) async-start(bf16[16,64,512]{2,1,0:T(8,128)(2,1)} %get-tuple-element.125), calls=%async_computation.4 | async-start | bytes 2097152 | tf_op jit(solution)/shard_map/all_to_all | solution.py:735
  203.3 8.1 %collective-permute-start.18 = (bf16[64,1024]{1,0:T(8,128)(2,1)S(1)}, bf16[64,1024]{1,0:T(8,128)(2,1)S(1)}, u32[]{:S(2)}, u32[]{:S(2)}) collective-permute-start(bf16[64,1024]{1,0:T(8,128)(2,1)S(1)} %copy-done.3), channel_id=1, source_target_pairs={{0,3},{1,2},{2,1},{3,0},{4,7},{5,6},{6,5},{7,4},{8,11},{9,10},{10,... | collective-permute-start | bytes 393224 | tf_op jit(solution)/shard_map/ppermute | solution.py:730
  205.0 6.3 %collective-permute-start.17 = (bf16[64,1024]{1,0:T(8,128)(2,1)S(1)}, bf16[64,1024]{1,0:T(8,128)(2,1)S(1)}, u32[]{:S(2)}, u32[]{:S(2)}) collective-permute-start(bf16[64,1024]{1,0:T(8,128)(2,1)S(1)} %copy-done.3), channel_id=1, source_target_pairs={{0,2},{1,3},{2,0},{3,1},{4,6},{5,7},{6,4},{7,5},{8,10},{9,11},{10,... | collective-permute-start | bytes 393224 | tf_op jit(solution)/shard_map/ppermute | solution.py:730
  205.4 7.2 %collective-permute-start.16 = (bf16[64,1024]{1,0:T(8,128)(2,1)S(1)}, bf16[64,1024]{1,0:T(8,128)(2,1)S(1)}, u32[]{:S(2)}, u32[]{:S(2)}) collective-permute-start(bf16[64,1024]{1,0:T(8,128)(2,1)S(1)} %copy-done.3), channel_id=1, source_target_pairs={{0,1},{1,0},{2,3},{3,2},{4,5},{5,4},{6,7},{7,6},{8,9},{9,8},{10,11... | collective-permute-start | bytes 393224 | tf_op jit(solution)/shard_map/ppermute | solution.py:730
  213.7 2.3 collective-permute-start.19
  221.6 10.7 %collective-permute-start.24 = (bf16[2,64,1024]{2,1,0:T(8,128)(2,1)}, bf16[2,64,1024]{2,1,0:T(8,128)(2,1)S(1)}, u32[]{:S(2)}, u32[]{:S(2)}) collective-permute-start(bf16[2,64,1024]{2,1,0:T(8,128)(2,1)} %get-tuple-element.138.refs_1_), channel_id=1, source_target_pairs={{0,4},{4,0},{1,5},{5,1},{2,6},{6,2},{3,7},{7,3},{8,12},{12,8},{9,1... | collective-permute-start | bytes 786440 | tf_op jit(solution)/shard_map/ppermute | solution.py:743
  224.6 7.4 %collective-permute-start.22 = (bf16[64,1024]{1,0:T(8,128)(2,1)S(1)}, bf16[64,1024]{1,0:T(8,128)(2,1)S(1)}, u32[]{:S(2)}, u32[]{:S(2)}) collective-permute-start(bf16[64,1024]{1,0:T(8,128)(2,1)S(1)} %get-tuple-element.130.refs_2_), channel_id=1, source_target_pairs={{0,3},{1,2},{2,1},{3,0},{4,7},{5,6},{6,5},{7,4},{8,11},{9,10},{10,... | collective-permute-start | bytes 393224 | tf_op jit(solution)/shard_map/ppermute | solution.py:730
  226.3 5.7 %collective-permute-start.21 = (bf16[64,1024]{1,0:T(8,128)(2,1)S(1)}, bf16[64,1024]{1,0:T(8,128)(2,1)S(1)}, u32[]{:S(2)}, u32[]{:S(2)}) collective-permute-start(bf16[64,1024]{1,0:T(8,128)(2,1)S(1)} %get-tuple-element.130.refs_2_), channel_id=1, source_target_pairs={{0,2},{1,3},{2,0},{3,1},{4,6},{5,7},{6,4},{7,5},{8,10},{9,11},{10,... | collective-permute-start | bytes 393224 | tf_op jit(solution)/shard_map/ppermute | solution.py:730
  227.2 5.1 %collective-permute-start.20 = (bf16[64,1024]{1,0:T(8,128)(2,1)S(1)}, bf16[64,1024]{1,0:T(8,128)(2,1)S(1)}, u32[]{:S(2)}, u32[]{:S(2)}) collective-permute-start(bf16[64,1024]{1,0:T(8,128)(2,1)S(1)} %get-tuple-element.130.refs_2_), channel_id=1, source_target_pairs={{0,1},{1,0},{2,3},{3,2},{4,5},{5,4},{6,7},{7,6},{8,9},{9,8},{10,11... | collective-permute-start | bytes 393224 | tf_op jit(solution)/shard_map/ppermute | solution.py:730
  236.1 29.7 %all-to-all-start.5 = ((bf16[16,128,512]{2,1,0:T(8,128)(2,1)}), bf16[16,128,512]{2,1,0:T(8,128)(2,1)}, u32[]{:S(2)}, u32[]{:S(2)}) async-start(bf16[16,128,512]{2,1,0:T(8,128)(2,1)} %get-tuple-element.145), calls=%async_computation.5 | async-start | bytes 4194304 | tf_op jit(solution)/shard_map/all_to_all | solution.py:735
  240.6 5.1 %collective-permute-start.27 = (bf16[64,1024]{1,0:T(8,128)(2,1)S(1)}, bf16[64,1024]{1,0:T(8,128)(2,1)S(1)}, u32[]{:S(2)}, u32[]{:S(2)}) collective-permute-start(bf16[64,1024]{1,0:T(8,128)(2,1)S(1)} %get-tuple-element.140.refs_2_), channel_id=1, source_target_pairs={{0,3},{1,2},{2,1},{3,0},{4,7},{5,6},{6,5},{7,4},{8,11},{9,10},{10,... | collective-permute-start | bytes 393224 | tf_op jit(solution)/shard_map/ppermute | solution.py:730
  242.2 5.3 %collective-permute-start.26 = (bf16[64,1024]{1,0:T(8,128)(2,1)S(1)}, bf16[64,1024]{1,0:T(8,128)(2,1)S(1)}, u32[]{:S(2)}, u32[]{:S(2)}) collective-permute-start(bf16[64,1024]{1,0:T(8,128)(2,1)S(1)} %get-tuple-element.140.refs_2_), channel_id=1, source_target_pairs={{0,2},{1,3},{2,0},{3,1},{4,6},{5,7},{6,4},{7,5},{8,10},{9,11},{10,... | collective-permute-start | bytes 393224 | tf_op jit(solution)/shard_map/ppermute | solution.py:730
  243.7 4.3 %collective-permute-start.25 = (bf16[64,1024]{1,0:T(8,128)(2,1)S(1)}, bf16[64,1024]{1,0:T(8,128)(2,1)S(1)}, u32[]{:S(2)}, u32[]{:S(2)}) collective-permute-start(bf16[64,1024]{1,0:T(8,128)(2,1)S(1)} %get-tuple-element.140.refs_2_), channel_id=1, source_target_pairs={{0,1},{1,0},{2,3},{3,2},{4,5},{5,4},{6,7},{7,6},{8,9},{9,8},{10,11... | collective-permute-start | bytes 393224 | tf_op jit(solution)/shard_map/ppermute | solution.py:730
  257.7 15.2 %collective-permute-start.28 = (bf16[8,2,128,512]{3,2,1,0:T(8,128)(2,1)}, bf16[8,2,128,512]{3,2,1,0:T(8,128)(2,1)}, u32[]{:S(2)}, u32[]{:S(2)}) collective-permute-start(bf16[8,2,128,512]{3,2,1,0:T(8,128)(2,1)} %get-tuple-element.152), channel_id=1, source_target_pairs={{0,64},{64,0},{1,65},{65,1},{2,66},{66,2},{3,67},{67,3},{4,68},{68... | collective-permute-start | bytes 6291464 | tf_op jit(solution)/shard_map/ppermute | solution.py:726
  264.7 8.1 %collective-permute-start.29 = (bf16[8,2,128,256]{3,2,1,0:T(8,128)(2,1)}, bf16[8,2,128,256]{3,2,1,0:T(8,128)(2,1)}, u32[]{:S(2)}, u32[]{:S(2)}) collective-permute-start(bf16[8,2,128,256]{3,2,1,0:T(8,128)(2,1)} %get-tuple-element.158), channel_id=1, source_target_pairs={{0,64},{64,0},{1,65},{65,1},{2,66},{66,2},{3,67},{67,3},{4,68},{68... | collective-permute-start | bytes 3145736 | tf_op jit(solution)/shard_map/ppermute | solution.py:726
  267.0 18.6 %all-to-all-start.6 = ((bf16[16,64,512]{2,1,0:T(8,128)(2,1)}), bf16[16,64,512]{2,1,0:T(8,128)(2,1)}, u32[]{:S(2)}, u32[]{:S(2)}) async-start(bf16[16,64,512]{2,1,0:T(8,128)(2,1)} %get-tuple-element.146), calls=%async_computation.6 | async-start | bytes 2097152 | tf_op jit(solution)/shard_map/all_to_all | solution.py:735
  288.5 15.1 %copy-start.2 = (bf16[2,64,1024]{2,1,0:T(8,128)(2,1)S(1)}, bf16[2,64,1024]{2,1,0:T(8,128)(2,1)}, u32[]{:S(2)}) copy-start(bf16[2,64,1024]{2,1,0:T(8,128)(2,1)} %get-tuple-element.138.refs_1_) | copy-start | bytes 786436
  288.5 42.2 %all-to-all-start.7 = ((bf16[16,128,768]{2,1,0:T(8,128)(2,1)}), bf16[16,128,768]{2,1,0:T(8,128)(2,1)}, u32[]{:S(2)}, u32[]{:S(2)}) async-start(bf16[16,128,768]{2,1,0:T(8,128)(2,1)} %get-tuple-element.176), calls=%async_computation.7 | async-start | bytes 6291456 | tf_op jit(solution)/shard_map/all_to_all | solution.py:735
  296.6 13.2 %collective-permute-start.33 = (bf16[8,2,128,256]{3,2,1,0:T(8,128)(2,1)S(1)}, bf16[8,2,128,256]{3,2,1,0:T(8,128)(2,1)S(1)}, u32[]{:S(2)}, u32[]{:S(2)}) collective-permute-start(bf16[8,2,128,256]{3,2,1,0:T(8,128)(2,1)S(1)} %get-tuple-element.165), channel_id=1, source_target_pairs={{0,64},{64,0},{1,65},{65,1},{2,66},{66,2},{3,67},{67,3},{4,68},{68... | collective-permute-start | bytes 3145736 | tf_op jit(solution)/shard_map/ppermute | solution.py:726
  300.3 9.0 %collective-permute-start.32 = (bf16[64,1024]{1,0:T(8,128)(2,1)S(1)}, bf16[64,1024]{1,0:T(8,128)(2,1)S(1)}, u32[]{:S(2)}, u32[]{:S(2)}) collective-permute-start(bf16[64,1024]{1,0:T(8,128)(2,1)S(1)} %get-tuple-element.159.refs_4_), channel_id=1, source_target_pairs={{0,3},{1,2},{2,1},{3,0},{4,7},{5,6},{6,5},{7,4},{8,11},{9,10},{10,... | collective-permute-start | bytes 393224 | tf_op jit(solution)/shard_map/ppermute | solution.py:730
  301.9 7.4 %collective-permute-start.31 = (bf16[64,1024]{1,0:T(8,128)(2,1)S(1)}, bf16[64,1024]{1,0:T(8,128)(2,1)S(1)}, u32[]{:S(2)}, u32[]{:S(2)}) collective-permute-start(bf16[64,1024]{1,0:T(8,128)(2,1)S(1)} %get-tuple-element.159.refs_4_), channel_id=1, source_target_pairs={{0,2},{1,3},{2,0},{3,1},{4,6},{5,7},{6,4},{7,5},{8,10},{9,11},{10,... | collective-permute-start | bytes 393224 | tf_op jit(solution)/shard_map/ppermute | solution.py:730
  303.1 6.7 %collective-permute-start.30 = (bf16[64,1024]{1,0:T(8,128)(2,1)S(1)}, bf16[64,1024]{1,0:T(8,128)(2,1)S(1)}, u32[]{:S(2)}, u32[]{:S(2)}) collective-permute-start(bf16[64,1024]{1,0:T(8,128)(2,1)S(1)} %get-tuple-element.159.refs_4_), channel_id=1, source_target_pairs={{0,1},{1,0},{2,3},{3,2},{4,5},{5,4},{6,7},{7,6},{8,9},{9,8},{10,11... | collective-permute-start | bytes 393224 | tf_op jit(solution)/shard_map/ppermute | solution.py:730
  330.7 19.2 %all-to-all-start.8 = ((bf16[16,144,256]{2,1,0:T(8,128)(2,1)}), bf16[16,144,256]{2,1,0:T(8,128)(2,1)S(1)}, u32[]{:S(2)}, u32[]{:S(2)}) async-start(bf16[16,144,256]{2,1,0:T(8,128)(2,1)} %get-tuple-element.180), calls=%async_computation.8 | async-start | bytes 2359296 | tf_op jit(solution)/shard_map/all_to_all | solution.py:735
  336.9 5.2 %collective-permute-start.34 = (bf16[64,1024]{1,0:T(8,128)(2,1)S(1)}, bf16[64,1024]{1,0:T(8,128)(2,1)S(1)}, u32[]{:S(2)}, u32[]{:S(2)}) collective-permute-start(bf16[64,1024]{1,0:T(8,128)(2,1)S(1)} %get-tuple-element.175), channel_id=1, source_target_pairs={{0,64},{64,0},{1,65},{65,1},{2,66},{66,2},{3,67},{67,3},{4,68},{68... | collective-permute-start | bytes 393224 | tf_op jit(solution)/shard_map/ppermute | solution.py:726
  342.1 15.8 %collective-permute-start.35 = (bf16[2,64,1024]{2,1,0:T(8,128)(2,1)S(1)}, bf16[2,64,1024]{2,1,0:T(8,128)(2,1)S(1)}, u32[]{:S(2)}, u32[]{:S(2)}) collective-permute-start(bf16[2,64,1024]{2,1,0:T(8,128)(2,1)S(1)} %shard_map.218.refs_1_), channel_id=1, source_target_pairs={{0,4},{4,0},{1,5},{5,1},{2,6},{6,2},{3,7},{7,3},{8,12},{12,8},{9,1... | collective-permute-start | bytes 786440 | tf_op jit(solution)/shard_map/ppermute | solution.py:743
  345.3 14.8 %copy-start.1 = (bf16[2,1,128,1024]{3,2,1,0:T(8,128)(2,1)S(1)}, bf16[2,1,128,1024]{3,2,1,0:T(8,128)(2,1)}, u32[]{:S(2)}) copy-start(bf16[2,1,128,1024]{3,2,1,0:T(8,128)(2,1)} %param.11) | copy-start | bytes 1572868
  348.6 10.4 %collective-permute-start.36 = (f32[128,512]{1,0:T(8,128)S(1)}, f32[128,512]{1,0:T(8,128)S(1)}, u32[]{:S(2)}, u32[]{:S(2)}) collective-permute-start(f32[128,512]{1,0:T(8,128)S(1)} %get-tuple-element.179), channel_id=1, source_target_pairs={{0,64},{64,0},{1,65},{65,1},{2,66},{66,2},{3,67},{67,3},{4,68},{68... | collective-permute-start | bytes 786440 | tf_op jit(solution)/shard_map/ppermute | solution.py:726
  350.0 8.9 %collective-permute-start.37 = (f32[136,256]{1,0:T(8,128)S(1)}, f32[136,256]{1,0:T(8,128)S(1)}, u32[]{:S(2)}, u32[]{:S(2)}) collective-permute-start(f32[136,256]{1,0:T(8,128)S(1)} %get-tuple-element.183), channel_id=1, source_target_pairs={{0,64},{64,0},{1,65},{65,1},{2,66},{66,2},{3,67},{67,3},{4,68},{68... | collective-permute-start | bytes 417800 | tf_op jit(solution)/shard_map/ppermute | solution.py:726
